TPU v7x, 32 devices: a whole 2x2x4 slice. The times are simulated.
32 devices in a mesh: section: 2 (over core), ctx: 4 (over z), dp: 4 (over y, x).
Axes of the slice: x: 2, y: 2, z: 4, core: 2. Of those that a mesh axis runs over, the one named last changes fastest.
Arguments:
- tokens: bfloat16 [8, 1024, 768], P('dp', 'ctx'), may hold values from -6 to 6
- seg_ids: int32 [8, 1024], P('dp'), may hold values from 0 to 15, as said below
- query_key_value_weight: bfloat16 [2, 768, 2304], P('section', 'dp'), may hold values from -0.21875 to 0.21875
- output_weight: bfloat16 [2, 768, 768], P('section', 'dp'), may hold values from -1.75 to 1.75
- gate_weight: bfloat16 [2, 768, 3072], P('section', 'dp'), may hold values from -0.21875 to 0.21875
- up_weight: bfloat16 [2, 768, 3072], P('section', 'dp'), may hold values from -0.21875 to 0.21875
- down_weight: bfloat16 [2, 3072, 768], P('section', 'dp'), may hold values from -0.109375 to 0.109375
- norm1_gain: bfloat16 [2, 768], P('section', 'dp'), may hold values from 0.5 to 1.5
- norm1_bias: bfloat16 [2, 768], P('section', 'dp'), may hold values from -1.5 to 1.5
- norm2_gain: bfloat16 [2, 768], P('section', 'dp'), may hold values from 0.5 to 1.5
- norm2_bias: bfloat16 [2, 768], P('section', 'dp'), may hold values from -1.5 to 1.5
- cotangent: bfloat16 [8, 1024, 768], P('dp', 'ctx'), may hold values from -6 to 6
Outputs:
- section_outputs: bfloat16 [2, 8, 1024, 768], P('section', 'dp', 'ctx')
- input_grads: float32 [2, 8, 1024, 768], P('section', 'dp', 'ctx')
- grad_qkv: float32 [2, 768, 2304], P('section', 'dp')
- grad_out: float32 [2, 768, 768], P('section', 'dp')
- grad_gate: float32 [2, 768, 3072], P('section', 'dp')
- grad_up: float32 [2, 768, 3072], P('section', 'dp')
- grad_down: float32 [2, 3072, 768], P('section', 'dp')
- grad_norm1_gain: float32 [2, 768], P('section', 'dp')
- grad_norm1_bias: float32 [2, 768], P('section', 'dp')
- grad_norm2_gain: float32 [2, 768], P('section', 'dp')
- grad_norm2_bias: float32 [2, 768], P('section', 'dp')
Inputs may be any that keep to these rules, and one draw needn't show every extreme that they name: `seg_ids`: in each sequence the ids start at 0 and rise by one where a document starts; documents hold 64 to 512 tokens, the last one cut by the sequence's end; of the 2 sequences of each index of dp, one is a single document, and in every draw one sequence is cut into 16 documents of 64 tokens.
All inputs are finite; a program needn't handle non-finite values.
Results may differ from a plain program's by a relative error of at most 0.022.
Values may be sent and summed in bfloat16 or wider, within the bound.
No kernel may reach another device: no remote copies, remote signals or barrier semaphores. Data moves between devices by JAX's collectives and lax.ppermute only.
A program may use at most 320 MiB of HBM per device.

v0:
```python
import jax
import jax.numpy as jnp
from jax import lax
from jax.sharding import PartitionSpec as P

HEAD = 64
MICRO = 2


EPS = 1e-05
NEG = -1e30


def passed_along(value, axis, steps):
    count = lax.axis_size(axis)
    first, last = (max(0, -steps), min(count, count - steps))
    return lax.ppermute(value, axis, [(source, source + steps) for source in range(first, last)])


def for_sending(array):
    return jax.tree.map(lambda a: a.astype(jnp.bfloat16) if a.dtype == jnp.float32 else a, array)


def positions(seg_ids):
    places = lax.broadcasted_iota(jnp.int32, seg_ids.shape, 1)
    begins = jnp.concatenate(
        [jnp.ones_like(seg_ids[:, :1]), (seg_ids[:, 1:] != seg_ids[:, :-1]).astype(jnp.int32)],
        axis=1,
    )
    return places - lax.cummax(places * begins, axis=1)


def rope_tables(places, half_dim):
    spread = 1000.0 ** (-2.0 * jnp.arange(half_dim, dtype=jnp.float32) / (2 * half_dim))
    angles = places.astype(jnp.float32)[..., None] * spread
    return (jnp.cos(angles), jnp.sin(angles))


def rotate(values, cosine, sine_table):
    half_dim = values.shape[-1] // 2
    former, latter = (values[..., :half_dim], values[..., half_dim:])
    cosine, sine_table = (cosine[..., None, :], sine_table[..., None, :])
    return jnp.concatenate(
        [former * cosine - latter * sine_table, latter * cosine + former * sine_table], axis=-1
    )


def unrotate(values, cosine, sine_table):
    half_dim = values.shape[-1] // 2
    former, latter = (values[..., :half_dim], values[..., half_dim:])
    cosine, sine_table = (cosine[..., None, :], sine_table[..., None, :])
    return jnp.concatenate(
        [former * cosine + latter * sine_table, latter * cosine - former * sine_table], axis=-1
    )


def norm_parts(resid, gain, bias):
    centred = resid - jnp.mean(resid, axis=-1, keepdims=True)
    scaling = lax.rsqrt(jnp.mean(centred * centred, axis=-1, keepdims=True) + EPS)
    unit_rows = centred * scaling
    return (unit_rows * gain + bias, unit_rows, scaling)


def norm_back(incoming, unit_rows, scaling, gain):
    scaled = incoming * gain
    inner = (
        scaled
        - jnp.mean(scaled, axis=-1, keepdims=True)
        - unit_rows * jnp.mean(scaled * unit_rows, axis=-1, keepdims=True)
    )
    return (
        scaling * inner,
        jnp.sum(incoming * unit_rows, axis=(0, 1)),
        jnp.sum(incoming, axis=(0, 1)),
    )


def masked_scores(queries, all_keys, seg_rows, seg_keys):
    row_count, model_width = queries.shape
    head_count = model_width // HEAD
    scores = jnp.einsum(
        "qhd,khd->hqk",
        queries.reshape(row_count, head_count, HEAD),
        all_keys.reshape(all_keys.shape[0], head_count, HEAD),
        preferred_element_type=jnp.float32,
    ) * HEAD ** (-0.5)
    return jnp.where((seg_rows[:, None] == seg_keys[None, :])[None], scores, NEG)


def attend(operands):
    queries, all_keys, all_values, seg_rows, seg_keys = operands
    row_count, model_width = queries.shape
    head_count = model_width // HEAD
    scores = masked_scores(queries, all_keys, seg_rows, seg_keys)
    row_max = jnp.max(scores, axis=-1, keepdims=True)
    exponent = jnp.exp(scores - row_max)
    row_sum = jnp.sum(exponent, axis=-1, keepdims=True)
    probs_low = (exponent / row_sum).astype(jnp.bfloat16)
    result = jnp.einsum(
        "hqk,khd->qhd",
        probs_low,
        all_values.reshape(all_values.shape[0], head_count, HEAD),
        preferred_element_type=jnp.float32,
    )
    return (result.reshape(row_count, model_width), (row_max + jnp.log(row_sum))[..., 0])


def attend_back(operands):
    queries, all_keys, all_values, seg_rows, seg_keys, log_sum, incoming = operands
    row_count, model_width = queries.shape
    head_count = model_width // HEAD
    key_count = all_keys.shape[0]
    probs = jnp.exp(masked_scores(queries, all_keys, seg_rows, seg_keys) - log_sum[..., None])
    heads_in = incoming.reshape(row_count, head_count, HEAD)
    dprobs = jnp.einsum(
        "qhd,khd->hqk",
        heads_in,
        all_values.reshape(key_count, head_count, HEAD),
        preferred_element_type=jnp.float32,
    )
    dscores = (probs * (dprobs - jnp.sum(probs * dprobs, axis=-1, keepdims=True))).astype(
        jnp.bfloat16
    )
    dquery = jnp.einsum(
        "hqk,khd->qhd",
        dscores,
        all_keys.reshape(key_count, head_count, HEAD),
        preferred_element_type=jnp.float32,
    ) * HEAD ** (-0.5)
    dkeys_part = jnp.einsum(
        "hqk,qhd->khd",
        dscores,
        queries.reshape(row_count, head_count, HEAD),
        preferred_element_type=jnp.float32,
    ) * HEAD ** (-0.5)
    dvalue = jnp.einsum(
        "hqk,qhd->khd", probs.astype(jnp.bfloat16), heads_in, preferred_element_type=jnp.float32
    )
    return (
        dquery.reshape(row_count, model_width),
        dkeys_part.reshape(key_count, model_width),
        dvalue.reshape(key_count, model_width),
    )


def layer_forward(hidden_state, weights_full, seg_rows, seg_keys, cosine, sine_table):
    query_key_value_weight, output_weight, gate_weight, up_weight, down_weight, norm_params = (
        weights_full
    )
    model_width = hidden_state.shape[-1]
    shaped = hidden_state.shape[:2] + (model_width // HEAD, HEAD)
    mixed_query_key_value = jnp.einsum(
        "bld,de->ble", hidden_state, query_key_value_weight, preferred_element_type=jnp.float32
    )
    queries = (
        rotate(mixed_query_key_value[..., :model_width].reshape(shaped), cosine, sine_table)
        .reshape(hidden_state.shape)
        .astype(jnp.bfloat16)
    )
    key_rows = (
        rotate(
            mixed_query_key_value[..., model_width : 2 * model_width].reshape(shaped),
            cosine,
            sine_table,
        )
        .reshape(hidden_state.shape)
        .astype(jnp.bfloat16)
    )
    value_rows = mixed_query_key_value[..., 2 * model_width :].astype(jnp.bfloat16)
    all_keys, all_values = (
        lax.all_gather(key_rows, "ctx", axis=1, tiled=True),
        lax.all_gather(value_rows, "ctx", axis=1, tiled=True),
    )
    attention_output, log_sum = lax.map(attend, (queries, all_keys, all_values, seg_rows, seg_keys))
    attention_output = attention_output.astype(jnp.bfloat16)
    residual_first = hidden_state.astype(jnp.float32) + jnp.einsum(
        "bld,de->ble", attention_output, output_weight, preferred_element_type=jnp.float32
    )
    normalized_rows, unit_one, scale_one = norm_parts(
        residual_first, norm_params[0], norm_params[1]
    )
    normalized_lowered = normalized_rows.astype(jnp.bfloat16)
    gate_projected = jnp.einsum(
        "bld,df->blf", normalized_lowered, gate_weight, preferred_element_type=jnp.float32
    )
    up_projected = jnp.einsum(
        "bld,df->blf", normalized_lowered, up_weight, preferred_element_type=jnp.float32
    )
    middle_state = (gate_projected * jax.nn.sigmoid(gate_projected) * up_projected).astype(
        jnp.bfloat16
    )
    residual_second = normalized_rows + jnp.einsum(
        "blf,fd->bld", middle_state, down_weight, preferred_element_type=jnp.float32
    )
    output, unit_two, scale_two = norm_parts(residual_second, norm_params[2], norm_params[3])
    extra = (all_keys, all_values)
    kept = (
        hidden_state,
        queries,
        key_rows,
        value_rows,
        log_sum,
        attention_output,
        unit_one,
        scale_one,
        gate_projected,
        up_projected,
        unit_two,
        scale_two,
    ) + extra
    return (output, kept)


def layer_backward(incoming, kept, weights_full, seg_rows, seg_keys, cosine, sine_table):
    query_key_value_weight, output_weight, gate_weight, up_weight, down_weight, norm_params = (
        weights_full
    )
    (
        hidden_state,
        queries,
        key_rows,
        value_rows,
        log_sum,
        attention_output,
        unit_one,
        scale_one,
        gate_projected,
        up_projected,
        unit_two,
        scale_two,
    ) = kept[:12]
    all_keys, all_values = (kept[12], kept[13])
    dresid_two, dgain_two, dbias_two = norm_back(incoming, unit_two, scale_two, norm_params[2])
    normalized_lowered = (unit_one * norm_params[0] + norm_params[1]).astype(jnp.bfloat16)
    sigmoid_gate = jax.nn.sigmoid(gate_projected)
    swish_gate = gate_projected * sigmoid_gate
    middle_state = (swish_gate * up_projected).astype(jnp.bfloat16)
    dout_two = dresid_two.astype(jnp.bfloat16)
    grad_down = jnp.einsum(
        "blf,bld->fd", middle_state, dout_two, preferred_element_type=jnp.float32
    )
    dmiddle = jnp.einsum("bld,fd->blf", dout_two, down_weight, preferred_element_type=jnp.float32)
    dgate_proj = (
        dmiddle * up_projected * sigmoid_gate * (1.0 + gate_projected * (1.0 - sigmoid_gate))
    ).astype(jnp.bfloat16)
    dup_proj = (dmiddle * swish_gate).astype(jnp.bfloat16)
    grad_gate = jnp.einsum(
        "bld,blf->df", normalized_lowered, dgate_proj, preferred_element_type=jnp.float32
    )
    grad_up = jnp.einsum(
        "bld,blf->df", normalized_lowered, dup_proj, preferred_element_type=jnp.float32
    )
    dnormed = (
        dresid_two
        + jnp.einsum("blf,df->bld", dgate_proj, gate_weight, preferred_element_type=jnp.float32)
        + jnp.einsum("blf,df->bld", dup_proj, up_weight, preferred_element_type=jnp.float32)
    )
    dresid_one, dgain_one, dbias_one = norm_back(dnormed, unit_one, scale_one, norm_params[0])
    dattn_out = dresid_one.astype(jnp.bfloat16)
    grad_out = jnp.einsum(
        "ble,bld->ed", attention_output, dattn_out, preferred_element_type=jnp.float32
    )
    dattended = jnp.einsum(
        "bld,ed->ble", dattn_out, output_weight, preferred_element_type=jnp.float32
    ).astype(jnp.bfloat16)
    dqueries, dkeys_all, dvalues_all = lax.map(
        attend_back, (queries, all_keys, all_values, seg_rows, seg_keys, log_sum, dattended)
    )
    dkey_rows, dvalue_rows = (
        lax.psum_scatter(
            dkeys_all.astype(jnp.bfloat16), "ctx", scatter_dimension=1, tiled=True
        ).astype(jnp.float32),
        lax.psum_scatter(
            dvalues_all.astype(jnp.bfloat16), "ctx", scatter_dimension=1, tiled=True
        ).astype(jnp.float32),
    )
    shaped = dqueries.shape[:2] + (dqueries.shape[2] // HEAD, HEAD)
    dmixed = jnp.concatenate(
        [
            unrotate(dqueries.reshape(shaped), cosine, sine_table).reshape(dqueries.shape),
            unrotate(dkey_rows.reshape(shaped), cosine, sine_table).reshape(dqueries.shape),
            dvalue_rows,
        ],
        axis=-1,
    ).astype(jnp.bfloat16)
    grad_qkv = jnp.einsum("bld,ble->de", hidden_state, dmixed, preferred_element_type=jnp.float32)
    dhidden = dresid_one + jnp.einsum(
        "ble,de->bld", dmixed, query_key_value_weight, preferred_element_type=jnp.float32
    )
    return (
        dhidden,
        (
            grad_qkv,
            grad_out,
            grad_gate,
            grad_up,
            grad_down,
            jnp.stack([dgain_one, dbias_one, dgain_two, dbias_two]),
        ),
    )


def on_device(
    tokens,
    seg_ids,
    query_key_value_weight,
    output_weight,
    gate_weight,
    up_weight,
    down_weight,
    norm1_gain,
    norm1_bias,
    norm2_gain,
    norm2_bias,
    cotangent,
):
    leading = lax.axis_index("section") == 0
    ctx_rank = lax.axis_index("ctx")
    span_len = tokens.shape[1]
    per_micro = tokens.shape[0] // MICRO
    seg_near = lax.dynamic_slice_in_dim(seg_ids, ctx_rank * span_len, span_len, 1)
    cosine_rows, sine_rows = rope_tables(
        lax.dynamic_slice_in_dim(positions(seg_ids), ctx_rank * span_len, span_len, 1), HEAD // 2
    )
    shards = (
        query_key_value_weight[0],
        output_weight[0],
        gate_weight[0],
        up_weight[0],
        down_weight[0],
        jnp.stack([norm1_gain[0], norm1_bias[0], norm2_gain[0], norm2_bias[0]]),
    )
    gathered = (
        lax.all_gather(shards[0], "dp", axis=0, tiled=True),
        lax.all_gather(shards[1], "dp", axis=0, tiled=True),
        lax.all_gather(shards[2], "dp", axis=0, tiled=True),
        lax.all_gather(shards[3], "dp", axis=0, tiled=True),
        lax.all_gather(shards[4], "dp", axis=0, tiled=True),
        lax.all_gather(shards[5], "dp", axis=1, tiled=True),
    )
    weights_full = gathered[:5] + (gathered[5].astype(jnp.float32),)

    def select(array, micro_idx):
        return lax.dynamic_slice_in_dim(array, micro_idx * per_micro, per_micro, 0)

    delay_fwd = jnp.where(leading, 0, 1)
    received = jnp.zeros((per_micro,) + tokens.shape[1:], jnp.bfloat16)
    outputs = []
    stored = []
    for tick_no in range(MICRO + 1):
        micro_idx = jnp.clip(tick_no - delay_fwd, 0, MICRO - 1)
        hidden_state = jnp.where(leading, select(tokens, micro_idx), received)
        output, kept = layer_forward(
            hidden_state,
            weights_full,
            select(seg_near, micro_idx),
            select(seg_ids, micro_idx),
            select(cosine_rows, micro_idx),
            select(sine_rows, micro_idx),
        )
        sent_rows = output.astype(jnp.bfloat16)
        outputs.append(sent_rows)
        stored.append(kept)
        if tick_no < MICRO:
            received = passed_along(sent_rows, "section", 1)
    gathered = (
        lax.all_gather(shards[0], "dp", axis=0, tiled=True),
        lax.all_gather(shards[1], "dp", axis=0, tiled=True),
        lax.all_gather(shards[2], "dp", axis=0, tiled=True),
        lax.all_gather(shards[3], "dp", axis=0, tiled=True),
        lax.all_gather(shards[4], "dp", axis=0, tiled=True),
        lax.all_gather(shards[5], "dp", axis=1, tiled=True),
    )
    weights_full = gathered[:5] + (gathered[5].astype(jnp.float32),)
    returned = jnp.zeros_like(received)
    totals = None
    input_parts = []
    for tick_no in range(MICRO + 1):
        micro_idx = jnp.clip(tick_no - 1 + delay_fwd, 0, MICRO - 1)
        active = jnp.where(leading, tick_no >= 1, tick_no < MICRO)
        incoming = jnp.where(
            leading, returned.astype(jnp.float32), select(cotangent, micro_idx).astype(jnp.float32)
        )
        incoming = jnp.where(active, incoming, 0.0)
        kept = jax.tree.map(
            lambda early, later: jnp.where(leading, early, later),
            stored[max(tick_no - 1, 0)],
            stored[min(tick_no + 1, MICRO)],
        )
        dhidden, grad_terms = layer_backward(
            incoming,
            kept,
            weights_full,
            select(seg_near, micro_idx),
            select(seg_ids, micro_idx),
            select(cosine_rows, micro_idx),
            select(sine_rows, micro_idx),
        )
        totals = (
            grad_terms
            if totals is None
            else tuple((early + later for early, later in zip(totals, grad_terms)))
        )
        input_parts.append(dhidden)
        if tick_no < MICRO:
            returned = passed_along(dhidden.astype(jnp.bfloat16), "section", -1)
    summed = (
        lax.psum_scatter(
            totals[0].astype(jnp.bfloat16), "dp", scatter_dimension=0, tiled=True
        ).astype(jnp.float32),
        lax.psum_scatter(
            totals[1].astype(jnp.bfloat16), "dp", scatter_dimension=0, tiled=True
        ).astype(jnp.float32),
        lax.psum_scatter(
            totals[2].astype(jnp.bfloat16), "dp", scatter_dimension=0, tiled=True
        ).astype(jnp.float32),
        lax.psum_scatter(
            totals[3].astype(jnp.bfloat16), "dp", scatter_dimension=0, tiled=True
        ).astype(jnp.float32),
        lax.psum_scatter(
            totals[4].astype(jnp.bfloat16), "dp", scatter_dimension=0, tiled=True
        ).astype(jnp.float32),
        lax.psum_scatter(
            totals[5].astype(jnp.bfloat16), "dp", scatter_dimension=1, tiled=True
        ).astype(jnp.float32),
    )
    summed = jax.tree.map(
        lambda part: part.astype(jnp.float32), lax.psum(for_sending(summed), "ctx")
    )
    last_rows = jnp.concatenate(
        [jnp.where(leading, outputs[micro_no], outputs[micro_no + 1]) for micro_no in range(MICRO)],
        axis=0,
    )
    input_grads = jnp.concatenate(
        [
            jnp.where(leading, input_parts[micro_no + 1], input_parts[micro_no])
            for micro_no in range(MICRO)
        ],
        axis=0,
    )
    norm_grads = summed[5]
    return (
        last_rows[None],
        input_grads[None],
        summed[0][None],
        summed[1][None],
        summed[2][None],
        summed[3][None],
        summed[4][None],
        norm_grads[0][None],
        norm_grads[1][None],
        norm_grads[2][None],
        norm_grads[3][None],
    )


def solution(mesh):
    placed = (
        P("dp", "ctx", None),
        P("dp", None),
        P("section", "dp", None),
        P("section", "dp", None),
        P("section", "dp", None),
        P("section", "dp", None),
        P("section", "dp", None),
        P("section", "dp"),
        P("section", "dp"),
        P("section", "dp"),
        P("section", "dp"),
        P("dp", "ctx", None),
    )
    return jax.shard_map(
        on_device,
        mesh=mesh,
        in_specs=placed,
        out_specs=(
            P("section", "dp", "ctx", None),
            P("section", "dp", "ctx", None),
            P("section", "dp", None),
            P("section", "dp", None),
            P("section", "dp", None),
            P("section", "dp", None),
            P("section", "dp", None),
            P("section", "dp"),
            P("section", "dp"),
            P("section", "dp"),
            P("section", "dp"),
        ),
        check_vma=False,
    )
```

profile of v0, /device:TPU:0, one launch (start us, length us, event | category | flops | bytes accessed | tf_op | source)
XLA Modules:
  0.0 1450.1 jit_solution(13203646358477306205)
XLA Ops:
  8.0 51.9 %all-gather.30.cloned.1.call-done = bf16[1,768,2304]{2,1,0:T(8,128)(2,1)} async-done(((bf16[1,192,2304]{2,1,0:T(8,128)(2,1)}), bf16[1,768,2304]{2,1,0:T(8,128)(2,1)}) %all-gather.30.cloned.1.call-update) | async-done | bytes 3538960 | tf_op jit(solution)/shard_map/all_gather | solution.py:334
  83.3 17.8 %all-gather.18.cloned.1.call-done = bf16[1,1024,768]{2,1,0:T(8,128)(2,1)} async-done(((bf16[1,256,768]{2,1,0:T(8,128)(2,1)}), bf16[1,1024,768]{2,1,0:T(8,128)(2,1)}) %all-gather.18.cloned.1.call-update) | async-done | bytes 1572880 | tf_op jit(solution)/shard_map/all_gather | solution.py:172
  103.7 35.6 %all-gather.20.cloned.1.call-done = bf16[1,1024,768]{2,1,0:T(8,128)(2,1)} async-done(((bf16[1,256,768]{2,1,0:T(8,128)(2,1)}), bf16[1,1024,768]{2,1,0:T(8,128)(2,1)}) %all-gather.20.cloned.1.call-update) | async-done | bytes 1572880 | tf_op jit(solution)/shard_map/all_gather | solution.py:171
  151.0 16.6 %all-gather.32.cloned.1.call-done = bf16[1,768,768]{2,1,0:T(8,128)(2,1)} async-done(((bf16[1,192,768]{2,1,0:T(8,128)(2,1)}), bf16[1,768,768]{2,1,0:T(8,128)(2,1)}) %all-gather.32.cloned.1.call-update) | async-done | bytes 1179664 | tf_op jit(solution)/shard_map/all_gather | solution.py:335
  169.7 56.6 %all-gather.36.cloned.1.call-done = bf16[1,768,3072]{2,1,0:T(8,128)(2,1)} async-done(((bf16[1,192,3072]{2,1,0:T(8,128)(2,1)}), bf16[1,768,3072]{2,1,0:T(8,128)(2,1)}) %all-gather.36.cloned.1.call-update) | async-done | bytes 4718608 | tf_op jit(solution)/shard_map/all_gather | solution.py:337
  230.4 54.7 %all-gather.34.cloned.1.call-done = bf16[1,768,3072]{2,1,0:T(8,128)(2,1)} async-done(((bf16[1,192,3072]{2,1,0:T(8,128)(2,1)}), bf16[1,768,3072]{2,1,0:T(8,128)(2,1)}) %all-gather.34.cloned.1.call-update) | async-done | bytes 4718608 | tf_op jit(solution)/shard_map/all_gather | solution.py:336
  290.9 53.2 %all-gather.38.cloned.1.call-done = bf16[1,3072,768]{2,1,0:T(8,128)(2,1)} async-done(((bf16[1,768,768]{2,1,0:T(8,128)(2,1)}), bf16[1,3072,768]{2,1,0:T(8,128)(2,1)}) %all-gather.38.cloned.1.call-update) | async-done | bytes 4718608 | tf_op jit(solution)/shard_map/all_gather | solution.py:338
  370.6 33.3 %all-gather.24.cloned.1.call-done = bf16[1,1024,768]{2,1,0:T(8,128)(2,1)} async-done(((bf16[1,256,768]{2,1,0:T(8,128)(2,1)}), bf16[1,1024,768]{2,1,0:T(8,128)(2,1)}) %all-gather.24.cloned.1.call-update) | async-done | bytes 1572880 | tf_op jit(solution)/shard_map/all_gather | solution.py:171
  419.3 22.7 %all-gather.22.cloned.1.call-done = bf16[1,1024,768]{2,1,0:T(8,128)(2,1)} async-done(((bf16[1,256,768]{2,1,0:T(8,128)(2,1)}), bf16[1,1024,768]{2,1,0:T(8,128)(2,1)}) %all-gather.22.cloned.1.call-update) | async-done | bytes 1572880 | tf_op jit(solution)/shard_map/all_gather | solution.py:172
  488.0 27.1 %all-gather.28.cloned.1.call-done = bf16[1,1024,768]{2,1,0:T(8,128)(2,1)} async-done(((bf16[1,256,768]{2,1,0:T(8,128)(2,1)}), bf16[1,1024,768]{2,1,0:T(8,128)(2,1)}) %all-gather.28.cloned.1.call-update) | async-done | bytes 1572880 | tf_op jit(solution)/shard_map/all_gather | solution.py:171
  527.7 25.6 %all-gather.26.cloned.1.call-done = bf16[1,1024,768]{2,1,0:T(8,128)(2,1)} async-done(((bf16[1,256,768]{2,1,0:T(8,128)(2,1)}), bf16[1,1024,768]{2,1,0:T(8,128)(2,1)}) %all-gather.26.cloned.1.call-update) | async-done | bytes 1572880 | tf_op jit(solution)/shard_map/all_gather | solution.py:172
  613.3 12.1 multiply_reduce_fusion.2
  674.9 33.2 %reduce-scatter.17.cloned.1.call-done = bf16[1,256,768]{1,2,0:T(8,128)(2,1)} async-done(((bf16[1,1024,768]{1,2,0:T(8,128)(2,1)}), bf16[1,256,768]{1,2,0:T(8,128)(2,1)}) %reduce-scatter.17.cloned.1.call-update) | async-done | bytes 393232 | tf_op jit(solution)/shard_map/reduce_scatter | solution.py:273
  740.8 12.3 multiply_reduce_fusion.1
  785.4 13.7 reduce-scatter.19.cloned.1.call-done
  803.2 33.0 %reduce-scatter.21.cloned.1.call-done = bf16[1,256,768]{1,2,0:T(8,128)(2,1)} async-done(((bf16[1,1024,768]{1,2,0:T(8,128)(2,1)}), bf16[1,256,768]{1,2,0:T(8,128)(2,1)}) %reduce-scatter.21.cloned.1.call-update) | async-done | bytes 393232 | tf_op jit(solution)/shard_map/reduce_scatter | solution.py:273
  873.1 12.3 multiply_reduce_fusion
  957.6 12.5 add_convert_fusion
  999.5 60.1 %reduce-scatter.31.cloned.1.call-done = bf16[192,3072]{1,0:T(8,128)(2,1)} async-done(((bf16[768,3072]{1,0:T(8,128)(2,1)}), bf16[192,3072]{1,0:T(8,128)(2,1)}) %reduce-scatter.31.cloned.1.call-update) | async-done | bytes 1179664 | tf_op jit(solution)/shard_map/reduce_scatter | solution.py:414
  1059.6 60.0 %reduce-scatter.33.cloned.1.call-done = bf16[192,3072]{1,0:T(8,128)(2,1)} async-done(((bf16[768,3072]{1,0:T(8,128)(2,1)}), bf16[192,3072]{1,0:T(8,128)(2,1)}) %reduce-scatter.33.cloned.1.call-update) | async-done | bytes 1179664 | tf_op jit(solution)/shard_map/reduce_scatter | solution.py:417
  1119.6 60.1 %reduce-scatter.35.cloned.1.call-done = bf16[768,768]{1,0:T(8,128)(2,1)} async-done(((bf16[3072,768]{1,0:T(8,128)(2,1)}), bf16[768,768]{1,0:T(8,128)(2,1)}) %reduce-scatter.35.cloned.1.call-update) | async-done | bytes 1179664 | tf_op jit(solution)/shard_map/reduce_scatter | solution.py:420
  1179.7 50.4 %reduce-scatter.27.cloned.1.call-done = bf16[192,2304]{1,0:T(8,128)(2,1)} async-done(((bf16[768,2304]{1,0:T(8,128)(2,1)}), bf16[192,2304]{1,0:T(8,128)(2,1)}) %reduce-scatter.27.cloned.1.call-update) | async-done | bytes 884752 | tf_op jit(solution)/shard_map/reduce_scatter | solution.py:408
  1233.7 23.7 %reduce-scatter.37.cloned.1.call-done = bf16[192,4]{1,0:T(8,128)(2,1)} async-done(((bf16[768,4]{1,0:T(8,128)(2,1)}), bf16[192,4]{1,0:T(8,128)(2,1)}) %reduce-scatter.37.cloned.1.call-update) | async-done | bytes 1552
  1274.7 158.7 %all-reduce.4.cloned.1.call-done = (bf16[1,192,2304]{2,1,0:T(8,128)(2,1)}, bf16[1,192,768]{2,1,0:T(8,128)(2,1)}, bf16[1,192,3072]{2,1,0:T(8,128)(2,1)}, bf16[1,192,3072]{2,1,0:T(8,128)(2,1)}, bf16[1,768,768]{2,1,0:T(8,128)(2,1)}) async-done(((bf16[1,192,2304]{2,1,0:T(8,128)(2,1)}, bf16[1,192,768]{2,1,0:T(8,128)(2,1)}, bf16[1,192,3072]{2,1,0:T(8,128)(2,1)}, bf16[1,192,3072]{2,1,0:T(8,128)(2,1)}, ...) | async-done | bytes 4718608 | tf_op jit(solution)/shard_map/psum | solution.py:428
  (764 shorter events, 494.7 us)
Async XLA Ops:
  7.2 52.7 %all-gather.30.cloned.1.call-start = ((), (), s32[]{:S(2)}) async-start(), calls=%async_computation.29 | async-start | bytes 4423680 | tf_op jit(solution)/shard_map/all_gather | solution.py:334
  7.9 93.2 %all-gather.18.cloned.1.call-start = ((), (), s32[]{:S(2)}) async-start(), calls=%async_computation.12 | async-start | bytes 1966080 | tf_op jit(solution)/shard_map/all_gather | solution.py:172
  63.9 75.4 %all-gather.20.cloned.1.call-start = ((), (), s32[]{:S(2)}) async-start(), calls=%async_computation.13 | async-start | bytes 1966080 | tf_op jit(solution)/shard_map/all_gather | solution.py:171
  70.8 96.8 %all-gather.32.cloned.1.call-start = ((), (), s32[]{:S(2)}) async-start(), calls=%async_computation.30 | async-start | bytes 1474560 | tf_op jit(solution)/shard_map/all_gather | solution.py:335
  71.4 155.0 %all-gather.36.cloned.1.call-start = ((), (), s32[]{:S(2)}) async-start(), calls=%async_computation.32 | async-start | bytes 5898240 | tf_op jit(solution)/shard_map/all_gather | solution.py:337
  72.0 213.2 %all-gather.34.cloned.1.call-start = ((), (), s32[]{:S(2)}) async-start(), calls=%async_computation.31 | async-start | bytes 5898240 | tf_op jit(solution)/shard_map/all_gather | solution.py:336
  72.6 271.5 %all-gather.38.cloned.1.call-start = ((), (), s32[]{:S(2)}) async-start(), calls=%async_computation.33 | async-start | bytes 5898240 | tf_op jit(solution)/shard_map/all_gather | solution.py:338
  73.3 330.5 %all-gather.24.cloned.1.call-start = ((), (), s32[]{:S(2)}) async-start(), calls=%async_computation.15 | async-start | bytes 1966080 | tf_op jit(solution)/shard_map/all_gather | solution.py:171
  366.5 75.4 %all-gather.22.cloned.1.call-start = ((), (), s32[]{:S(2)}) async-start(), calls=%async_computation.14 | async-start | bytes 1966080 | tf_op jit(solution)/shard_map/all_gather | solution.py:172
  368.5 146.6 %all-gather.28.cloned.1.call-start = ((), (), s32[]{:S(2)}) async-start(), calls=%async_computation.17 | async-start | bytes 1966080 | tf_op jit(solution)/shard_map/all_gather | solution.py:171
  478.7 74.5 %all-gather.26.cloned.1.call-start = ((), (), s32[]{:S(2)}) async-start(), calls=%async_computation.16 | async-start | bytes 1966080 | tf_op jit(solution)/shard_map/all_gather | solution.py:172
  482.3 188.6 %reduce-scatter.15.cloned.1.call-start = ((), (), s32[]{:S(2)}) async-start(), calls=%async_computation.18 | async-start | bytes 1966080 | tf_op jit(solution)/shard_map/reduce_scatter | solution.py:270
  636.6 71.5 %reduce-scatter.17.cloned.1.call-start = ((), (), s32[]{:S(2)}) async-start(), calls=%async_computation.19 | async-start | bytes 1966080 | tf_op jit(solution)/shard_map/reduce_scatter | solution.py:273
  645.6 153.6 %reduce-scatter.19.cloned.1.call-start = ((), (), s32[]{:S(2)}) async-start(), calls=%async_computation.20 | async-start | bytes 1966080 | tf_op jit(solution)/shard_map/reduce_scatter | solution.py:270
  764.0 72.2 %reduce-scatter.21.cloned.1.call-start = ((), (), s32[]{:S(2)}) async-start(), calls=%async_computation.21 | async-start | bytes 1966080 | tf_op jit(solution)/shard_map/reduce_scatter | solution.py:273
  773.1 208.8 %reduce-scatter.23.cloned.1.call-start = ((), (), s32[]{:S(2)}) async-start(), calls=%async_computation.22 | async-start | bytes 1966080 | tf_op jit(solution)/shard_map/reduce_scatter | solution.py:270
  896.4 87.0 %reduce-scatter.25.cloned.1.call-start = ((), (), s32[]{:S(2)}) async-start(), calls=%async_computation.23 | async-start | bytes 1966080 | tf_op jit(solution)/shard_map/reduce_scatter | solution.py:273
  905.5 94.1 %reduce-scatter.29.cloned.1.call-start = ((), (), s32[]{:S(2)}) async-start(), calls=%async_computation.25 | async-start | bytes 1474560 | tf_op jit(solution)/shard_map/reduce_scatter | solution.py:411
  909.4 150.2 %reduce-scatter.31.cloned.1.call-start = ((), (), s32[]{:S(2)}) async-start(), calls=%async_computation.26 | async-start | bytes 5898240 | tf_op jit(solution)/shard_map/reduce_scatter | solution.py:414
  925.8 193.8 %reduce-scatter.33.cloned.1.call-start = ((), (), s32[]{:S(2)}) async-start(), calls=%async_computation.27 | async-start | bytes 5898240 | tf_op jit(solution)/shard_map/reduce_scatter | solution.py:417
  941.8 237.9 %reduce-scatter.35.cloned.1.call-start = ((), (), s32[]{:S(2)}) async-start(), calls=%async_computation.28 | async-start | bytes 5898240 | tf_op jit(solution)/shard_map/reduce_scatter | solution.py:420
  970.2 259.9 %reduce-scatter.27.cloned.1.call-start = ((), (), s32[]{:S(2)}) async-start(), calls=%async_computation.24 | async-start | bytes 4423680 | tf_op jit(solution)/shard_map/reduce_scatter | solution.py:408
  992.0 265.5 %reduce-scatter.37.cloned.1.call-start = ((), (), s32[]{:S(2)}) async-start(), calls=%async_computation.34 | async-start | bytes 245760
  993.6 439.8 %all-reduce.4.cloned.1.call-start = ((), (), s32[]{:S(2)}) async-start(), calls=%async_computation.35 | async-start | bytes 9437184 | tf_op jit(solution)/shard_map/psum | solution.py:428
  (246 other events, 3479.0 us)
Sparse Core Ops, SparseCore 0:
  9.9 49.9 all-gather.29
  64.0 37.0 all-gather.17
  103.3 35.9 all-gather.19
  141.0 26.5 all-gather.31
  169.3 57.0 all-gather.35
  228.1 57.0 all-gather.33
  287.0 57.0 all-gather.37
  366.7 37.1 all-gather.23
  406.0 35.9 all-gather.21
  478.8 36.2 all-gather.27
  517.3 35.9 all-gather.25
  636.7 34.1 reduce-scatter.14
  673.7 34.2 reduce-scatter.16
  764.1 35.0 reduce-scatter.18
  801.9 34.2 reduce-scatter.20
  896.5 35.0 reduce-scatter.22
  934.3 34.2 reduce-scatter.24
  972.0 27.5 reduce-scatter.28
  1002.5 57.0 reduce-scatter.30
  1062.5 57.0 reduce-scatter.32
  1122.6 57.0 reduce-scatter.34
  1182.8 47.2 reduce-scatter.26
  1233.4 23.9 reduce-scatter.36
  1260.0 173.3 all-reduce.3
where the time goes:
time: 1460 us; the launch traced here: 1450 us
  waiting for transfers between devices  912 us (62%)
  matrix products  313 us (21%)
  other arithmetic  89.9 us (6%)
  local copies, waits for them, and re-layouts  88.6 us (6%)
  blocking collectives  20.1 us (1%)
  between operations  18.2 us (1%)
    psum x1, waiting for transfers between devices, on_device(): lax.psum(for_sending(summed), 'ctx')  159 us
    all_gather x3, waiting for transfers between devices, layer_forward(): lax.all_gather(key_rows, 'ctx', axis=1, tiled=True)  95.9 us
    reduce_scatter x3, waiting for transfers between devices, layer_backward(): lax.psum_scatter(dvalues_all.astype(jnp.bfloat16), 'ctx', scatter_dimensi...  66.2 us
    all_gather x3, waiting for transfers between devices, layer_forward(): lax.all_gather(value_rows, 'ctx', axis=1, tiled=True)  66.1 us
    reduce_scatter x1, waiting for transfers between devices, on_device(): lax.psum_scatter(totals[4].astype(jnp.bfloat16), 'dp', scatter_dimension=...  60.1 us
    reduce_scatter x1, waiting for transfers between devices, on_device(): lax.psum_scatter(totals[2].astype(jnp.bfloat16), 'dp', scatter_dimension=...  60.1 us
    reduce_scatter x1, waiting for transfers between devices, on_device(): lax.psum_scatter(totals[3].astype(jnp.bfloat16), 'dp', scatter_dimension=...  60 us
    all_gather x1, waiting for transfers between devices, on_device(): lax.all_gather(shards[3], 'dp', axis=0, tiled=True)  56.6 us
  transfers between devices with their start and end apart: 28, of which 24 were waited for; matrix products, arithmetic and copies ran while one was open for 16% of the time, Pallas kernels for 0%

commit v1 on v0

--- a/solution.py
+++ b/solution.py
@@ -300,7 +300,7 @@
     )
 
 
-def on_device(
+def relay_on_device(
     tokens,
     seg_ids,
     query_key_value_weight,
@@ -454,6 +454,268 @@
     )
 
 
+def other_core(value, pairs=((0, 1), (1, 0))):
+    return lax.ppermute(value, "section", list(pairs))
+
+
+def along_x(value):
+    return lax.ppermute(value, "dp", [(i, i ^ 1) for i in range(4)])
+
+
+def along_y(value):
+    return lax.ppermute(value, "dp", [(i, i ^ 2) for i in range(4)])
+
+
+def along_z(value):
+    return lax.ppermute(value, "ctx", [(i, i ^ 1) for i in range(4)])
+
+
+def z_swap(value):
+    pairs = [(4 + i, 4 + (i ^ 2)) for i in range(4)]
+    return lax.ppermute(value, ("section", "ctx"), pairs)
+
+
+def lowered(value):
+    return value.astype(jnp.bfloat16)
+
+
+def by_core(core, mine, theirs, axis):
+    return jnp.where(
+        core == 0,
+        jnp.concatenate([mine, theirs], axis=axis),
+        jnp.concatenate([theirs, mine], axis=axis),
+    )
+
+
+def half_of(array, which):
+    width = array.shape[-1] // 2
+    return lax.dynamic_slice_in_dim(array, which * width, width, array.ndim - 1)
+
+
+def gather_half(piece, dp_rank):
+    rows = piece.shape[0] // 2
+    from_x, from_y = along_x(piece), along_y(piece)
+    diag = jnp.concatenate([along_x(from_y[:rows]), along_y(from_x[rows:])], axis=0)
+    odd, high = (dp_rank & 1) == 1, (dp_rank & 2) == 2
+    near = jnp.where(odd, jnp.concatenate([from_x, piece]), jnp.concatenate([piece, from_x]))
+    far = jnp.where(odd, jnp.concatenate([diag, from_y]), jnp.concatenate([from_y, diag]))
+    return jnp.where(high, jnp.concatenate([far, near]), jnp.concatenate([near, far]))
+
+
+def reduce_half(partial, dp_rank, ctx_rank):
+    count = partial.shape[0] // 4
+    rows = count // 2
+
+    def part(flip, begin, size):
+        return lax.dynamic_slice_in_dim(partial, (dp_rank ^ flip) * count + begin, size, 0)
+
+    to_x, to_y = along_x(part(3, 0, rows)), along_y(part(3, rows, rows))
+    x_first, y_last = along_x(part(1, 0, rows)), along_y(part(2, rows, rows))
+    x_last = along_x(lowered(part(1, rows, rows).astype(jnp.float32) + to_y.astype(jnp.float32)))
+    y_first = along_y(lowered(part(2, 0, rows).astype(jnp.float32) + to_x.astype(jnp.float32)))
+    own = part(0, 0, count).astype(jnp.float32)
+    summed = lowered(
+        own
+        + jnp.concatenate([x_first, x_last]).astype(jnp.float32)
+        + jnp.concatenate([y_first, y_last]).astype(jnp.float32)
+    )
+    inner = lax.ppermute(summed, "ctx", [(0, 1), (3, 2)])
+    pair = lowered(summed.astype(jnp.float32) + inner.astype(jnp.float32))
+    across = lax.ppermute(pair, "ctx", [(1, 2), (2, 1)])
+    total = lowered(pair.astype(jnp.float32) + across.astype(jnp.float32))
+    outer = lax.ppermute(total, "ctx", [(1, 0), (2, 3)])
+    return jnp.where((ctx_rank == 0) | (ctx_rank == 3), outer, total)
+
+
+def forward_rows(hidden, weights, seg_rows, seg_keys, cosine, sine):
+    qkv_weight, output_weight, gate_weight, up_weight, down_weight, norm_params = weights
+    rows, width = hidden.shape
+    shaped = (rows, width // HEAD, HEAD)
+    dot = lambda a, b: jnp.dot(a, b, preferred_element_type=jnp.float32)
+    mixed = dot(hidden, qkv_weight)
+    queries = lowered(rotate(mixed[:, :width].reshape(shaped), cosine, sine).reshape(rows, width))
+    keys = lowered(
+        rotate(mixed[:, width : 2 * width].reshape(shaped), cosine, sine).reshape(rows, width)
+    )
+    own = jnp.concatenate([keys, lowered(mixed[:, 2 * width :])], axis=1)
+    from_z = along_z(own)
+    blocks = jnp.concatenate([own, other_core(own), from_z, other_core(from_z)], axis=0)
+    all_keys, all_values = blocks[:, :width], blocks[:, width:]
+    attended, log_sum = attend((queries, all_keys, all_values, seg_rows, seg_keys))
+    attended = lowered(attended)
+    resid_one = hidden.astype(jnp.float32) + dot(attended, output_weight)
+    normed, unit_one, scale_one = norm_parts(resid_one, norm_params[0], norm_params[1])
+    normed_low = lowered(normed)
+    gate_proj, up_proj = dot(normed_low, gate_weight), dot(normed_low, up_weight)
+    middle = lowered(gate_proj * jax.nn.sigmoid(gate_proj) * up_proj)
+    resid_two = normed + dot(middle, down_weight)
+    output, unit_two, scale_two = norm_parts(resid_two, norm_params[2], norm_params[3])
+    kept = (
+        hidden, queries, all_keys, all_values, log_sum, attended, unit_one, scale_one,
+        normed_low, gate_proj, up_proj, middle, unit_two, scale_two,
+    )
+    return output, kept
+
+
+def backward_rows(incoming, kept, weights, seg_rows, seg_keys, cosine, sine, core):
+    qkv_weight, output_weight, gate_weight, up_weight, down_weight, norm_params = weights
+    (
+        hidden, queries, all_keys, all_values, log_sum, attended, unit_one, scale_one,
+        normed_low, gate_proj, up_proj, middle, unit_two, scale_two,
+    ) = kept
+    rows, width = hidden.shape
+    shaped = (rows, width // HEAD, HEAD)
+    dot_t = lambda a, b: lax.dot_general(
+        a, b, (((1,), (1,)), ((), ())), preferred_element_type=jnp.float32
+    )
+
+    def weight_grad(left, right):
+        left_all = jnp.concatenate([left, other_core(left)], axis=0)
+        right_all = jnp.concatenate(
+            [half_of(right, core), other_core(half_of(right, 1 - core))], axis=0
+        )
+        return lowered(
+            lax.dot_general(
+                left_all, right_all, (((0,), (0,)), ((), ())), preferred_element_type=jnp.float32
+            )
+        )
+
+    def norm_back_rows(grad, unit, scale, gain):
+        result, dgain, dbias = norm_back(grad[None], unit[None], scale[None], gain)
+        return result[0], dgain, dbias
+
+    dresid_two, dgain_two, dbias_two = norm_back_rows(incoming, unit_two, scale_two, norm_params[2])
+    dout_two = lowered(dresid_two)
+    grad_down = weight_grad(middle, dout_two)
+    dmiddle = dot_t(dout_two, down_weight)
+    sig = jax.nn.sigmoid(gate_proj)
+    dgate = lowered(dmiddle * up_proj * sig * (1.0 + gate_proj * (1.0 - sig)))
+    dup = lowered(dmiddle * (gate_proj * sig))
+    grad_gate, grad_up = weight_grad(normed_low, dgate), weight_grad(normed_low, dup)
+    dnormed = dresid_two + dot_t(dgate, gate_weight) + dot_t(dup, up_weight)
+    dresid_one, dgain_one, dbias_one = norm_back_rows(dnormed, unit_one, scale_one, norm_params[0])
+    dattn_out = lowered(dresid_one)
+    grad_out = weight_grad(attended, dattn_out)
+    dattended = lowered(dot_t(dattn_out, output_weight))
+    dqueries, dkeys, dvalues = attend_back(
+        (queries, all_keys, all_values, seg_rows, seg_keys, log_sum, dattended)
+    )
+    parts = lowered(jnp.concatenate([dkeys, dvalues], axis=1)).reshape(4, rows, 2 * width)
+    from_core = other_core(jnp.stack([parts[1], parts[3]])).astype(jnp.float32)
+    from_z = along_z(lowered(parts[2].astype(jnp.float32) + from_core[1])).astype(jnp.float32)
+    dkv = parts[0].astype(jnp.float32) + from_core[0] + from_z
+    dmixed = lowered(
+        jnp.concatenate(
+            [
+                unrotate(dqueries.reshape(shaped), cosine, sine).reshape(rows, width),
+                unrotate(dkv[:, :width].reshape(shaped), cosine, sine).reshape(rows, width),
+                dkv[:, width:],
+            ],
+            axis=1,
+        )
+    )
+    grad_qkv = weight_grad(hidden, dmixed)
+    dhidden = dresid_one + dot_t(dmixed, qkv_weight)
+    return (
+        dhidden,
+        (grad_qkv, grad_out, grad_gate, grad_up, grad_down),
+        jnp.stack([dgain_one, dbias_one, dgain_two, dbias_two]),
+    )
+
+
+def paired_on_device(
+    tokens,
+    seg_ids,
+    query_key_value_weight,
+    output_weight,
+    gate_weight,
+    up_weight,
+    down_weight,
+    norm1_gain,
+    norm1_bias,
+    norm2_gain,
+    norm2_bias,
+    cotangent,
+):
+    core, ctx_rank, dp_rank = (lax.axis_index(a) for a in ("section", "ctx", "dp"))
+    span = tokens.shape[1]
+    sequence = ctx_rank // 2
+    block = ctx_rank ^ (2 * core)
+    pick = lambda array, index: lax.dynamic_index_in_dim(array, index, 0, keepdims=False)
+
+    def rows_of(array):
+        return jnp.where(core == 0, pick(array, sequence), z_swap(pick(array, 1 - sequence)))
+
+    seg = pick(seg_ids, sequence)
+    places = pick(positions(seg_ids), sequence)
+    seg_rows = lax.dynamic_slice_in_dim(seg, block * span, span, 0)
+    seg_keys = jnp.concatenate(
+        [lax.dynamic_slice_in_dim(seg, (block ^ flip) * span, span, 0) for flip in (0, 2, 1, 3)]
+    )
+    cosine, sine = rope_tables(lax.dynamic_slice_in_dim(places, block * span, span, 0), HEAD // 2)
+
+    shards = (query_key_value_weight, output_weight, gate_weight, up_weight, down_weight)
+    norm_shard = jnp.concatenate([norm1_gain, norm1_bias, norm2_gain, norm2_bias], axis=0)
+    norms = lax.all_gather(norm_shard, "section", axis=0)
+    norms = lax.all_gather(norms, "dp", axis=2, tiled=True).astype(jnp.float32)
+
+    weights = [[], []]
+    own_half = [half_of(shard[0], core) for shard in shards]
+    sent_half = [other_core(half_of(shard[0], 1 - core)) for shard in shards]
+    for layer in range(2):
+        for own, received in zip(own_half, sent_half):
+            piece = jnp.where(core == layer, own, received)
+            mine = gather_half(piece, dp_rank)
+            weights[layer].append(by_core(core, mine, other_core(mine), 1))
+        weights[layer].append(norms[layer])
+
+    hidden = rows_of(tokens)
+    incoming = rows_of(cotangent).astype(jnp.float32)
+    kept, outputs = [], []
+    for layer in range(2):
+        output, keep = forward_rows(hidden, weights[layer], seg_rows, seg_keys, cosine, sine)
+        hidden = lowered(output)
+        kept.append(keep)
+        outputs.append(hidden)
+    totals, norm_sums, input_rows = [None, None], [None, None], [None, None]
+    for layer in (1, 0):
+        dhidden, grads, norm_sums[layer] = backward_rows(
+            incoming, kept[layer], weights[layer], seg_rows, seg_keys, cosine, sine, core
+        )
+        totals[layer] = [reduce_half(grad, dp_rank, ctx_rank) for grad in grads]
+        input_rows[layer] = dhidden
+        incoming = lowered(dhidden).astype(jnp.float32)
+
+    def whole(first, second):
+        from_first = other_core(first, ((1, 0),))
+        from_second = other_core(second, ((0, 1),))
+        mine = jnp.where(core == 0, first, second)
+        theirs = jnp.where(core == 0, from_first, from_second)
+        return by_core(core, mine, theirs, 1).astype(jnp.float32)[None]
+
+    grads = [whole(first, second) for first, second in zip(*totals)]
+    norm_sums = lax.psum(jnp.stack(norm_sums), ("section", "dp", "ctx"))
+    norm_grads = lax.dynamic_slice_in_dim(
+        pick(norm_sums, core), dp_rank * norm1_gain.shape[1], norm1_gain.shape[1], 1
+    )
+
+    def placed_rows(first, second):
+        first, second = lowered(first), lowered(second)
+        near = jnp.where(
+            core == 0, first, other_core(second, ((0, 1),))
+        )
+        swapped = z_swap(jnp.stack([first, second]))
+        far = jnp.where(core == 0, other_core(swapped[0], ((1, 0),)), swapped[1])
+        return jnp.where(sequence == 0, jnp.stack([near, far]), jnp.stack([far, near]))[None]
+
+    return (
+        placed_rows(*outputs),
+        placed_rows(*input_rows).astype(jnp.float32),
+        *grads,
+        *(norm_grads[i][None] for i in range(4)),
+    )
+
+
 def solution(mesh):
     placed = (
         P("dp", "ctx", None),
@@ -469,8 +731,9 @@
         P("section", "dp"),
         P("dp", "ctx", None),
     )
+    paired = mesh.shape["section"] == 2 and mesh.shape["ctx"] == 4 and mesh.shape["dp"] == 4
     return jax.shard_map(
-        on_device,
+        paired_on_device if paired else relay_on_device,
         mesh=mesh,
         in_specs=placed,
         out_specs=(

time: 1460 us -> 992 us (0.68)
  waiting for transfers between devices: 912 us -> 320 us
  starting transfers between devices: 8.68 us -> 233 us
  matrix products: 313 us -> 167 us
  blocking collectives: 20.1 us -> 52.2 us
  other arithmetic: 89.9 us -> 118 us
    all_gather x11 -> x0, waiting for transfers between devices: 395 us -> none  [the longest x3 95.9 us: layer_forward(): lax.all_gather(key_rows, 'ctx', axis=1, tiled=True)]
    reduce_scatter x11 -> x0, waiting for transfers between devices: 328 us -> none  [the longest x3 66.2 us: layer_backward(): lax.psum_scatter(dvalues_all.astype(jnp.bfloat16), 'ctx', scatter_dimensi...]
    ppermute x4 -> x191, waiting for transfers between devices: 2.44 us -> 320 us  [the longest x50 88.6 us: along_x(): return lax.ppermute(value, 'dp', [(i, i ^ 1) for i in range(4)])]
    ppermute x4 -> x191, starting transfers between devices: 6.54 us -> 233 us  [the longest x50 55.3 us: along_y(): return lax.ppermute(value, 'dp', [(i, i ^ 2) for i in range(4)])]
    psum x1 -> x0, waiting for transfers between devices: 159 us -> none  [on_device(): lax.psum(for_sending(summed), 'ctx')]
    dot_general x45 -> x30, matrix products: 174 us -> 109 us  [the longest x10 47.5 us: forward_rows(): dot = lambda a, b: jnp.dot(a, b, preferred_element_type=jnp.float32)]
    slice x15 -> x41, local copies, waits for them, and re-layouts: 19.9 us -> 51.5 us  [the longest x1 21.5 us: forward_rows(): norm_params[2]]
    psum x1, blocking collectives: 11.9 us -> 40.8 us  [paired_on_device(): norm_sums = lax.psum(jnp.stack(norm_sums), ('section', 'dp', 'ctx'))]
  transfers between devices with their start and end apart: 28 -> 191, of which waited for: 24 -> 64; matrix products, arithmetic and copies ran while one was open for 16% -> 31% of each run, Pallas kernels for 0% -> 0%
where the time goes in v1:
time: 992 us; the launch traced here: 981 us
  waiting for transfers between devices  320 us (32%)
  starting transfers between devices  233 us (23%)
  matrix products  167 us (17%)
  other arithmetic  118 us (12%)
  local copies, waits for them, and re-layouts  87.9 us (9%)
  blocking collectives  52.2 us (5%)
    ppermute x50, waiting for transfers between devices, along_x(): return lax.ppermute(value, 'dp', [(i, i ^ 1) for i in range(4)])  88.6 us
    ppermute x50, waiting for transfers between devices, along_y(): return lax.ppermute(value, 'dp', [(i, i ^ 2) for i in range(4)])  79.3 us
    ppermute x10, waiting for transfers between devices, reduce_half(): outer = lax.ppermute(total, 'ctx', [(1, 0), (2, 3)])  76.5 us
    ppermute x50, starting transfers between devices, along_y(): return lax.ppermute(value, 'dp', [(i, i ^ 2) for i in range(4)])  55.3 us
    ppermute x50, starting transfers between devices, along_x(): return lax.ppermute(value, 'dp', [(i, i ^ 1) for i in range(4)])  52.4 us
    ppermute x53, starting transfers between devices, other_core(): return lax.ppermute(value, 'section', list(pairs))  50 us
    dot_general x10, matrix products, forward_rows(): dot = lambda a, b: jnp.dot(a, b, preferred_element_type=jnp.float32)  47.5 us
    dot_general x10, matrix products, backward_rows(): lax.dot_general(a, b, (((1,), (1,)), ((), ())), preferred_element_type=jn...  46.1 us
  transfers between devices with their start and end apart: 191, of which 64 were waited for; matrix products, arithmetic and copies ran while one was open for 31% of the time, Pallas kernels for 0%

profile of v1, /device:TPU:0, one launch (start us, length us, event | category | flops | bytes accessed | tf_op | source)
XLA Modules:
  0.0 981.4 jit_solution(11369768033056479845)
XLA Ops:
  16.4 9.7 all_gather.11
  26.4 21.5 %slice_reduce_fusion.1 = (f32[768]{0:T(1024)}, f32[768]{0:T(1024)}, f32[768]{0:T(1024)}, f32[768]{0:T(1024)S(1)}, f32[768]{0:T(1024)S(1)}, /*index=5*/f32[768]{0:T(1024)S(1)}, f32[768]{0:T(1024)}, f32[768]{0:T(1024)S(1)}) fusion(f32[2,4,768]{1,0,2:T(2,128)S(1)} %convert_element_type.744), kind=kLoop, calls=%fused_computation.332 | loop fusion | bytes 49152 | tf_op jit(solution)/shard_map/slice | solution.py:552
  94.9 7.7 collective-permute-done.36
  105.0 15.0 %collective-permute-done.3 = bf16[96,1152]{1,0:T(8,128)(2,1)S(1)} collective-permute-done((bf16[96,1152]{1,0:T(8,128)(2,1)S(1)}, bf16[96,1152]{1,0:T(8,128)(2,1)S(1)}, u32[]{:S(2)}, u32[]{:S(2)}) %collective-permute-start.3) | collective-permute-done | bytes 221216 | tf_op jit(solution)/shard_map/ppermute | solution.py:462
  129.0 7.5 collective-permute-done.37
  145.3 7.4 collective-permute-done.29
  157.8 7.5 collective-permute-done.47
  231.3 11.1 %collective-permute-done.8 = bf16[256,1536]{1,0:T(8,128)(2,1)S(1)} collective-permute-done((bf16[256,1536]{1,0:T(8,128)(2,1)S(1)}, bf16[256,1536]{1,0:T(8,128)(2,1)S(1)}, u32[]{:S(2)}, u32[]{:S(2)}) %collective-permute-start.8) | collective-permute-done | bytes 786464 | tf_op jit(solution)/shard_map/ppermute | solution.py:470
  280.2 9.2 multiply_convert_fusion.9
  310.7 12.5 %collective-permute-done.40 = bf16[256,1536]{1,0:T(8,128)(2,1)S(1)} collective-permute-done((bf16[256,1536]{1,0:T(8,128)(2,1)S(1)}, bf16[256,1536]{1,0:T(8,128)(2,1)S(1)}, u32[]{:S(2)}, u32[]{:S(2)}) %collective-permute-start.40) | collective-permute-done | bytes 786464 | tf_op jit(solution)/shard_map/ppermute | solution.py:470
  395.5 10.9 %multiply_reduce_fusion.1 = (f32[12,256]{1,0:T(8,128)S(1)}, f32[12,256,1024]{2,1,0:T(8,128)}) fusion(f32[12,256]{1,0:T(8,128)S(1)} %log_add_fusion.1, f32[12,256,1024]{2,1,0:T(8,128)} %copy-done.1, pred[256,1024]{1,0:T(8,128)(4,1)S(1)} %broadcast_compare_fusion, bf16[256,12,64]{0,2,1:T(8,128)(2,1)} %bitcast.261, bf16[1024,12,64]{0,2,1:T(8,128)(2,1)} %bitcast.240), kind=kOutput, calls=%fused_computation.4 | convolution fusion | flops 418378752 | bytes 27418624 | tf_op jit(solution)/shard_map/qhd,khd->hqk/dot_general | solution.py:115
  468.6 11.9 %collective-permute-start.66 = (bf16[2,256,1536]{1,2,0:T(8,128)(2,1)S(1)}, bf16[2,256,1536]{1,2,0:T(8,128)(2,1)S(1)}, u32[]{:S(2)}, u32[]{:S(2)}) collective-permute-start(bf16[2,256,1536]{1,2,0:T(8,128)(2,1)S(1)} %pad_maximum_fusion.2), channel_id=1, source_target_pairs={{0,16},{16,0},{1,17},{17,1},{2,18},{18,2},{3,19},{19,3},{4,20},{20... | collective-permute-start | bytes 4718600 | tf_op jit(solution)/shard_map/ppermute | solution.py:458
  527.4 9.7 collective-permute-done.140
  585.4 10.4 %multiply_reduce_fusion = (f32[12,256]{1,0:T(8,128)S(1)}, f32[12,256,1024]{2,1,0:T(8,128)}) fusion(f32[12,256]{1,0:T(8,128)S(1)} %copy-done.88, f32[12,256,1024]{2,1,0:T(8,128)} %copy-done, pred[256,1024]{1,0:T(8,128)(4,1)S(1)} %broadcast_compare_fusion, bf16[256,12,64]{0,2,1:T(8,128)(2,1)S(1)} %bitcast.263, bf16[1024,12,64]{0,2,1:T(8,128)(2,1)S(1)} %bitcast.239), kind=kOutput, calls=%fused_computation.1 | convolution fusion | flops 418378752 | bytes 27418624 | tf_op jit(solution)/shard_map/qhd,khd->hqk/dot_general | solution.py:115
  595.8 8.0 fusion.25
  619.2 40.8 %psum.7 = f32[2,4,768]{2,1,0:T(4,128)} all-reduce(f32[2,4,768]{2,1,0:T(4,128)} %pad_maximum_fusion.30), channel_id=1, replica_groups=mesh['section'=2,'ctx'=4,'dp'=4] {'section','dp','ctx'}, use_global_device_ids=true, to_apply=%region_32.33 | all-reduce | flops 6144 | bytes 49152 | tf_op jit(solution)/shard_map/psum | solution.py:697
  737.4 7.7 collective-permute-done.88
  789.7 17.7 %collective-permute-start.129 = (bf16[192,1536]{1,0:T(8,128)(2,1)S(1)}, bf16[192,1536]{1,0:T(8,128)(2,1)S(1)}, u32[]{:S(2)}, u32[]{:S(2)}) collective-permute-start(bf16[192,1536]{1,0:T(8,128)(2,1)S(1)} %add_convert_fusion.17), channel_id=1, source_target_pairs={{0,4},{12,8},{1,5},{13,9},{2,6},{14,10},{3,7},{15,11},{16,20},{28,... | collective-permute-start | bytes 1769480 | tf_op jit(solution)/shard_map/ppermute | solution.py:522
  809.9 11.2 %collective-permute-done.129 = bf16[192,1536]{1,0:T(8,128)(2,1)S(1)} collective-permute-done((bf16[192,1536]{1,0:T(8,128)(2,1)S(1)}, bf16[192,1536]{1,0:T(8,128)(2,1)S(1)}, u32[]{:S(2)}, u32[]{:S(2)}) %collective-permute-start.129) | collective-permute-done | bytes 589856 | tf_op jit(solution)/shard_map/ppermute | solution.py:522
  822.5 11.6 %collective-permute-done.69 = bf16[256,1536]{0,1:T(8,128)(2,1)S(1)} collective-permute-done((bf16[256,1536]{0,1:T(8,128)(2,1)S(1)}, bf16[256,1536]{0,1:T(8,128)(2,1)S(1)}, u32[]{:S(2)}, u32[]{:S(2)}) %collective-permute-start.69) | collective-permute-done | bytes 786464 | tf_op jit(solution)/shard_map/ppermute | solution.py:470
  843.2 9.0 collective-permute-done.188
  853.6 10.3 %collective-permute-done.177 = bf16[768,384]{0,1:T(8,128)(2,1)S(1)} collective-permute-done((bf16[768,384]{0,1:T(8,128)(2,1)S(1)}, bf16[768,384]{0,1:T(8,128)(2,1)S(1)}, u32[]{:S(2)}, u32[]{:S(2)}) %collective-permute-start.177) | collective-permute-done | bytes 589856 | tf_op jit(solution)/shard_map/ppermute | solution.py:526
  873.5 25.8 %collective-permute-done.154 = bf16[192,1536]{1,0:T(8,128)(2,1)S(1)} collective-permute-done((bf16[192,1536]{1,0:T(8,128)(2,1)S(1)}, bf16[192,1536]{1,0:T(8,128)(2,1)S(1)}, u32[]{:S(2)}, u32[]{:S(2)}) %collective-permute-start.154) | collective-permute-done | bytes 589856 | tf_op jit(solution)/shard_map/ppermute | solution.py:526
  948.3 23.4 %collective-permute-done.83 = bf16[192,1152]{1,0:T(8,128)(2,1)S(1)} collective-permute-done((bf16[192,1152]{1,0:T(8,128)(2,1)S(1)}, bf16[192,1152]{1,0:T(8,128)(2,1)S(1)}, u32[]{:S(2)}, u32[]{:S(2)}) %collective-permute-start.83) | collective-permute-done | bytes 442400 | tf_op jit(solution)/shard_map/ppermute | solution.py:526
  (918 shorter events, 659.6 us)
Async XLA Ops:
  2.4 76.9 %collective-permute-start = (bf16[256,768]{1,0:T(8,128)(2,1)}, bf16[256,768]{1,0:T(8,128)(2,1)}, u32[]{:S(2)}, u32[]{:S(2)}) collective-permute-start(bf16[256,768]{1,0:T(8,128)(2,1)} %dynamic-slice_bitcast_fusion.4), channel_id=1, source_target_pairs={{16,24},{20,28},{24,16},{28,20},{17,25},{21,29},{25,17},{29,21},{1... | collective-permute-start | bytes 1179656 | tf_op jit(solution)/shard_map/ppermute | solution.py:475
  5.5 47.5 %collective-permute-start.10 = (bf16[192,384]{1,0:T(8,128)(2,1)}, bf16[192,384]{1,0:T(8,128)(2,1)}, u32[]{:S(2)}, u32[]{:S(2)}) collective-permute-start(bf16[192,384]{1,0:T(8,128)(2,1)} %dynamic-slice_bitcast_fusion.5), channel_id=1, source_target_pairs={{0,16},{16,0},{1,17},{17,1},{2,18},{18,2},{3,19},{19,3},{4,20},{20... | collective-permute-start | bytes 442376 | tf_op jit(solution)/shard_map/ppermute | solution.py:458
  84.3 52.8 %collective-permute-start.17 = (bf16[192,1536]{1,0:T(8,128)(2,1)S(1)}, bf16[192,1536]{1,0:T(8,128)(2,1)S(1)}, u32[]{:S(2)}, u32[]{:S(2)}) collective-permute-start(bf16[192,1536]{1,0:T(8,128)(2,1)S(1)} %get-tuple-element.164), channel_id=1, source_target_pairs={{0,2},{1,3},{2,0},{3,1},{4,6},{5,7},{6,4},{7,5},{8,10},{9,11},{10,... | collective-permute-start | bytes 1769480 | tf_op jit(solution)/shard_map/ppermute | solution.py:466
  92.3 46.5 %collective-permute-start.19 = (bf16[192,1536]{1,0:T(8,128)(2,1)S(1)}, bf16[192,1536]{1,0:T(8,128)(2,1)S(1)}, u32[]{:S(2)}, u32[]{:S(2)}) collective-permute-start(bf16[192,1536]{1,0:T(8,128)(2,1)S(1)} %get-tuple-element.164), channel_id=1, source_target_pairs={{0,1},{1,0},{2,3},{3,2},{4,5},{5,4},{6,7},{7,6},{8,9},{9,8},{10,11... | collective-permute-start | bytes 1769480 | tf_op jit(solution)/shard_map/ppermute | solution.py:462
  156.5 53.0 %collective-permute-start.6 = (bf16[768,1152]{1,0:T(8,128)(2,1)S(1)}, bf16[768,1152]{1,0:T(8,128)(2,1)S(1)}, u32[]{:S(2)}, u32[]{:S(2)}) collective-permute-start(bf16[768,1152]{1,0:T(8,128)(2,1)S(1)} %maximum_select_fusion.14), channel_id=1, source_target_pairs={{0,16},{16,0},{1,17},{17,1},{2,18},{18,2},{3,19},{19,3},{4,20},{20... | collective-permute-start | bytes 5308424 | tf_op jit(solution)/shard_map/ppermute | solution.py:458
  203.2 165.6 %collective-permute-start.65 = (bf16[256,768]{1,0:T(8,128)(2,1)}, bf16[256,768]{1,0:T(8,128)(2,1)}, u32[]{:S(2)}, u32[]{:S(2)}) collective-permute-start(bf16[256,768]{1,0:T(8,128)(2,1)} %dynamic-slice_bitcast_fusion.3), channel_id=1, source_target_pairs={{16,24},{20,28},{24,16},{28,20},{17,25},{21,29},{25,17},{29,21},{1... | collective-permute-start | bytes 1179656 | tf_op jit(solution)/shard_map/ppermute | solution.py:475
  204.6 63.8 %collective-permute-start.15 = (bf16[768,384]{1,0:T(8,128)(2,1)}, bf16[768,384]{1,0:T(8,128)(2,1)}, u32[]{:S(2)}, u32[]{:S(2)}) collective-permute-start(bf16[768,384]{1,0:T(8,128)(2,1)} %maximum_select_fusion.56), channel_id=1, source_target_pairs={{0,16},{16,0},{1,17},{17,1},{2,18},{18,2},{3,19},{19,3},{4,20},{20... | collective-permute-start | bytes 1769480 | tf_op jit(solution)/shard_map/ppermute | solution.py:458
  230.8 63.0 %collective-permute-start.38 = (bf16[768,1152]{1,0:T(8,128)(2,1)}, bf16[768,1152]{1,0:T(8,128)(2,1)}, u32[]{:S(2)}, u32[]{:S(2)}) collective-permute-start(bf16[768,1152]{1,0:T(8,128)(2,1)} %maximum_select_fusion.15), channel_id=1, source_target_pairs={{0,16},{16,0},{1,17},{17,1},{2,18},{18,2},{3,19},{19,3},{4,20},{20... | collective-permute-start | bytes 5308424 | tf_op jit(solution)/shard_map/ppermute | solution.py:458
  303.1 43.8 %collective-permute-start.46 = (bf16[768,384]{1,0:T(8,128)(2,1)}, bf16[768,384]{1,0:T(8,128)(2,1)}, u32[]{:S(2)}, u32[]{:S(2)}) collective-permute-start(bf16[768,384]{1,0:T(8,128)(2,1)} %maximum_select_fusion.57), channel_id=1, source_target_pairs={{0,16},{16,0},{1,17},{17,1},{2,18},{18,2},{3,19},{19,3},{4,20},{20... | collective-permute-start | bytes 1769480 | tf_op jit(solution)/shard_map/ppermute | solution.py:458
  306.9 42.6 %collective-permute-start.51 = (bf16[768,1536]{1,0:T(8,128)(2,1)}, bf16[768,1536]{1,0:T(8,128)(2,1)}, u32[]{:S(2)}, u32[]{:S(2)}) collective-permute-start(bf16[768,1536]{1,0:T(8,128)(2,1)} %maximum_select_fusion.11), channel_id=1, source_target_pairs={{0,16},{16,0},{1,17},{17,1},{2,18},{18,2},{3,19},{19,3},{4,20},{20... | collective-permute-start | bytes 7077896 | tf_op jit(solution)/shard_map/ppermute | solution.py:458
  326.4 36.6 %collective-permute-start.61 = (bf16[3072,384]{0,1:T(8,128)(2,1)}, bf16[3072,384]{0,1:T(8,128)(2,1)}, u32[]{:S(2)}, u32[]{:S(2)}) collective-permute-start(bf16[3072,384]{0,1:T(8,128)(2,1)} %maximum_select_fusion.13), channel_id=1, source_target_pairs={{0,16},{16,0},{1,17},{17,1},{2,18},{18,2},{3,19},{19,3},{4,20},{20... | collective-permute-start | bytes 7077896 | tf_op jit(solution)/shard_map/ppermute | solution.py:458
  440.2 72.6 %collective-permute-start.178 = (bf16[256,3072]{1,0:T(8,128)(2,1)S(1)}, bf16[256,3072]{1,0:T(8,128)(2,1)S(1)}, u32[]{:S(2)}, u32[]{:S(2)}) collective-permute-start(bf16[256,3072]{1,0:T(8,128)(2,1)S(1)} %copy-done.113), channel_id=1, source_target_pairs={{0,16},{16,0},{1,17},{17,1},{2,18},{18,2},{3,19},{19,3},{4,20},{20... | collective-permute-start | bytes 4718600 | tf_op jit(solution)/shard_map/ppermute | solution.py:458
  468.6 47.8 %collective-permute-start.66 = (bf16[2,256,1536]{1,2,0:T(8,128)(2,1)S(1)}, bf16[2,256,1536]{1,2,0:T(8,128)(2,1)S(1)}, u32[]{:S(2)}, u32[]{:S(2)}) collective-permute-start(bf16[2,256,1536]{1,2,0:T(8,128)(2,1)S(1)} %pad_maximum_fusion.2), channel_id=1, source_target_pairs={{0,16},{16,0},{1,17},{17,1},{2,18},{18,2},{3,19},{19,3},{4,20},{20... | collective-permute-start | bytes 4718600 | tf_op jit(solution)/shard_map/ppermute | solution.py:458
  538.7 133.8 %collective-permute-start.167 = (bf16[256,3072]{1,0:T(8,128)(2,1)}, bf16[256,3072]{1,0:T(8,128)(2,1)}, u32[]{:S(2)}, u32[]{:S(2)}) collective-permute-start(bf16[256,3072]{1,0:T(8,128)(2,1)} %get-tuple-element.247), channel_id=1, source_target_pairs={{0,16},{16,0},{1,17},{17,1},{2,18},{18,2},{3,19},{19,3},{4,20},{20... | collective-permute-start | bytes 4718600 | tf_op jit(solution)/shard_map/ppermute | solution.py:458
  538.7 122.7 %collective-permute-start.97 = (bf16[256,768]{0,1:T(8,128)(2,1)}, bf16[256,768]{0,1:T(8,128)(2,1)}, u32[]{:S(2)}, u32[]{:S(2)}) collective-permute-start(bf16[256,768]{0,1:T(8,128)(2,1)} %bitcast.15), channel_id=1, source_target_pairs={{0,16},{16,0},{1,17},{17,1},{2,18},{18,2},{3,19},{19,3},{4,20},{20... | collective-permute-start | bytes 1179656 | tf_op jit(solution)/shard_map/ppermute | solution.py:458
  539.3 126.0 %collective-permute-start.163 = (bf16[192,1536]{1,0:T(8,128)(2,1)}, bf16[192,1536]{1,0:T(8,128)(2,1)}, u32[]{:S(2)}, u32[]{:S(2)}) collective-permute-start(bf16[192,1536]{1,0:T(8,128)(2,1)} %add_convert_fusion.7), channel_id=1, source_target_pairs={{4,8},{8,4},{5,9},{9,5},{6,10},{10,6},{7,11},{11,7},{20,24},{24,20... | collective-permute-start | bytes 1769480 | tf_op jit(solution)/shard_map/ppermute | solution.py:524
  544.4 124.9 %collective-permute-start.141 = (bf16[192,1536]{1,0:T(8,128)(2,1)}, bf16[192,1536]{1,0:T(8,128)(2,1)}, u32[]{:S(2)}, u32[]{:S(2)}) collective-permute-start(bf16[192,1536]{1,0:T(8,128)(2,1)} %add_convert_fusion.13), channel_id=1, source_target_pairs={{4,8},{8,4},{5,9},{9,5},{6,10},{10,6},{7,11},{11,7},{20,24},{24,20... | collective-permute-start | bytes 1769480 | tf_op jit(solution)/shard_map/ppermute | solution.py:524
  615.9 47.4 %collective-permute-start.98 = (bf16[256,384]{1,0:T(8,128)(2,1)}, bf16[256,384]{1,0:T(8,128)(2,1)}, u32[]{:S(2)}, u32[]{:S(2)}) collective-permute-start(bf16[256,384]{1,0:T(8,128)(2,1)} %get-tuple-element.222), channel_id=1, source_target_pairs={{0,16},{16,0},{1,17},{17,1},{2,18},{18,2},{3,19},{19,3},{4,20},{20... | collective-permute-start | bytes 589832 | tf_op jit(solution)/shard_map/ppermute | solution.py:458
  777.6 87.7 %collective-permute-start.73 = (bf16[256,768]{1,0:T(8,128)(2,1)S(1)}, bf16[256,768]{1,0:T(8,128)(2,1)S(1)}, u32[]{:S(2)}, u32[]{:S(2)}) collective-permute-start(bf16[256,768]{1,0:T(8,128)(2,1)S(1)} %copy-done.80), channel_id=1, source_target_pairs={{0,16},{16,0},{1,17},{17,1},{2,18},{18,2},{3,19},{19,3},{4,20},{20... | collective-permute-start | bytes 1179656 | tf_op jit(solution)/shard_map/ppermute | solution.py:458
  777.8 61.2 %collective-permute-start.70 = (bf16[256,768]{1,0:T(8,128)(2,1)S(1)}, bf16[256,768]{1,0:T(8,128)(2,1)S(1)}, u32[]{:S(2)}, u32[]{:S(2)}) collective-permute-start(bf16[256,768]{1,0:T(8,128)(2,1)S(1)} %copy-done.40), channel_id=1, source_target_pairs={{0,16},{1,17},{2,18},{3,19},{4,20},{5,21},{6,22},{7,23},{8,24},{9,... | collective-permute-start | bytes 1179656 | tf_op jit(solution)/shard_map/ppermute | solution.py:458
  808.4 63.6 %collective-permute-start.164 = (bf16[192,1536]{1,0:T(8,128)(2,1)S(1)}, bf16[192,1536]{1,0:T(8,128)(2,1)S(1)}, u32[]{:S(2)}, u32[]{:S(2)}) collective-permute-start(bf16[192,1536]{1,0:T(8,128)(2,1)S(1)} %add_convert_fusion.6), channel_id=1, source_target_pairs={{4,0},{8,12},{5,1},{9,13},{6,2},{10,14},{7,3},{11,15},{20,16},{24,... | collective-permute-start | bytes 1769480 | tf_op jit(solution)/shard_map/ppermute | solution.py:526
  852.3 74.3 %collective-permute-start.142 = (bf16[192,1536]{1,0:T(8,128)(2,1)}, bf16[192,1536]{1,0:T(8,128)(2,1)}, u32[]{:S(2)}, u32[]{:S(2)}) collective-permute-start(bf16[192,1536]{1,0:T(8,128)(2,1)} %add_convert_fusion.12), channel_id=1, source_target_pairs={{4,0},{8,12},{5,1},{9,13},{6,2},{10,14},{7,3},{11,15},{20,16},{24,... | collective-permute-start | bytes 1769480 | tf_op jit(solution)/shard_map/ppermute | solution.py:526
  865.3 36.6 %collective-permute-start.189 = (bf16[768,384]{0,1:T(8,128)(2,1)S(1)}, bf16[768,384]{0,1:T(8,128)(2,1)S(1)}, u32[]{:S(2)}, u32[]{:S(2)}) collective-permute-start(bf16[768,384]{0,1:T(8,128)(2,1)S(1)} %get-tuple-element.81), channel_id=1, source_target_pairs={{16,0},{17,1},{18,2},{19,3},{20,4},{21,5},{22,6},{23,7},{24,8},{25... | collective-permute-start | bytes 1769480 | tf_op jit(solution)/shard_map/ppermute | solution.py:458
  872.0 40.7 %collective-permute-start.71 = (bf16[2,256,768]{2,1,0:T(8,128)(2,1)}, bf16[2,256,768]{2,1,0:T(8,128)(2,1)}, u32[]{:S(2)}, u32[]{:S(2)}) collective-permute-start(bf16[2,256,768]{2,1,0:T(8,128)(2,1)} %pad_maximum_fusion.11), channel_id=1, source_target_pairs={{16,24},{20,28},{24,16},{28,20},{17,25},{21,29},{25,17},{29,21},{1... | collective-permute-start | bytes 2359304 | tf_op jit(solution)/shard_map/ppermute | solution.py:475
  (292 other events, 4184.6 us)

commit v2 on v0

--- a/solution.py
+++ b/solution.py
@@ -1,6 +1,8 @@
 import jax
 import jax.numpy as jnp
 from jax import lax
+from jax.experimental import pallas as pl
+from jax.experimental.pallas import tpu as pltpu
 from jax.sharding import PartitionSpec as P
 
 HEAD = 64
@@ -300,7 +302,7 @@
     )
 
 
-def on_device(
+def relay_on_device(
     tokens,
     seg_ids,
     query_key_value_weight,
@@ -454,6 +456,712 @@
     )
 
 
+NT = (((1,), (1,)), ((), ()))
+TN = (((0,), (0,)), ((), ()))
+
+
+def mm(left, right, dims=(((1,), (0,)), ((), ()))):
+    return lax.dot_general(left, right, dims, preferred_element_type=jnp.float32)
+
+
+def in_vmem():
+    return pl.BlockSpec(memory_space=pltpu.VMEM)
+
+
+def anywhere():
+    return pl.BlockSpec(memory_space=pl.ANY)
+
+
+def in_smem():
+    return pl.BlockSpec(memory_space=pltpu.SMEM)
+
+
+def kernel_call(body, out_shapes, in_specs, scratch, mbytes, cost, name, out_specs=None, grid=None):
+    return pl.pallas_call(
+        body,
+        out_shape=out_shapes,
+        in_specs=in_specs,
+        out_specs=[in_vmem()] * len(out_shapes) if out_specs is None else out_specs,
+        scratch_shapes=scratch,
+        **({} if grid is None else {"grid": grid}),
+        compiler_params=pltpu.CompilerParams(vmem_limit_bytes=mbytes * 2**20),
+        cost_estimate=pl.CostEstimate(flops=cost[0], bytes_accessed=cost[1], transcendentals=0),
+        name=name,
+    )
+
+
+def shape_of(shape, dtype):
+    return jax.ShapeDtypeStruct(shape, dtype)
+
+
+def start_loads(place, pieces, first, width, scratch, sems, begin, rows=None):
+    dp_rank, core = place[0], place[1]
+    count = pieces[0].shape[0]
+    copies = []
+    for index, piece in enumerate(pieces):
+        kind = index % 5
+        flip = min(kind, 3)
+        half = core if index < 5 else 1 - core
+        row = (dp_rank ^ flip) * count + (count // 2 if kind == 4 else 0)
+        copies.append(
+            pltpu.make_async_copy(
+                piece.at[:, pl.ds(first, width)],
+                scratch.at[
+                    pl.ds(pl.multiple_of(row, count // 2), piece.shape[0]),
+                    pl.ds(pl.multiple_of(half * width, 128), width),
+                ],
+                sems.at[begin + index],
+            )
+        )
+    for copy in copies:
+        copy.start()
+    return copies
+
+
+def wait_all(copies):
+    for copy in copies:
+        copy.wait()
+
+
+def turn(values, cosine, sine):
+    lane = lax.broadcasted_iota(jnp.int32, values.shape, 1)
+    swapped = jnp.where(
+        lane % 64 < 32, pltpu.roll(values, 96, 1), pltpu.roll(values, 32, 1)
+    )
+    return values * cosine + swapped * sine
+
+
+def project_rows(place, hidden, cosine, sine, pieces):
+    rows, width = hidden.shape
+    half = 3 * width // 2
+
+    def body(place_ref, hidden_ref, cos_ref, sin_ref, *refs):
+        parts, (q_ref, kv_ref, weight, sems) = refs[:10], refs[10:]
+        wait_all(start_loads(place_ref, parts, 0, half, weight, sems, 0))
+        for step in range(3 * width // 256):
+            mixed = mm(hidden_ref[...], weight[:, step * 256 : step * 256 + 256])
+            for pair in range(2):
+                column = step * 256 + pair * 128
+                part = mixed[:, pair * 128 : pair * 128 + 128]
+                which, lane = column // width, column % width
+                if which < 2:
+                    part = turn(part, cos_ref[...], sin_ref[...])
+                if which == 0:
+                    q_ref[:, lane : lane + 128] = (
+                        part.astype(jnp.bfloat16).astype(jnp.float32) * HEAD**-0.5
+                    ).astype(jnp.bfloat16)
+                else:
+                    kv_ref[which - 1, :, lane : lane + 128] = part.astype(jnp.bfloat16)
+
+    return kernel_call(
+        body,
+        [shape_of((rows, width), jnp.bfloat16), shape_of((2, rows, width), jnp.bfloat16)],
+        [in_smem()] + [in_vmem()] * 3 + [anywhere()] * 10,
+        [pltpu.VMEM((width, 3 * width), jnp.bfloat16), pltpu.SemaphoreType.DMA((10,))],
+        32,
+        (6 * rows * width * width, 6 * width * width + 8 * rows * width),
+        "project_rows",
+    )(place, hidden, cosine, sine, *pieces)
+
+
+def attend_rows(queries, blocks, seg_column, seg_row):
+    rows, width = queries.shape
+    keys = 4 * rows
+
+    def body(col_ref, row_ref, q_ref, b0, b1, b2, b3, out_ref, bias):
+        @pl.when(pl.program_id(0) == 0)
+        def _():
+            bias[...] = jnp.where(col_ref[...] == row_ref[...], 0.0, NEG)
+
+        lane = lax.broadcasted_iota(jnp.int32, (rows, 128), 1)
+        query = q_ref[...]
+        key = jnp.concatenate([b[0] for b in (b0, b1, b2, b3)], axis=0)
+        value = jnp.concatenate([b[1] for b in (b0, b1, b2, b3)], axis=0)
+        results = []
+        for head in range(2):
+            own = (lane < 64) if head == 0 else (lane >= 64)
+            scores = mm(jnp.where(own, query, jnp.zeros_like(query)), key, NT) + bias[...]
+            top = jnp.max(scores, axis=1, keepdims=True)
+            exponent = jnp.exp(scores - top)
+            total = jnp.sum(exponent, axis=1, keepdims=True)
+            results.append(mm(exponent.astype(jnp.bfloat16), value) / total)
+        out_ref[...] = jnp.where(lane < 64, results[0], results[1]).astype(jnp.bfloat16)
+
+    block = pl.BlockSpec((2, rows, 128), lambda j: (0, 0, j))
+    return kernel_call(
+        body,
+        [shape_of((rows, width), jnp.bfloat16)],
+        [
+            pl.BlockSpec((rows, 1), lambda j: (0, 0)),
+            pl.BlockSpec((1, keys), lambda j: (0, 0)),
+            pl.BlockSpec((rows, 128), lambda j: (0, j)),
+            block, block, block, block,
+        ],
+        [pltpu.VMEM((rows, keys), jnp.float32)],
+        48,
+        (16 * rows * keys * width, 24 * rows * width),
+        "attend_rows",
+        [pl.BlockSpec((rows, 128), lambda j: (0, j))],
+        (width // 128,),
+    )(seg_column, seg_row, queries, *blocks)[0]
+
+
+def attend_rows_back(queries, blocks, seg_row, seg_column, incoming):
+    rows, width = queries.shape
+    keys = 4 * rows
+
+    def body(row_ref, col_ref, q_ref, in_ref, b0, b1, b2, b3, dq_ref, own_ref, z_ref, core_ref, bias):
+        @pl.when(pl.program_id(0) == 0)
+        def _():
+            bias[...] = jnp.where(col_ref[...] == row_ref[...], 0.0, NEG)
+
+        lane = lax.broadcasted_iota(jnp.int32, (rows, 128), 1)
+        query, given = q_ref[...], in_ref[...]
+        key = jnp.concatenate([b[0] for b in (b0, b1, b2, b3)], axis=0)
+        value = jnp.concatenate([b[1] for b in (b0, b1, b2, b3)], axis=0)
+        key_t = key.T
+        dkeys, dvalues, dqueries = [], [], []
+        for head in range(2):
+            own = (lane < 64) if head == 0 else (lane >= 64)
+            scores = mm(key, jnp.where(own, query, jnp.zeros_like(query)), NT) + bias[...]
+            exponent = jnp.exp(scores - jnp.max(scores, axis=0, keepdims=True))
+            probs = exponent * (1.0 / jnp.sum(exponent, axis=0, keepdims=True))
+            dvalues.append(mm(probs.astype(jnp.bfloat16), given))
+            dprobs = probs * mm(value, jnp.where(own, given, jnp.zeros_like(given)), NT)
+            dscores = dprobs - probs * jnp.sum(dprobs, axis=0, keepdims=True)
+            dscores = dscores.astype(jnp.bfloat16)
+            dkeys.append(mm(dscores, query))
+            dqueries.append(mm(key_t[64 * head : 64 * head + 64], dscores))
+        dq_ref[...] = jnp.concatenate(dqueries, axis=0).T * HEAD**-0.5
+        wide = lax.broadcasted_iota(jnp.int32, (keys, 128), 1) < 64
+        for which, pair in enumerate((dkeys, dvalues)):
+            both = jnp.where(wide, pair[0], pair[1]).astype(jnp.bfloat16)
+            own_ref[which] = both[:rows]
+            core_ref[0, which] = both[rows : 2 * rows]
+            z_ref[which] = both[2 * rows : 3 * rows]
+            core_ref[1, which] = both[3 * rows :]
+
+    block = pl.BlockSpec((2, rows, 128), lambda j: (0, 0, j))
+    columns = pl.BlockSpec((rows, 128), lambda j: (0, j))
+    pair_shape = shape_of((2, rows, width), jnp.bfloat16)
+    return kernel_call(
+        body,
+        [
+            shape_of((rows, width), jnp.float32),
+            pair_shape,
+            pair_shape,
+            shape_of((2, 2, rows, width), jnp.bfloat16),
+        ],
+        [
+            pl.BlockSpec((1, rows), lambda j: (0, 0)),
+            pl.BlockSpec((keys, 1), lambda j: (0, 0)),
+            columns, columns, block, block, block, block,
+        ],
+        [pltpu.VMEM((keys, rows), jnp.float32)],
+        56,
+        (40 * rows * keys * width, 48 * rows * width),
+        "attend_rows_back",
+        [columns, block, block, pl.BlockSpec((2, 2, rows, 128), lambda j: (0, 0, 0, j))],
+        (width // 128,),
+    )(seg_row, seg_column, queries, incoming, *blocks)
+
+
+def unit_of(resid):
+    centred = resid - jnp.mean(resid, axis=1, keepdims=True)
+    scaling = lax.rsqrt(jnp.mean(centred * centred, axis=1, keepdims=True) + EPS)
+    return centred * scaling, scaling
+
+
+def norm_rows_back(incoming, unit, scaling, gain):
+    scaled = incoming * gain
+    return scaling * (
+        scaled
+        - jnp.mean(scaled, axis=1, keepdims=True)
+        - unit * jnp.mean(scaled * unit, axis=1, keepdims=True)
+    )
+
+
+FF_STEP = 512
+
+
+def mlp_scratch(width, hidden_width):
+    return [
+        pltpu.VMEM((width, width), jnp.bfloat16),
+        pltpu.VMEM((width, hidden_width), jnp.bfloat16),
+        pltpu.VMEM((width, hidden_width), jnp.bfloat16),
+        pltpu.VMEM((hidden_width, width), jnp.bfloat16),
+        pltpu.VMEM((width, 256), jnp.bfloat16),
+        pltpu.VMEM((128, width), jnp.float32),
+        pltpu.SemaphoreType.DMA((50,)),
+    ]
+
+
+def mlp_rows(place, hidden, attended, first_parts, gate_up_parts, down_parts):
+    rows, width = hidden.shape
+    ff_half = gate_up_parts[0].shape[1] // 2
+    ff = 2 * ff_half
+
+    def body(place_ref, hidden_ref, att_ref, *refs):
+        parts, rest = refs[:30], refs[30:]
+        out_ref, one_ref, two_ref, acts_ref, gate_ref, up_ref = rest[:6]
+        w_out, w_gate, w_up, w_down, w_norm, norm_ref, sems = rest[6:]
+        normed_ref = acts_ref.at[:, :width]
+        norm_loads = start_loads(place_ref, parts[:10], 2 * width, 128, w_norm, sems, 40)
+        loads = [
+            start_loads(place_ref, parts[:10], 3 * width // 2, width // 2, w_out, sems, 0),
+            start_loads(place_ref, parts[10:20], 0, ff_half, w_gate, sems, 10),
+            start_loads(place_ref, parts[10:20], ff_half, ff_half, w_up, sems, 20),
+            start_loads(place_ref, parts[20:30], 0, width // 2, w_down, sems, 30),
+        ]
+        wait_all(norm_loads)
+        norm_ref[...] = w_norm[:, :128].astype(jnp.float32).T
+        wait_all(loads[0])
+        resid = hidden_ref[...].astype(jnp.float32) + mm(att_ref[...], w_out[...])
+        one_ref[...] = resid
+        normed = unit_of(resid)[0] * norm_ref[0:1] + norm_ref[1:2]
+        normed_ref[...] = normed.astype(jnp.bfloat16)
+        two_ref[...] = normed
+        wait_all(loads[1])
+        wait_all(loads[2])
+        wait_all(loads[3])
+
+        @pl.loop(0, ff // FF_STEP)
+        def _(step):
+            span = pl.ds(pl.multiple_of(step * FF_STEP, FF_STEP), FF_STEP)
+            gate = mm(normed_ref[...], w_gate[:, span])
+            up = mm(normed_ref[...], w_up[:, span])
+            gate_ref[:, span] = gate
+            up_ref[:, span] = up
+            middle = (gate * jax.nn.sigmoid(gate) * up).astype(jnp.bfloat16)
+            acts_ref[:, pl.ds(pl.multiple_of(width + step * FF_STEP, 128), FF_STEP)] = middle
+            two_ref[...] += mm(middle, w_down[span, :])
+
+        out_ref[...] = (unit_of(two_ref[...])[0] * norm_ref[2:3] + norm_ref[3:4]).astype(jnp.bfloat16)
+
+    return kernel_call(
+        body,
+        [
+            shape_of((rows, width), jnp.bfloat16),
+            shape_of((rows, width), jnp.float32),
+            shape_of((rows, width), jnp.float32),
+            shape_of((rows, width + ff), jnp.bfloat16),
+            shape_of((rows, ff), jnp.float32),
+            shape_of((rows, ff), jnp.float32),
+        ],
+        [in_smem()] + [in_vmem()] * 2 + [anywhere()] * 30,
+        mlp_scratch(width, ff),
+        56,
+        (2 * rows * width * (width + 3 * ff), 2 * width * (width + 3 * ff)),
+        "mlp_rows",
+    )(place, hidden, attended, *first_parts, *gate_up_parts, *down_parts)
+
+
+def mlp_rows_back(place, incoming, one, two, gate, up, first_parts, gate_up_parts, down_parts):
+    rows, width = incoming.shape
+    ff_half = gate_up_parts[0].shape[1] // 2
+    ff = 2 * ff_half
+
+    def body(place_ref, in_ref, one_ref, two_ref, gate_ref, up_ref, *refs):
+        parts, rest = refs[:30], refs[30:]
+        keep_ref, send_ref, dresid_ref, datt_ref, sums_ref = rest[:5]
+        w_out, w_gate, w_up, w_down, w_norm, norm_ref, sems, low_ref = rest[5:]
+        core = place_ref[1]
+        norm_loads = start_loads(place_ref, parts[:10], 2 * width, 128, w_norm, sems, 40)
+
+        def share(half, columns, value):
+            @pl.when(half == core)
+            def _():
+                keep_ref[:, columns] = value
+
+            @pl.when(half != core)
+            def _():
+                send_ref[:, columns] = value
+
+        loads = [
+            start_loads(place_ref, parts[20:30], 0, width // 2, w_down, sems, 30),
+            start_loads(place_ref, parts[10:20], 0, ff_half, w_gate, sems, 10),
+            start_loads(place_ref, parts[10:20], ff_half, ff_half, w_up, sems, 20),
+            start_loads(place_ref, parts[:10], 3 * width // 2, width // 2, w_out, sems, 0),
+        ]
+        wait_all(norm_loads)
+        norm_ref[...] = w_norm[:, :128].astype(jnp.float32).T
+        sums_ref[...] = jnp.zeros_like(sums_ref)
+        given = in_ref[...].astype(jnp.float32)
+        unit, scaling = unit_of(two_ref[...])
+        sums_ref[2:3] = jnp.sum(given * unit, axis=0, keepdims=True)
+        sums_ref[3:4] = jnp.sum(given, axis=0, keepdims=True)
+        dresid_two = norm_rows_back(given, unit, scaling, norm_ref[2:3])
+        dresid_ref[...] = dresid_two
+        low_ref[...] = dresid_two.astype(jnp.bfloat16)
+        for half in range(2):
+            span = slice(half * width // 2, (half + 1) * width // 2)
+            share(half, slice(ff, ff + width // 2), low_ref[:, span])
+        for copies in loads:
+            wait_all(copies)
+
+        @pl.loop(0, ff // FF_STEP)
+        def _(step):
+            span = pl.ds(pl.multiple_of(step * FF_STEP, FF_STEP), FF_STEP)
+            dmiddle = mm(low_ref[...], w_down[span, :], NT)
+            gate_block = gate_ref[:, span]
+            sig = jax.nn.sigmoid(gate_block)
+            dgate = (dmiddle * up_ref[:, span] * sig * (1.0 + gate_block * (1.0 - sig))).astype(jnp.bfloat16)
+            dup = (dmiddle * (gate_block * sig)).astype(jnp.bfloat16)
+            half, column = step // (ff_half // FF_STEP), step % (ff_half // FF_STEP) * FF_STEP
+            share(half, pl.ds(pl.multiple_of(column, 128), FF_STEP), dgate)
+            share(half, pl.ds(pl.multiple_of(column + ff_half, 128), FF_STEP), dup)
+            dresid_ref[...] += mm(dgate, w_gate[:, span], NT) + mm(dup, w_up[:, span], NT)
+
+        dnormed = dresid_ref[...]
+        unit, scaling = unit_of(one_ref[...])
+        sums_ref[0:1] = jnp.sum(dnormed * unit, axis=0, keepdims=True)
+        sums_ref[1:2] = jnp.sum(dnormed, axis=0, keepdims=True)
+        dresid_one = norm_rows_back(dnormed, unit, scaling, norm_ref[0:1])
+        dresid_ref[...] = dresid_one
+        low_ref[...] = dresid_one.astype(jnp.bfloat16)
+        for half in range(2):
+            span = slice(half * width // 2, (half + 1) * width // 2)
+            share(half, slice(ff + width // 2, ff + width), low_ref[:, span])
+        datt_ref[...] = mm(low_ref[...], w_out[...], NT).astype(jnp.bfloat16)
+
+    return kernel_call(
+        body,
+        [
+            shape_of((rows, ff + width), jnp.bfloat16),
+            shape_of((rows, ff + width), jnp.bfloat16),
+            shape_of((rows, width), jnp.float32),
+            shape_of((rows, width), jnp.bfloat16),
+            shape_of((8, width), jnp.float32),
+        ],
+        [in_smem()] + [in_vmem()] * 5 + [anywhere()] * 30,
+        mlp_scratch(width, ff) + [pltpu.VMEM((rows, width), jnp.bfloat16)],
+        56,
+        (2 * rows * width * (width + 3 * ff), 2 * width * (width + 3 * ff)),
+        "mlp_rows_back",
+    )(place, incoming, one, two, gate, up, *first_parts, *gate_up_parts, *down_parts)
+
+
+def project_rows_back(place, dqueries, sums, dresid_one, cosine, sine, pieces):
+    rows, width = dqueries.shape
+    half = 3 * width // 2
+    count = len(sums)
+
+    def body(place_ref, dq_ref, resid_ref, cos_ref, sin_ref, *refs):
+        parts, rest = refs[:10], refs[10:]
+        sum_refs, (keep_ref, send_ref, dhidden_ref, weight, sems, dmixed_ref) = rest[:count], rest[count:]
+        core = place_ref[1]
+        loads = start_loads(place_ref, parts, 0, half, weight, sems, 0)
+        for column in range(0, 3 * width, 128):
+            which, lane = column // width, column % width
+            span = slice(lane, lane + 128)
+            if which == 0:
+                part = dq_ref[:, span]
+            else:
+                part = sum(ref[which - 1, :, span].astype(jnp.float32) for ref in sum_refs)
+            if which < 2:
+                part = turn(part, cos_ref[...], -sin_ref[...])
+            dmixed_ref[:, column : column + 128] = part.astype(jnp.bfloat16)
+        for index in range(2):
+            @pl.when(core == index)
+            def _():
+                keep_ref[...] = dmixed_ref[:, index * half : (index + 1) * half]
+                send_ref[...] = dmixed_ref[:, (1 - index) * half : (2 - index) * half]
+
+        wait_all(loads)
+        dhidden_ref[...] = resid_ref[...] + mm(dmixed_ref[...], weight[...], NT)
+
+    return kernel_call(
+        body,
+        [
+            shape_of((rows, half), jnp.bfloat16),
+            shape_of((rows, half), jnp.bfloat16),
+            shape_of((rows, width), jnp.float32),
+        ],
+        [in_smem()] + [in_vmem()] * 4 + [anywhere()] * 10 + [in_vmem()] * count,
+        [
+            pltpu.VMEM((width, 3 * width), jnp.bfloat16),
+            pltpu.SemaphoreType.DMA((10,)),
+            pltpu.VMEM((rows, 3 * width), jnp.bfloat16),
+        ],
+        48,
+        (6 * rows * width * width, 6 * width * width + 8 * rows * width),
+        "project_rows_back",
+    )(place, dqueries, dresid_one, cosine, sine, *pieces, *sums)
+
+
+def grad_parts(place, lefts, rights, left_span, right_span, sums=()):
+    rows = lefts[0].shape[0]
+    depth = left_span[1] - left_span[0]
+    width = right_span[1] - right_span[0]
+    extra = 128 if sums else 0
+    count = depth // 4
+    tile = min(width, 512) if width % 512 == 0 else 384
+
+    def body(place_ref, l0, l1, r0, r1, *refs):
+        sum_refs, refs = refs[: len(sums)], refs[len(sums) :]
+        own_ref, x_ref, y_ref, xl_ref, yu_ref, left_t, right, block = refs[:8]
+        left_t[:, :rows] = l0[:, left_span[0] : left_span[1]].T
+        left_t[:, rows:] = l1[:, left_span[0] : left_span[1]].T
+        right[:rows] = r0[:, right_span[0] : right_span[1]]
+        right[rows:] = r1[:, right_span[0] : right_span[1]]
+        if sums:
+            padded, turned = refs[8:]
+            padded[...] = jnp.zeros_like(padded)
+            padded[:8] = sum_refs[0][...] + sum_refs[1][...]
+            turned[...] = padded[...].T
+        upper, lower = slice(0, count // 2), slice(count // 2, count)
+        for flip in range(4):
+            begin = pl.multiple_of((place_ref[0] ^ flip) * count, count)
+            for column in range(0, width, tile):
+                span = slice(column, column + tile)
+                block[:, span] = mm(left_t[pl.ds(begin, count), :], right[:, span]).astype(jnp.bfloat16)
+            if sums:
+                block[:, width:] = turned[pl.ds(begin, count), :].astype(jnp.bfloat16)
+            if flip == 0:
+                own_ref[...] = block[...]
+            elif flip == 1:
+                x_ref[upper] = block[upper]
+                xl_ref[...] = block[lower]
+            elif flip == 2:
+                y_ref[upper] = block[lower]
+                yu_ref[...] = block[upper]
+            else:
+                x_ref[lower] = block[upper]
+                y_ref[lower] = block[lower]
+
+    out_width = width + extra
+    return kernel_call(
+        body,
+        [
+            shape_of((count, out_width), jnp.bfloat16),
+            shape_of((count, out_width), jnp.bfloat16),
+            shape_of((count, out_width), jnp.bfloat16),
+            shape_of((count // 2, out_width), jnp.bfloat16),
+            shape_of((count // 2, out_width), jnp.bfloat16),
+        ],
+        [in_smem()] + [in_vmem()] * (4 + len(sums)),
+        [
+            pltpu.VMEM((depth, 2 * rows), jnp.bfloat16),
+            pltpu.VMEM((2 * rows, width), jnp.bfloat16),
+            pltpu.VMEM((count, out_width), jnp.bfloat16),
+        ]
+        + ([pltpu.VMEM((128, depth), jnp.float32), pltpu.VMEM((depth, 128), jnp.float32)] if sums else []),
+        56,
+        (4 * rows * depth * width, 4 * rows * (depth + width) + 2 * depth * width),
+        "grad_parts",
+    )(place, *lefts, *rights, *sums)
+
+
+def to_core(value, pairs=((0, 1), (1, 0))):
+    return lax.ppermute(value, "section", list(pairs))
+
+
+def along_x(value):
+    return lax.ppermute(value, "dp", [(i, i ^ 1) for i in range(4)])
+
+
+def along_y(value):
+    return lax.ppermute(value, "dp", [(i, i ^ 2) for i in range(4)])
+
+
+def along_z(value):
+    return lax.ppermute(value, "ctx", [(i, i ^ 1) for i in range(4)])
+
+
+def z_swap(value):
+    pairs = [(4 + i, 4 + (i ^ 2)) for i in range(4)]
+    return lax.ppermute(value, ("section", "ctx"), pairs)
+
+
+def lowered(value):
+    return value.astype(jnp.bfloat16)
+
+
+def wide(value):
+    return value.astype(jnp.float32)
+
+
+def by_core(core, mine, theirs, axis):
+    return jnp.where(
+        core == 0,
+        jnp.concatenate([mine, theirs], axis=axis),
+        jnp.concatenate([theirs, mine], axis=axis),
+    )
+
+
+def half_of(array, which):
+    width = array.shape[-1] // 2
+    return lax.dynamic_slice_in_dim(array, which * width, width, array.ndim - 1)
+
+
+def gathered(piece):
+    rows = piece.shape[0] // 2
+    from_x, from_y = along_x(piece), along_y(piece)
+    upper, lower = along_x(from_y[:rows]), along_y(from_x[rows:])
+    mine = [piece, from_x, from_y, upper, lower]
+    return mine + [to_core(part) for part in mine]
+
+
+def reduced(parts, ctx_rank):
+    own, x_message, y_message, x_lower, y_upper = parts
+    rows = own.shape[0] // 2
+    from_x, from_y = along_x(x_message), along_y(y_message)
+    x_last = along_x(lowered(wide(x_lower) + wide(from_y[rows:])))
+    y_last = along_y(lowered(wide(y_upper) + wide(from_x[rows:])))
+    summed = lowered(
+        wide(own)
+        + jnp.concatenate(
+            [wide(from_x[:rows]) + wide(y_last), wide(from_y[:rows]) + wide(x_last)], axis=0
+        )
+    )
+    inner = lax.ppermute(summed, "ctx", [(0, 1), (3, 2)])
+    pair = lowered(wide(summed) + wide(inner))
+    across = lax.ppermute(pair, "ctx", [(1, 2), (2, 1)])
+    total = lowered(wide(pair) + wide(across))
+    outer = lax.ppermute(total, "ctx", [(1, 0), (2, 3)])
+    return jnp.where((ctx_rank == 0) | (ctx_rank == 3), outer, total)
+
+
+def paired_on_device(
+    tokens,
+    seg_ids,
+    query_key_value_weight,
+    output_weight,
+    gate_weight,
+    up_weight,
+    down_weight,
+    norm1_gain,
+    norm1_bias,
+    norm2_gain,
+    norm2_bias,
+    cotangent,
+):
+    core, ctx_rank, dp_rank = (lax.axis_index(a) for a in ("section", "ctx", "dp"))
+    span, width = tokens.shape[1], tokens.shape[2]
+    sequence = ctx_rank // 2
+    block = ctx_rank ^ (2 * core)
+    place = jnp.stack([dp_rank, core]).astype(jnp.int32)
+    pick = lambda array, index: lax.dynamic_index_in_dim(array, index, 0, keepdims=False)
+
+    def rows_of(array):
+        return jnp.where(core == 0, pick(array, sequence), z_swap(pick(array, 1 - sequence)))
+
+    norm_columns = jnp.concatenate([norm1_gain, norm1_bias, norm2_gain, norm2_bias], axis=0).T
+    norm_columns = jnp.pad(norm_columns, ((0, 0), (0, 124)))
+
+    def packs(which):
+        return (
+            jnp.concatenate(
+                [half_of(query_key_value_weight[0], which), half_of(output_weight[0], which), norm_columns],
+                axis=1,
+            ),
+            jnp.concatenate([half_of(gate_weight[0], which), half_of(up_weight[0], which)], axis=1),
+            half_of(down_weight[0], which),
+        )
+
+    own_packs = packs(core)
+    sent_packs = [to_core(pack) for pack in packs(1 - core)]
+    weights = [
+        [gathered(jnp.where(core == layer, own, sent)) for own, sent in zip(own_packs, sent_packs)]
+        for layer in range(2)
+    ]
+
+    seg = pick(seg_ids, sequence)
+    seg_rows = lax.dynamic_slice_in_dim(seg, block * span, span, 0)
+    seg_keys = jnp.concatenate(
+        [lax.dynamic_slice_in_dim(seg, (block ^ flip) * span, span, 0) for flip in (0, 2, 1, 3)]
+    )
+    begins = jnp.sum((seg[None, :] < seg_rows[:, None]).astype(jnp.int32), axis=1)
+    places = block * span + jnp.arange(span, dtype=jnp.int32) - begins
+    lanes = jnp.arange(128, dtype=jnp.int32) % HEAD
+    half = HEAD // 2
+    spread = 1000.0 ** (-2.0 * (lanes % half).astype(jnp.float32) / HEAD)
+    angles = places.astype(jnp.float32)[:, None] * spread[None, :]
+    cosine, sine = jnp.cos(angles), jnp.where(lanes < half, -1.0, 1.0) * jnp.sin(angles)
+
+    hidden = rows_of(tokens)
+    incoming = rows_of(cotangent)
+    kept, outputs = [], []
+    for layer in range(2):
+        first, gate_up, down = weights[layer]
+        queries, own = project_rows(place, hidden, cosine, sine, first)
+        from_z = along_z(own)
+        blocks = [own, to_core(own), from_z, to_core(from_z)]
+        attended = attend_rows(queries, blocks, seg_rows[:, None], seg_keys[None, :])
+        output, one, two, acts, gate, up = mlp_rows(place, hidden, attended, first, gate_up, down)
+        kept.append((hidden, queries, blocks, attended, one, two, acts, gate, up))
+        outputs.append(output)
+        hidden = output
+
+    totals, input_rows = [None, None], [None, None]
+    ff = acts.shape[1] - width
+    for layer in (1, 0):
+        first, gate_up, down = weights[layer]
+        hidden, queries, blocks, attended, one, two, acts, gate, up = kept[layer]
+        both = lambda value: (value, to_core(value))
+        keep, send, dresid_one, dattended, sums = mlp_rows_back(
+            place, incoming, one, two, gate, up, first, gate_up, down
+        )
+        right = (keep, to_core(send))
+        acts = both(acts)
+        low = lambda value: (value, wide(to_core(lowered(value))))
+        totals[layer] = [
+            reduced(grad_parts(place, acts, right, (0, width), (0, ff)), ctx_rank),
+            reduced(grad_parts(place, acts, right, (width, width + ff), (ff, ff + width // 2)), ctx_rank),
+            reduced(
+                grad_parts(
+                    place, both(attended), right, (0, width), (ff + width // 2, ff + width), low(sums)
+                ),
+                ctx_rank,
+            ),
+        ]
+        dqueries, own, near, across = attend_rows_back(
+            queries, blocks, seg_rows[None, :], seg_keys[:, None], dattended
+        )
+        across = to_core(across)
+        from_z = along_z(lowered(wide(near) + wide(across[1])))
+        keep, send, dhidden = project_rows_back(
+            place, dqueries, (own, across[0], from_z), dresid_one, cosine, sine, first
+        )
+        totals[layer].append(
+            reduced(
+                grad_parts(place, both(hidden), (keep, to_core(send)), (0, width), (0, 3 * width // 2)),
+                ctx_rank,
+            )
+        )
+        input_rows[layer] = dhidden
+        incoming = lowered(dhidden)
+
+    def whole(first, second):
+        from_first = to_core(first, ((1, 0),))
+        from_second = to_core(second, ((0, 1),))
+        return jnp.where(core == 0, first, second), jnp.where(core == 0, from_first, from_second)
+
+    pairs = [whole(first, second) for first, second in zip(*totals)]
+    joined = lambda index, begin, end: wide(
+        by_core(core, pairs[index][0][:, begin:end], pairs[index][1][:, begin:end], 1)
+    )[None]
+    norm_grads = wide(pairs[2][0][:, width // 2 : width // 2 + 4]).T
+
+    def placed_rows(first, second):
+        first, second = lowered(first), lowered(second)
+        near = jnp.where(core == 0, first, to_core(second, ((0, 1),)))
+        swapped = z_swap(jnp.stack([first, second]))
+        far = jnp.where(core == 0, to_core(swapped[0], ((1, 0),)), swapped[1])
+        return jnp.where(sequence == 0, jnp.stack([near, far]), jnp.stack([far, near]))[None]
+
+    return (
+        placed_rows(*outputs),
+        wide(placed_rows(*input_rows)),
+        joined(3, 0, 3 * width // 2),
+        joined(2, 0, width // 2),
+        joined(0, 0, ff // 2),
+        joined(0, ff // 2, ff),
+        joined(1, 0, width // 2),
+        *(norm_grads[i : i + 1] for i in range(4)),
+    )
+
+
 def solution(mesh):
     placed = (
         P("dp", "ctx", None),
@@ -469,8 +1177,9 @@
         P("section", "dp"),
         P("dp", "ctx", None),
     )
+    paired = mesh.shape["section"] == 2 and mesh.shape["ctx"] == 4 and mesh.shape["dp"] == 4
     return jax.shard_map(
-        on_device,
+        paired_on_device if paired else relay_on_device,
         mesh=mesh,
         in_specs=placed,
         out_specs=(

time: 1460 us -> 880 us (0.60)
  waiting for transfers between devices: 912 us -> 413 us
  matrix products: 313 us -> 0 us
  Pallas kernels: 0 us -> 190 us
  starting transfers between devices: 8.68 us -> 169 us
  local copies, waits for them, and re-layouts: 88.6 us -> 45.9 us
  other arithmetic: 89.9 us -> 52.2 us
  blocking collectives: 20.1 us -> 0 us
    ppermute x4 -> x151, waiting for transfers between devices: 2.44 us -> 413 us  [the longest x28 164 us: along_y(): return lax.ppermute(value, 'dp', [(i, i ^ 2) for i in range(4)])]
    all_gather x11 -> x0, waiting for transfers between devices: 395 us -> none  [the longest x3 95.9 us: layer_forward(): lax.all_gather(key_rows, 'ctx', axis=1, tiled=True)]
    reduce_scatter x11 -> x0, waiting for transfers between devices: 328 us -> none  [the longest x3 66.2 us: layer_backward(): lax.psum_scatter(dvalues_all.astype(jnp.bfloat16), 'ctx', scatter_dimensi...]
    dot_general x66 -> x0, matrix products: 313 us -> none  [the longest x3 36.7 us: attend_back(): jnp.einsum('qhd,khd->hqk', heads_in, all_values.reshape(key_count, head_c...]
    pallas_call x0 -> x20, Pallas kernels: none -> 190 us  [the longest x8 46 us: grad_parts(): kernel_call(body, [shape_of((count, out_width), jnp.bfloat16), shape_of((...]
    ppermute x4 -> x151, starting transfers between devices: 6.54 us -> 169 us  [the longest x63 55.7 us: to_core(): return lax.ppermute(value, 'section', list(pairs))]
    psum x1 -> x0, waiting for transfers between devices: 159 us -> none  [on_device(): lax.psum(for_sending(summed), 'ctx')]
    unnamed x25 -> x0, waiting for transfers between devices: 27 us -> none
  transfers between devices with their start and end apart: 28 -> 151, of which waited for: 24 -> 48; matrix products, arithmetic and copies ran while one was open for 16% -> 8% of each run, Pallas kernels for 0% -> 20%
where the time goes in v2:
time: 880 us; the launch traced here: 873 us
  waiting for transfers between devices  413 us (47%)
  Pallas kernels  190 us (22%)
  starting transfers between devices  169 us (19%)
  other arithmetic  52.2 us (6%)
  local copies, waits for them, and re-layouts  45.9 us (5%)
    ppermute x28, waiting for transfers between devices, along_y(): return lax.ppermute(value, 'dp', [(i, i ^ 2) for i in range(4)])  164 us
    ppermute x28, waiting for transfers between devices, along_x(): return lax.ppermute(value, 'dp', [(i, i ^ 1) for i in range(4)])  106 us
    ppermute x8, waiting for transfers between devices, reduced(): outer = lax.ppermute(total, 'ctx', [(1, 0), (2, 3)])  75.9 us
    ppermute x63, starting transfers between devices, to_core(): return lax.ppermute(value, 'section', list(pairs))  55.7 us
    ppermute x8, waiting for transfers between devices, reduced(): inner = lax.ppermute(summed, 'ctx', [(0, 1), (3, 2)])  47.5 us
    pallas_call x8, Pallas kernels, grad_parts(): kernel_call(body, [shape_of((count, out_width), jnp.bfloat16), shape_of((...  46 us
    pallas_call x2, Pallas kernels, mlp_rows_back(): kernel_call(body, [shape_of((rows, ff + width), jnp.bfloat16), shape_of((...  41.7 us
    ppermute x28, starting transfers between devices, along_y(): return lax.ppermute(value, 'dp', [(i, i ^ 2) for i in range(4)])  38.1 us
  transfers between devices with their start and end apart: 151, of which 48 were waited for; matrix products, arithmetic and copies ran while one was open for 8% of the time, Pallas kernels for 20%

profile of v2, /device:TPU:0, one launch (start us, length us, event | category | flops | bytes accessed | tf_op | source)
XLA Modules:
  0.0 872.9 jit_solution(12996934406812506512)
XLA Ops:
  17.9 8.6 collective-permute-start.29
  38.5 22.7 %collective-permute-done.56.refs_22_ = bf16[768,384]{1,0:T(8,128)(2,1)S(1)} collective-permute-done((bf16[768,384]{1,0:T(8,128)(2,1)}, bf16[768,384]{1,0:T(8,128)(2,1)S(1)}, u32[]{:S(2)}, u32[]{:S(2)}) %collective-permute-start.56) | collective-permute-done | bytes 589856 | tf_op jit(solution)/shard_map/ppermute | solution.py:964
  116.8 17.6 %collective-permute-done.16.refs_12_ = bf16[192,3072]{1,0:T(8,128)(2,1)} collective-permute-done((bf16[192,3072]{1,0:T(8,128)(2,1)S(1)}, bf16[192,3072]{1,0:T(8,128)(2,1)}, u32[]{:S(2)}, u32[]{:S(2)}) %collective-permute-start.16) | collective-permute-done | bytes 1179680 | tf_op jit(solution)/shard_map/ppermute | solution.py:964
  142.0 9.3 %collective-permute-done.17.refs_13_ = bf16[96,3072]{1,0:T(8,128)(2,1)S(1)} collective-permute-done((bf16[96,3072]{1,0:T(8,128)(2,1)S(1)}, bf16[96,3072]{1,0:T(8,128)(2,1)S(1)}, u32[]{:S(2)}, u32[]{:S(2)}) %collective-permute-start.17) | collective-permute-done | bytes 589856 | tf_op jit(solution)/shard_map/ppermute | solution.py:960
  175.1 16.1 %mlp_rows.2 = (bf16[256,768]{1,0:T(8,128)(2,1)}, f32[256,768]{1,0:T(8,128)}, f32[256,768]{1,0:T(8,128)}, bf16[256,3840]{1,0:T(8,128)(2,1)}, f32[256,3072]{1,0:T(8,128)}, /*index=5*/f32[256,3072]{1,0:T(8,128)}) custom-call(s32[2]{0:T(128)} %copy-done.58, bf16[256,768]{1,0:T(8,128)(2,1)} %copy-done.44, bf16[256,768]{1,0:T(8,128)(2,1)} %copy-done.52, ...), custom_call_target="tpu_custom_call" | custom-call | flops 3925868544 | bytes 15335424 | tf_op jit(solution)/shard_map/mlp_rows/pallas_call | solution.py:741
  203.0 11.7 %collective-permute-done.44.b2 = bf16[2,256,768]{2,1,0:T(8,128)(2,1)S(1)} collective-permute-done((bf16[2,256,768]{2,1,0:T(8,128)(2,1)S(1)}, bf16[2,256,768]{2,1,0:T(8,128)(2,1)S(1)}, u32[]{:S(2)}, u32[]{:S(2)}) %collective-permute-start.44) | collective-permute-done | bytes 786464 | tf_op jit(solution)/shard_map/ppermute | solution.py:968
  230.6 16.4 %mlp_rows.3 = (bf16[256,768]{1,0:T(8,128)(2,1)}, f32[256,768]{1,0:T(8,128)}, f32[256,768]{1,0:T(8,128)}, bf16[256,3840]{1,0:T(8,128)(2,1)}, f32[256,3072]{1,0:T(8,128)}, /*index=5*/f32[256,3072]{1,0:T(8,128)}) custom-call(s32[2]{0:T(128)} %copy-done.58, bf16[256,768]{1,0:T(8,128)(2,1)} %get-tuple-element.93.hidden_ref.l0, bf16[256,768]{1,0:T(8,128)(2,1)} %copy-done.54, ...), custom_call_target="tpu_custom_call" | custom-call | flops 3925868544 | bytes 15335424 | tf_op jit(solution)/shard_map/mlp_rows/pallas_call | solution.py:741
  248.8 20.8 %mlp_rows_back.2 = (bf16[256,3840]{1,0:T(8,128)(2,1)}, bf16[256,3840]{1,0:T(8,128)(2,1)}, f32[256,768]{1,0:T(8,128)}, bf16[256,768]{1,0:T(8,128)(2,1)}, f32[8,768]{1,0:T(8,128)}) custom-call(s32[2]{0:T(128)} %copy-done.58, bf16[256,768]{1,0:T(8,128)(2,1)} %bitcast_select_fusion.2.in_ref, f32[256,768]{1,0:T(8,128)} %get-tuple-element.97.one_ref, ...), custom_call_target="tpu_custom_call" | custom-call | flops 3925868544 | bytes 15335424 | tf_op jit(solution)/shard_map/mlp_rows_back/pallas_call | solution.py:827
  269.7 18.4 %attend_rows_back.2 = (f32[256,768]{1,0:T(8,128)}, bf16[2,256,768]{2,1,0:T(8,128)(2,1)}, bf16[2,256,768]{2,1,0:T(8,128)(2,1)}, bf16[2,2,256,768]{3,2,1,0:T(8,128)(2,1)}) custom-call(s32[1,256]{1,0:T(1,128)} %copy-done.157, s32[1024,1]{1,0:T(8,128)} %copy.56.col_ref, bf16[256,768]{1,0:T(8,128)(2,1)} %copy-done.80, ...), custom_call_target="tpu_custom_call" | custom-call | flops 8053063680 | bytes 9437184 | tf_op jit(solution)/shard_map/attend_rows_back/pallas_call | solution.py:647
  367.0 20.9 %mlp_rows_back.3 = (bf16[256,3840]{1,0:T(8,128)(2,1)}, bf16[256,3840]{1,0:T(8,128)(2,1)}, f32[256,768]{1,0:T(8,128)}, bf16[256,768]{1,0:T(8,128)(2,1)}, f32[8,768]{1,0:T(8,128)}) custom-call(s32[2]{0:T(128)} %copy-done.58, bf16[256,768]{1,0:T(8,128)(2,1)} %convert_element_type.563.in_ref, f32[256,768]{1,0:T(8,128)} %get-tuple-element.108.one_ref, ...), custom_call_target="tpu_custom_call" | custom-call | flops 3925868544 | bytes 15335424 | tf_op jit(solution)/shard_map/mlp_rows_back/pallas_call | solution.py:827
  388.7 18.4 %attend_rows_back.3 = (f32[256,768]{1,0:T(8,128)}, bf16[2,256,768]{2,1,0:T(8,128)(2,1)}, bf16[2,256,768]{2,1,0:T(8,128)(2,1)}, bf16[2,2,256,768]{3,2,1,0:T(8,128)(2,1)}) custom-call(s32[1,256]{1,0:T(1,128)} %copy-done.157, s32[1024,1]{1,0:T(8,128)} %copy.56.col_ref, bf16[256,768]{1,0:T(8,128)(2,1)} %copy-done.78, ...), custom_call_target="tpu_custom_call" | custom-call | flops 8053063680 | bytes 9437184 | tf_op jit(solution)/shard_map/attend_rows_back/pallas_call | solution.py:647
  421.0 21.9 %collective-permute-done.145 = bf16[384,384]{1,0:T(8,128)(2,1)S(1)} collective-permute-done((bf16[384,384]{1,0:T(8,128)(2,1)S(1)}, bf16[384,384]{1,0:T(8,128)(2,1)S(1)}, u32[]{:S(2)}, u32[]{:S(2)}) %collective-permute-start.145) | collective-permute-done | bytes 294944 | tf_op jit(solution)/shard_map/ppermute | solution.py:960
  452.4 17.7 %collective-permute-done.128 = bf16[192,3072]{1,0:T(8,128)(2,1)S(1)} collective-permute-done((bf16[192,3072]{1,0:T(8,128)(2,1)}, bf16[192,3072]{1,0:T(8,128)(2,1)S(1)}, u32[]{:S(2)}, u32[]{:S(2)}) %collective-permute-start.128) | collective-permute-done | bytes 1179680 | tf_op jit(solution)/shard_map/ppermute | solution.py:964
  471.2 9.2 %collective-permute-done.86 = bf16[192,1152]{1,0:T(8,128)(2,1)S(1)} collective-permute-done((bf16[192,1152]{1,0:T(8,128)(2,1)S(1)}, bf16[192,1152]{1,0:T(8,128)(2,1)S(1)}, u32[]{:S(2)}, u32[]{:S(2)}) %collective-permute-start.86) | collective-permute-done | bytes 442400 | tf_op jit(solution)/shard_map/ppermute | solution.py:960
  506.1 12.9 %collective-permute-done.127 = bf16[96,3072]{1,0:T(8,128)(2,1)S(1)} collective-permute-done((bf16[96,3072]{1,0:T(8,128)(2,1)S(1)}, bf16[96,3072]{1,0:T(8,128)(2,1)S(1)}, u32[]{:S(2)}, u32[]{:S(2)}) %collective-permute-start.127) | collective-permute-done | bytes 589856 | tf_op jit(solution)/shard_map/ppermute | solution.py:964
  520.0 12.1 %collective-permute-done.129 = bf16[96,3072]{1,0:T(8,128)(2,1)S(1)} collective-permute-done((bf16[96,3072]{1,0:T(8,128)(2,1)S(1)}, bf16[96,3072]{1,0:T(8,128)(2,1)S(1)}, u32[]{:S(2)}, u32[]{:S(2)}) %collective-permute-start.129) | collective-permute-done | bytes 589856 | tf_op jit(solution)/shard_map/ppermute | solution.py:960
  608.5 11.9 %collective-permute-done.102 = bf16[192,512]{1,0:T(8,128)(2,1)S(1)} collective-permute-done((bf16[192,512]{1,0:T(8,128)(2,1)S(1)}, bf16[192,512]{1,0:T(8,128)(2,1)S(1)}, u32[]{:S(2)}, u32[]{:S(2)}) %collective-permute-start.102) | collective-permute-done | bytes 196640 | tf_op jit(solution)/shard_map/ppermute | solution.py:1017
  623.9 9.6 %collective-permute-done.137 = bf16[768,384]{1,0:T(8,128)(2,1)S(1)} collective-permute-done((bf16[768,384]{1,0:T(8,128)(2,1)S(1)}, bf16[768,384]{1,0:T(8,128)(2,1)S(1)}, u32[]{:S(2)}, u32[]{:S(2)}) %collective-permute-start.137) | collective-permute-done | bytes 589856 | tf_op jit(solution)/shard_map/ppermute | solution.py:964
  681.5 8.5 collective-permute-done.77
  692.3 18.7 %collective-permute-done.78 = bf16[96,1152]{1,0:T(8,128)(2,1)S(1)} collective-permute-done((bf16[96,1152]{1,0:T(8,128)(2,1)S(1)}, bf16[96,1152]{1,0:T(8,128)(2,1)S(1)}, u32[]{:S(2)}, u32[]{:S(2)}) %collective-permute-start.78) | collective-permute-done | bytes 221216 | tf_op jit(solution)/shard_map/ppermute | solution.py:964
  720.5 10.0 %collective-permute-done.121 = bf16[96,3072]{1,0:T(8,128)(2,1)S(1)} collective-permute-done((bf16[96,3072]{1,0:T(8,128)(2,1)S(1)}, bf16[96,3072]{1,0:T(8,128)(2,1)S(1)}, u32[]{:S(2)}, u32[]{:S(2)}) %collective-permute-start.121) | collective-permute-done | bytes 589856 | tf_op jit(solution)/shard_map/ppermute | solution.py:960
  736.0 31.4 %collective-permute-done.81 = bf16[192,1152]{1,0:T(8,128)(2,1)S(1)} collective-permute-done((bf16[192,1152]{1,0:T(8,128)(2,1)S(1)}, bf16[192,1152]{1,0:T(8,128)(2,1)S(1)}, u32[]{:S(2)}, u32[]{:S(2)}) %collective-permute-start.81) | collective-permute-done | bytes 442400 | tf_op jit(solution)/shard_map/ppermute | solution.py:1017
  776.5 50.3 %collective-permute-done.141 = bf16[768,384]{1,0:T(8,128)(2,1)S(1)} collective-permute-done((bf16[768,384]{1,0:T(8,128)(2,1)S(1)}, bf16[768,384]{1,0:T(8,128)(2,1)S(1)}, u32[]{:S(2)}, u32[]{:S(2)}) %collective-permute-start.141) | collective-permute-done | bytes 589856 | tf_op jit(solution)/shard_map/ppermute | solution.py:1021
  843.6 18.0 %collective-permute-done.124 = bf16[192,3072]{1,0:T(8,128)(2,1)S(1)} collective-permute-done((bf16[192,3072]{1,0:T(8,128)(2,1)S(1)}, bf16[192,3072]{1,0:T(8,128)(2,1)S(1)}, u32[]{:S(2)}, u32[]{:S(2)}) %collective-permute-start.124) | collective-permute-done | bytes 1179680 | tf_op jit(solution)/shard_map/ppermute | solution.py:1021
  (770 shorter events, 455.8 us)
Async XLA Ops:
  37.0 40.3 %collective-permute-start.34 = (bf16[192,1664]{1,0:T(8,128)(2,1)S(1)}, bf16[192,1664]{1,0:T(8,128)(2,1)S(1)}, u32[]{:S(2)}, u32[]{:S(2)}) collective-permute-start(bf16[192,1664]{1,0:T(8,128)(2,1)S(1)} %get-tuple-element.231.refs_0_), channel_id=1, source_target_pairs={{0,1},{1,0},{2,3},{3,2},{4,5},{5,4},{6,7},{7,6},{8,9},{9,8},{10,11... | collective-permute-start | bytes 1916936 | tf_op jit(solution)/shard_map/ppermute | solution.py:960
  155.4 41.2 %collective-permute-start.47 = (bf16[192,3072]{1,0:T(8,128)(2,1)}, bf16[192,3072]{1,0:T(8,128)(2,1)}, u32[]{:S(2)}, u32[]{:S(2)}) collective-permute-start(bf16[192,3072]{1,0:T(8,128)(2,1)} %get-tuple-element.227.refs_10_), channel_id=1, source_target_pairs={{0,2},{1,3},{2,0},{3,1},{4,6},{5,7},{6,4},{7,5},{8,10},{9,11},{10,... | collective-permute-start | bytes 3538952 | tf_op jit(solution)/shard_map/ppermute | solution.py:964
  156.9 40.1 %collective-permute-start.46 = (bf16[192,3072]{1,0:T(8,128)(2,1)}, bf16[192,3072]{1,0:T(8,128)(2,1)}, u32[]{:S(2)}, u32[]{:S(2)}) collective-permute-start(bf16[192,3072]{1,0:T(8,128)(2,1)} %get-tuple-element.227.refs_10_), channel_id=1, source_target_pairs={{0,1},{1,0},{2,3},{3,2},{4,5},{5,4},{6,7},{7,6},{8,9},{9,8},{10,11... | collective-permute-start | bytes 3538952 | tf_op jit(solution)/shard_map/ppermute | solution.py:960
  248.1 47.1 %collective-permute-start.65 = (bf16[2,256,768]{2,1,0:T(8,128)(2,1)S(1)}, bf16[2,256,768]{2,1,0:T(8,128)(2,1)S(1)}, u32[]{:S(2)}, u32[]{:S(2)}) collective-permute-start(bf16[2,256,768]{2,1,0:T(8,128)(2,1)S(1)} %pad_maximum_fusion.2), channel_id=1, source_target_pairs={{16,24},{20,28},{24,16},{28,20},{17,25},{21,29},{25,17},{29,21},{1... | collective-permute-start | bytes 2359304 | tf_op jit(solution)/shard_map/ppermute | solution.py:973
  302.9 351.3 %collective-permute-start.75 = (bf16[256,768]{1,0:T(8,128)(2,1)S(1)}, bf16[256,768]{1,0:T(8,128)(2,1)}, u32[]{:S(2)}, u32[]{:S(2)}) collective-permute-start(bf16[256,768]{1,0:T(8,128)(2,1)S(1)} %copy-done.45), channel_id=1, source_target_pairs={{0,16},{16,0},{1,17},{17,1},{2,18},{18,2},{3,19},{19,3},{4,20},{20... | collective-permute-start | bytes 1179656 | tf_op jit(solution)/shard_map/ppermute | solution.py:956
  310.2 48.4 %collective-permute-start.69 = (bf16[2,256,768]{2,1,0:T(8,128)(2,1)}, bf16[2,256,768]{2,1,0:T(8,128)(2,1)}, u32[]{:S(2)}, u32[]{:S(2)}) collective-permute-start(bf16[2,256,768]{2,1,0:T(8,128)(2,1)} %fusion.3), channel_id=1, source_target_pairs={{0,4},{4,0},{8,12},{12,8},{1,5},{5,1},{9,13},{13,9},{2,6},{6,2},{1... | collective-permute-start | bytes 2359304 | tf_op jit(solution)/shard_map/ppermute | solution.py:968
  322.3 87.1 %collective-permute-start.142 = (bf16[768,384]{1,0:T(8,128)(2,1)}, bf16[768,384]{1,0:T(8,128)(2,1)}, u32[]{:S(2)}, u32[]{:S(2)}) collective-permute-start(bf16[768,384]{1,0:T(8,128)(2,1)} %get-tuple-element.167), channel_id=1, source_target_pairs={{0,1},{1,0},{2,3},{3,2},{4,5},{5,4},{6,7},{7,6},{8,9},{9,8},{10,11... | collective-permute-start | bytes 1769480 | tf_op jit(solution)/shard_map/ppermute | solution.py:960
  323.1 88.0 %collective-permute-start.144 = (bf16[768,384]{1,0:T(8,128)(2,1)}, bf16[768,384]{1,0:T(8,128)(2,1)}, u32[]{:S(2)}, u32[]{:S(2)}) collective-permute-start(bf16[768,384]{1,0:T(8,128)(2,1)} %get-tuple-element.169), channel_id=1, source_target_pairs={{0,2},{1,3},{2,0},{3,1},{4,6},{5,7},{6,4},{7,5},{8,10},{9,11},{10,... | collective-permute-start | bytes 1769480 | tf_op jit(solution)/shard_map/ppermute | solution.py:964
  356.2 52.2 %collective-permute-start.112 = (bf16[192,512]{1,0:T(8,128)(2,1)S(1)}, bf16[192,512]{1,0:T(8,128)(2,1)S(1)}, u32[]{:S(2)}, u32[]{:S(2)}) collective-permute-start(bf16[192,512]{1,0:T(8,128)(2,1)S(1)} %fusion.21), channel_id=1, source_target_pairs={{0,4},{12,8},{1,5},{13,9},{2,6},{14,10},{3,7},{15,11},{16,20},{28,... | collective-permute-start | bytes 589832 | tf_op jit(solution)/shard_map/ppermute | solution.py:1017
  408.4 42.3 %collective-permute-start.126 = (bf16[192,3072]{1,0:T(8,128)(2,1)}, bf16[192,3072]{1,0:T(8,128)(2,1)S(1)}, u32[]{:S(2)}, u32[]{:S(2)}) collective-permute-start(bf16[192,3072]{1,0:T(8,128)(2,1)} %get-tuple-element.157), channel_id=1, source_target_pairs={{0,1},{1,0},{2,3},{3,2},{4,5},{5,4},{6,7},{7,6},{8,9},{9,8},{10,11... | collective-permute-start | bytes 3538952 | tf_op jit(solution)/shard_map/ppermute | solution.py:960
  445.1 107.6 %collective-permute-start.117 = (bf16[256,3840]{1,0:T(8,128)(2,1)}, bf16[256,3840]{1,0:T(8,128)(2,1)}, u32[]{:S(2)}, u32[]{:S(2)}) collective-permute-start(bf16[256,3840]{1,0:T(8,128)(2,1)} %get-tuple-element.149.l0), channel_id=1, source_target_pairs={{0,16},{16,0},{1,17},{17,1},{2,18},{18,2},{3,19},{19,3},{4,20},{20... | collective-permute-start | bytes 5898248 | tf_op jit(solution)/shard_map/ppermute | solution.py:956
  445.8 101.3 %collective-permute-start.96 = (bf16[256,3840]{1,0:T(8,128)(2,1)}, bf16[256,3840]{1,0:T(8,128)(2,1)S(1)}, u32[]{:S(2)}, u32[]{:S(2)}) collective-permute-start(bf16[256,3840]{1,0:T(8,128)(2,1)} %get-tuple-element.134), channel_id=1, source_target_pairs={{0,16},{16,0},{1,17},{17,1},{2,18},{18,2},{3,19},{19,3},{4,20},{20... | collective-permute-start | bytes 5898248 | tf_op jit(solution)/shard_map/ppermute | solution.py:956
  489.8 43.5 %collective-permute-start.70 = (bf16[2,2,256,768]{3,2,1,0:T(8,128)(2,1)S(1)}, bf16[2,2,256,768]{3,2,1,0:T(8,128)(2,1)S(1)}, u32[]{:S(2)}, u32[]{:S(2)}) collective-permute-start(bf16[2,2,256,768]{3,2,1,0:T(8,128)(2,1)S(1)} %copy-done.159), channel_id=1, source_target_pairs={{0,16},{16,0},{1,17},{17,1},{2,18},{18,2},{3,19},{19,3},{4,20},{20... | collective-permute-start | bytes 4718600 | tf_op jit(solution)/shard_map/ppermute | solution.py:956
  544.3 59.8 %collective-permute-start.72 = (bf16[256,768]{1,0:T(8,128)(2,1)S(1)}, bf16[256,768]{1,0:T(8,128)(2,1)}, u32[]{:S(2)}, u32[]{:S(2)}) collective-permute-start(bf16[256,768]{1,0:T(8,128)(2,1)S(1)} %copy-done.106), channel_id=1, source_target_pairs={{0,16},{1,17},{2,18},{3,19},{4,20},{5,21},{6,22},{7,23},{8,24},{9,... | collective-permute-start | bytes 1179656 | tf_op jit(solution)/shard_map/ppermute | solution.py:956
  547.1 97.6 %collective-permute-start.114 = (bf16[192,512]{1,0:T(8,128)(2,1)S(1)}, bf16[192,512]{1,0:T(8,128)(2,1)S(1)}, u32[]{:S(2)}, u32[]{:S(2)}) collective-permute-start(bf16[192,512]{1,0:T(8,128)(2,1)S(1)} %add_convert_fusion.24), channel_id=1, source_target_pairs={{4,0},{8,12},{5,1},{9,13},{6,2},{10,14},{7,3},{11,15},{20,16},{24,... | collective-permute-start | bytes 589832 | tf_op jit(solution)/shard_map/ppermute | solution.py:1021
  552.6 44.7 %collective-permute-start.71 = (bf16[2,256,768]{2,1,0:T(8,128)(2,1)}, bf16[2,256,768]{2,1,0:T(8,128)(2,1)}, u32[]{:S(2)}, u32[]{:S(2)}) collective-permute-start(bf16[2,256,768]{2,1,0:T(8,128)(2,1)} %fusion.2), channel_id=1, source_target_pairs={{0,4},{4,0},{8,12},{12,8},{1,5},{5,1},{9,13},{13,9},{2,6},{6,2},{1... | collective-permute-start | bytes 2359304 | tf_op jit(solution)/shard_map/ppermute | solution.py:968
  621.5 50.5 %collective-permute-start.118 = (bf16[192,3072]{1,0:T(8,128)(2,1)}, bf16[192,3072]{1,0:T(8,128)(2,1)}, u32[]{:S(2)}, u32[]{:S(2)}) collective-permute-start(bf16[192,3072]{1,0:T(8,128)(2,1)} %get-tuple-element.151), channel_id=1, source_target_pairs={{0,1},{1,0},{2,3},{3,2},{4,5},{5,4},{6,7},{7,6},{8,9},{9,8},{10,11... | collective-permute-start | bytes 3538952 | tf_op jit(solution)/shard_map/ppermute | solution.py:960
  662.3 112.8 %collective-permute-start.148 = (bf16[768,384]{1,0:T(8,128)(2,1)S(1)}, bf16[768,384]{1,0:T(8,128)(2,1)S(1)}, u32[]{:S(2)}, u32[]{:S(2)}) collective-permute-start(bf16[768,384]{1,0:T(8,128)(2,1)S(1)} %add_convert_fusion.4), channel_id=1, source_target_pairs={{4,0},{8,12},{5,1},{9,13},{6,2},{10,14},{7,3},{11,15},{20,16},{24,... | collective-permute-start | bytes 1769480 | tf_op jit(solution)/shard_map/ppermute | solution.py:1021
  668.0 160.4 %collective-permute-start.92 = (bf16[192,1152]{1,0:T(8,128)(2,1)S(1)}, bf16[192,1152]{1,0:T(8,128)(2,1)S(1)}, u32[]{:S(2)}, u32[]{:S(2)}) collective-permute-start(bf16[192,1152]{1,0:T(8,128)(2,1)S(1)} %copy-done.104), channel_id=1, source_target_pairs={{4,0},{8,12},{5,1},{9,13},{6,2},{10,14},{7,3},{11,15},{20,16},{24,... | collective-permute-start | bytes 1327112 | tf_op jit(solution)/shard_map/ppermute | solution.py:1021
  672.0 61.7 %collective-permute-start.139 = (bf16[768,384]{1,0:T(8,128)(2,1)S(1)}, bf16[768,384]{1,0:T(8,128)(2,1)S(1)}, u32[]{:S(2)}, u32[]{:S(2)}) collective-permute-start(bf16[768,384]{1,0:T(8,128)(2,1)S(1)} %fusion.7), channel_id=1, source_target_pairs={{0,4},{12,8},{1,5},{13,9},{2,6},{14,10},{3,7},{15,11},{16,20},{28,... | collective-permute-start | bytes 1769480 | tf_op jit(solution)/shard_map/ppermute | solution.py:1017
  770.5 73.2 %collective-permute-start.132 = (bf16[192,3072]{1,0:T(8,128)(2,1)S(1)}, bf16[192,3072]{1,0:T(8,128)(2,1)S(1)}, u32[]{:S(2)}, u32[]{:S(2)}) collective-permute-start(bf16[192,3072]{1,0:T(8,128)(2,1)S(1)} %add_convert_fusion), channel_id=1, source_target_pairs={{4,0},{8,12},{5,1},{9,13},{6,2},{10,14},{7,3},{11,15},{20,16},{24,... | collective-permute-start | bytes 3538952 | tf_op jit(solution)/shard_map/ppermute | solution.py:1021
  771.9 54.9 %collective-permute-start.141 = (bf16[768,384]{1,0:T(8,128)(2,1)S(1)}, bf16[768,384]{1,0:T(8,128)(2,1)S(1)}, u32[]{:S(2)}, u32[]{:S(2)}) collective-permute-start(bf16[768,384]{1,0:T(8,128)(2,1)S(1)} %add_convert_fusion.6), channel_id=1, source_target_pairs={{4,0},{8,12},{5,1},{9,13},{6,2},{10,14},{7,3},{11,15},{20,16},{24,... | collective-permute-start | bytes 1769480 | tf_op jit(solution)/shard_map/ppermute | solution.py:1021
  773.4 63.0 %collective-permute-start.83 = (bf16[192,1152]{1,0:T(8,128)(2,1)S(1)}, bf16[192,1152]{1,0:T(8,128)(2,1)S(1)}, u32[]{:S(2)}, u32[]{:S(2)}) collective-permute-start(bf16[192,1152]{1,0:T(8,128)(2,1)S(1)} %add_convert_fusion.14), channel_id=1, source_target_pairs={{4,0},{8,12},{5,1},{9,13},{6,2},{10,14},{7,3},{11,15},{20,16},{24,... | collective-permute-start | bytes 1327112 | tf_op jit(solution)/shard_map/ppermute | solution.py:1021
  775.1 86.5 %collective-permute-start.124 = (bf16[192,3072]{1,0:T(8,128)(2,1)S(1)}, bf16[192,3072]{1,0:T(8,128)(2,1)S(1)}, u32[]{:S(2)}, u32[]{:S(2)}) collective-permute-start(bf16[192,3072]{1,0:T(8,128)(2,1)S(1)} %add_convert_fusion.2), channel_id=1, source_target_pairs={{4,0},{8,12},{5,1},{9,13},{6,2},{10,14},{7,3},{11,15},{20,16},{24,... | collective-permute-start | bytes 3538952 | tf_op jit(solution)/shard_map/ppermute | solution.py:1021
  (295 other events, 4602.9 us)

commit v3 on v2

--- a/solution.py
+++ b/solution.py
@@ -485,7 +485,7 @@
         scratch_shapes=scratch,
         **({} if grid is None else {"grid": grid}),
         compiler_params=pltpu.CompilerParams(vmem_limit_bytes=mbytes * 2**20),
-        cost_estimate=pl.CostEstimate(flops=cost[0], bytes_accessed=cost[1], transcendentals=0),
+        cost_estimate=pl.CostEstimate(flops=0, bytes_accessed=3 * 10**6 * cost, transcendentals=0),
         name=name,
     )
 
@@ -494,25 +494,27 @@
     return jax.ShapeDtypeStruct(shape, dtype)
 
 
-def start_loads(place, pieces, first, width, scratch, sems, begin, rows=None):
+def start_loads(place, pieces, first, width, scratch, sems, begin, blocks=1):
     dp_rank, core = place[0], place[1]
     count = pieces[0].shape[0]
     copies = []
-    for index, piece in enumerate(pieces):
-        kind = index % 5
-        flip = min(kind, 3)
-        half = core if index < 5 else 1 - core
-        row = (dp_rank ^ flip) * count + (count // 2 if kind == 4 else 0)
-        copies.append(
-            pltpu.make_async_copy(
-                piece.at[:, pl.ds(first, width)],
-                scratch.at[
-                    pl.ds(pl.multiple_of(row, count // 2), piece.shape[0]),
-                    pl.ds(pl.multiple_of(half * width, 128), width),
-                ],
-                sems.at[begin + index],
+    cuts = ((0, 0, 2, 0, 0, 0), (1, 0, 2, 1, 0, 0), (2, 0, 2, 2, 0, 0), (3, 0, 1, 3, 0, 0), (4, 0, 1, 3, 1, 0))
+    cuts += ((5, 0, 2, 0, 0, 1), (6, 0, 2, 1, 0, 1), (6, 2, 2, 2, 0, 1), (7, 0, 2, 3, 0, 1))
+    unit = count // 2
+    for piece, source, size, flip, target, other in cuts:
+        half = 1 - core if other else core
+        for block in range(blocks):
+            row = ((dp_rank ^ flip) * blocks + block) * count + target * unit
+            copies.append(
+                pltpu.make_async_copy(
+                    pieces[piece].at[pl.ds(source * unit, size * unit), pl.ds(first + block * width, width)],
+                    scratch.at[
+                        pl.ds(pl.multiple_of(row, unit), size * unit),
+                        pl.ds(pl.multiple_of(half * width, 128), width),
+                    ],
+                    sems.at[begin + len(copies)],
+                )
             )
-        )
     for copy in copies:
         copy.start()
     return copies
@@ -536,7 +538,7 @@
     half = 3 * width // 2
 
     def body(place_ref, hidden_ref, cos_ref, sin_ref, *refs):
-        parts, (q_ref, kv_ref, weight, sems) = refs[:10], refs[10:]
+        parts, (q_ref, kv_ref, weight, sems) = refs[:8], refs[8:]
         wait_all(start_loads(place_ref, parts, 0, half, weight, sems, 0))
         for step in range(3 * width // 256):
             mixed = mm(hidden_ref[...], weight[:, step * 256 : step * 256 + 256])
@@ -556,27 +558,27 @@
     return kernel_call(
         body,
         [shape_of((rows, width), jnp.bfloat16), shape_of((2, rows, width), jnp.bfloat16)],
-        [in_smem()] + [in_vmem()] * 3 + [anywhere()] * 10,
+        [in_smem()] + [in_vmem()] * 3 + [anywhere()] * 8,
         [pltpu.VMEM((width, 3 * width), jnp.bfloat16), pltpu.SemaphoreType.DMA((10,))],
-        32,
-        (6 * rows * width * width, 6 * width * width + 8 * rows * width),
+        60,
+        3,
         "project_rows",
     )(place, hidden, cosine, sine, *pieces)
 
 
 def attend_rows(queries, blocks, seg_column, seg_row):
     rows, width = queries.shape
-    keys = 4 * rows
-
-    def body(col_ref, row_ref, q_ref, b0, b1, b2, b3, out_ref, bias):
+    keys = 2 * rows
+
+    def body(col_ref, row_ref, q_ref, b0, b1, out_ref, bias):
         @pl.when(pl.program_id(0) == 0)
         def _():
             bias[...] = jnp.where(col_ref[...] == row_ref[...], 0.0, NEG)
 
         lane = lax.broadcasted_iota(jnp.int32, (rows, 128), 1)
         query = q_ref[...]
-        key = jnp.concatenate([b[0] for b in (b0, b1, b2, b3)], axis=0)
-        value = jnp.concatenate([b[1] for b in (b0, b1, b2, b3)], axis=0)
+        key = jnp.concatenate([b[0] for b in (b0, b1)], axis=0)
+        value = jnp.concatenate([b[1] for b in (b0, b1)], axis=0)
         results = []
         for head in range(2):
             own = (lane < 64) if head == 0 else (lane >= 64)
@@ -595,11 +597,11 @@
             pl.BlockSpec((rows, 1), lambda j: (0, 0)),
             pl.BlockSpec((1, keys), lambda j: (0, 0)),
             pl.BlockSpec((rows, 128), lambda j: (0, j)),
-            block, block, block, block,
+            block, block,
         ],
         [pltpu.VMEM((rows, keys), jnp.float32)],
-        48,
-        (16 * rows * keys * width, 24 * rows * width),
+        60,
+        8,
         "attend_rows",
         [pl.BlockSpec((rows, 128), lambda j: (0, j))],
         (width // 128,),
@@ -608,17 +610,17 @@
 
 def attend_rows_back(queries, blocks, seg_row, seg_column, incoming):
     rows, width = queries.shape
-    keys = 4 * rows
-
-    def body(row_ref, col_ref, q_ref, in_ref, b0, b1, b2, b3, dq_ref, own_ref, z_ref, core_ref, bias):
+    keys = 2 * rows
+
+    def body(row_ref, col_ref, q_ref, in_ref, b0, b1, dq_ref, own_ref, core_ref, bias):
         @pl.when(pl.program_id(0) == 0)
         def _():
             bias[...] = jnp.where(col_ref[...] == row_ref[...], 0.0, NEG)
 
         lane = lax.broadcasted_iota(jnp.int32, (rows, 128), 1)
         query, given = q_ref[...], in_ref[...]
-        key = jnp.concatenate([b[0] for b in (b0, b1, b2, b3)], axis=0)
-        value = jnp.concatenate([b[1] for b in (b0, b1, b2, b3)], axis=0)
+        key = jnp.concatenate([b[0] for b in (b0, b1)], axis=0)
+        value = jnp.concatenate([b[1] for b in (b0, b1)], axis=0)
         key_t = key.T
         dkeys, dvalues, dqueries = [], [], []
         for head in range(2):
@@ -637,9 +639,7 @@
         for which, pair in enumerate((dkeys, dvalues)):
             both = jnp.where(wide, pair[0], pair[1]).astype(jnp.bfloat16)
             own_ref[which] = both[:rows]
-            core_ref[0, which] = both[rows : 2 * rows]
-            z_ref[which] = both[2 * rows : 3 * rows]
-            core_ref[1, which] = both[3 * rows :]
+            core_ref[which] = both[rows:]
 
     block = pl.BlockSpec((2, rows, 128), lambda j: (0, 0, j))
     columns = pl.BlockSpec((rows, 128), lambda j: (0, j))
@@ -650,18 +650,17 @@
             shape_of((rows, width), jnp.float32),
             pair_shape,
             pair_shape,
-            shape_of((2, 2, rows, width), jnp.bfloat16),
         ],
         [
             pl.BlockSpec((1, rows), lambda j: (0, 0)),
             pl.BlockSpec((keys, 1), lambda j: (0, 0)),
-            columns, columns, block, block, block, block,
+            columns, columns, block, block,
         ],
         [pltpu.VMEM((keys, rows), jnp.float32)],
-        56,
-        (40 * rows * keys * width, 48 * rows * width),
+        60,
+        18,
         "attend_rows_back",
-        [columns, block, block, pl.BlockSpec((2, 2, rows, 128), lambda j: (0, 0, 0, j))],
+        [columns, block, block],
         (width // 128,),
     )(seg_row, seg_column, queries, incoming, *blocks)
 
@@ -692,26 +691,26 @@
         pltpu.VMEM((hidden_width, width), jnp.bfloat16),
         pltpu.VMEM((width, 256), jnp.bfloat16),
         pltpu.VMEM((128, width), jnp.float32),
-        pltpu.SemaphoreType.DMA((50,)),
+        pltpu.SemaphoreType.DMA((80,)),
     ]
 
 
-def mlp_rows(place, hidden, attended, first_parts, gate_up_parts, down_parts):
+def mlp_rows(place, hidden, attended, first_parts, rest_parts):
     rows, width = hidden.shape
-    ff_half = gate_up_parts[0].shape[1] // 2
+    ff_half = (rest_parts[0].shape[1] - 2 * width) // 2
     ff = 2 * ff_half
 
     def body(place_ref, hidden_ref, att_ref, *refs):
-        parts, rest = refs[:30], refs[30:]
+        parts, rest = refs[:16], refs[16:]
         out_ref, one_ref, two_ref, acts_ref, gate_ref, up_ref = rest[:6]
         w_out, w_gate, w_up, w_down, w_norm, norm_ref, sems = rest[6:]
         normed_ref = acts_ref.at[:, :width]
-        norm_loads = start_loads(place_ref, parts[:10], 2 * width, 128, w_norm, sems, 40)
+        norm_loads = start_loads(place_ref, parts[:8], 2 * width, 128, w_norm, sems, 70)
         loads = [
-            start_loads(place_ref, parts[:10], 3 * width // 2, width // 2, w_out, sems, 0),
-            start_loads(place_ref, parts[10:20], 0, ff_half, w_gate, sems, 10),
-            start_loads(place_ref, parts[10:20], ff_half, ff_half, w_up, sems, 20),
-            start_loads(place_ref, parts[20:30], 0, width // 2, w_down, sems, 30),
+            start_loads(place_ref, parts[:8], 3 * width // 2, width // 2, w_out, sems, 0),
+            start_loads(place_ref, parts[8:], 0, ff_half, w_gate, sems, 10),
+            start_loads(place_ref, parts[8:], ff_half, ff_half, w_up, sems, 20),
+            start_loads(place_ref, parts[8:], 2 * ff_half, width // 2, w_down, sems, 30, 4),
         ]
         wait_all(norm_loads)
         norm_ref[...] = w_norm[:, :128].astype(jnp.float32).T
@@ -748,40 +747,40 @@
             shape_of((rows, ff), jnp.float32),
             shape_of((rows, ff), jnp.float32),
         ],
-        [in_smem()] + [in_vmem()] * 2 + [anywhere()] * 30,
+        [in_smem()] + [in_vmem()] * 2 + [anywhere()] * 16,
         mlp_scratch(width, ff),
-        56,
-        (2 * rows * width * (width + 3 * ff), 2 * width * (width + 3 * ff)),
+        60,
+        16,
         "mlp_rows",
-    )(place, hidden, attended, *first_parts, *gate_up_parts, *down_parts)
-
-
-def mlp_rows_back(place, incoming, one, two, gate, up, first_parts, gate_up_parts, down_parts):
+    )(place, hidden, attended, *first_parts, *rest_parts)
+
+
+def mlp_rows_back(place, incoming, one, two, gate, up, first_parts, rest_parts):
     rows, width = incoming.shape
-    ff_half = gate_up_parts[0].shape[1] // 2
+    ff_half = (rest_parts[0].shape[1] - 2 * width) // 2
     ff = 2 * ff_half
 
     def body(place_ref, in_ref, one_ref, two_ref, gate_ref, up_ref, *refs):
-        parts, rest = refs[:30], refs[30:]
-        keep_ref, send_ref, dresid_ref, datt_ref, sums_ref = rest[:5]
-        w_out, w_gate, w_up, w_down, w_norm, norm_ref, sems, low_ref = rest[5:]
+        parts, rest = refs[:16], refs[16:]
+        keep_ref, send_ref, keep_ff, send_ff, dresid_ref, datt_ref = rest[:6]
+        w_out, w_gate, w_up, w_down, w_norm, norm_ref, sems, low_ref, sums_ref = rest[6:]
         core = place_ref[1]
-        norm_loads = start_loads(place_ref, parts[:10], 2 * width, 128, w_norm, sems, 40)
-
-        def share(half, columns, value):
+        norm_loads = start_loads(place_ref, parts[:8], 2 * width, 128, w_norm, sems, 70)
+
+        def share(half, columns, value, keep, send):
             @pl.when(half == core)
             def _():
-                keep_ref[:, columns] = value
+                keep[:rows, columns] = value
 
             @pl.when(half != core)
             def _():
-                send_ref[:, columns] = value
+                send[:rows, columns] = value
 
         loads = [
-            start_loads(place_ref, parts[20:30], 0, width // 2, w_down, sems, 30),
-            start_loads(place_ref, parts[10:20], 0, ff_half, w_gate, sems, 10),
-            start_loads(place_ref, parts[10:20], ff_half, ff_half, w_up, sems, 20),
-            start_loads(place_ref, parts[:10], 3 * width // 2, width // 2, w_out, sems, 0),
+            start_loads(place_ref, parts[8:], 2 * ff_half, width // 2, w_down, sems, 30, 4),
+            start_loads(place_ref, parts[8:], 0, ff_half, w_gate, sems, 10),
+            start_loads(place_ref, parts[8:], ff_half, ff_half, w_up, sems, 20),
+            start_loads(place_ref, parts[:8], 3 * width // 2, width // 2, w_out, sems, 0),
         ]
         wait_all(norm_loads)
         norm_ref[...] = w_norm[:, :128].astype(jnp.float32).T
@@ -795,7 +794,7 @@
         low_ref[...] = dresid_two.astype(jnp.bfloat16)
         for half in range(2):
             span = slice(half * width // 2, (half + 1) * width // 2)
-            share(half, slice(ff, ff + width // 2), low_ref[:, span])
+            share(half, slice(0, width // 2), low_ref[:, span], keep_ref, send_ref)
         for copies in loads:
             wait_all(copies)
 
@@ -808,8 +807,8 @@
             dgate = (dmiddle * up_ref[:, span] * sig * (1.0 + gate_block * (1.0 - sig))).astype(jnp.bfloat16)
             dup = (dmiddle * (gate_block * sig)).astype(jnp.bfloat16)
             half, column = step // (ff_half // FF_STEP), step % (ff_half // FF_STEP) * FF_STEP
-            share(half, pl.ds(pl.multiple_of(column, 128), FF_STEP), dgate)
-            share(half, pl.ds(pl.multiple_of(column + ff_half, 128), FF_STEP), dup)
+            share(half, pl.ds(pl.multiple_of(column, 128), FF_STEP), dgate, keep_ff, send_ff)
+            share(half, pl.ds(pl.multiple_of(column + ff_half, 128), FF_STEP), dup, keep_ff, send_ff)
             dresid_ref[...] += mm(dgate, w_gate[:, span], NT) + mm(dup, w_up[:, span], NT)
 
         dnormed = dresid_ref[...]
@@ -821,24 +820,28 @@
         low_ref[...] = dresid_one.astype(jnp.bfloat16)
         for half in range(2):
             span = slice(half * width // 2, (half + 1) * width // 2)
-            share(half, slice(ff + width // 2, ff + width), low_ref[:, span])
+            share(half, slice(width // 2, width), low_ref[:, span], keep_ref, send_ref)
         datt_ref[...] = mm(low_ref[...], w_out[...], NT).astype(jnp.bfloat16)
+        for ref in (keep_ref, send_ref):
+            ref[rows:] = sums_ref[...].astype(jnp.bfloat16)
 
     return kernel_call(
         body,
         [
-            shape_of((rows, ff + width), jnp.bfloat16),
-            shape_of((rows, ff + width), jnp.bfloat16),
+            shape_of((rows + 16, width), jnp.bfloat16),
+            shape_of((rows + 16, width), jnp.bfloat16),
+            shape_of((rows, ff), jnp.bfloat16),
+            shape_of((rows, ff), jnp.bfloat16),
             shape_of((rows, width), jnp.float32),
             shape_of((rows, width), jnp.bfloat16),
-            shape_of((8, width), jnp.float32),
         ],
-        [in_smem()] + [in_vmem()] * 5 + [anywhere()] * 30,
-        mlp_scratch(width, ff) + [pltpu.VMEM((rows, width), jnp.bfloat16)],
-        56,
-        (2 * rows * width * (width + 3 * ff), 2 * width * (width + 3 * ff)),
+        [in_smem()] + [in_vmem()] * 5 + [anywhere()] * 16,
+        mlp_scratch(width, ff)
+        + [pltpu.VMEM((rows, width), jnp.bfloat16), pltpu.VMEM((16, width), jnp.float32)],
+        60,
+        21,
         "mlp_rows_back",
-    )(place, incoming, one, two, gate, up, *first_parts, *gate_up_parts, *down_parts)
+    )(place, incoming, one, two, gate, up, *first_parts, *rest_parts)
 
 
 def project_rows_back(place, dqueries, sums, dresid_one, cosine, sine, pieces):
@@ -847,7 +850,7 @@
     count = len(sums)
 
     def body(place_ref, dq_ref, resid_ref, cos_ref, sin_ref, *refs):
-        parts, rest = refs[:10], refs[10:]
+        parts, rest = refs[:8], refs[8:]
         sum_refs, (keep_ref, send_ref, dhidden_ref, weight, sems, dmixed_ref) = rest[:count], rest[count:]
         core = place_ref[1]
         loads = start_loads(place_ref, parts, 0, half, weight, sems, 0)
@@ -877,83 +880,105 @@
             shape_of((rows, half), jnp.bfloat16),
             shape_of((rows, width), jnp.float32),
         ],
-        [in_smem()] + [in_vmem()] * 4 + [anywhere()] * 10 + [in_vmem()] * count,
+        [in_smem()] + [in_vmem()] * 4 + [anywhere()] * 8 + [in_vmem()] * count,
         [
             pltpu.VMEM((width, 3 * width), jnp.bfloat16),
             pltpu.SemaphoreType.DMA((10,)),
             pltpu.VMEM((rows, 3 * width), jnp.bfloat16),
         ],
-        48,
-        (6 * rows * width * width, 6 * width * width + 8 * rows * width),
+        60,
+        6,
         "project_rows_back",
     )(place, dqueries, dresid_one, cosine, sine, *pieces, *sums)
 
 
-def grad_parts(place, lefts, rights, left_span, right_span, sums=()):
-    rows = lefts[0].shape[0]
-    depth = left_span[1] - left_span[0]
-    width = right_span[1] - right_span[0]
-    extra = 128 if sums else 0
-    count = depth // 4
-    tile = min(width, 512) if width % 512 == 0 else 384
-
-    def body(place_ref, l0, l1, r0, r1, *refs):
-        sum_refs, refs = refs[: len(sums)], refs[len(sums) :]
-        own_ref, x_ref, y_ref, xl_ref, yu_ref, left_t, right, block = refs[:8]
-        left_t[:, :rows] = l0[:, left_span[0] : left_span[1]].T
-        left_t[:, rows:] = l1[:, left_span[0] : left_span[1]].T
-        right[:rows] = r0[:, right_span[0] : right_span[1]]
-        right[rows:] = r1[:, right_span[0] : right_span[1]]
-        if sums:
-            padded, turned = refs[8:]
+def grad_parts(place, groups, sums=None):
+    jobs = [job for group in groups for job in group]
+    rows = jobs[0][0][0].shape[0]
+    lefts, rights, arrays = [], [], []
+    for left, left_span, right, right_span, blocks in jobs:
+        for known, entry in ((lefts, (left, left_span)), (rights, (right, right_span))):
+            if not any(entry[0] is other[0] and entry[1] == other[1] for other in known):
+                known.append(entry)
+        for array in (*left, *right):
+            if not any(array is other for other in arrays):
+                arrays.append(array)
+    where = lambda array: next(i for i, other in enumerate(arrays) if other is array)
+    slot = lambda known, pair, span: next(
+        i for i, other in enumerate(known) if other[0] is pair and other[1] == span
+    )
+    count = (jobs[0][1][1] - jobs[0][1][0]) // 4 // jobs[0][4]
+    totals = [sum((job[3][1] - job[3][0]) * job[4] for job in group) for group in groups]
+    widths = list(totals)
+    if sums is not None:
+        widths[0] += 128
+
+    def body(place_ref, *refs):
+        inputs, refs = refs[: len(arrays)], refs[len(arrays) :]
+        outs, refs = refs[: 5 * len(groups)], refs[5 * len(groups) :]
+        block, left_refs, right_refs = refs[0], refs[1 : 1 + len(lefts)], refs[1 + len(lefts) :]
+        for ref, (pair, span) in zip(left_refs, lefts):
+            for core in range(2):
+                ref[:, core * rows : (core + 1) * rows] = inputs[where(pair[core])][:rows, span[0] : span[1]].T
+        for ref, (pair, span) in zip(right_refs, rights):
+            for core in range(2):
+                ref[core * rows : (core + 1) * rows] = inputs[where(pair[core])][:rows, span[0] : span[1]]
+        if sums is not None:
+            padded, turned = refs[-2:]
             padded[...] = jnp.zeros_like(padded)
-            padded[:8] = sum_refs[0][...] + sum_refs[1][...]
+            padded[:16] = sum(
+                inputs[where(array)][rows:, : 4 * count].astype(jnp.float32) for array in jobs[sums][2]
+            )
             turned[...] = padded[...].T
         upper, lower = slice(0, count // 2), slice(count // 2, count)
-        for flip in range(4):
-            begin = pl.multiple_of((place_ref[0] ^ flip) * count, count)
-            for column in range(0, width, tile):
-                span = slice(column, column + tile)
-                block[:, span] = mm(left_t[pl.ds(begin, count), :], right[:, span]).astype(jnp.bfloat16)
-            if sums:
-                block[:, width:] = turned[pl.ds(begin, count), :].astype(jnp.bfloat16)
-            if flip == 0:
-                own_ref[...] = block[...]
-            elif flip == 1:
-                x_ref[upper] = block[upper]
-                xl_ref[...] = block[lower]
-            elif flip == 2:
-                y_ref[upper] = block[lower]
-                yu_ref[...] = block[upper]
-            else:
-                x_ref[lower] = block[upper]
-                y_ref[lower] = block[lower]
-
-    out_width = width + extra
-    return kernel_call(
-        body,
-        [
-            shape_of((count, out_width), jnp.bfloat16),
-            shape_of((count, out_width), jnp.bfloat16),
-            shape_of((count, out_width), jnp.bfloat16),
-            shape_of((count // 2, out_width), jnp.bfloat16),
-            shape_of((count // 2, out_width), jnp.bfloat16),
-        ],
-        [in_smem()] + [in_vmem()] * (4 + len(sums)),
-        [
-            pltpu.VMEM((depth, 2 * rows), jnp.bfloat16),
-            pltpu.VMEM((2 * rows, width), jnp.bfloat16),
-            pltpu.VMEM((count, out_width), jnp.bfloat16),
-        ]
-        + ([pltpu.VMEM((128, depth), jnp.float32), pltpu.VMEM((depth, 128), jnp.float32)] if sums else []),
-        56,
-        (4 * rows * depth * width, 4 * rows * (depth + width) + 2 * depth * width),
-        "grad_parts",
-    )(place, *lefts, *rights, *sums)
-
-
-def to_core(value, pairs=((0, 1), (1, 0))):
-    return lax.ppermute(value, "section", list(pairs))
+        for index, group in enumerate(groups):
+            own_ref, x_ref, y_ref, xl_ref, yu_ref = outs[5 * index : 5 * index + 5]
+            end = widths[index]
+            for flip in range(4):
+                target = 0
+                for left, left_span, right, right_span, blocks in group:
+                    left_t, right_all = left_refs[slot(lefts, left, left_span)], right_refs[slot(rights, right, right_span)]
+                    width = right_span[1] - right_span[0]
+                    tile = 512 if width % 512 == 0 else 384
+                    for part in range(blocks):
+                        begin = ((place_ref[0] ^ flip) * blocks + part) * count
+                        rows_t = left_t[pl.ds(pl.multiple_of(begin, count), count), :]
+                        for column in range(0, width, tile):
+                            block[:, target : target + tile] = mm(
+                                rows_t, right_all[:, column : column + tile]
+                            ).astype(jnp.bfloat16)
+                            target += tile
+                if target < end:
+                    begin = pl.multiple_of((place_ref[0] ^ flip) * count, count)
+                    block[:, target:end] = turned[pl.ds(begin, count), :].astype(jnp.bfloat16)
+                if flip == 0:
+                    own_ref[...] = block[:, :end]
+                elif flip == 1:
+                    x_ref[upper] = block[upper, :end]
+                    xl_ref[...] = block[lower, :end]
+                elif flip == 2:
+                    y_ref[upper] = block[lower, :end]
+                    yu_ref[...] = block[upper, :end]
+                else:
+                    x_ref[lower] = block[upper, :end]
+                    y_ref[lower] = block[lower, :end]
+
+    scratch = [pltpu.VMEM((count, max(widths)), jnp.bfloat16)]
+    scratch += [pltpu.VMEM((span[1] - span[0], 2 * rows), jnp.bfloat16) for _, span in lefts]
+    scratch += [pltpu.VMEM((2 * rows, span[1] - span[0]), jnp.bfloat16) for _, span in rights]
+    if sums is not None:
+        scratch += [pltpu.VMEM((128, 4 * count), jnp.float32), pltpu.VMEM((4 * count, 128), jnp.float32)]
+    shapes = []
+    for width in widths:
+        shapes += [shape_of((count, width), jnp.bfloat16)] * 3 + [shape_of((count // 2, width), jnp.bfloat16)] * 2
+    made = kernel_call(
+        body, shapes, [in_smem()] + [in_vmem()] * len(arrays), scratch, 60, 7, "grad_parts"
+    )(place, *arrays)
+    return [made[5 * index : 5 * index + 5] for index in range(len(groups))]
+
+
+def to_core(value):
+    return lax.ppermute(value, "section", [(0, 1), (1, 0)])
 
 
 def along_x(value):
@@ -968,9 +993,17 @@
     return lax.ppermute(value, "ctx", [(i, i ^ 1) for i in range(4)])
 
 
-def z_swap(value):
-    pairs = [(4 + i, 4 + (i ^ 2)) for i in range(4)]
+def near_blocks(value):
+    pairs = [(i, i ^ 1) for i in range(4)] + [(4 + i, 4 + (i ^ 2)) for i in range(4)]
     return lax.ppermute(value, ("section", "ctx"), pairs)
+
+
+def far_blocks(value):
+    return lax.ppermute(value, ("section", "ctx"), [(4 + i, 4 + (i ^ 3)) for i in range(4)])
+
+
+def same_role(value):
+    return lax.ppermute(value, "ctx", [(i, i ^ 3) for i in range(4)])
 
 
 def lowered(value):
@@ -994,32 +1027,59 @@
     return lax.dynamic_slice_in_dim(array, which * width, width, array.ndim - 1)
 
 
-def gathered(piece):
-    rows = piece.shape[0] // 2
-    from_x, from_y = along_x(piece), along_y(piece)
-    upper, lower = along_x(from_y[:rows]), along_y(from_x[rows:])
-    mine = [piece, from_x, from_y, upper, lower]
-    return mine + [to_core(part) for part in mine]
-
-
-def reduced(parts, ctx_rank):
-    own, x_message, y_message, x_lower, y_upper = parts
-    rows = own.shape[0] // 2
-    from_x, from_y = along_x(x_message), along_y(y_message)
-    x_last = along_x(lowered(wide(x_lower) + wide(from_y[rows:])))
-    y_last = along_y(lowered(wide(y_upper) + wide(from_x[rows:])))
-    summed = lowered(
-        wide(own)
+def after(value, *others):
+    return lax.optimization_barrier((value, *others))[0]
+
+
+def gather_near(pieces, *others):
+    own = after(pieces[0], *others)
+    return [own, along_x(own), along_y(own), pieces[1]]
+
+
+def gather_far(near, *others):
+    rows = near[0].shape[0] // 2
+    return [along_x(after(near[2][:rows], *others)), along_y(after(near[1][rows:], *others))]
+
+
+def both_cores(near, far):
+    return [
+        *near[:3],
+        *far,
+        near[3],
+        to_core(jnp.concatenate(near[1:3], axis=0)),
+        to_core(jnp.concatenate(far, axis=0)),
+    ]
+
+
+def reduce_first(parts, *others):
+    return along_x(after(parts[1], *others)), along_y(after(parts[2], *others))
+
+
+def reduce_second(parts, first, *others):
+    _, _, _, x_lower, y_upper = after(tuple(parts), *others)
+    from_x, from_y = first
+    rows = x_lower.shape[0]
+    return (
+        along_x(lowered(wide(x_lower) + wide(from_y[rows:]))),
+        along_y(lowered(wide(y_upper) + wide(from_x[rows:]))),
+    )
+
+
+def reduce_last(parts, first, second):
+    from_x, from_y = first
+    rows = second[0].shape[0]
+    return lowered(
+        wide(parts[0])
         + jnp.concatenate(
-            [wide(from_x[:rows]) + wide(y_last), wide(from_y[:rows]) + wide(x_last)], axis=0
+            [wide(from_x[:rows]) + wide(second[1]), wide(from_y[:rows]) + wide(second[0])], axis=0
         )
     )
-    inner = lax.ppermute(summed, "ctx", [(0, 1), (3, 2)])
-    pair = lowered(wide(summed) + wide(inner))
-    across = lax.ppermute(pair, "ctx", [(1, 2), (2, 1)])
-    total = lowered(wide(pair) + wide(across))
-    outer = lax.ppermute(total, "ctx", [(1, 0), (2, 3)])
-    return jnp.where((ctx_rank == 0) | (ctx_rank == 3), outer, total)
+
+
+def reduce_ctx(piece, middle, *others):
+    mine = lowered(wide(piece) + wide(same_role(piece)))
+    other = along_z(after(mine, *others))
+    return jnp.where(middle, other, mine), jnp.where(middle, mine, other)
 
 
 def paired_on_device(
@@ -1039,12 +1099,36 @@
     core, ctx_rank, dp_rank = (lax.axis_index(a) for a in ("section", "ctx", "dp"))
     span, width = tokens.shape[1], tokens.shape[2]
     sequence = ctx_rank // 2
-    block = ctx_rank ^ (2 * core)
+    middle = (ctx_rank == 1) | (ctx_rank == 2)
+    role = jnp.where(middle, 1, 0)
+    even = ctx_rank % 2 == 0
     place = jnp.stack([dp_rank, core]).astype(jnp.int32)
     pick = lambda array, index: lax.dynamic_index_in_dim(array, index, 0, keepdims=False)
 
-    def rows_of(array):
-        return jnp.where(core == 0, pick(array, sequence), z_swap(pick(array, 1 - sequence)))
+    def in_order(left, right):
+        return jnp.where(even, jnp.concatenate([left, right]), jnp.concatenate([right, left]))
+
+    def to_rows():
+        mine, theirs = jnp.where(middle, cotangent, tokens), jnp.where(middle, tokens, cotangent)
+        first = near_blocks(jnp.where(core == 0, pick(theirs, sequence), pick(theirs, 1 - sequence)))
+        second = far_blocks(pick(mine, 1 - sequence))
+        return in_order(
+            jnp.where(core == 0, pick(mine, sequence), first), jnp.where(core == 0, first, second)
+        )
+
+    def send_rows(rows):
+        halves = rows.reshape(2, span, width)
+        left, right = pick(halves, jnp.where(even, 0, 1)), pick(halves, jnp.where(even, 1, 0))
+        return left, near_blocks(jnp.where(core == 0, right, left)), far_blocks(right)
+
+    def placed_rows(left, first, second):
+        same = jnp.where(core == 0, left, second)
+        first_layer, second_layer = jnp.where(middle, first, same), jnp.where(middle, same, first)
+        other = to_core(jnp.where(core == 0, second_layer, first_layer))
+        mine = jnp.where(core == 0, first_layer, second_layer)
+        return jnp.where(
+            sequence == core, jnp.stack([mine, other]), jnp.stack([other, mine])
+        )[None]
 
     norm_columns = jnp.concatenate([norm1_gain, norm1_bias, norm2_gain, norm2_bias], axis=0).T
     norm_columns = jnp.pad(norm_columns, ((0, 0), (0, 124)))
@@ -1055,109 +1139,132 @@
                 [half_of(query_key_value_weight[0], which), half_of(output_weight[0], which), norm_columns],
                 axis=1,
             ),
-            jnp.concatenate([half_of(gate_weight[0], which), half_of(up_weight[0], which)], axis=1),
-            half_of(down_weight[0], which),
+            jnp.concatenate(
+                [half_of(gate_weight[0], which), half_of(up_weight[0], which)]
+                + jnp.split(half_of(down_weight[0], which), down_weight.shape[1] // gate_weight.shape[1]),
+                axis=1,
+            ),
         )
 
-    own_packs = packs(core)
-    sent_packs = [to_core(pack) for pack in packs(1 - core)]
-    weights = [
-        [gathered(jnp.where(core == layer, own, sent)) for own, sent in zip(own_packs, sent_packs)]
-        for layer in range(2)
+    own_halves, other_halves = packs(core), packs(1 - core)
+    sent = [to_core(pack) for pack in other_halves]
+    sent += [to_core(after(pack, *sent)) for pack in own_halves]
+    count = len(own_halves)
+    pieces = [
+        (
+            jnp.where(core == role, own_halves[index], sent[index]),
+            jnp.where(core == role, other_halves[index], sent[count + index]),
+        )
+        for index in range(count)
     ]
 
     seg = pick(seg_ids, sequence)
-    seg_rows = lax.dynamic_slice_in_dim(seg, block * span, span, 0)
-    seg_keys = jnp.concatenate(
-        [lax.dynamic_slice_in_dim(seg, (block ^ flip) * span, span, 0) for flip in (0, 2, 1, 3)]
-    )
+    rows = 2 * span
+    begin = (sequence ^ core) * rows
+    seg_rows = lax.dynamic_slice_in_dim(seg, begin, rows, 0)
+    seg_keys = jnp.concatenate([seg_rows, lax.dynamic_slice_in_dim(seg, rows - begin, rows, 0)])
     begins = jnp.sum((seg[None, :] < seg_rows[:, None]).astype(jnp.int32), axis=1)
-    places = block * span + jnp.arange(span, dtype=jnp.int32) - begins
+    places = begin + jnp.arange(rows, dtype=jnp.int32) - begins
     lanes = jnp.arange(128, dtype=jnp.int32) % HEAD
     half = HEAD // 2
     spread = 1000.0 ** (-2.0 * (lanes % half).astype(jnp.float32) / HEAD)
     angles = places.astype(jnp.float32)[:, None] * spread[None, :]
     cosine, sine = jnp.cos(angles), jnp.where(lanes < half, -1.0, 1.0) * jnp.sin(angles)
 
-    hidden = rows_of(tokens)
-    incoming = rows_of(cotangent)
-    kept, outputs = [], []
-    for layer in range(2):
-        first, gate_up, down = weights[layer]
+    def attention(hidden):
         queries, own = project_rows(place, hidden, cosine, sine, first)
-        from_z = along_z(own)
-        blocks = [own, to_core(own), from_z, to_core(from_z)]
-        attended = attend_rows(queries, blocks, seg_rows[:, None], seg_keys[None, :])
-        output, one, two, acts, gate, up = mlp_rows(place, hidden, attended, first, gate_up, down)
-        kept.append((hidden, queries, blocks, attended, one, two, acts, gate, up))
-        outputs.append(output)
-        hidden = output
-
-    totals, input_rows = [None, None], [None, None]
-    ff = acts.shape[1] - width
-    for layer in (1, 0):
-        first, gate_up, down = weights[layer]
-        hidden, queries, blocks, attended, one, two, acts, gate, up = kept[layer]
-        both = lambda value: (value, to_core(value))
-        keep, send, dresid_one, dattended, sums = mlp_rows_back(
-            place, incoming, one, two, gate, up, first, gate_up, down
-        )
-        right = (keep, to_core(send))
-        acts = both(acts)
-        low = lambda value: (value, wide(to_core(lowered(value))))
-        totals[layer] = [
-            reduced(grad_parts(place, acts, right, (0, width), (0, ff)), ctx_rank),
-            reduced(grad_parts(place, acts, right, (width, width + ff), (ff, ff + width // 2)), ctx_rank),
-            reduced(
-                grad_parts(
-                    place, both(attended), right, (0, width), (ff + width // 2, ff + width), low(sums)
-                ),
-                ctx_rank,
-            ),
-        ]
-        dqueries, own, near, across = attend_rows_back(
-            queries, blocks, seg_rows[None, :], seg_keys[:, None], dattended
-        )
-        across = to_core(across)
-        from_z = along_z(lowered(wide(near) + wide(across[1])))
-        keep, send, dhidden = project_rows_back(
-            place, dqueries, (own, across[0], from_z), dresid_one, cosine, sine, first
-        )
-        totals[layer].append(
-            reduced(
-                grad_parts(place, both(hidden), (keep, to_core(send)), (0, width), (0, 3 * width // 2)),
-                ctx_rank,
+        blocks = [own, to_core(own)]
+        return queries, blocks, attend_rows(queries, blocks, seg_rows[:, None], seg_keys[None, :])
+
+    given = to_rows()
+    near = gather_near(pieces[0])
+    far = gather_far(near)
+    near_mlp = gather_near(pieces[1], *far)
+    first = both_cores(near, far)
+    queries, blocks, attended = attention(given)
+    near_mlp = [after(part, attended) for part in near_mlp]
+    rest = both_cores(near_mlp, gather_far(near_mlp))
+    output = mlp_rows(place, given, attended, first, rest)[0]
+
+    hidden = jnp.where(middle, along_z(output), given)
+    queries, blocks, attended = attention(hidden)
+    output, one, two, acts, gate, up = mlp_rows(place, hidden, attended, first, rest)
+
+    _, _, _, _, dresid_one, dattended = mlp_rows_back(place, given, one, two, gate, up, first, rest)
+    sent_outputs = send_rows(output)
+    dqueries, own, across = attend_rows_back(
+        queries, blocks, seg_rows[None, :], seg_keys[:, None], after(dattended, *sent_outputs)
+    )
+    dhidden = project_rows_back(
+        place, dqueries, (own, to_core(across)), dresid_one, cosine, sine, first
+    )[2]
+    incoming = jnp.where(middle, given, along_z(lowered(dhidden)))
+
+    both = lambda value: (value, to_core(value))
+    acts, attended, hidden = both(acts), both(attended), both(hidden)
+    keep, send, keep_ff, send_ff, dresid_one, dattended = mlp_rows_back(
+        place, incoming, one, two, gate, up, first, rest
+    )
+    ff = keep_ff.shape[1]
+    right, right_ff = (keep, to_core(send)), (keep_ff, to_core(send_ff))
+    parts = grad_parts(
+        place,
+        [
+            [
+                (acts, (width, width + ff), right, (0, width // 2), ff // width),
+                (attended, (0, width), right, (width // 2, width), 1),
+            ]
+        ],
+        1,
+    )
+    right_ff = (after(right_ff[0], *parts[0]), right_ff[1])
+    parts += grad_parts(
+        place, [[(acts, (0, width), right_ff, (half * ff // 2, (half + 1) * ff // 2), 1)] for half in range(2)]
+    )
+    dqueries, own, across = attend_rows_back(
+        queries, blocks, seg_rows[None, :], seg_keys[:, None], after(dattended, *(x for part in parts for x in part))
+    )
+    near = [reduce_first(parts[0])]
+    near.append(reduce_first(parts[1]))
+    across = to_core(after(across, *near[0], *near[1]))
+    far = [reduce_second(parts[0], near[0], across)]
+    near.append(reduce_first(parts[2], across))
+    keep, send, dhidden = project_rows_back(place, dqueries, (own, across), dresid_one, cosine, sine, first)
+    keep = after(keep, *far[0])
+    parts += grad_parts(place, [[(hidden, (0, width), (keep, to_core(send)), (0, 3 * width // 2), 1)]])
+    near.append(reduce_first(parts[3]))
+    far.append(reduce_second(parts[1], near[1], *parts[3]))
+    far.append(reduce_second(parts[2], near[2], *parts[3]))
+    far.append(reduce_second(parts[3], near[3]))
+    pieces = [reduce_last(*group) for group in zip(parts, near, far)]
+    pieces[0] = after(pieces[0], *parts[3])
+    totals = [reduce_ctx(piece, middle, *far[3]) for piece in pieces]
+
+    pairs = []
+    for first_layer, second_layer in totals:
+        pairs.append(
+            (
+                jnp.where(core == 0, first_layer, second_layer),
+                to_core(jnp.where(core == 0, second_layer, first_layer)),
             )
         )
-        input_rows[layer] = dhidden
-        incoming = lowered(dhidden)
-
-    def whole(first, second):
-        from_first = to_core(first, ((1, 0),))
-        from_second = to_core(second, ((0, 1),))
-        return jnp.where(core == 0, first, second), jnp.where(core == 0, from_first, from_second)
-
-    pairs = [whole(first, second) for first, second in zip(*totals)]
     joined = lambda index, begin, end: wide(
         by_core(core, pairs[index][0][:, begin:end], pairs[index][1][:, begin:end], 1)
     )[None]
-    norm_grads = wide(pairs[2][0][:, width // 2 : width // 2 + 4]).T
-
-    def placed_rows(first, second):
-        first, second = lowered(first), lowered(second)
-        near = jnp.where(core == 0, first, to_core(second, ((0, 1),)))
-        swapped = z_swap(jnp.stack([first, second]))
-        far = jnp.where(core == 0, to_core(swapped[0], ((1, 0),)), swapped[1])
-        return jnp.where(sequence == 0, jnp.stack([near, far]), jnp.stack([far, near]))[None]
+    norm_grads = wide(pairs[0][0][:, 5 * width // 2 : 5 * width // 2 + 4]).T
+    pick_down = lambda which: jnp.concatenate(
+        [pairs[0][which][:, i * width // 2 : (i + 1) * width // 2] for i in range(ff // width)]
+    )
+    grad_down = wide(by_core(core, pick_down(0), pick_down(1), 1))[None]
 
     return (
-        placed_rows(*outputs),
-        wide(placed_rows(*input_rows)),
+        placed_rows(*after(sent_outputs, *far[3])),
+        wide(placed_rows(*send_rows(after(lowered(dhidden), *far[3])))),
         joined(3, 0, 3 * width // 2),
-        joined(2, 0, width // 2),
-        joined(0, 0, ff // 2),
-        joined(0, ff // 2, ff),
-        joined(1, 0, width // 2),
+        joined(0, 2 * width, 5 * width // 2),
+        joined(1, 0, ff // 2),
+        joined(2, 0, ff // 2),
+        grad_down,
         *(norm_grads[i : i + 1] for i in range(4)),
     )
 

time: 880 us -> 650 us (0.74)
  waiting for transfers between devices: 413 us -> 173 us
  Pallas kernels: 190 us -> 256 us
  starting transfers between devices: 169 us -> 119 us
  local copies, waits for them, and re-layouts: 45.9 us -> 33.4 us
    ppermute x28 -> x12, waiting for transfers between devices: 164 us -> 38.1 us  [along_y(): return lax.ppermute(value, 'dp', [(i, i ^ 2) for i in range(4)])]
    ppermute x91 -> x34, waiting for transfers between devices: 131 us -> 39.8 us  [the longest x24 21.4 us: to_core(): return lax.ppermute(value, 'section', [(0, 1), (1, 0)])]
    ppermute x28 -> x12, waiting for transfers between devices: 106 us -> 25.1 us  [along_x(): return lax.ppermute(value, 'dp', [(i, i ^ 1) for i in range(4)])]
    ppermute x4 -> x6, waiting for transfers between devices: 11.7 us -> 70.3 us  [along_z(): return lax.ppermute(value, 'ctx', [(i, i ^ 1) for i in range(4)])]
    ppermute x91 -> x34, starting transfers between devices: 92.8 us -> 39.8 us  [the longest x24 25.3 us: to_core(): return lax.ppermute(value, 'section', [(0, 1), (1, 0)])]
    ppermute x4 -> x6, starting transfers between devices: 8.79 us -> 52.3 us  [along_z(): return lax.ppermute(value, 'ctx', [(i, i ^ 1) for i in range(4)])]
    ppermute x28 -> x12, starting transfers between devices: 38.1 us -> 13.5 us  [along_y(): return lax.ppermute(value, 'dp', [(i, i ^ 2) for i in range(4)])]
    pallas_call x2, Pallas kernels: 36.8 us -> 54.1 us  [attend_rows_back(): kernel_call(body, [shape_of((rows, width), jnp.float32), pair_shape, pair...]
  transfers between devices with their start and end apart: 151 -> 64, of which waited for: 48 -> 26; matrix products, arithmetic and copies ran while one was open for 8% -> 9% of each run, Pallas kernels for 20% -> 24%
where the time goes in v3:
time: 650 us; the launch traced here: 640 us
  Pallas kernels  256 us (39%)
  waiting for transfers between devices  173 us (27%)
  starting transfers between devices  119 us (18%)
  other arithmetic  56.1 us (9%)
  local copies, waits for them, and re-layouts  33.4 us (5%)
    ppermute x6, waiting for transfers between devices, along_z(): return lax.ppermute(value, 'ctx', [(i, i ^ 1) for i in range(4)])  70.3 us
    pallas_call x2, Pallas kernels, mlp_rows_back(): kernel_call(body, [shape_of((rows + 16, width), jnp.bfloat16), shape_of((...  62.9 us
    pallas_call x2, Pallas kernels, attend_rows_back(): kernel_call(body, [shape_of((rows, width), jnp.float32), pair_shape, pair...  54.1 us
    ppermute x6, starting transfers between devices, along_z(): return lax.ppermute(value, 'ctx', [(i, i ^ 1) for i in range(4)])  52.3 us
    pallas_call x2, Pallas kernels, mlp_rows(): kernel_call(body, [shape_of((rows, width), jnp.bfloat16), shape_of((rows,...  46 us
    ppermute x12, waiting for transfers between devices, along_y(): return lax.ppermute(value, 'dp', [(i, i ^ 2) for i in range(4)])  38.1 us
    pallas_call x2, Pallas kernels, attend_rows(): kernel_call(body, [shape_of((rows, width), jnp.bfloat16)], [pl.BlockSpec(...  30.4 us
    pallas_call x3, Pallas kernels, grad_parts(): kernel_call(body, shapes, [in_smem()] + [in_vmem()] * len(arrays), scratc...  29.5 us
  transfers between devices with their start and end apart: 64, of which 26 were waited for; matrix products, arithmetic and copies ran while one was open for 9% of the time, Pallas kernels for 24%

profile of v3, /device:TPU:0, one launch (start us, length us, event | category | flops | bytes accessed | tf_op | source)
XLA Modules:
  0.0 639.8 jit_solution(14213652087105304919)
XLA Ops:
  65.7 15.2 %attend_rows.2.att_ref = bf16[512,768]{1,0:T(8,128)(2,1)} custom-call(s32[512,1]{1,0:T(8,128)} %copy.53.col_ref, s32[1,1024]{1,0:T(1,128)} %bitcast.117, bf16[512,768]{1,0:T(8,128)(2,1)} %get-tuple-element.94.q_ref, bf16[2,512,768]{2,1,0:T(8,128)(2,1)} %get-tuple-element.95.b0, bf16[2,512,768]{2,1,0:T(8,128)(2,1)} %copy-done.16), custom_call_target="tpu_custom_call" | custom-call | bytes 24000000 | tf_op jit(solution)/shard_map/attend_rows/pallas_call | solution.py:593
  80.9 10.3 %collective-permute-done.13.refs_10_ = bf16[192,4608]{1,0:T(8,128)(2,1)} collective-permute-done((bf16[192,4608]{1,0:T(8,128)(2,1)}, bf16[192,4608]{1,0:T(8,128)(2,1)}, u32[]{:S(2)}, u32[]{:S(2)}) %collective-permute-start.13) | collective-permute-done | bytes 1769504 | tf_op jit(solution)/shard_map/ppermute | solution.py:989
  99.3 19.8 %collective-permute-done.14.refs_11_ = bf16[96,4608]{1,0:T(8,128)(2,1)S(1)} collective-permute-done((bf16[96,4608]{1,0:T(8,128)(2,1)S(1)}, bf16[96,4608]{1,0:T(8,128)(2,1)S(1)}, u32[]{:S(2)}, u32[]{:S(2)}) %collective-permute-start.14) | collective-permute-done | bytes 884768 | tf_op jit(solution)/shard_map/ppermute | solution.py:985
  126.1 23.0 %mlp_rows.2 = (bf16[512,768]{1,0:T(8,128)(2,1)}, f32[512,768]{1,0:T(8,128)}, f32[512,768]{1,0:T(8,128)}, bf16[512,3840]{1,0:T(8,128)(2,1)}, f32[512,3072]{1,0:T(8,128)}, /*index=5*/f32[512,3072]{1,0:T(8,128)}) custom-call(s32[2]{0:T(128)} %pad_add_fusion.1.place_ref, bf16[512,768]{1,0:T(8,128)(2,1)} %maximum_select_fusion.4.hidden_ref.in_ref, ...), custom_call_target="tpu_custom_call" | custom-call | bytes 48000000 | tf_op jit(solution)/shard_map/mlp_rows/pallas_call | solution.py:740
  152.3 18.1 %collective-permute-done.19 = bf16[512,768]{1,0:T(8,128)(2,1)S(1)} collective-permute-done((bf16[512,768]{1,0:T(8,128)(2,1)}, bf16[512,768]{1,0:T(8,128)(2,1)S(1)}, u32[]{:S(2)}, u32[]{:S(2)}) %collective-permute-start.19) | collective-permute-done | bytes 786464 | tf_op jit(solution)/shard_map/ppermute | solution.py:993
  172.4 6.5 %project_rows.3 = (bf16[512,768]{1,0:T(8,128)(2,1)}, bf16[2,512,768]{2,1,0:T(8,128)(2,1)}) custom-call(s32[2]{0:T(128)} %pad_add_fusion.1.place_ref, bf16[512,768]{1,0:T(8,128)(2,1)} %broadcast_select_fusion.9.hidden_ref.refs_0_, f32[512,128]{1,0:T(8,128)} %get-tuple-element.271.cos_ref, f32[512,128]{1,0:T(8,128)} %get-tuple-element.270.sin_ref, ...), custom_call_target="tpu_custom_call" | custom-call | bytes 9000000 | tf_op jit(solution)/shard_map/project_rows/pallas_call | solution.py:558
  183.8 15.2 %attend_rows.3.att_ref.refs_4_ = bf16[512,768]{1,0:T(8,128)(2,1)} custom-call(s32[512,1]{1,0:T(8,128)} %copy.53.col_ref, s32[1,1024]{1,0:T(1,128)} %bitcast.118, bf16[512,768]{1,0:T(8,128)(2,1)} %get-tuple-element.103.q_ref, bf16[2,512,768]{2,1,0:T(8,128)(2,1)} %get-tuple-element.104.b0, bf16[2,512,768]{2,1,0:T(8,128)(2,1)} %copy-done.12), custom_call_target="tpu_custom_call" | custom-call | bytes 24000000 | tf_op jit(solution)/shard_map/attend_rows/pallas_call | solution.py:593
  199.0 23.0 %mlp_rows.3 = (bf16[512,768]{1,0:T(8,128)(2,1)}, f32[512,768]{1,0:T(8,128)}, f32[512,768]{1,0:T(8,128)}, bf16[512,3840]{1,0:T(8,128)(2,1)}, f32[512,3072]{1,0:T(8,128)}, /*index=5*/f32[512,3072]{1,0:T(8,128)}) custom-call(s32[2]{0:T(128)} %pad_add_fusion.1.place_ref, bf16[512,768]{1,0:T(8,128)(2,1)} %broadcast_select_fusion.9.hidden_ref.refs_0_, ...), custom_call_target="tpu_custom_call" | custom-call | bytes 48000000 | tf_op jit(solution)/shard_map/mlp_rows/pallas_call | solution.py:740
  226.4 31.4 %mlp_rows_back.2 = (bf16[528,768]{1,0:T(8,128)(2,1)}, bf16[528,768]{1,0:T(8,128)(2,1)}, bf16[512,3072]{1,0:T(8,128)(2,1)}, bf16[512,3072]{1,0:T(8,128)(2,1)}, f3...) custom-call(s32[2]{0:T(128)} %pad_add_fusion.1.place_ref, bf16[512,768]{1,0:T(8,128)(2,1)} %maximum_select_fusion.4.hidden_ref.in_ref, ...), custom_call_target="tpu_custom_call" | custom-call | bytes 63000000 | tf_op jit(solution)/shard_map/mlp_rows_back/pallas_call | solution.py:828
  257.9 27.0 %attend_rows_back.2 = (f32[512,768]{1,0:T(8,128)}, bf16[2,512,768]{2,1,0:T(8,128)(2,1)}, bf16[2,512,768]{2,1,0:T(8,128)(2,1)}) custom-call(s32[1,512]{1,0:T(1,128)} %copy-done.46, s32[1024,1]{1,0:T(8,128)} %copy.56.col_ref, bf16[512,768]{1,0:T(8,128)(2,1)} %get-tuple-element.103.q_ref, bf16[512,768]{1,0:T(8,128)(2,1)} %get-tuple-element.111.in_ref, ...), custom_call_target="tpu_custom_call" | custom-call | bytes 54000000 | tf_op jit(solution)/shard_map/attend_rows_back/pallas_call | solution.py:647
  293.4 10.0 %project_rows_back.2 = (bf16[512,1152]{1,0:T(8,128)(2,1)}, bf16[512,1152]{1,0:T(8,128)(2,1)}, f32[512,768]{1,0:T(8,128)}) custom-call(s32[2]{0:T(128)} %pad_add_fusion.1.place_ref, f32[512,768]{1,0:T(8,128)} %get-tuple-element.112.dq_ref, f32[512,768]{1,0:T(8,128)} %get-tuple-element.113.resid_ref, f32[512,128]{1,0:T(8,128)} %get-tuple-element.271.cos_ref, ...), custom_call_target="tpu_custom_call" | custom-call | bytes 18000000 | tf_op jit(solution)/shard_map/project_rows_back/pallas_call | solution.py:876
  305.8 19.2 %collective-permute-done.25 = bf16[512,768]{1,0:T(8,128)(2,1)S(1)} collective-permute-done((bf16[512,768]{1,0:T(8,128)(2,1)S(1)}, bf16[512,768]{1,0:T(8,128)(2,1)S(1)}, u32[]{:S(2)}, u32[]{:S(2)}) %collective-permute-start.25) | collective-permute-done | bytes 786464 | tf_op jit(solution)/shard_map/ppermute | solution.py:993
  325.9 31.5 %mlp_rows_back.3 = (bf16[528,768]{1,0:T(8,128)(2,1)}, bf16[528,768]{1,0:T(8,128)(2,1)}, bf16[512,3072]{1,0:T(8,128)(2,1)}, bf16[512,3072]{1,0:T(8,128)(2,1)}, f3...) custom-call(s32[2]{0:T(128)} %pad_add_fusion.1.place_ref, bf16[512,768]{1,0:T(8,128)(2,1)} %broadcast_select_fusion.8.in_ref, ...), custom_call_target="tpu_custom_call" | custom-call | bytes 63000000 | tf_op jit(solution)/shard_map/mlp_rows_back/pallas_call | solution.py:828
  358.0 7.2 %collective-permute-done.28.refs_5_ = bf16[512,768]{1,0:T(8,128)(2,1)S(1)} collective-permute-done((bf16[512,768]{1,0:T(8,128)(2,1)}, bf16[512,768]{1,0:T(8,128)(2,1)S(1)}, u32[]{:S(2)}, u32[]{:S(2)}) %collective-permute-start.28) | collective-permute-done | bytes 786464 | tf_op jit(solution)/shard_map/ppermute | solution.py:981
  366.4 11.6 %grad_parts.3 = (bf16[192,2048]{1,0:T(8,128)(2,1)}, bf16[192,2048]{1,0:T(8,128)(2,1)}, bf16[192,2048]{1,0:T(8,128)(2,1)}, bf16[96,2048]{1,0:T(8,128)(2,1)}, bf16[96,2048]{1,0:T(8,128)(2,1)}) custom-call(s32[2]{0:T(128)} %pad_add_fusion.1.place_ref, bf16[512,3840]{1,0:T(8,128)(2,1)} %get-tuple-element.118.refs_0_, ...), custom_call_target="tpu_custom_call" | custom-call | bytes 21000000 | tf_op jit(solution)/shard_map/grad_parts/pallas_call | solution.py:974
  380.0 11.7 %grad_parts.4 = (bf16[192,1536]{1,0:T(8,128)(2,1)}, bf16[192,1536]{1,0:T(8,128)(2,1)}, bf16[192,1536]{1,0:T(8,128)(2,1)}, bf16[96,1536]{1,0:T(8,128)(2,1)}, bf16...) custom-call(s32[2]{0:T(128)} %pad_add_fusion.1.place_ref, ...), custom_call_target="tpu_custom_call" | custom-call | bytes 21000000 | tf_op jit(solution)/shard_map/grad_parts/pallas_call | solution.py:974
  393.7 27.1 %attend_rows_back.3 = (f32[512,768]{1,0:T(8,128)}, bf16[2,512,768]{2,1,0:T(8,128)(2,1)}, bf16[2,512,768]{2,1,0:T(8,128)(2,1)}) custom-call(s32[1,512]{1,0:T(1,128)} %copy-done.46, s32[1024,1]{1,0:T(8,128)} %copy.56.col_ref, bf16[512,768]{1,0:T(8,128)(2,1)} %get-tuple-element.103.q_ref, bf16[512,768]{1,0:T(8,128)(2,1)} %get-tuple-element.139.in_ref, ...), custom_call_target="tpu_custom_call" | custom-call | bytes 54000000 | tf_op jit(solution)/shard_map/attend_rows_back/pallas_call | solution.py:647
  433.9 9.8 %project_rows_back.3 = (bf16[512,1152]{1,0:T(8,128)(2,1)}, bf16[512,1152]{1,0:T(8,128)(2,1)}, f32[512,768]{1,0:T(8,128)}) custom-call(s32[2]{0:T(128)} %pad_add_fusion.1.place_ref, f32[512,768]{1,0:T(8,128)} %get-tuple-element.140.dq_ref, f32[512,768]{1,0:T(8,128)} %get-tuple-element.141.resid_ref, f32[512,128]{1,0:T(8,128)} %get-tuple-element.271.cos_ref, ...), custom_call_target="tpu_custom_call" | custom-call | bytes 18000000 | tf_op jit(solution)/shard_map/project_rows_back/pallas_call | solution.py:876
  466.3 12.8 %collective-permute-done.58 = bf16[96,1536]{1,0:T(8,128)(2,1)S(1)} collective-permute-done((bf16[96,1536]{1,0:T(8,128)(2,1)S(1)}, bf16[96,1536]{1,0:T(8,128)(2,1)S(1)}, u32[]{:S(2)}, u32[]{:S(2)}) %collective-permute-start.58) | collective-permute-done | bytes 294944 | tf_op jit(solution)/shard_map/ppermute | solution.py:989
  504.8 12.5 %collective-permute-done.54 = bf16[192,1536]{1,0:T(8,128)(2,1)S(1)} collective-permute-done((bf16[192,1536]{1,0:T(8,128)(2,1)S(1)}, bf16[192,1536]{1,0:T(8,128)(2,1)S(1)}, u32[]{:S(2)}, u32[]{:S(2)}) %collective-permute-start.54) | collective-permute-done | bytes 589856 | tf_op jit(solution)/shard_map/ppermute | solution.py:1006
  517.3 46.1 %collective-permute-start.50 = (bf16[192,2048]{1,0:T(8,128)(2,1)S(1)}, bf16[192,2048]{1,0:T(8,128)(2,1)S(1)}, u32[]{:S(2)}, u32[]{:S(2)}) collective-permute-start(bf16[192,2048]{1,0:T(8,128)(2,1)S(1)} %add_convert_fusion), channel_id=1, source_target_pairs={{0,4},{4,0},{8,12},{12,8},{1,5},{5,1},{9,13},{13,9},{2,6},{6,2},{1... | collective-permute-start | bytes 2359304 | tf_op jit(solution)/shard_map/ppermute | solution.py:993
  565.8 14.5 %collective-permute-start.45 = (bf16[256,768]{1,0:T(8,128)(2,1)S(1)}, bf16[256,768]{1,0:T(8,128)(2,1)S(1)}, u32[]{:S(2)}, u32[]{:S(2)}) collective-permute-start(bf16[256,768]{1,0:T(8,128)(2,1)S(1)} %get-tuple-element.225), channel_id=1, source_target_pairs={{0,16},{16,0},{1,17},{17,1},{2,18},{18,2},{3,19},{19,3},{4,20},{20... | collective-permute-start | bytes 1179656 | tf_op jit(solution)/shard_map/ppermute | solution.py:981
  583.0 15.7 %collective-permute-done.62 = bf16[192,1536]{1,0:T(8,128)(2,1)S(1)} collective-permute-done((bf16[192,1536]{1,0:T(8,128)(2,1)S(1)}, bf16[192,1536]{1,0:T(8,128)(2,1)S(1)}, u32[]{:S(2)}, u32[]{:S(2)}) %collective-permute-start.62) | collective-permute-done | bytes 589856 | tf_op jit(solution)/shard_map/ppermute | solution.py:993
  599.7 11.7 %collective-permute-done.55 = bf16[192,1536]{1,0:T(8,128)(2,1)S(1)} collective-permute-done((bf16[192,1536]{1,0:T(8,128)(2,1)S(1)}, bf16[192,1536]{1,0:T(8,128)(2,1)S(1)}, u32[]{:S(2)}, u32[]{:S(2)}) %collective-permute-start.55) | collective-permute-done | bytes 589856 | tf_op jit(solution)/shard_map/ppermute | solution.py:993
  (317 shorter events, 207.0 us)
Async XLA Ops:
  8.4 38.6 %collective-permute-start.7 = (bf16[192,4608]{1,0:T(8,128)(2,1)}, bf16[192,4608]{1,0:T(8,128)(2,1)}, u32[]{:S(2)}, u32[]{:S(2)}) collective-permute-start(bf16[192,4608]{1,0:T(8,128)(2,1)} %fusion.18), channel_id=1, source_target_pairs={{0,16},{16,0},{1,17},{17,1},{2,18},{18,2},{3,19},{19,3},{4,20},{20... | collective-permute-start | bytes 5308424 | tf_op jit(solution)/shard_map/ppermute | solution.py:981
  49.9 41.3 %collective-permute-start.13 = (bf16[192,4608]{1,0:T(8,128)(2,1)}, bf16[192,4608]{1,0:T(8,128)(2,1)}, u32[]{:S(2)}, u32[]{:S(2)}) collective-permute-start(bf16[192,4608]{1,0:T(8,128)(2,1)} %broadcast_select_fusion.1.refs_8_), channel_id=1, source_target_pairs={{0,2},{1,3},{2,0},{3,1},{4,6},{5,7},{6,4},{7,5},{8,10},{9,11},{10,... | collective-permute-start | bytes 5308424 | tf_op jit(solution)/shard_map/ppermute | solution.py:989
  51.2 41.0 %collective-permute-start.12 = (bf16[192,4608]{1,0:T(8,128)(2,1)}, bf16[192,4608]{1,0:T(8,128)(2,1)}, u32[]{:S(2)}, u32[]{:S(2)}) collective-permute-start(bf16[192,4608]{1,0:T(8,128)(2,1)} %broadcast_select_fusion.1.refs_8_), channel_id=1, source_target_pairs={{0,1},{1,0},{2,3},{3,2},{4,5},{5,4},{6,7},{7,6},{8,9},{9,8},{10,11... | collective-permute-start | bytes 5308424 | tf_op jit(solution)/shard_map/ppermute | solution.py:985
  94.5 29.8 %collective-permute-start.17 = (bf16[384,4608]{1,0:T(8,128)(2,1)S(1)}, bf16[384,4608]{1,0:T(8,128)(2,1)S(1)}, u32[]{:S(2)}, u32[]{:S(2)}) collective-permute-start(bf16[384,4608]{1,0:T(8,128)(2,1)S(1)} %pad_maximum_fusion), channel_id=1, source_target_pairs={{0,16},{16,0},{1,17},{17,1},{2,18},{18,2},{3,19},{19,3},{4,20},{20... | collective-permute-start | bytes 10616840 | tf_op jit(solution)/shard_map/ppermute | solution.py:981
  224.1 33.8 %collective-permute-start.21 = (bf16[256,768]{1,0:T(8,128)(2,1)S(1)}, bf16[256,768]{1,0:T(8,128)(2,1)S(1)}, u32[]{:S(2)}, u32[]{:S(2)}) collective-permute-start(bf16[256,768]{1,0:T(8,128)(2,1)S(1)} %get-tuple-element.219), channel_id=1, source_target_pairs={{0,4},{4,0},{8,12},{12,8},{16,24},{20,28},{24,16},{28,20},{1,5},{5... | collective-permute-start | bytes 1179656 | tf_op jit(solution)/shard_map/ppermute | solution.py:998
  224.7 33.2 %collective-permute-start.22 = (bf16[256,768]{1,0:T(8,128)(2,1)S(1)}, bf16[256,768]{1,0:T(8,128)(2,1)S(1)}, u32[]{:S(2)}, u32[]{:S(2)}) collective-permute-start(bf16[256,768]{1,0:T(8,128)(2,1)S(1)} %get-tuple-element.220), channel_id=1, source_target_pairs={{16,28},{20,24},{24,20},{28,16},{17,29},{21,25},{25,21},{29,17},{1... | collective-permute-start | bytes 1179656 | tf_op jit(solution)/shard_map/ppermute | solution.py:1002
  305.7 59.5 %collective-permute-start.26 = (bf16[512,3840]{1,0:T(8,128)(2,1)S(1)}, bf16[512,3840]{1,0:T(8,128)(2,1)}, u32[]{:S(2)}, u32[]{:S(2)}) collective-permute-start(bf16[512,3840]{1,0:T(8,128)(2,1)S(1)} %copy-done.11), channel_id=1, source_target_pairs={{0,16},{16,0},{1,17},{17,1},{2,18},{18,2},{3,19},{19,3},{4,20},{20... | collective-permute-start | bytes 11796488 | tf_op jit(solution)/shard_map/ppermute | solution.py:981
  377.9 42.9 %collective-permute-start.30 = (bf16[192,2048]{1,0:T(8,128)(2,1)}, bf16[192,2048]{1,0:T(8,128)(2,1)S(1)}, u32[]{:S(2)}, u32[]{:S(2)}) collective-permute-start(bf16[192,2048]{1,0:T(8,128)(2,1)} %get-tuple-element.122), channel_id=1, source_target_pairs={{0,1},{1,0},{2,3},{3,2},{4,5},{5,4},{6,7},{7,6},{8,9},{9,8},{10,11... | collective-permute-start | bytes 2359304 | tf_op jit(solution)/shard_map/ppermute | solution.py:985
  379.3 41.5 %collective-permute-start.31 = (bf16[192,2048]{1,0:T(8,128)(2,1)}, bf16[192,2048]{1,0:T(8,128)(2,1)S(1)}, u32[]{:S(2)}, u32[]{:S(2)}) collective-permute-start(bf16[192,2048]{1,0:T(8,128)(2,1)} %get-tuple-element.123), channel_id=1, source_target_pairs={{0,2},{1,3},{2,0},{3,1},{4,6},{5,7},{6,4},{7,5},{8,10},{9,11},{10,... | collective-permute-start | bytes 2359304 | tf_op jit(solution)/shard_map/ppermute | solution.py:989
  391.8 29.1 %collective-permute-start.32 = (bf16[192,1536]{1,0:T(8,128)(2,1)}, bf16[192,1536]{1,0:T(8,128)(2,1)S(1)}, u32[]{:S(2)}, u32[]{:S(2)}) collective-permute-start(bf16[192,1536]{1,0:T(8,128)(2,1)} %get-tuple-element.130), channel_id=1, source_target_pairs={{0,1},{1,0},{2,3},{3,2},{4,5},{5,4},{6,7},{7,6},{8,9},{9,8},{10,11... | collective-permute-start | bytes 1769480 | tf_op jit(solution)/shard_map/ppermute | solution.py:985
  393.2 27.6 %collective-permute-start.33 = (bf16[192,1536]{1,0:T(8,128)(2,1)}, bf16[192,1536]{1,0:T(8,128)(2,1)S(1)}, u32[]{:S(2)}, u32[]{:S(2)}) collective-permute-start(bf16[192,1536]{1,0:T(8,128)(2,1)} %get-tuple-element.131), channel_id=1, source_target_pairs={{0,2},{1,3},{2,0},{3,1},{4,6},{5,7},{6,4},{7,5},{8,10},{9,11},{10,... | collective-permute-start | bytes 1769480 | tf_op jit(solution)/shard_map/ppermute | solution.py:989
  457.0 43.3 %collective-permute-start.49 = (bf16[192,2048]{1,0:T(8,128)(2,1)S(1)}, bf16[192,2048]{1,0:T(8,128)(2,1)S(1)}, u32[]{:S(2)}, u32[]{:S(2)}) collective-permute-start(bf16[192,2048]{1,0:T(8,128)(2,1)S(1)} %fusion), channel_id=1, source_target_pairs={{0,12},{4,8},{8,4},{12,0},{1,13},{5,9},{9,5},{13,1},{2,14},{6,10},... | collective-permute-start | bytes 2359304 | tf_op jit(solution)/shard_map/ppermute | solution.py:1006
  459.8 30.9 %collective-permute-start.40 = (bf16[192,1152]{1,0:T(8,128)(2,1)}, bf16[192,1152]{1,0:T(8,128)(2,1)S(1)}, u32[]{:S(2)}, u32[]{:S(2)}) collective-permute-start(bf16[192,1152]{1,0:T(8,128)(2,1)} %get-tuple-element.155), channel_id=1, source_target_pairs={{0,1},{1,0},{2,3},{3,2},{4,5},{5,4},{6,7},{7,6},{8,9},{9,8},{10,11... | collective-permute-start | bytes 1327112 | tf_op jit(solution)/shard_map/ppermute | solution.py:985
  461.2 31.2 %collective-permute-start.38 = (bf16[192,1152]{1,0:T(8,128)(2,1)}, bf16[192,1152]{1,0:T(8,128)(2,1)S(1)}, u32[]{:S(2)}, u32[]{:S(2)}) collective-permute-start(bf16[192,1152]{1,0:T(8,128)(2,1)} %get-tuple-element.153), channel_id=1, source_target_pairs={{0,2},{1,3},{2,0},{3,1},{4,6},{5,7},{6,4},{7,5},{8,10},{9,11},{10,... | collective-permute-start | bytes 1327112 | tf_op jit(solution)/shard_map/ppermute | solution.py:989
  489.4 27.9 %collective-permute-start.54 = (bf16[192,1536]{1,0:T(8,128)(2,1)S(1)}, bf16[192,1536]{1,0:T(8,128)(2,1)S(1)}, u32[]{:S(2)}, u32[]{:S(2)}) collective-permute-start(bf16[192,1536]{1,0:T(8,128)(2,1)S(1)} %fusion.2), channel_id=1, source_target_pairs={{0,12},{4,8},{8,4},{12,0},{1,13},{5,9},{9,5},{13,1},{2,14},{6,10},... | collective-permute-start | bytes 1769480 | tf_op jit(solution)/shard_map/ppermute | solution.py:1006
  498.6 82.7 %collective-permute-start.46 = (bf16[192,1152]{1,0:T(8,128)(2,1)S(1)}, bf16[192,1152]{1,0:T(8,128)(2,1)S(1)}, u32[]{:S(2)}, u32[]{:S(2)}) collective-permute-start(bf16[192,1152]{1,0:T(8,128)(2,1)S(1)} %fusion.7), channel_id=1, source_target_pairs={{0,12},{4,8},{8,4},{12,0},{1,13},{5,9},{9,5},{13,1},{2,14},{6,10},... | collective-permute-start | bytes 1327112 | tf_op jit(solution)/shard_map/ppermute | solution.py:1006
  500.1 63.5 %collective-permute-start.43 = (bf16[256,768]{1,0:T(8,128)(2,1)S(1)}, bf16[256,768]{1,0:T(8,128)(2,1)S(1)}, u32[]{:S(2)}, u32[]{:S(2)}) collective-permute-start(bf16[256,768]{1,0:T(8,128)(2,1)S(1)} %get-tuple-element.217), channel_id=1, source_target_pairs={{0,4},{4,0},{8,12},{12,8},{16,24},{20,28},{24,16},{28,20},{1,5},{5... | collective-permute-start | bytes 1179656 | tf_op jit(solution)/shard_map/ppermute | solution.py:998
  500.3 63.3 %collective-permute-start.44 = (bf16[256,768]{1,0:T(8,128)(2,1)S(1)}, bf16[256,768]{1,0:T(8,128)(2,1)S(1)}, u32[]{:S(2)}, u32[]{:S(2)}) collective-permute-start(bf16[256,768]{1,0:T(8,128)(2,1)S(1)} %get-tuple-element.218), channel_id=1, source_target_pairs={{16,28},{20,24},{24,20},{28,16},{17,29},{21,25},{25,21},{29,17},{1... | collective-permute-start | bytes 1179656 | tf_op jit(solution)/shard_map/ppermute | solution.py:1002
  504.6 61.1 %collective-permute-start.42 = (bf16[256,768]{1,0:T(8,128)(2,1)S(1)}, bf16[256,768]{1,0:T(8,128)(2,1)S(1)}, u32[]{:S(2)}, u32[]{:S(2)}) collective-permute-start(bf16[256,768]{1,0:T(8,128)(2,1)S(1)} %get-tuple-element.233), channel_id=1, source_target_pairs={{0,16},{16,0},{1,17},{17,1},{2,18},{18,2},{3,19},{19,3},{4,20},{20... | collective-permute-start | bytes 1179656 | tf_op jit(solution)/shard_map/ppermute | solution.py:981
  517.3 101.6 %collective-permute-start.50 = (bf16[192,2048]{1,0:T(8,128)(2,1)S(1)}, bf16[192,2048]{1,0:T(8,128)(2,1)S(1)}, u32[]{:S(2)}, u32[]{:S(2)}) collective-permute-start(bf16[192,2048]{1,0:T(8,128)(2,1)S(1)} %add_convert_fusion), channel_id=1, source_target_pairs={{0,4},{4,0},{8,12},{12,8},{1,5},{5,1},{9,13},{13,9},{2,6},{6,2},{1... | collective-permute-start | bytes 2359304 | tf_op jit(solution)/shard_map/ppermute | solution.py:993
  563.6 35.2 %collective-permute-start.62 = (bf16[192,1536]{1,0:T(8,128)(2,1)S(1)}, bf16[192,1536]{1,0:T(8,128)(2,1)S(1)}, u32[]{:S(2)}, u32[]{:S(2)}) collective-permute-start(bf16[192,1536]{1,0:T(8,128)(2,1)S(1)} %add_convert_fusion.1), channel_id=1, source_target_pairs={{0,4},{4,0},{8,12},{12,8},{1,5},{5,1},{9,13},{13,9},{2,6},{6,2},{1... | collective-permute-start | bytes 1769480 | tf_op jit(solution)/shard_map/ppermute | solution.py:993
  563.7 47.7 %collective-permute-start.55 = (bf16[192,1536]{1,0:T(8,128)(2,1)S(1)}, bf16[192,1536]{1,0:T(8,128)(2,1)S(1)}, u32[]{:S(2)}, u32[]{:S(2)}) collective-permute-start(bf16[192,1536]{1,0:T(8,128)(2,1)S(1)} %add_convert_fusion.2), channel_id=1, source_target_pairs={{0,4},{4,0},{8,12},{12,8},{1,5},{5,1},{9,13},{13,9},{2,6},{6,2},{1... | collective-permute-start | bytes 1769480 | tf_op jit(solution)/shard_map/ppermute | solution.py:993
  581.4 36.6 %collective-permute-start.47 = (bf16[192,1152]{1,0:T(8,128)(2,1)S(1)}, bf16[192,1152]{1,0:T(8,128)(2,1)S(1)}, u32[]{:S(2)}, u32[]{:S(2)}) collective-permute-start(bf16[192,1152]{1,0:T(8,128)(2,1)S(1)} %add_convert_fusion.3), channel_id=1, source_target_pairs={{0,4},{4,0},{8,12},{12,8},{1,5},{5,1},{9,13},{13,9},{2,6},{6,2},{1... | collective-permute-start | bytes 1327112 | tf_op jit(solution)/shard_map/ppermute | solution.py:993
  599.7 31.3 %collective-permute-start.63 = (bf16[192,1536]{1,0:T(8,128)(2,1)}, bf16[192,1536]{1,0:T(8,128)(2,1)}, u32[]{:S(2)}, u32[]{:S(2)}) collective-permute-start(bf16[192,1536]{1,0:T(8,128)(2,1)} %get-tuple-element.229), channel_id=1, source_target_pairs={{0,16},{16,0},{1,17},{17,1},{2,18},{18,2},{3,19},{19,3},{4,20},{20... | collective-permute-start | bytes 1769480 | tf_op jit(solution)/shard_map/ppermute | solution.py:981
  (93 other events, 870.0 us)

commit v4 on v3

--- a/solution.py
+++ b/solution.py
@@ -476,14 +476,24 @@
     return pl.BlockSpec(memory_space=pltpu.SMEM)
 
 
-def kernel_call(body, out_shapes, in_specs, scratch, mbytes, cost, name, out_specs=None, grid=None):
+def kernel_call(
+    body, out_shapes, in_specs, scratch, mbytes, cost, name, out_specs=None, grid=None, prefetch=False
+):
+    out_specs = [in_vmem()] * len(out_shapes) if out_specs is None else out_specs
+    if prefetch:
+        spec = {
+            "grid_spec": pltpu.PrefetchScalarGridSpec(
+                num_scalar_prefetch=1, grid=grid, in_specs=in_specs, out_specs=out_specs, scratch_shapes=scratch
+            )
+        }
+    else:
+        spec = {"in_specs": in_specs, "out_specs": out_specs, "scratch_shapes": scratch}
+        if grid is not None:
+            spec["grid"] = grid
     return pl.pallas_call(
         body,
         out_shape=out_shapes,
-        in_specs=in_specs,
-        out_specs=[in_vmem()] * len(out_shapes) if out_specs is None else out_specs,
-        scratch_shapes=scratch,
-        **({} if grid is None else {"grid": grid}),
+        **spec,
         compiler_params=pltpu.CompilerParams(vmem_limit_bytes=mbytes * 2**20),
         cost_estimate=pl.CostEstimate(flops=0, bytes_accessed=3 * 10**6 * cost, transcendentals=0),
         name=name,
@@ -494,7 +504,7 @@
     return jax.ShapeDtypeStruct(shape, dtype)
 
 
-def start_loads(place, pieces, first, width, scratch, sems, begin, blocks=1):
+def loads_of(place, pieces, first, width, scratch, sems, begin, blocks=1):
     dp_rank, core = place[0], place[1]
     count = pieces[0].shape[0]
     copies = []
@@ -515,9 +525,18 @@
                     sems.at[begin + len(copies)],
                 )
             )
+    return copies
+
+
+def start_loads(*arguments):
+    copies = loads_of(*arguments)
+    start_all(copies)
+    return copies
+
+
+def start_all(copies):
     for copy in copies:
         copy.start()
-    return copies
 
 
 def wait_all(copies):
@@ -570,10 +589,13 @@
     rows, width = queries.shape
     keys = 2 * rows
 
-    def body(col_ref, row_ref, q_ref, b0, b1, out_ref, bias):
-        @pl.when(pl.program_id(0) == 0)
+    def body(col_ref, row_ref, q_ref, b0, b1, out_ref, sum_ref, bias, sums):
+        step = pl.program_id(0)
+
+        @pl.when(step == 0)
         def _():
             bias[...] = jnp.where(col_ref[...] == row_ref[...], 0.0, NEG)
+            sums[...] = jnp.zeros_like(sums)
 
         lane = lax.broadcasted_iota(jnp.int32, (rows, 128), 1)
         query = q_ref[...]
@@ -587,33 +609,40 @@
             exponent = jnp.exp(scores - top)
             total = jnp.sum(exponent, axis=1, keepdims=True)
             results.append(mm(exponent.astype(jnp.bfloat16), value) / total)
+            sums[...] = jnp.where(lane == 2 * step + head, top + jnp.log(total), sums[...])
         out_ref[...] = jnp.where(lane < 64, results[0], results[1]).astype(jnp.bfloat16)
+
+        @pl.when(step == width // 128 - 1)
+        def _():
+            sum_ref[...] = sums[...].T
 
     block = pl.BlockSpec((2, rows, 128), lambda j: (0, 0, j))
     return kernel_call(
         body,
-        [shape_of((rows, width), jnp.bfloat16)],
+        [shape_of((rows, width), jnp.bfloat16), shape_of((128, rows), jnp.float32)],
         [
             pl.BlockSpec((rows, 1), lambda j: (0, 0)),
             pl.BlockSpec((1, keys), lambda j: (0, 0)),
             pl.BlockSpec((rows, 128), lambda j: (0, j)),
             block, block,
         ],
-        [pltpu.VMEM((rows, keys), jnp.float32)],
+        [pltpu.VMEM((rows, keys), jnp.float32), pltpu.VMEM((rows, 128), jnp.float32)],
         60,
         8,
         "attend_rows",
-        [pl.BlockSpec((rows, 128), lambda j: (0, j))],
+        [pl.BlockSpec((rows, 128), lambda j: (0, j)), pl.BlockSpec((128, rows), lambda j: (0, 0))],
         (width // 128,),
-    )(seg_column, seg_row, queries, *blocks)[0]
-
-
-def attend_rows_back(queries, blocks, seg_row, seg_column, incoming):
+    )(seg_column, seg_row, queries, *blocks)
+
+
+def attend_rows_back(queries, blocks, seg_row, seg_column, attended, sums, incoming):
     rows, width = queries.shape
     keys = 2 * rows
 
-    def body(row_ref, col_ref, q_ref, in_ref, b0, b1, dq_ref, own_ref, core_ref, bias):
-        @pl.when(pl.program_id(0) == 0)
+    def body(row_ref, col_ref, sum_ref, q_ref, att_ref, in_ref, b0, b1, dq_ref, own_ref, core_ref, bias):
+        step = pl.program_id(0)
+
+        @pl.when(step == 0)
         def _():
             bias[...] = jnp.where(col_ref[...] == row_ref[...], 0.0, NEG)
 
@@ -622,16 +651,16 @@
         key = jnp.concatenate([b[0] for b in (b0, b1)], axis=0)
         value = jnp.concatenate([b[1] for b in (b0, b1)], axis=0)
         key_t = key.T
+        inner = (given.astype(jnp.float32) * att_ref[...].astype(jnp.float32)).T
         dkeys, dvalues, dqueries = [], [], []
         for head in range(2):
             own = (lane < 64) if head == 0 else (lane >= 64)
             scores = mm(key, jnp.where(own, query, jnp.zeros_like(query)), NT) + bias[...]
-            exponent = jnp.exp(scores - jnp.max(scores, axis=0, keepdims=True))
-            probs = exponent * (1.0 / jnp.sum(exponent, axis=0, keepdims=True))
+            probs = jnp.exp(scores - sum_ref[pl.ds(2 * step + head, 1), :])
             dvalues.append(mm(probs.astype(jnp.bfloat16), given))
-            dprobs = probs * mm(value, jnp.where(own, given, jnp.zeros_like(given)), NT)
-            dscores = dprobs - probs * jnp.sum(dprobs, axis=0, keepdims=True)
-            dscores = dscores.astype(jnp.bfloat16)
+            dprobs = mm(value, jnp.where(own, given, jnp.zeros_like(given)), NT)
+            inner_row = jnp.sum(inner[64 * head : 64 * head + 64], axis=0, keepdims=True)
+            dscores = (probs * (dprobs - inner_row)).astype(jnp.bfloat16)
             dkeys.append(mm(dscores, query))
             dqueries.append(mm(key_t[64 * head : 64 * head + 64], dscores))
         dq_ref[...] = jnp.concatenate(dqueries, axis=0).T * HEAD**-0.5
@@ -654,7 +683,8 @@
         [
             pl.BlockSpec((1, rows), lambda j: (0, 0)),
             pl.BlockSpec((keys, 1), lambda j: (0, 0)),
-            columns, columns, block, block,
+            pl.BlockSpec((128, rows), lambda j: (0, 0)),
+            columns, columns, columns, block, block,
         ],
         [pltpu.VMEM((keys, rows), jnp.float32)],
         60,
@@ -662,7 +692,7 @@
         "attend_rows_back",
         [columns, block, block],
         (width // 128,),
-    )(seg_row, seg_column, queries, incoming, *blocks)
+    )(seg_row, seg_column, sums, queries, attended, incoming, *blocks)
 
 
 def unit_of(resid):
@@ -695,152 +725,203 @@
     ]
 
 
+def mlp_loads(place_ref, parts, scratch, width, ff_half):
+    w_out, w_gate, w_up, w_down, w_norm, _, sems = scratch
+    return (
+        loads_of(place_ref, parts[:8], 2 * width, 128, w_norm, sems, 70),
+        loads_of(place_ref, parts[:8], 3 * width // 2, width // 2, w_out, sems, 0),
+        loads_of(place_ref, parts[8:], 0, ff_half, w_gate, sems, 10),
+        loads_of(place_ref, parts[8:], ff_half, ff_half, w_up, sems, 20),
+        loads_of(place_ref, parts[8:], 2 * ff_half, width // 2, w_down, sems, 30, 4),
+    )
+
+
+MINE = 5
+
+
+def mlp_blocks(ff):
+    steps = ff // FF_STEP
+    return steps, lambda j, place: (place[1] ^ (j // (steps // 2))) * (steps // 2) + j % (steps // 2)
+
+
 def mlp_rows(place, hidden, attended, first_parts, rest_parts):
     rows, width = hidden.shape
     ff_half = (rest_parts[0].shape[1] - 2 * width) // 2
     ff = 2 * ff_half
+    steps, block_of = mlp_blocks(ff)
 
     def body(place_ref, hidden_ref, att_ref, *refs):
         parts, rest = refs[:16], refs[16:]
-        out_ref, one_ref, two_ref, acts_ref, gate_ref, up_ref = rest[:6]
-        w_out, w_gate, w_up, w_down, w_norm, norm_ref, sems = rest[6:]
-        normed_ref = acts_ref.at[:, :width]
-        norm_loads = start_loads(place_ref, parts[:8], 2 * width, 128, w_norm, sems, 70)
-        loads = [
-            start_loads(place_ref, parts[:8], 3 * width // 2, width // 2, w_out, sems, 0),
-            start_loads(place_ref, parts[8:], 0, ff_half, w_gate, sems, 10),
-            start_loads(place_ref, parts[8:], ff_half, ff_half, w_up, sems, 20),
-            start_loads(place_ref, parts[8:], 2 * ff_half, width // 2, w_down, sems, 30, 4),
-        ]
-        wait_all(norm_loads)
-        norm_ref[...] = w_norm[:, :128].astype(jnp.float32).T
-        wait_all(loads[0])
-        resid = hidden_ref[...].astype(jnp.float32) + mm(att_ref[...], w_out[...])
-        one_ref[...] = resid
-        normed = unit_of(resid)[0] * norm_ref[0:1] + norm_ref[1:2]
-        normed_ref[...] = normed.astype(jnp.bfloat16)
-        two_ref[...] = normed
-        wait_all(loads[1])
-        wait_all(loads[2])
-        wait_all(loads[3])
-
-        @pl.loop(0, ff // FF_STEP)
-        def _(step):
-            span = pl.ds(pl.multiple_of(step * FF_STEP, FF_STEP), FF_STEP)
-            gate = mm(normed_ref[...], w_gate[:, span])
-            up = mm(normed_ref[...], w_up[:, span])
-            gate_ref[:, span] = gate
-            up_ref[:, span] = up
-            middle = (gate * jax.nn.sigmoid(gate) * up).astype(jnp.bfloat16)
-            acts_ref[:, pl.ds(pl.multiple_of(width + step * FF_STEP, 128), FF_STEP)] = middle
-            two_ref[...] += mm(middle, w_down[span, :])
-
-        out_ref[...] = (unit_of(two_ref[...])[0] * norm_ref[2:3] + norm_ref[3:4]).astype(jnp.bfloat16)
-
+        out_ref, one_ref, two_ref, normed_ref, mid_ref, gate_ref, up_ref = rest[:7]
+        w_out, w_gate, w_up, w_down, w_norm, norm_ref, _ = rest[7:]
+        step = pl.program_id(0)
+        norm, out, gates, ups, downs = mlp_loads(place_ref, parts, rest[7:], width, ff_half)
+
+        @pl.when(step == 0)
+        def _():
+            for copies in (norm, out, gates[:MINE], ups[:MINE], downs, gates[MINE:], ups[MINE:]):
+                start_all(copies)
+            wait_all(norm)
+            norm_ref[...] = w_norm[:, :128].astype(jnp.float32).T
+            wait_all(out)
+            resid = hidden_ref[...].astype(jnp.float32) + mm(att_ref[...], w_out[...])
+            one_ref[...] = resid
+            normed = unit_of(resid)[0] * norm_ref[0:1] + norm_ref[1:2]
+            normed_ref[...] = normed.astype(jnp.bfloat16)
+            two_ref[...] = normed
+            wait_all(gates[:MINE])
+            wait_all(ups[:MINE])
+
+        @pl.when(step == steps // 2)
+        def _():
+            wait_all(gates[MINE:])
+            wait_all(ups[MINE:])
+
+        span = pl.ds(pl.multiple_of(block_of(step, place_ref) * FF_STEP, FF_STEP), FF_STEP)
+        gate = mm(normed_ref[...], w_gate[:, span])
+        up = mm(normed_ref[...], w_up[:, span])
+        gate_ref[...] = gate.astype(jnp.bfloat16)
+        up_ref[...] = up.astype(jnp.bfloat16)
+        middle = (gate * jax.nn.sigmoid(gate) * up).astype(jnp.bfloat16)
+        mid_ref[...] = middle
+
+        @pl.when(step == 0)
+        def _():
+            wait_all(downs)
+
+        two_ref[...] += mm(middle, w_down[span, :])
+
+        @pl.when(step == steps - 1)
+        def _():
+            out_ref[...] = (unit_of(two_ref[...])[0] * norm_ref[2:3] + norm_ref[3:4]).astype(jnp.bfloat16)
+
+    whole = pl.BlockSpec((rows, width), lambda j, place: (0, 0))
+    part = pl.BlockSpec((rows, FF_STEP), lambda j, place: (0, block_of(j, place)))
     return kernel_call(
         body,
         [
             shape_of((rows, width), jnp.bfloat16),
             shape_of((rows, width), jnp.float32),
             shape_of((rows, width), jnp.float32),
-            shape_of((rows, width + ff), jnp.bfloat16),
-            shape_of((rows, ff), jnp.float32),
-            shape_of((rows, ff), jnp.float32),
+            shape_of((rows, width), jnp.bfloat16),
+            shape_of((rows, ff), jnp.bfloat16),
+            shape_of((rows, ff), jnp.bfloat16),
+            shape_of((rows, ff), jnp.bfloat16),
         ],
-        [in_smem()] + [in_vmem()] * 2 + [anywhere()] * 16,
+        [whole, whole] + [anywhere()] * 16,
         mlp_scratch(width, ff),
         60,
         16,
         "mlp_rows",
+        [whole] * 4 + [part] * 3,
+        (steps,),
+        True,
     )(place, hidden, attended, *first_parts, *rest_parts)
 
 
-def mlp_rows_back(place, incoming, one, two, gate, up, first_parts, rest_parts):
+def mlp_rows_back(place, incoming, one, two, gate, up, first_parts, rest_parts, for_weights):
     rows, width = incoming.shape
     ff_half = (rest_parts[0].shape[1] - 2 * width) // 2
     ff = 2 * ff_half
+    steps, block_of = mlp_blocks(ff)
+    extra = 6 if for_weights else 0
 
     def body(place_ref, in_ref, one_ref, two_ref, gate_ref, up_ref, *refs):
-        parts, rest = refs[:16], refs[16:]
-        keep_ref, send_ref, keep_ff, send_ff, dresid_ref, datt_ref = rest[:6]
-        w_out, w_gate, w_up, w_down, w_norm, norm_ref, sems, low_ref, sums_ref = rest[6:]
-        core = place_ref[1]
-        norm_loads = start_loads(place_ref, parts[:8], 2 * width, 128, w_norm, sems, 70)
-
-        def share(half, columns, value, keep, send):
-            @pl.when(half == core)
+        parts, outs, rest = refs[:16], refs[16 : 18 + extra], refs[18 + extra :]
+        dresid_ref, datt_ref = outs[:2]
+        w_out, w_gate, w_up, w_down, w_norm, norm_ref, _, low_ref, sums_ref = rest
+        step = pl.program_id(0)
+        norm, out, gates, ups, downs = mlp_loads(place_ref, parts, rest[:7], width, ff_half)
+
+        def share(column):
+            half = width // 2
+            low, first = low_ref[...], place_ref[1] == 0
+            for ref, mine in ((outs[2], True), (outs[3], False)):
+                ref[:rows, column : column + half] = jnp.where(
+                    first == mine, low[:, :half], low[:, half:]
+                )
+
+        @pl.when(step == 0)
+        def _():
+            for copies in (norm, downs, gates[:MINE], ups[:MINE], gates[MINE:], ups[MINE:], out):
+                start_all(copies)
+            wait_all(norm)
+            norm_ref[...] = w_norm[:, :128].astype(jnp.float32).T
+            given = in_ref[...].astype(jnp.float32)
+            unit, scaling = unit_of(two_ref[...])
+            dresid_two = norm_rows_back(given, unit, scaling, norm_ref[2:3])
+            dresid_ref[...] = dresid_two
+            low_ref[...] = dresid_two.astype(jnp.bfloat16)
+            if for_weights:
+                sums_ref[...] = jnp.zeros_like(sums_ref)
+                sums_ref[2:3] = jnp.sum(given * unit, axis=0, keepdims=True)
+                sums_ref[3:4] = jnp.sum(given, axis=0, keepdims=True)
+                share(0)
+            wait_all(downs)
+            wait_all(gates[:MINE])
+            wait_all(ups[:MINE])
+
+        @pl.when(step == steps // 2)
+        def _():
+            wait_all(gates[MINE:])
+            wait_all(ups[MINE:])
+
+        span = pl.ds(pl.multiple_of(block_of(step, place_ref) * FF_STEP, FF_STEP), FF_STEP)
+        dmiddle = mm(low_ref[...], w_down[span, :], NT)
+        gate_block = gate_ref[...].astype(jnp.float32)
+        sig = jax.nn.sigmoid(gate_block)
+        swish = gate_block * sig
+        dup = (dmiddle * swish).astype(jnp.bfloat16)
+        dgate = (dmiddle * up_ref[...].astype(jnp.float32) * (sig + swish * (1.0 - sig))).astype(jnp.bfloat16)
+        if for_weights:
+            @pl.when(step < steps // 2)
             def _():
-                keep[:rows, columns] = value
-
-            @pl.when(half != core)
+                outs[4][...], outs[5][...] = dgate, dup
+
+            @pl.when(step >= steps // 2)
             def _():
-                send[:rows, columns] = value
-
-        loads = [
-            start_loads(place_ref, parts[8:], 2 * ff_half, width // 2, w_down, sems, 30, 4),
-            start_loads(place_ref, parts[8:], 0, ff_half, w_gate, sems, 10),
-            start_loads(place_ref, parts[8:], ff_half, ff_half, w_up, sems, 20),
-            start_loads(place_ref, parts[:8], 3 * width // 2, width // 2, w_out, sems, 0),
-        ]
-        wait_all(norm_loads)
-        norm_ref[...] = w_norm[:, :128].astype(jnp.float32).T
-        sums_ref[...] = jnp.zeros_like(sums_ref)
-        given = in_ref[...].astype(jnp.float32)
-        unit, scaling = unit_of(two_ref[...])
-        sums_ref[2:3] = jnp.sum(given * unit, axis=0, keepdims=True)
-        sums_ref[3:4] = jnp.sum(given, axis=0, keepdims=True)
-        dresid_two = norm_rows_back(given, unit, scaling, norm_ref[2:3])
-        dresid_ref[...] = dresid_two
-        low_ref[...] = dresid_two.astype(jnp.bfloat16)
-        for half in range(2):
-            span = slice(half * width // 2, (half + 1) * width // 2)
-            share(half, slice(0, width // 2), low_ref[:, span], keep_ref, send_ref)
-        for copies in loads:
-            wait_all(copies)
-
-        @pl.loop(0, ff // FF_STEP)
-        def _(step):
-            span = pl.ds(pl.multiple_of(step * FF_STEP, FF_STEP), FF_STEP)
-            dmiddle = mm(low_ref[...], w_down[span, :], NT)
-            gate_block = gate_ref[:, span]
-            sig = jax.nn.sigmoid(gate_block)
-            dgate = (dmiddle * up_ref[:, span] * sig * (1.0 + gate_block * (1.0 - sig))).astype(jnp.bfloat16)
-            dup = (dmiddle * (gate_block * sig)).astype(jnp.bfloat16)
-            half, column = step // (ff_half // FF_STEP), step % (ff_half // FF_STEP) * FF_STEP
-            share(half, pl.ds(pl.multiple_of(column, 128), FF_STEP), dgate, keep_ff, send_ff)
-            share(half, pl.ds(pl.multiple_of(column + ff_half, 128), FF_STEP), dup, keep_ff, send_ff)
-            dresid_ref[...] += mm(dgate, w_gate[:, span], NT) + mm(dup, w_up[:, span], NT)
-
-        dnormed = dresid_ref[...]
-        unit, scaling = unit_of(one_ref[...])
-        sums_ref[0:1] = jnp.sum(dnormed * unit, axis=0, keepdims=True)
-        sums_ref[1:2] = jnp.sum(dnormed, axis=0, keepdims=True)
-        dresid_one = norm_rows_back(dnormed, unit, scaling, norm_ref[0:1])
-        dresid_ref[...] = dresid_one
-        low_ref[...] = dresid_one.astype(jnp.bfloat16)
-        for half in range(2):
-            span = slice(half * width // 2, (half + 1) * width // 2)
-            share(half, slice(width // 2, width), low_ref[:, span], keep_ref, send_ref)
-        datt_ref[...] = mm(low_ref[...], w_out[...], NT).astype(jnp.bfloat16)
-        for ref in (keep_ref, send_ref):
-            ref[rows:] = sums_ref[...].astype(jnp.bfloat16)
-
+                outs[6][...], outs[7][...] = dgate, dup
+
+        dresid_ref[...] += mm(dgate, w_gate[:, span], NT) + mm(dup, w_up[:, span], NT)
+
+        @pl.when(step == steps - 1)
+        def _():
+            wait_all(out)
+            dnormed = dresid_ref[...]
+            unit, scaling = unit_of(one_ref[...])
+            dresid_one = norm_rows_back(dnormed, unit, scaling, norm_ref[0:1])
+            dresid_ref[...] = dresid_one
+            low_ref[...] = dresid_one.astype(jnp.bfloat16)
+            if for_weights:
+                sums_ref[0:1] = jnp.sum(dnormed * unit, axis=0, keepdims=True)
+                sums_ref[1:2] = jnp.sum(dnormed, axis=0, keepdims=True)
+                share(width // 2)
+                for ref in outs[2:4]:
+                    ref[rows:] = sums_ref[...].astype(jnp.bfloat16)
+            datt_ref[...] = mm(low_ref[...], w_out[...], NT).astype(jnp.bfloat16)
+
+    half_steps = steps // 2
+    whole = pl.BlockSpec((rows, width), lambda j, place: (0, 0))
+    longer = pl.BlockSpec((rows + 16, width), lambda j, place: (0, 0))
+    part = pl.BlockSpec((rows, FF_STEP), lambda j, place: (0, block_of(j, place)))
+    mine = pl.BlockSpec((rows, FF_STEP), lambda j, place: (0, jnp.minimum(j, half_steps - 1)))
+    theirs = pl.BlockSpec((rows, FF_STEP), lambda j, place: (0, jnp.maximum(j - half_steps, 0)))
+    shapes = [shape_of((rows, width), jnp.float32), shape_of((rows, width), jnp.bfloat16)]
+    specs = [whole, whole]
+    if for_weights:
+        shapes += [shape_of((rows + 16, width), jnp.bfloat16)] * 2 + [shape_of((rows, ff_half), jnp.bfloat16)] * 4
+        specs += [longer] * 2 + [mine] * 2 + [theirs] * 2
     return kernel_call(
         body,
-        [
-            shape_of((rows + 16, width), jnp.bfloat16),
-            shape_of((rows + 16, width), jnp.bfloat16),
-            shape_of((rows, ff), jnp.bfloat16),
-            shape_of((rows, ff), jnp.bfloat16),
-            shape_of((rows, width), jnp.float32),
-            shape_of((rows, width), jnp.bfloat16),
-        ],
-        [in_smem()] + [in_vmem()] * 5 + [anywhere()] * 16,
-        mlp_scratch(width, ff)
-        + [pltpu.VMEM((rows, width), jnp.bfloat16), pltpu.VMEM((16, width), jnp.float32)],
+        shapes,
+        [whole, whole, whole, part, part] + [anywhere()] * 16,
+        mlp_scratch(width, ff) + [pltpu.VMEM((rows, width), jnp.bfloat16), pltpu.VMEM((16, width), jnp.float32)],
         60,
         21,
         "mlp_rows_back",
+        specs,
+        (steps,),
+        True,
     )(place, incoming, one, two, gate, up, *first_parts, *rest_parts)
 
 
@@ -1076,10 +1157,19 @@
     )
 
 
-def reduce_ctx(piece, middle, *others):
-    mine = lowered(wide(piece) + wide(same_role(piece)))
-    other = along_z(after(mine, *others))
-    return jnp.where(middle, other, mine), jnp.where(middle, mine, other)
+def reduce_ctx(pieces, middle, last):
+    received = [same_role(pieces[0])]
+    mine, others = [], []
+    for index, piece in enumerate(pieces):
+        mine.append(lowered(wide(piece) + wide(after(received[index], *last))))
+        last = (mine[index],)
+        others.append(along_z(mine[index]))
+        if index + 1 < len(pieces):
+            ready = pieces[index + 1] if index == 0 else after(pieces[index + 1], received[index - 1], mine[index - 1])
+            received.append(same_role(ready))
+    return [
+        (jnp.where(middle, theirs, own), jnp.where(middle, own, theirs)) for own, theirs in zip(mine, others)
+    ]
 
 
 def paired_on_device(
@@ -1133,30 +1223,28 @@
     norm_columns = jnp.concatenate([norm1_gain, norm1_bias, norm2_gain, norm2_bias], axis=0).T
     norm_columns = jnp.pad(norm_columns, ((0, 0), (0, 124)))
 
-    def packs(which):
-        return (
-            jnp.concatenate(
-                [half_of(query_key_value_weight[0], which), half_of(output_weight[0], which), norm_columns],
-                axis=1,
-            ),
-            jnp.concatenate(
-                [half_of(gate_weight[0], which), half_of(up_weight[0], which)]
-                + jnp.split(half_of(down_weight[0], which), down_weight.shape[1] // gate_weight.shape[1]),
-                axis=1,
-            ),
+    def first_pack(which):
+        return jnp.concatenate(
+            [half_of(query_key_value_weight[0], which), half_of(output_weight[0], which), norm_columns], axis=1
         )
 
-    own_halves, other_halves = packs(core), packs(1 - core)
-    sent = [to_core(pack) for pack in other_halves]
-    sent += [to_core(after(pack, *sent)) for pack in own_halves]
-    count = len(own_halves)
-    pieces = [
-        (
-            jnp.where(core == role, own_halves[index], sent[index]),
-            jnp.where(core == role, other_halves[index], sent[count + index]),
+    def rest_pack(which, *others):
+        gate, up, down = after((gate_weight[0], up_weight[0], down_weight[0]), *others)
+        return jnp.concatenate(
+            [half_of(gate, which), half_of(up, which)]
+            + jnp.split(half_of(down, which), down.shape[0] // gate.shape[0]),
+            axis=1,
         )
-        for index in range(count)
-    ]
+
+    def choose(own, other, other_sent, own_sent):
+        return jnp.where(core == role, own, other_sent), jnp.where(core == role, other, own_sent)
+
+    own, other = first_pack(core), first_pack(1 - core)
+    other_sent = to_core(other)
+    first_pieces = choose(own, other, other_sent, to_core(after(own, other_sent)))
+    own, other = rest_pack(core, other_sent), rest_pack(1 - core, other_sent)
+    rest_pieces = choose(own, other, to_core(other), to_core(after(own, other_sent)))
+    tokens, cotangent = after((tokens, cotangent), other_sent)
 
     seg = pick(seg_ids, sequence)
     rows = 2 * span
@@ -1174,26 +1262,26 @@
     def attention(hidden):
         queries, own = project_rows(place, hidden, cosine, sine, first)
         blocks = [own, to_core(own)]
-        return queries, blocks, attend_rows(queries, blocks, seg_rows[:, None], seg_keys[None, :])
+        return queries, blocks, *attend_rows(queries, blocks, seg_rows[:, None], seg_keys[None, :])
 
     given = to_rows()
-    near = gather_near(pieces[0])
+    near = gather_near(first_pieces)
     far = gather_far(near)
-    near_mlp = gather_near(pieces[1], *far)
+    near_mlp = gather_near(rest_pieces, *far)
     first = both_cores(near, far)
-    queries, blocks, attended = attention(given)
+    queries, blocks, attended, sums = attention(given)
     near_mlp = [after(part, attended) for part in near_mlp]
     rest = both_cores(near_mlp, gather_far(near_mlp))
     output = mlp_rows(place, given, attended, first, rest)[0]
 
     hidden = jnp.where(middle, along_z(output), given)
-    queries, blocks, attended = attention(hidden)
-    output, one, two, acts, gate, up = mlp_rows(place, hidden, attended, first, rest)
-
-    _, _, _, _, dresid_one, dattended = mlp_rows_back(place, given, one, two, gate, up, first, rest)
+    queries, blocks, attended, sums = attention(hidden)
+    output, one, two, normed, mids, gate, up = mlp_rows(place, hidden, attended, first, rest)
+
+    dresid_one, dattended = mlp_rows_back(place, given, one, two, gate, up, first, rest, False)
     sent_outputs = send_rows(output)
     dqueries, own, across = attend_rows_back(
-        queries, blocks, seg_rows[None, :], seg_keys[:, None], after(dattended, *sent_outputs)
+        queries, blocks, seg_rows[None, :], seg_keys[:, None], attended, sums, after(dattended, *sent_outputs)
     )
     dhidden = project_rows_back(
         place, dqueries, (own, to_core(across)), dresid_one, cosine, sine, first
@@ -1201,28 +1289,26 @@
     incoming = jnp.where(middle, given, along_z(lowered(dhidden)))
 
     both = lambda value: (value, to_core(value))
-    acts, attended, hidden = both(acts), both(attended), both(hidden)
-    keep, send, keep_ff, send_ff, dresid_one, dattended = mlp_rows_back(
-        place, incoming, one, two, gate, up, first, rest
-    )
-    ff = keep_ff.shape[1]
-    right, right_ff = (keep, to_core(send)), (keep_ff, to_core(send_ff))
+    mids, normed, attended, hidden = both(mids), both(normed), both(attended), both(hidden)
+    dresid_one, dattended, keep, send, keep_gate, keep_up, send_gate, send_up = mlp_rows_back(
+        place, incoming, one, two, gate, up, first, rest, True
+    )
+    ff = mids[0].shape[1]
+    right, right_gate, right_up = (keep, to_core(send)), (keep_gate, to_core(send_gate)), (keep_up, to_core(send_up))
     parts = grad_parts(
         place,
         [
             [
-                (acts, (width, width + ff), right, (0, width // 2), ff // width),
+                (mids, (0, ff), right, (0, width // 2), ff // width),
                 (attended, (0, width), right, (width // 2, width), 1),
             ]
         ],
         1,
     )
-    right_ff = (after(right_ff[0], *parts[0]), right_ff[1])
-    parts += grad_parts(
-        place, [[(acts, (0, width), right_ff, (half * ff // 2, (half + 1) * ff // 2), 1)] for half in range(2)]
-    )
+    normed = (after(normed[0], *parts[0]), normed[1])
+    parts += grad_parts(place, [[(normed, (0, width), pair, (0, ff // 2), 1)] for pair in (right_gate, right_up)])
     dqueries, own, across = attend_rows_back(
-        queries, blocks, seg_rows[None, :], seg_keys[:, None], after(dattended, *(x for part in parts for x in part))
+        queries, blocks, seg_rows[None, :], seg_keys[:, None], attended[0], sums, after(dattended, *(x for part in parts for x in part))
     )
     near = [reduce_first(parts[0])]
     near.append(reduce_first(parts[1]))
@@ -1237,8 +1323,8 @@
     far.append(reduce_second(parts[2], near[2], *parts[3]))
     far.append(reduce_second(parts[3], near[3]))
     pieces = [reduce_last(*group) for group in zip(parts, near, far)]
-    pieces[0] = after(pieces[0], *parts[3])
-    totals = [reduce_ctx(piece, middle, *far[3]) for piece in pieces]
+    pieces[1:] = [after(piece, *parts[3]) for piece in pieces[1:]]
+    totals = reduce_ctx(pieces, middle, parts[3])
 
     pairs = []
     for first_layer, second_layer in totals:

time: 650 us -> 594 us (0.914)
  waiting for transfers between devices: 173 us -> 140 us
  Pallas kernels: 256 us -> 224 us
  starting transfers between devices: 119 us -> 129 us
    ppermute x12, waiting for transfers between devices: 38.1 us -> 18.1 us  [along_y(): return lax.ppermute(value, 'dp', [(i, i ^ 2) for i in range(4)])]
    pallas_call x2, Pallas kernels: 54.1 us -> 39.9 us  [attend_rows_back(): kernel_call(body, [shape_of((rows, width), jnp.float32), pair_shape, pair...]
    ppermute x6, waiting for transfers between devices: 70.3 us -> 58.6 us  [along_z(): return lax.ppermute(value, 'ctx', [(i, i ^ 1) for i in range(4)])]
    pallas_call x4, Pallas kernels: 93.3 us -> 81.7 us  [the longest x2 50.1 us: mlp_rows_back(): kernel_call(body, shapes, [whole, whole, whole, part, part] + [anywhere()...]
    unnamed x115 -> x105, local copies, waits for them, and re-layouts: 24.7 us -> 20.7 us
    ppermute x24 -> x26, starting transfers between devices: 25.3 us -> 28.4 us  [to_core(): return lax.ppermute(value, 'section', [(0, 1), (1, 0)])]
    ppermute x24 -> x26, waiting for transfers between devices: 21.4 us -> 22.6 us  [to_core(): return lax.ppermute(value, 'section', [(0, 1), (1, 0)])]
  transfers between devices with their start and end apart: 64 -> 66, of which waited for: 26 -> 23; matrix products, arithmetic and copies ran while one was open for 9% -> 11% of each run, Pallas kernels for 24% -> 24%
where the time goes in v4:
time: 594 us; the launch traced here: 583 us
  Pallas kernels  224 us (38%)
  waiting for transfers between devices  140 us (24%)
  starting transfers between devices  129 us (22%)
  other arithmetic  57.2 us (10%)
  local copies, waits for them, and re-layouts  31.6 us (5%)
    ppermute x6, starting transfers between devices, along_z(): return lax.ppermute(value, 'ctx', [(i, i ^ 1) for i in range(4)])  58.6 us
    ppermute x6, waiting for transfers between devices, along_z(): return lax.ppermute(value, 'ctx', [(i, i ^ 1) for i in range(4)])  58.6 us
    pallas_call x2, Pallas kernels, mlp_rows_back(): kernel_call(body, shapes, [whole, whole, whole, part, part] + [anywhere()...  50.1 us
    pallas_call x2, Pallas kernels, mlp_rows(): kernel_call(body, [shape_of((rows, width), jnp.bfloat16), shape_of((rows,...  42.2 us
    pallas_call x2, Pallas kernels, attend_rows_back(): kernel_call(body, [shape_of((rows, width), jnp.float32), pair_shape, pair...  39.9 us
    pallas_call x2, Pallas kernels, attend_rows(): kernel_call(body, [shape_of((rows, width), jnp.bfloat16), shape_of((128,...  31.6 us
    ppermute x26, starting transfers between devices, to_core(): return lax.ppermute(value, 'section', [(0, 1), (1, 0)])  28.4 us
    pallas_call x3, Pallas kernels, grad_parts(): kernel_call(body, shapes, [in_smem()] + [in_vmem()] * len(arrays), scratc...  27.2 us
  transfers between devices with their start and end apart: 66, of which 23 were waited for; matrix products, arithmetic and copies ran while one was open for 11% of the time, Pallas kernels for 24%

profile of v4, /device:TPU:0, one launch (start us, length us, event | category | flops | bytes accessed | tf_op | source)
XLA Modules:
  0.0 583.5 jit_solution(2705644603688915246)
XLA Ops:
  37.5 8.1 %collective-permute-start.8 = (bf16[384,1664]{1,0:T(8,128)(2,1)S(1)}, bf16[384,1664]{1,0:T(8,128)(2,1)S(1)}, u32[]{:S(2)}, u32[]{:S(2)}) collective-permute-start(bf16[384,1664]{1,0:T(8,128)(2,1)S(1)} %pad_maximum_fusion.2), channel_id=1, source_target_pairs={{0,16},{16,0},{1,17},{17,1},{2,18},{18,2},{3,19},{19,3},{4,20},{20... | collective-permute-start | bytes 3833864 | tf_op jit(solution)/shard_map/ppermute | solution.py:1062
  57.2 6.5 %project_rows.2 = (bf16[512,768]{1,0:T(8,128)(2,1)}, bf16[2,512,768]{2,1,0:T(8,128)(2,1)}) custom-call(s32[2]{0:T(128)} %pad_add_fusion.1.place_ref, bf16[512,768]{1,0:T(8,128)(2,1)} %maximum_select_fusion.4.hidden_ref.in_ref, f32[512,128]{1,0:T(8,128)} %get-tuple-element.301.cos_ref, f32[512,128]{1,0:T(8,128)} %get-tuple-element.300.sin_ref, ...), custom_call_target="tpu_custom_call" | custom-call | bytes 9000000 | tf_op jit(solution)/shard_map/project_rows/pallas_call | solution.py:577
  68.5 15.8 %attend_rows.2 = (bf16[512,768]{1,0:T(8,128)(2,1)}, f32[128,512]{1,0:T(8,128)}) custom-call(s32[512,1]{1,0:T(8,128)} %copy.53.col_ref, s32[1,1024]{1,0:T(1,128)} %bitcast.89, bf16[512,768]{1,0:T(8,128)(2,1)} %get-tuple-element.111.q_ref, bf16[2,512,768]{2,1,0:T(8,128)(2,1)} %get-tuple-element.112.b0, bf16[2,512,768]{2,1,0:T(8,128)(2,1)} %copy-done.18), custom_call_target="tpu_custom_call" | custom-call | bytes 24000000 | tf_op jit(solution)/shard_map/attend_rows/pallas_call | solution.py:620
  84.3 9.5 %collective-permute-done.13.refs_10_ = bf16[192,4608]{1,0:T(8,128)(2,1)} collective-permute-done((bf16[192,4608]{1,0:T(8,128)(2,1)}, bf16[192,4608]{1,0:T(8,128)(2,1)}, u32[]{:S(2)}, u32[]{:S(2)}) %collective-permute-start.13) | collective-permute-done | bytes 1769504 | tf_op jit(solution)/shard_map/ppermute | solution.py:1070
  101.9 19.0 %collective-permute-done.14.refs_11_ = bf16[96,4608]{1,0:T(8,128)(2,1)S(1)} collective-permute-done((bf16[96,4608]{1,0:T(8,128)(2,1)S(1)}, bf16[96,4608]{1,0:T(8,128)(2,1)S(1)}, u32[]{:S(2)}, u32[]{:S(2)}) %collective-permute-start.14) | collective-permute-done | bytes 884768 | tf_op jit(solution)/shard_map/ppermute | solution.py:1066
  128.6 21.2 %mlp_rows.2 = (bf16[512,768]{1,0:T(8,128)(2,1)}, f32[512,768]{1,0:T(8,128)}, f32[512,768]{1,0:T(8,128)}, bf16[512,768]{1,0:T(8,128)(2,1)}, bf16[512,3072]{1,0:T(...) custom-call(s32[2]{0:T(128)} %pad_add_fusion.1.place_ref, ...), custom_call_target="tpu_custom_call" | custom-call | bytes 48000000 | tf_op jit(solution)/shard_map/mlp_rows/pallas_call | solution.py:800
  149.9 19.7 %collective-permute-done.19 = bf16[512,768]{1,0:T(8,128)(2,1)S(1)} collective-permute-done((bf16[512,768]{1,0:T(8,128)(2,1)}, bf16[512,768]{1,0:T(8,128)(2,1)S(1)}, u32[]{:S(2)}, u32[]{:S(2)}) %collective-permute-start.19) | collective-permute-done | bytes 786464 | tf_op jit(solution)/shard_map/ppermute | solution.py:1074
  171.8 6.5 %project_rows.3 = (bf16[512,768]{1,0:T(8,128)(2,1)}, bf16[2,512,768]{2,1,0:T(8,128)(2,1)}) custom-call(s32[2]{0:T(128)} %pad_add_fusion.1.place_ref, bf16[512,768]{1,0:T(8,128)(2,1)} %broadcast_select_fusion.9.hidden_ref.refs_0_, f32[512,128]{1,0:T(8,128)} %get-tuple-element.301.cos_ref, f32[512,128]{1,0:T(8,128)} %get-tuple-element.300.sin_ref, ...), custom_call_target="tpu_custom_call" | custom-call | bytes 9000000 | tf_op jit(solution)/shard_map/project_rows/pallas_call | solution.py:577
  183.2 15.8 %attend_rows.3 = (bf16[512,768]{1,0:T(8,128)(2,1)}, f32[128,512]{1,0:T(8,128)}) custom-call(s32[512,1]{1,0:T(8,128)} %copy.53.col_ref, s32[1,1024]{1,0:T(1,128)} %bitcast.90, bf16[512,768]{1,0:T(8,128)(2,1)} %get-tuple-element.124.q_ref, bf16[2,512,768]{2,1,0:T(8,128)(2,1)} %get-tuple-element.125.b0, bf16[2,512,768]{2,1,0:T(8,128)(2,1)} %copy-done.11), custom_call_target="tpu_custom_call" | custom-call | bytes 24000000 | tf_op jit(solution)/shard_map/attend_rows/pallas_call | solution.py:620
  199.0 21.0 %mlp_rows.3 = (bf16[512,768]{1,0:T(8,128)(2,1)}, f32[512,768]{1,0:T(8,128)}, f32[512,768]{1,0:T(8,128)}, bf16[512,768]{1,0:T(8,128)(2,1)}, bf16[512,3072]{1,0:T(...) custom-call(s32[2]{0:T(128)} %pad_add_fusion.1.place_ref, ...), custom_call_target="tpu_custom_call" | custom-call | bytes 48000000 | tf_op jit(solution)/shard_map/mlp_rows/pallas_call | solution.py:800
  223.0 23.0 %mlp_rows_back.2 = (f32[512,768]{1,0:T(8,128)}, bf16[512,768]{1,0:T(8,128)(2,1)}) custom-call(s32[2]{0:T(128)} %pad_add_fusion.1.place_ref, bf16[512,768]{1,0:T(8,128)(2,1)} %maximum_select_fusion.4.hidden_ref.in_ref, f32[512,768]{1,0:T(8,128)} %get-tuple-element.129.one_ref, f32[512,768]{1,0:T(8,128)} %get-tuple-element.130.two_ref, ...), custom_call_target="tpu_custom_call" | custom-call | bytes 63000000 | tf_op jit(solution)/shard_map/mlp_rows_back/pallas_call | solution.py:914
  246.1 19.9 %attend_rows_back.2 = (f32[512,768]{1,0:T(8,128)}, bf16[2,512,768]{2,1,0:T(8,128)(2,1)}, bf16[2,512,768]{2,1,0:T(8,128)(2,1)}) custom-call(s32[1,512]{1,0:T(1,128)} %copy-done.43, s32[1024,1]{1,0:T(8,128)} %copy.56.col_ref, f32[128,512]{1,0:T(8,128)} %get-tuple-element.128.sum_ref, bf16[512,768]{1,0:T(8,128)(2,1)} %get-tuple-element.124.q_ref, ...), custom_call_target="tpu_custom_call" | custom-call | bytes 54000000 | tf_op jit(solution)/shard_map/attend_rows_back/pallas_call | solution.py:676
  275.6 9.8 %project_rows_back.2 = (bf16[512,1152]{1,0:T(8,128)(2,1)}, bf16[512,1152]{1,0:T(8,128)(2,1)}, f32[512,768]{1,0:T(8,128)}) custom-call(s32[2]{0:T(128)} %pad_add_fusion.1.place_ref, f32[512,768]{1,0:T(8,128)} %get-tuple-element.135.dq_ref, f32[512,768]{1,0:T(8,128)} %get-tuple-element.136.resid_ref, f32[512,128]{1,0:T(8,128)} %get-tuple-element.301.cos_ref, ...), custom_call_target="tpu_custom_call" | custom-call | bytes 18000000 | tf_op jit(solution)/shard_map/project_rows_back/pallas_call | solution.py:957
  287.9 19.1 %collective-permute-done.25 = bf16[512,768]{1,0:T(8,128)(2,1)S(1)} collective-permute-done((bf16[512,768]{1,0:T(8,128)(2,1)S(1)}, bf16[512,768]{1,0:T(8,128)(2,1)S(1)}, u32[]{:S(2)}, u32[]{:S(2)}) %collective-permute-start.25) | collective-permute-done | bytes 786464 | tf_op jit(solution)/shard_map/ppermute | solution.py:1074
  307.9 27.1 %mlp_rows_back.3 = (f32[512,768]{1,0:T(8,128)}, bf16[512,768]{1,0:T(8,128)(2,1)}, bf16[528,768]{1,0:T(8,128)(2,1)}, bf16[528,768]{1,0:T(8,128)(2,1)}, bf16[512,1...) custom-call(s32[2]{0:T(128)} %pad_add_fusion.1.place_ref, ...), custom_call_target="tpu_custom_call" | custom-call | bytes 63000000 | tf_op jit(solution)/shard_map/mlp_rows_back/pallas_call | solution.py:914
  336.2 6.4 %collective-permute-done.27.refs_3_ = bf16[528,768]{1,0:T(8,128)(2,1)S(1)} collective-permute-done((bf16[528,768]{1,0:T(8,128)(2,1)}, bf16[528,768]{1,0:T(8,128)(2,1)S(1)}, u32[]{:S(2)}, u32[]{:S(2)}) %collective-permute-start.27) | collective-permute-done | bytes 811040 | tf_op jit(solution)/shard_map/ppermute | solution.py:1062
  343.4 11.1 %grad_parts.3 = (bf16[192,2048]{1,0:T(8,128)(2,1)}, bf16[192,2048]{1,0:T(8,128)(2,1)}, bf16[192,2048]{1,0:T(8,128)(2,1)}, bf16[96,2048]{1,0:T(8,128)(2,1)}, bf16[96,2048]{1,0:T(8,128)(2,1)}) custom-call(s32[2]{0:T(128)} %pad_add_fusion.1.place_ref, bf16[512,3072]{1,0:T(8,128)(2,1)} %get-tuple-element.141.refs_0_, ...), custom_call_target="tpu_custom_call" | custom-call | bytes 21000000 | tf_op jit(solution)/shard_map/grad_parts/pallas_call | solution.py:1055
  357.8 9.9 %grad_parts.4 = (bf16[192,1536]{1,0:T(8,128)(2,1)}, bf16[192,1536]{1,0:T(8,128)(2,1)}, bf16[192,1536]{1,0:T(8,128)(2,1)}, bf16[96,1536]{1,0:T(8,128)(2,1)}, bf16...) custom-call(s32[2]{0:T(128)} %pad_add_fusion.1.place_ref, ...), custom_call_target="tpu_custom_call" | custom-call | bytes 21000000 | tf_op jit(solution)/shard_map/grad_parts/pallas_call | solution.py:1055
  369.7 19.9 %attend_rows_back.3 = (f32[512,768]{1,0:T(8,128)}, bf16[2,512,768]{2,1,0:T(8,128)(2,1)}, bf16[2,512,768]{2,1,0:T(8,128)(2,1)}) custom-call(s32[1,512]{1,0:T(1,128)} %copy-done.43, s32[1024,1]{1,0:T(8,128)} %copy.56.col_ref, f32[128,512]{1,0:T(8,128)} %get-tuple-element.128.sum_ref, bf16[512,768]{1,0:T(8,128)(2,1)} %get-tuple-element.124.q_ref, ...), custom_call_target="tpu_custom_call" | custom-call | bytes 54000000 | tf_op jit(solution)/shard_map/attend_rows_back/pallas_call | solution.py:676
  400.7 9.8 %project_rows_back.3 = (bf16[512,1152]{1,0:T(8,128)(2,1)}, bf16[512,1152]{1,0:T(8,128)(2,1)}, f32[512,768]{1,0:T(8,128)}) custom-call(s32[2]{0:T(128)} %pad_add_fusion.1.place_ref, f32[512,768]{1,0:T(8,128)} %get-tuple-element.166.dq_ref, f32[512,768]{1,0:T(8,128)} %get-tuple-element.167.resid_ref, f32[512,128]{1,0:T(8,128)} %get-tuple-element.301.cos_ref, ...), custom_call_target="tpu_custom_call" | custom-call | bytes 18000000 | tf_op jit(solution)/shard_map/project_rows_back/pallas_call | solution.py:957
  423.4 10.7 %collective-permute-done.51 = bf16[192,2048]{1,0:T(8,128)(2,1)S(1)} collective-permute-done((bf16[192,2048]{1,0:T(8,128)(2,1)S(1)}, bf16[192,2048]{1,0:T(8,128)(2,1)S(1)}, u32[]{:S(2)}, u32[]{:S(2)}) %collective-permute-start.51) | collective-permute-done | bytes 786464 | tf_op jit(solution)/shard_map/ppermute | solution.py:1087
  434.4 15.7 %collective-permute-start.60 = (bf16[192,2048]{1,0:T(8,128)(2,1)S(1)}, bf16[192,2048]{1,0:T(8,128)(2,1)S(1)}, u32[]{:S(2)}, u32[]{:S(2)}) collective-permute-start(bf16[192,2048]{1,0:T(8,128)(2,1)S(1)} %add_convert_fusion), channel_id=1, source_target_pairs={{0,4},{4,0},{8,12},{12,8},{1,5},{5,1},{9,13},{13,9},{2,6},{6,2},{1... | collective-permute-start | bytes 2359304 | tf_op jit(solution)/shard_map/ppermute | solution.py:1074
  505.0 37.2 %collective-permute-start.62 = (bf16[192,1536]{1,0:T(8,128)(2,1)S(1)}, bf16[192,1536]{1,0:T(8,128)(2,1)S(1)}, u32[]{:S(2)}, u32[]{:S(2)}) collective-permute-start(bf16[192,1536]{1,0:T(8,128)(2,1)S(1)} %add_convert_fusion.2), channel_id=1, source_target_pairs={{0,4},{4,0},{8,12},{12,8},{1,5},{5,1},{9,13},{13,9},{2,6},{6,2},{1... | collective-permute-start | bytes 1769480 | tf_op jit(solution)/shard_map/ppermute | solution.py:1074
  554.7 14.2 %collective-permute-done.64 = bf16[192,1536]{1,0:T(8,128)(2,1)S(1)} collective-permute-done((bf16[192,1536]{1,0:T(8,128)(2,1)S(1)}, bf16[192,1536]{1,0:T(8,128)(2,1)S(1)}, u32[]{:S(2)}, u32[]{:S(2)}) %collective-permute-start.64) | collective-permute-done | bytes 589856 | tf_op jit(solution)/shard_map/ppermute | solution.py:1074
  (311 shorter events, 204.3 us)
Async XLA Ops:
  7.0 27.9 %collective-permute-start.4 = (bf16[192,1664]{1,0:T(8,128)(2,1)S(1)}, bf16[192,1664]{1,0:T(8,128)(2,1)S(1)}, u32[]{:S(2)}, u32[]{:S(2)}) collective-permute-start(bf16[192,1664]{1,0:T(8,128)(2,1)S(1)} %get-tuple-element.289.refs_0_), channel_id=1, source_target_pairs={{0,2},{1,3},{2,0},{3,1},{4,6},{5,7},{6,4},{7,5},{8,10},{9,11},{10,... | collective-permute-start | bytes 1916936 | tf_op jit(solution)/shard_map/ppermute | solution.py:1070
  10.0 25.6 %collective-permute-start.3 = (bf16[192,1664]{1,0:T(8,128)(2,1)S(1)}, bf16[192,1664]{1,0:T(8,128)(2,1)S(1)}, u32[]{:S(2)}, u32[]{:S(2)}) collective-permute-start(bf16[192,1664]{1,0:T(8,128)(2,1)S(1)} %get-tuple-element.289.refs_0_), channel_id=1, source_target_pairs={{0,1},{1,0},{2,3},{3,2},{4,5},{5,4},{6,7},{7,6},{8,9},{9,8},{10,11... | collective-permute-start | bytes 1916936 | tf_op jit(solution)/shard_map/ppermute | solution.py:1066
  18.4 31.5 %collective-permute-start.11 = (bf16[192,4608]{1,0:T(8,128)(2,1)}, bf16[192,4608]{1,0:T(8,128)(2,1)}, u32[]{:S(2)}, u32[]{:S(2)}) collective-permute-start(bf16[192,4608]{1,0:T(8,128)(2,1)} %get-tuple-element.264), channel_id=1, source_target_pairs={{0,16},{16,0},{1,17},{17,1},{2,18},{18,2},{3,19},{19,3},{4,20},{20... | collective-permute-start | bytes 5308424 | tf_op jit(solution)/shard_map/ppermute | solution.py:1062
  27.8 27.1 %collective-permute-start.7 = (bf16[192,1664]{1,0:T(8,128)(2,1)S(1)}, bf16[192,1664]{1,0:T(8,128)(2,1)S(1)}, u32[]{:S(2)}, u32[]{:S(2)}) collective-permute-start(bf16[192,1664]{1,0:T(8,128)(2,1)S(1)} %get-tuple-element.110), channel_id=1, source_target_pairs={{0,16},{16,0},{1,17},{17,1},{2,18},{18,2},{3,19},{19,3},{4,20},{20... | collective-permute-start | bytes 1916936 | tf_op jit(solution)/shard_map/ppermute | solution.py:1062
  52.8 41.0 %collective-permute-start.13 = (bf16[192,4608]{1,0:T(8,128)(2,1)}, bf16[192,4608]{1,0:T(8,128)(2,1)}, u32[]{:S(2)}, u32[]{:S(2)}) collective-permute-start(bf16[192,4608]{1,0:T(8,128)(2,1)} %broadcast_select_fusion.1.refs_8_), channel_id=1, source_target_pairs={{0,2},{1,3},{2,0},{3,1},{4,6},{5,7},{6,4},{7,5},{8,10},{9,11},{10,... | collective-permute-start | bytes 5308424 | tf_op jit(solution)/shard_map/ppermute | solution.py:1070
  53.3 40.7 %collective-permute-start.12 = (bf16[192,4608]{1,0:T(8,128)(2,1)}, bf16[192,4608]{1,0:T(8,128)(2,1)}, u32[]{:S(2)}, u32[]{:S(2)}) collective-permute-start(bf16[192,4608]{1,0:T(8,128)(2,1)} %broadcast_select_fusion.1.refs_8_), channel_id=1, source_target_pairs={{0,1},{1,0},{2,3},{3,2},{4,5},{5,4},{6,7},{7,6},{8,9},{9,8},{10,11... | collective-permute-start | bytes 5308424 | tf_op jit(solution)/shard_map/ppermute | solution.py:1066
  96.3 30.6 %collective-permute-start.17 = (bf16[384,4608]{1,0:T(8,128)(2,1)S(1)}, bf16[384,4608]{1,0:T(8,128)(2,1)S(1)}, u32[]{:S(2)}, u32[]{:S(2)}) collective-permute-start(bf16[384,4608]{1,0:T(8,128)(2,1)S(1)} %pad_maximum_fusion), channel_id=1, source_target_pairs={{0,16},{16,0},{1,17},{17,1},{2,18},{18,2},{3,19},{19,3},{4,20},{20... | collective-permute-start | bytes 10616840 | tf_op jit(solution)/shard_map/ppermute | solution.py:1062
  269.7 66.5 %collective-permute-start.26 = (bf16[512,3072]{1,0:T(8,128)(2,1)}, bf16[512,3072]{1,0:T(8,128)(2,1)}, u32[]{:S(2)}, u32[]{:S(2)}) collective-permute-start(bf16[512,3072]{1,0:T(8,128)(2,1)} %get-tuple-element.141.refs_0_), channel_id=1, source_target_pairs={{0,16},{16,0},{1,17},{17,1},{2,18},{18,2},{3,19},{19,3},{4,20},{20... | collective-permute-start | bytes 9437192 | tf_op jit(solution)/shard_map/ppermute | solution.py:1062
  287.8 47.9 %collective-permute-start.28 = (bf16[512,768]{1,0:T(8,128)(2,1)S(1)}, bf16[512,768]{1,0:T(8,128)(2,1)}, u32[]{:S(2)}, u32[]{:S(2)}) collective-permute-start(bf16[512,768]{1,0:T(8,128)(2,1)S(1)} %copy-done.13), channel_id=1, source_target_pairs={{0,16},{16,0},{1,17},{17,1},{2,18},{18,2},{3,19},{19,3},{4,20},{20... | collective-permute-start | bytes 2359304 | tf_op jit(solution)/shard_map/ppermute | solution.py:1062
  354.6 35.1 %collective-permute-start.32 = (bf16[192,2048]{1,0:T(8,128)(2,1)}, bf16[192,2048]{1,0:T(8,128)(2,1)S(1)}, u32[]{:S(2)}, u32[]{:S(2)}) collective-permute-start(bf16[192,2048]{1,0:T(8,128)(2,1)} %get-tuple-element.145), channel_id=1, source_target_pairs={{0,1},{1,0},{2,3},{3,2},{4,5},{5,4},{6,7},{7,6},{8,9},{9,8},{10,11... | collective-permute-start | bytes 2359304 | tf_op jit(solution)/shard_map/ppermute | solution.py:1066
  355.1 34.5 %collective-permute-start.33 = (bf16[192,2048]{1,0:T(8,128)(2,1)}, bf16[192,2048]{1,0:T(8,128)(2,1)S(1)}, u32[]{:S(2)}, u32[]{:S(2)}) collective-permute-start(bf16[192,2048]{1,0:T(8,128)(2,1)} %get-tuple-element.146), channel_id=1, source_target_pairs={{0,2},{1,3},{2,0},{3,1},{4,6},{5,7},{6,4},{7,5},{8,10},{9,11},{10,... | collective-permute-start | bytes 2359304 | tf_op jit(solution)/shard_map/ppermute | solution.py:1070
  390.5 26.7 %collective-permute-start.23 = (bf16[512,768]{1,0:T(8,128)(2,1)S(1)}, bf16[512,768]{1,0:T(8,128)(2,1)}, u32[]{:S(2)}, u32[]{:S(2)}) collective-permute-start(bf16[512,768]{1,0:T(8,128)(2,1)S(1)} %copy-done.12), channel_id=1, source_target_pairs={{0,16},{16,0},{1,17},{17,1},{2,18},{18,2},{3,19},{19,3},{4,20},{20... | collective-permute-start | bytes 2359304 | tf_op jit(solution)/shard_map/ppermute | solution.py:1062
  413.8 36.3 %collective-permute-start.53 = (bf16[192,1536]{1,0:T(8,128)(2,1)}, bf16[192,1536]{1,0:T(8,128)(2,1)}, u32[]{:S(2)}, u32[]{:S(2)}) collective-permute-start(bf16[192,1536]{1,0:T(8,128)(2,1)} %get-tuple-element.195), channel_id=1, source_target_pairs={{0,1},{1,0},{2,3},{3,2},{4,5},{5,4},{6,7},{7,6},{8,9},{9,8},{10,11... | collective-permute-start | bytes 1769480 | tf_op jit(solution)/shard_map/ppermute | solution.py:1066
  415.2 36.5 %collective-permute-start.55 = (bf16[192,1536]{1,0:T(8,128)(2,1)}, bf16[192,1536]{1,0:T(8,128)(2,1)}, u32[]{:S(2)}, u32[]{:S(2)}) collective-permute-start(bf16[192,1536]{1,0:T(8,128)(2,1)} %get-tuple-element.197), channel_id=1, source_target_pairs={{0,2},{1,3},{2,0},{3,1},{4,6},{5,7},{6,4},{7,5},{8,10},{9,11},{10,... | collective-permute-start | bytes 1769480 | tf_op jit(solution)/shard_map/ppermute | solution.py:1070
  434.4 53.8 %collective-permute-start.60 = (bf16[192,2048]{1,0:T(8,128)(2,1)S(1)}, bf16[192,2048]{1,0:T(8,128)(2,1)S(1)}, u32[]{:S(2)}, u32[]{:S(2)}) collective-permute-start(bf16[192,2048]{1,0:T(8,128)(2,1)S(1)} %add_convert_fusion), channel_id=1, source_target_pairs={{0,4},{4,0},{8,12},{12,8},{1,5},{5,1},{9,13},{13,9},{2,6},{6,2},{1... | collective-permute-start | bytes 2359304 | tf_op jit(solution)/shard_map/ppermute | solution.py:1074
  467.5 32.1 %collective-permute-start.57 = (bf16[192,1536]{1,0:T(8,128)(2,1)S(1)}, bf16[192,1536]{1,0:T(8,128)(2,1)}, u32[]{:S(2)}, u32[]{:S(2)}) collective-permute-start(bf16[192,1536]{1,0:T(8,128)(2,1)S(1)} %fusion.3), channel_id=1, source_target_pairs={{0,12},{4,8},{8,4},{12,0},{1,13},{5,9},{9,5},{13,1},{2,14},{6,10},... | collective-permute-start | bytes 1769480 | tf_op jit(solution)/shard_map/ppermute | solution.py:1087
  472.3 26.1 %collective-permute-start.50 = (bf16[192,1536]{1,0:T(8,128)(2,1)S(1)}, bf16[192,1536]{1,0:T(8,128)(2,1)}, u32[]{:S(2)}, u32[]{:S(2)}) collective-permute-start(bf16[192,1536]{1,0:T(8,128)(2,1)S(1)} %fusion.2), channel_id=1, source_target_pairs={{0,12},{4,8},{8,4},{12,0},{1,13},{5,9},{9,5},{13,1},{2,14},{6,10},... | collective-permute-start | bytes 1769480 | tf_op jit(solution)/shard_map/ppermute | solution.py:1087
  485.9 56.3 %collective-permute-start.46 = (bf16[256,768]{1,0:T(8,128)(2,1)}, bf16[256,768]{1,0:T(8,128)(2,1)}, u32[]{:S(2)}, u32[]{:S(2)}) collective-permute-start(bf16[256,768]{1,0:T(8,128)(2,1)} %get-tuple-element.248), channel_id=1, source_target_pairs={{16,28},{20,24},{24,20},{28,16},{17,29},{21,25},{25,21},{29,17},{1... | collective-permute-start | bytes 1179656 | tf_op jit(solution)/shard_map/ppermute | solution.py:1083
  488.3 55.1 %collective-permute-start.44 = (bf16[256,768]{1,0:T(8,128)(2,1)}, bf16[256,768]{1,0:T(8,128)(2,1)}, u32[]{:S(2)}, u32[]{:S(2)}) collective-permute-start(bf16[256,768]{1,0:T(8,128)(2,1)} %get-tuple-element.263), channel_id=1, source_target_pairs={{0,16},{16,0},{1,17},{17,1},{2,18},{18,2},{3,19},{19,3},{4,20},{20... | collective-permute-start | bytes 1179656 | tf_op jit(solution)/shard_map/ppermute | solution.py:1062
  498.4 71.4 %collective-permute-start.61 = (bf16[192,2048]{1,0:T(8,128)(2,1)S(1)}, bf16[192,2048]{1,0:T(8,128)(2,1)S(1)}, u32[]{:S(2)}, u32[]{:S(2)}) collective-permute-start(bf16[192,2048]{1,0:T(8,128)(2,1)S(1)} %copy-done.25), channel_id=1, source_target_pairs={{0,16},{16,0},{1,17},{17,1},{2,18},{18,2},{3,19},{19,3},{4,20},{20... | collective-permute-start | bytes 2359304 | tf_op jit(solution)/shard_map/ppermute | solution.py:1062
  499.6 48.9 %collective-permute-start.52 = (bf16[192,1152]{1,0:T(8,128)(2,1)S(1)}, bf16[192,1152]{1,0:T(8,128)(2,1)S(1)}, u32[]{:S(2)}, u32[]{:S(2)}) collective-permute-start(bf16[192,1152]{1,0:T(8,128)(2,1)S(1)} %fusion.7), channel_id=1, source_target_pairs={{0,12},{4,8},{8,4},{12,0},{1,13},{5,9},{9,5},{13,1},{2,14},{6,10},... | collective-permute-start | bytes 1327112 | tf_op jit(solution)/shard_map/ppermute | solution.py:1087
  505.0 64.2 %collective-permute-start.62 = (bf16[192,1536]{1,0:T(8,128)(2,1)S(1)}, bf16[192,1536]{1,0:T(8,128)(2,1)S(1)}, u32[]{:S(2)}, u32[]{:S(2)}) collective-permute-start(bf16[192,1536]{1,0:T(8,128)(2,1)S(1)} %add_convert_fusion.2), channel_id=1, source_target_pairs={{0,4},{4,0},{8,12},{12,8},{1,5},{5,1},{9,13},{13,9},{2,6},{6,2},{1... | collective-permute-start | bytes 1769480 | tf_op jit(solution)/shard_map/ppermute | solution.py:1074
  542.2 26.7 %collective-permute-start.64 = (bf16[192,1536]{1,0:T(8,128)(2,1)S(1)}, bf16[192,1536]{1,0:T(8,128)(2,1)S(1)}, u32[]{:S(2)}, u32[]{:S(2)}) collective-permute-start(bf16[192,1536]{1,0:T(8,128)(2,1)S(1)} %add_convert_fusion.1), channel_id=1, source_target_pairs={{0,4},{4,0},{8,12},{12,8},{1,5},{5,1},{9,13},{13,9},{2,6},{6,2},{1... | collective-permute-start | bytes 1769480 | tf_op jit(solution)/shard_map/ppermute | solution.py:1074
  548.6 29.4 %collective-permute-start.58 = (bf16[192,1152]{1,0:T(8,128)(2,1)S(1)}, bf16[192,1152]{1,0:T(8,128)(2,1)S(1)}, u32[]{:S(2)}, u32[]{:S(2)}) collective-permute-start(bf16[192,1152]{1,0:T(8,128)(2,1)S(1)} %add_convert_fusion.3), channel_id=1, source_target_pairs={{0,4},{4,0},{8,12},{12,8},{1,5},{5,1},{9,13},{13,9},{2,6},{6,2},{1... | collective-permute-start | bytes 1327112 | tf_op jit(solution)/shard_map/ppermute | solution.py:1074
  (90 other events, 1031.2 us)

commit v5 on v4

--- a/solution.py
+++ b/solution.py
@@ -710,7 +710,7 @@
     )
 
 
-FF_STEP = 512
+FF_STEP = 768
 
 
 def mlp_scratch(width, hidden_width):
@@ -744,7 +744,7 @@
     return steps, lambda j, place: (place[1] ^ (j // (steps // 2))) * (steps // 2) + j % (steps // 2)
 
 
-def mlp_rows(place, hidden, attended, first_parts, rest_parts):
+def mlp_rows(place, hidden, attended, first_parts, rest_parts, keep_all):
     rows, width = hidden.shape
     ff_half = (rest_parts[0].shape[1] - 2 * width) // 2
     ff = 2 * ff_half
@@ -752,10 +752,13 @@
 
     def body(place_ref, hidden_ref, att_ref, *refs):
         parts, rest = refs[:16], refs[16:]
-        out_ref, one_ref, two_ref, normed_ref, mid_ref, gate_ref, up_ref = rest[:7]
-        w_out, w_gate, w_up, w_down, w_norm, norm_ref, _ = rest[7:]
+        if keep_all:
+            (out_ref, one_ref, two_ref, normed_ref, mid_ref, gate_ref, up_ref), rest = rest[:7], rest[7:]
+        else:
+            out_ref, rest, (two_ref, normed_ref) = rest[0], rest[1:-2], rest[-2:]
+        w_out, w_gate, w_up, w_down, w_norm, norm_ref, _ = rest
         step = pl.program_id(0)
-        norm, out, gates, ups, downs = mlp_loads(place_ref, parts, rest[7:], width, ff_half)
+        norm, out, gates, ups, downs = mlp_loads(place_ref, parts, rest, width, ff_half)
 
         @pl.when(step == 0)
         def _():
@@ -765,7 +768,8 @@
             norm_ref[...] = w_norm[:, :128].astype(jnp.float32).T
             wait_all(out)
             resid = hidden_ref[...].astype(jnp.float32) + mm(att_ref[...], w_out[...])
-            one_ref[...] = resid
+            if keep_all:
+                one_ref[...] = resid
             normed = unit_of(resid)[0] * norm_ref[0:1] + norm_ref[1:2]
             normed_ref[...] = normed.astype(jnp.bfloat16)
             two_ref[...] = normed
@@ -780,10 +784,9 @@
         span = pl.ds(pl.multiple_of(block_of(step, place_ref) * FF_STEP, FF_STEP), FF_STEP)
         gate = mm(normed_ref[...], w_gate[:, span])
         up = mm(normed_ref[...], w_up[:, span])
-        gate_ref[...] = gate.astype(jnp.bfloat16)
-        up_ref[...] = up.astype(jnp.bfloat16)
         middle = (gate * jax.nn.sigmoid(gate) * up).astype(jnp.bfloat16)
-        mid_ref[...] = middle
+        if keep_all:
+            gate_ref[...], up_ref[...], mid_ref[...] = gate.astype(jnp.bfloat16), up.astype(jnp.bfloat16), middle
 
         @pl.when(step == 0)
         def _():
@@ -797,23 +800,21 @@
 
     whole = pl.BlockSpec((rows, width), lambda j, place: (0, 0))
     part = pl.BlockSpec((rows, FF_STEP), lambda j, place: (0, block_of(j, place)))
+    shapes, scratch = [shape_of((rows, width), jnp.bfloat16)], mlp_scratch(width, ff)
+    if keep_all:
+        shapes += [shape_of((rows, width), jnp.float32)] * 2 + [shape_of((rows, width), jnp.bfloat16)]
+        shapes += [shape_of((rows, ff), jnp.bfloat16)] * 3
+    else:
+        scratch += [pltpu.VMEM((rows, width), jnp.float32), pltpu.VMEM((rows, width), jnp.bfloat16)]
     return kernel_call(
         body,
-        [
-            shape_of((rows, width), jnp.bfloat16),
-            shape_of((rows, width), jnp.float32),
-            shape_of((rows, width), jnp.float32),
-            shape_of((rows, width), jnp.bfloat16),
-            shape_of((rows, ff), jnp.bfloat16),
-            shape_of((rows, ff), jnp.bfloat16),
-            shape_of((rows, ff), jnp.bfloat16),
-        ],
+        shapes,
         [whole, whole] + [anywhere()] * 16,
-        mlp_scratch(width, ff),
+        scratch,
         60,
         16,
         "mlp_rows",
-        [whole] * 4 + [part] * 3,
+        [whole] * 4 + [part] * 3 if keep_all else [whole],
         (steps,),
         True,
     )(place, hidden, attended, *first_parts, *rest_parts)
@@ -1058,6 +1059,19 @@
     return [made[5 * index : 5 * index + 5] for index in range(len(groups))]
 
 
+def first_columns(values):
+    rows = values.shape[0]
+
+    def body(values_ref, *refs):
+        turned = values_ref[...].astype(jnp.float32).T
+        for index, ref in enumerate(refs):
+            ref[...] = turned[index : index + 1]
+
+    return kernel_call(
+        body, [shape_of((1, rows), jnp.float32)] * 4, [in_vmem()], [], 16, 1, "first_columns"
+    )(values)
+
+
 def to_core(value):
     return lax.ppermute(value, "section", [(0, 1), (1, 0)])
 
@@ -1112,9 +1126,9 @@
     return lax.optimization_barrier((value, *others))[0]
 
 
-def gather_near(pieces, *others):
-    own = after(pieces[0], *others)
-    return [own, along_x(own), along_y(own), pieces[1]]
+def gather_near(piece, *others):
+    own = after(piece, *others)
+    return [own, along_x(own), along_y(own)]
 
 
 def gather_far(near, *others):
@@ -1122,11 +1136,11 @@
     return [along_x(after(near[2][:rows], *others)), along_y(after(near[1][rows:], *others))]
 
 
-def both_cores(near, far):
+def both_cores(near, far, other):
     return [
-        *near[:3],
+        *near,
         *far,
-        near[3],
+        other,
         to_core(jnp.concatenate(near[1:3], axis=0)),
         to_core(jnp.concatenate(far, axis=0)),
     ]
@@ -1158,18 +1172,16 @@
 
 
 def reduce_ctx(pieces, middle, last):
-    received = [same_role(pieces[0])]
+    received = [same_role(pieces[0]), same_role(pieces[1])]
     mine, others = [], []
     for index, piece in enumerate(pieces):
         mine.append(lowered(wide(piece) + wide(after(received[index], *last))))
         last = (mine[index],)
         others.append(along_z(mine[index]))
-        if index + 1 < len(pieces):
-            ready = pieces[index + 1] if index == 0 else after(pieces[index + 1], received[index - 1], mine[index - 1])
-            received.append(same_role(ready))
-    return [
-        (jnp.where(middle, theirs, own), jnp.where(middle, own, theirs)) for own, theirs in zip(mine, others)
-    ]
+        if index + 2 < len(pieces):
+            received.append(same_role(after(pieces[index + 2], received[index])))
+    sums = [(jnp.where(middle, theirs, own), jnp.where(middle, own, theirs)) for own, theirs in zip(mine, others)]
+    return sums, mine[-2]
 
 
 def paired_on_device(
@@ -1198,10 +1210,11 @@
     def in_order(left, right):
         return jnp.where(even, jnp.concatenate([left, right]), jnp.concatenate([right, left]))
 
-    def to_rows():
+    def to_rows(tokens, cotangent, others):
         mine, theirs = jnp.where(middle, cotangent, tokens), jnp.where(middle, tokens, cotangent)
         first = near_blocks(jnp.where(core == 0, pick(theirs, sequence), pick(theirs, 1 - sequence)))
         second = far_blocks(pick(mine, 1 - sequence))
+        first, second = after((first, second), *others)
         return in_order(
             jnp.where(core == 0, pick(mine, sequence), first), jnp.where(core == 0, first, second)
         )
@@ -1236,15 +1249,20 @@
             axis=1,
         )
 
-    def choose(own, other, other_sent, own_sent):
-        return jnp.where(core == role, own, other_sent), jnp.where(core == role, other, own_sent)
+    def halves(own, other, other_sent):
+        return jnp.where(core == role, own, other_sent), lambda near: jnp.where(
+            core == role, other, to_core(after(own, *near[1:3]))
+        )
 
     own, other = first_pack(core), first_pack(1 - core)
     other_sent = to_core(other)
-    first_pieces = choose(own, other, other_sent, to_core(after(own, other_sent)))
+    first_piece, first_other = halves(own, other, other_sent)
+    near = gather_near(first_piece)
+    far = gather_far(near)
     own, other = rest_pack(core, other_sent), rest_pack(1 - core, other_sent)
-    rest_pieces = choose(own, other, to_core(other), to_core(after(own, other_sent)))
-    tokens, cotangent = after((tokens, cotangent), other_sent)
+    rest_piece, rest_other = halves(own, other, to_core(other))
+    near_mlp = gather_near(rest_piece, *near[1:3])
+    given = to_rows(*after((tokens, cotangent), first_piece), far)
 
     seg = pick(seg_ids, sequence)
     rows = 2 * span
@@ -1264,19 +1282,15 @@
         blocks = [own, to_core(own)]
         return queries, blocks, *attend_rows(queries, blocks, seg_rows[:, None], seg_keys[None, :])
 
-    given = to_rows()
-    near = gather_near(first_pieces)
-    far = gather_far(near)
-    near_mlp = gather_near(rest_pieces, *far)
-    first = both_cores(near, far)
+    first = both_cores(near, far, first_other(near))
     queries, blocks, attended, sums = attention(given)
     near_mlp = [after(part, attended) for part in near_mlp]
-    rest = both_cores(near_mlp, gather_far(near_mlp))
-    output = mlp_rows(place, given, attended, first, rest)[0]
+    rest = both_cores(near_mlp, gather_far(near_mlp), rest_other(near_mlp))
+    output = mlp_rows(place, given, attended, first, rest, False)[0]
 
     hidden = jnp.where(middle, along_z(output), given)
     queries, blocks, attended, sums = attention(hidden)
-    output, one, two, normed, mids, gate, up = mlp_rows(place, hidden, attended, first, rest)
+    output, one, two, normed, mids, gate, up = mlp_rows(place, hidden, attended, first, rest, True)
 
     dresid_one, dattended = mlp_rows_back(place, given, one, two, gate, up, first, rest, False)
     sent_outputs = send_rows(output)
@@ -1290,12 +1304,24 @@
 
     both = lambda value: (value, to_core(value))
     mids, normed, attended, hidden = both(mids), both(normed), both(attended), both(hidden)
+    incoming = after(incoming, mids[1], normed[1], attended[1], hidden[1])
     dresid_one, dattended, keep, send, keep_gate, keep_up, send_gate, send_up = mlp_rows_back(
         place, incoming, one, two, gate, up, first, rest, True
     )
     ff = mids[0].shape[1]
     right, right_gate, right_up = (keep, to_core(send)), (keep_gate, to_core(send_gate)), (keep_up, to_core(send_up))
-    parts = grad_parts(
+    parts = grad_parts(place, [[(normed, (0, width), right_gate, (0, ff // 2), 1)]])
+    near = [reduce_first(parts[0])]
+    normed = (after(normed[0], *parts[0]), normed[1])
+    parts += grad_parts(place, [[(normed, (0, width), right_up, (0, ff // 2), 1)]])
+    near.append(reduce_first(parts[1]))
+    dqueries, own, across = attend_rows_back(
+        queries, blocks, seg_rows[None, :], seg_keys[:, None], attended[0], sums, after(dattended, *parts[1])
+    )
+    across = to_core(after(across, *near[0], *near[1]))
+    far = [reduce_second(parts[0], near[0], dqueries), reduce_second(parts[1], near[1], dqueries)]
+    mids = (after(mids[0], dqueries), mids[1])
+    parts += grad_parts(
         place,
         [
             [
@@ -1305,26 +1331,17 @@
         ],
         1,
     )
-    normed = (after(normed[0], *parts[0]), normed[1])
-    parts += grad_parts(place, [[(normed, (0, width), pair, (0, ff // 2), 1)] for pair in (right_gate, right_up)])
-    dqueries, own, across = attend_rows_back(
-        queries, blocks, seg_rows[None, :], seg_keys[:, None], attended[0], sums, after(dattended, *(x for part in parts for x in part))
-    )
-    near = [reduce_first(parts[0])]
-    near.append(reduce_first(parts[1]))
-    across = to_core(after(across, *near[0], *near[1]))
-    far = [reduce_second(parts[0], near[0], across)]
-    near.append(reduce_first(parts[2], across))
-    keep, send, dhidden = project_rows_back(place, dqueries, (own, across), dresid_one, cosine, sine, first)
-    keep = after(keep, *far[0])
+    keep, send, dhidden = project_rows_back(
+        place, dqueries, (own, across), after(dresid_one, *parts[2], *far[0], *far[1]), cosine, sine, first
+    )
+    near.append(reduce_first(parts[2], *far[0], *far[1]))
     parts += grad_parts(place, [[(hidden, (0, width), (keep, to_core(send)), (0, 3 * width // 2), 1)]])
     near.append(reduce_first(parts[3]))
-    far.append(reduce_second(parts[1], near[1], *parts[3]))
     far.append(reduce_second(parts[2], near[2], *parts[3]))
     far.append(reduce_second(parts[3], near[3]))
     pieces = [reduce_last(*group) for group in zip(parts, near, far)]
-    pieces[1:] = [after(piece, *parts[3]) for piece in pieces[1:]]
-    totals = reduce_ctx(pieces, middle, parts[3])
+    totals, nearly = reduce_ctx(pieces, middle, parts[3])
+    sent_grads = send_rows(after(lowered(dhidden), nearly))
 
     pairs = []
     for first_layer, second_layer in totals:
@@ -1337,21 +1354,21 @@
     joined = lambda index, begin, end: wide(
         by_core(core, pairs[index][0][:, begin:end], pairs[index][1][:, begin:end], 1)
     )[None]
-    norm_grads = wide(pairs[0][0][:, 5 * width // 2 : 5 * width // 2 + 4]).T
+    norm_grads = first_columns(pairs[2][0][:, 5 * width // 2 :])
     pick_down = lambda which: jnp.concatenate(
-        [pairs[0][which][:, i * width // 2 : (i + 1) * width // 2] for i in range(ff // width)]
+        [pairs[2][which][:, i * width // 2 : (i + 1) * width // 2] for i in range(ff // width)]
     )
     grad_down = wide(by_core(core, pick_down(0), pick_down(1), 1))[None]
 
     return (
         placed_rows(*after(sent_outputs, *far[3])),
-        wide(placed_rows(*send_rows(after(lowered(dhidden), *far[3])))),
+        wide(placed_rows(*sent_grads)),
         joined(3, 0, 3 * width // 2),
-        joined(0, 2 * width, 5 * width // 2),
+        joined(2, 2 * width, 5 * width // 2),
+        joined(0, 0, ff // 2),
         joined(1, 0, ff // 2),
-        joined(2, 0, ff // 2),
         grad_down,
-        *(norm_grads[i : i + 1] for i in range(4)),
+        *norm_grads,
     )
 
 

time: 594 us -> 548 us (0.923)
  starting transfers between devices: 129 us -> 109 us
  other arithmetic: 57.2 us -> 40.4 us
  local copies, waits for them, and re-layouts: 31.6 us -> 21.1 us
  waiting for transfers between devices: 140 us -> 146 us
    ppermute x3, waiting for transfers between devices: 1.59 us -> 24.9 us  [near_blocks(): return lax.ppermute(value, ('section', 'ctx'), pairs)]
    ppermute x12, waiting for transfers between devices: 23.9 us -> 44 us  [along_x(): return lax.ppermute(value, 'dp', [(i, i ^ 1) for i in range(4)])]
    ppermute x26, starting transfers between devices: 28.4 us -> 9.75 us  [to_core(): return lax.ppermute(value, 'section', [(0, 1), (1, 0)])]
    ppermute x4, waiting for transfers between devices: 15.5 us -> 0.01 us  [same_role(): return lax.ppermute(value, 'ctx', [(i, i ^ 3) for i in range(4)])]
    ppermute x6, starting transfers between devices: 58.6 us -> 43.7 us  [along_z(): return lax.ppermute(value, 'ctx', [(i, i ^ 1) for i in range(4)])]
    ppermute x6, waiting for transfers between devices: 58.6 us -> 44.9 us  [along_z(): return lax.ppermute(value, 'ctx', [(i, i ^ 1) for i in range(4)])]
    ppermute x4, starting transfers between devices: 7.95 us -> 21.6 us  [same_role(): return lax.ppermute(value, 'ctx', [(i, i ^ 3) for i in range(4)])]
    ppermute x26, waiting for transfers between devices: 22.6 us -> 14.6 us  [to_core(): return lax.ppermute(value, 'section', [(0, 1), (1, 0)])]
  transfers between devices with their start and end apart: 66 -> 66, of which waited for: 23 -> 20; matrix products, arithmetic and copies ran while one was open for 11% -> 7% of each run, Pallas kernels for 24% -> 25%
where the time goes in v5:
time: 548 us; the launch traced here: 541 us
  Pallas kernels  222 us (41%)
  waiting for transfers between devices  146 us (27%)
  starting transfers between devices  109 us (20%)
  other arithmetic  40.4 us (7%)
  local copies, waits for them, and re-layouts  21.1 us (4%)
    pallas_call x2, Pallas kernels, mlp_rows_back(): kernel_call(body, shapes, [whole, whole, whole, part, part] + [anywhere()...  48.8 us
    ppermute x6, waiting for transfers between devices, along_z(): return lax.ppermute(value, 'ctx', [(i, i ^ 1) for i in range(4)])  44.9 us
    ppermute x12, waiting for transfers between devices, along_x(): return lax.ppermute(value, 'dp', [(i, i ^ 1) for i in range(4)])  44 us
    ppermute x6, starting transfers between devices, along_z(): return lax.ppermute(value, 'ctx', [(i, i ^ 1) for i in range(4)])  43.7 us
    pallas_call x2, Pallas kernels, attend_rows_back(): kernel_call(body, [shape_of((rows, width), jnp.float32), pair_shape, pair...  39.7 us
    pallas_call x2, Pallas kernels, mlp_rows(): kernel_call(body, shapes, [whole, whole] + [anywhere()] * 16, scratch, 60...  37.8 us
    pallas_call x2, Pallas kernels, attend_rows(): kernel_call(body, [shape_of((rows, width), jnp.bfloat16), shape_of((128,...  32 us
    pallas_call x4, Pallas kernels, grad_parts(): kernel_call(body, shapes, [in_smem()] + [in_vmem()] * len(arrays), scratc...  30.3 us
  transfers between devices with their start and end apart: 66, of which 20 were waited for; matrix products, arithmetic and copies ran while one was open for 7% of the time, Pallas kernels for 25%

profile of v5, /device:TPU:0, one launch (start us, length us, event | category | flops | bytes accessed | tf_op | source)
XLA Modules:
  0.0 541.4 jit_solution(10950971629933927871)
XLA Ops:
  19.6 7.8 %collective-permute-done.5.refs_1_ = bf16[192,1664]{1,0:T(8,128)(2,1)S(1)} collective-permute-done((bf16[192,1664]{1,0:T(8,128)(2,1)S(1)}, bf16[192,1664]{1,0:T(8,128)(2,1)S(1)}, u32[]{:S(2)}, u32[]{:S(2)}) %collective-permute-start.5) | collective-permute-done | bytes 639008 | tf_op jit(solution)/shard_map/ppermute | solution.py:1080
  47.8 6.5 %project_rows.2 = (bf16[512,768]{1,0:T(8,128)(2,1)}, bf16[2,512,768]{2,1,0:T(8,128)(2,1)}) custom-call(s32[2]{0:T(128)} %pad_add_fusion.1.place_ref, bf16[512,768]{1,0:T(8,128)(2,1)} %maximum_select_fusion.4.hidden_ref.in_ref, f32[512,128]{1,0:T(8,128)} %get-tuple-element.259.cos_ref, f32[512,128]{1,0:T(8,128)} %get-tuple-element.258.sin_ref, ...), custom_call_target="tpu_custom_call" | custom-call | bytes 9000000 | tf_op jit(solution)/shard_map/project_rows/pallas_call | solution.py:577
  58.1 16.0 %attend_rows.2 = (bf16[512,768]{1,0:T(8,128)(2,1)}, f32[128,512]{1,0:T(8,128)}) custom-call(s32[512,1]{1,0:T(8,128)} %copy.41.col_ref, s32[1,1024]{1,0:T(1,128)} %bitcast.88, bf16[512,768]{1,0:T(8,128)(2,1)} %get-tuple-element.116.q_ref, bf16[2,512,768]{2,1,0:T(8,128)(2,1)} %get-tuple-element.117.b0, bf16[2,512,768]{2,1,0:T(8,128)(2,1)} %collective-permute-done.10.b1), custom_call_target="tpu_custom_call" | custom-call | bytes 24000000 | tf_op jit(solution)/shard_map/attend_rows/pallas_call | solution.py:620
  74.2 10.2 %collective-permute-done.13.refs_10_ = bf16[192,4608]{1,0:T(8,128)(2,1)S(1)} collective-permute-done((bf16[192,4608]{1,0:T(8,128)(2,1)}, bf16[192,4608]{1,0:T(8,128)(2,1)S(1)}, u32[]{:S(2)}, u32[]{:S(2)}) %collective-permute-start.13) | collective-permute-done | bytes 1769504 | tf_op jit(solution)/shard_map/ppermute | solution.py:1084
  92.1 20.1 %collective-permute-done.14.refs_11_ = bf16[96,4608]{1,0:T(8,128)(2,1)S(1)} collective-permute-done((bf16[96,4608]{1,0:T(8,128)(2,1)S(1)}, bf16[96,4608]{1,0:T(8,128)(2,1)S(1)}, u32[]{:S(2)}, u32[]{:S(2)}) %collective-permute-start.14) | collective-permute-done | bytes 884768 | tf_op jit(solution)/shard_map/ppermute | solution.py:1080
  119.7 17.7 %mlp_rows.2 = bf16[512,768]{1,0:T(8,128)(2,1)} custom-call(s32[2]{0:T(128)} %pad_add_fusion.1.place_ref, bf16[512,768]{1,0:T(8,128)(2,1)} %maximum_select_fusion.4.hidden_ref.in_ref, bf16[512,768]{1,0:T(8,128)(2,1)} %get-tuple-element.118.att_ref, bf16[192,1664]{1,0:T(8,128)(2,1)} %copy-done.5, bf16[192,1664]{1,0:T(8,128)(2,1)} %copy-done.1, ...), custom_call_target="tpu_custom_call" | custom-call | bytes 48000000 | tf_op jit(solution)/shard_map/mlp_rows/pallas_call | solution.py:809
  137.5 19.8 %collective-permute-done.19 = bf16[512,768]{1,0:T(8,128)(2,1)S(1)} collective-permute-done((bf16[512,768]{1,0:T(8,128)(2,1)}, bf16[512,768]{1,0:T(8,128)(2,1)S(1)}, u32[]{:S(2)}, u32[]{:S(2)}) %collective-permute-start.19) | collective-permute-done | bytes 786464 | tf_op jit(solution)/shard_map/ppermute | solution.py:1088
  159.4 6.5 %project_rows.3 = (bf16[512,768]{1,0:T(8,128)(2,1)}, bf16[2,512,768]{2,1,0:T(8,128)(2,1)}) custom-call(s32[2]{0:T(128)} %pad_add_fusion.1.place_ref, bf16[512,768]{1,0:T(8,128)(2,1)} %broadcast_select_fusion.9.hidden_ref.refs_0_, f32[512,128]{1,0:T(8,128)} %get-tuple-element.259.cos_ref, f32[512,128]{1,0:T(8,128)} %get-tuple-element.258.sin_ref, ...), custom_call_target="tpu_custom_call" | custom-call | bytes 9000000 | tf_op jit(solution)/shard_map/project_rows/pallas_call | solution.py:577
  170.8 16.0 %attend_rows.3 = (bf16[512,768]{1,0:T(8,128)(2,1)}, f32[128,512]{1,0:T(8,128)}) custom-call(s32[512,1]{1,0:T(8,128)} %copy.41.col_ref, s32[1,1024]{1,0:T(1,128)} %bitcast.89, bf16[512,768]{1,0:T(8,128)(2,1)} %get-tuple-element.127.q_ref, bf16[2,512,768]{2,1,0:T(8,128)(2,1)} %get-tuple-element.128.b0, bf16[2,512,768]{2,1,0:T(8,128)(2,1)} %copy-done.12), custom_call_target="tpu_custom_call" | custom-call | bytes 24000000 | tf_op jit(solution)/shard_map/attend_rows/pallas_call | solution.py:620
  186.8 20.0 %mlp_rows.3 = (bf16[512,768]{1,0:T(8,128)(2,1)}, f32[512,768]{1,0:T(8,128)}, f32[512,768]{1,0:T(8,128)}, bf16[512,768]{1,0:T(8,128)(2,1)}, bf16[512,3072]{1,0:T(...) custom-call(s32[2]{0:T(128)} %pad_add_fusion.1.place_ref, ...), custom_call_target="tpu_custom_call" | custom-call | bytes 48000000 | tf_op jit(solution)/shard_map/mlp_rows/pallas_call | solution.py:809
  210.1 22.3 %mlp_rows_back.2 = (f32[512,768]{1,0:T(8,128)}, bf16[512,768]{1,0:T(8,128)(2,1)}) custom-call(s32[2]{0:T(128)} %pad_add_fusion.1.place_ref, bf16[512,768]{1,0:T(8,128)(2,1)} %maximum_select_fusion.4.hidden_ref.in_ref, f32[512,768]{1,0:T(8,128)} %get-tuple-element.132.one_ref, f32[512,768]{1,0:T(8,128)} %get-tuple-element.133.two_ref, ...), custom_call_target="tpu_custom_call" | custom-call | bytes 63000000 | tf_op jit(solution)/shard_map/mlp_rows_back/pallas_call | solution.py:915
  232.5 19.9 %attend_rows_back.2 = (f32[512,768]{1,0:T(8,128)}, bf16[2,512,768]{2,1,0:T(8,128)(2,1)}, bf16[2,512,768]{2,1,0:T(8,128)(2,1)}) custom-call(s32[1,512]{1,0:T(1,128)} %copy-done.58, s32[1024,1]{1,0:T(8,128)} %copy.44.col_ref, f32[128,512]{1,0:T(8,128)} %get-tuple-element.131.sum_ref, bf16[512,768]{1,0:T(8,128)(2,1)} %get-tuple-element.127.q_ref, ...), custom_call_target="tpu_custom_call" | custom-call | bytes 54000000 | tf_op jit(solution)/shard_map/attend_rows_back/pallas_call | solution.py:676
  261.8 10.0 %project_rows_back.2 = (bf16[512,1152]{1,0:T(8,128)(2,1)}, bf16[512,1152]{1,0:T(8,128)(2,1)}, f32[512,768]{1,0:T(8,128)}) custom-call(s32[2]{0:T(128)} %pad_add_fusion.1.place_ref, f32[512,768]{1,0:T(8,128)} %get-tuple-element.138.dq_ref, f32[512,768]{1,0:T(8,128)} %get-tuple-element.139.resid_ref, f32[512,128]{1,0:T(8,128)} %get-tuple-element.259.cos_ref, ...), custom_call_target="tpu_custom_call" | custom-call | bytes 18000000 | tf_op jit(solution)/shard_map/project_rows_back/pallas_call | solution.py:958
  274.6 18.7 %collective-permute-done.25 = bf16[512,768]{1,0:T(8,128)(2,1)S(1)} collective-permute-done((bf16[512,768]{1,0:T(8,128)(2,1)S(1)}, bf16[512,768]{1,0:T(8,128)(2,1)S(1)}, u32[]{:S(2)}, u32[]{:S(2)}) %collective-permute-start.25) | collective-permute-done | bytes 786464 | tf_op jit(solution)/shard_map/ppermute | solution.py:1088
  295.4 26.5 %mlp_rows_back.3 = (f32[512,768]{1,0:T(8,128)}, bf16[512,768]{1,0:T(8,128)(2,1)}, bf16[528,768]{1,0:T(8,128)(2,1)}, bf16[528,768]{1,0:T(8,128)(2,1)}, bf16[512,1...) custom-call(s32[2]{0:T(128)} %pad_add_fusion.1.place_ref, ...), custom_call_target="tpu_custom_call" | custom-call | bytes 63000000 | tf_op jit(solution)/shard_map/mlp_rows_back/pallas_call | solution.py:915
  326.8 6.5 %grad_parts.4 = (bf16[192,1536]{1,0:T(8,128)(2,1)}, bf16[192,1536]{1,0:T(8,128)(2,1)}, bf16[192,1536]{1,0:T(8,128)(2,1)}, bf16[96,1536]{1,0:T(8,128)(2,1)}, bf16[96,1536]{1,0:T(8,128)(2,1)}) custom-call(s32[2]{0:T(128)} %pad_add_fusion.1.place_ref, bf16[512,768]{1,0:T(8,128)(2,1)} %get-tuple-element.154.refs_0_, bf16[512,768]{1,0:T(8,128)(2,1)} %copy-done.18, ...), custom_call_target="tpu_custom_call" | custom-call | bytes 21000000 | tf_op jit(solution)/shard_map/grad_parts/pallas_call | solution.py:1056
  342.8 19.8 %attend_rows_back.3 = (f32[512,768]{1,0:T(8,128)}, bf16[2,512,768]{2,1,0:T(8,128)(2,1)}, bf16[2,512,768]{2,1,0:T(8,128)(2,1)}) custom-call(s32[1,512]{1,0:T(1,128)} %copy-done.58, s32[1024,1]{1,0:T(8,128)} %copy.44.col_ref, f32[128,512]{1,0:T(8,128)} %get-tuple-element.131.sum_ref, bf16[512,768]{1,0:T(8,128)(2,1)} %get-tuple-element.127.q_ref, ...), custom_call_target="tpu_custom_call" | custom-call | bytes 54000000 | tf_op jit(solution)/shard_map/attend_rows_back/pallas_call | solution.py:676
  364.8 11.2 %grad_parts.6 = (bf16[192,2048]{1,0:T(8,128)(2,1)}, bf16[192,2048]{1,0:T(8,128)(2,1)}, bf16[192,2048]{1,0:T(8,128)(2,1)}, bf16[96,2048]{1,0:T(8,128)(2,1)}, bf16[96,2048]{1,0:T(8,128)(2,1)}) custom-call(s32[2]{0:T(128)} %pad_add_fusion.1.place_ref, bf16[512,3072]{1,0:T(8,128)(2,1)} %get-tuple-element.165.refs_0_, ...), custom_call_target="tpu_custom_call" | custom-call | bytes 21000000 | tf_op jit(solution)/shard_map/grad_parts/pallas_call | solution.py:1056
  393.5 9.8 %project_rows_back.3 = (bf16[512,1152]{1,0:T(8,128)(2,1)}, bf16[512,1152]{1,0:T(8,128)(2,1)}, f32[512,768]{1,0:T(8,128)}) custom-call(s32[2]{0:T(128)} %pad_add_fusion.1.place_ref, f32[512,768]{1,0:T(8,128)} %get-tuple-element.163.dq_ref, f32[512,768]{1,0:T(8,128)} %get-tuple-element.177.resid_ref, f32[512,128]{1,0:T(8,128)} %get-tuple-element.259.cos_ref, ...), custom_call_target="tpu_custom_call" | custom-call | bytes 18000000 | tf_op jit(solution)/shard_map/project_rows_back/pallas_call | solution.py:958
  415.6 12.6 %collective-permute-start.62 = (bf16[192,1536]{1,0:T(8,128)(2,1)S(1)}, bf16[192,1536]{1,0:T(8,128)(2,1)S(1)}, u32[]{:S(2)}, u32[]{:S(2)}) collective-permute-start(bf16[192,1536]{1,0:T(8,128)(2,1)S(1)} %add_convert_fusion.2), channel_id=1, source_target_pairs={{0,4},{4,0},{8,12},{12,8},{1,5},{5,1},{9,13},{13,9},{2,6},{6,2},{1... | collective-permute-start | bytes 1769480 | tf_op jit(solution)/shard_map/ppermute | solution.py:1088
  441.3 9.5 %collective-permute-start.64 = (bf16[192,1536]{1,0:T(8,128)(2,1)S(1)}, bf16[192,1536]{1,0:T(8,128)(2,1)S(1)}, u32[]{:S(2)}, u32[]{:S(2)}) collective-permute-start(bf16[192,1536]{1,0:T(8,128)(2,1)S(1)} %add_convert_fusion.1), channel_id=1, source_target_pairs={{0,4},{4,0},{8,12},{12,8},{1,5},{5,1},{9,13},{13,9},{2,6},{6,2},{1... | collective-permute-start | bytes 1769480 | tf_op jit(solution)/shard_map/ppermute | solution.py:1088
  466.2 15.9 %collective-permute-start.57 = (bf16[192,1152]{1,0:T(8,128)(2,1)S(1)}, bf16[192,1152]{1,0:T(8,128)(2,1)S(1)}, u32[]{:S(2)}, u32[]{:S(2)}) collective-permute-start(bf16[192,1152]{1,0:T(8,128)(2,1)S(1)} %fusion.7), channel_id=1, source_target_pairs={{0,12},{4,8},{8,4},{12,0},{1,13},{5,9},{9,5},{13,1},{2,14},{6,10},... | collective-permute-start | bytes 1327112 | tf_op jit(solution)/shard_map/ppermute | solution.py:1101
  485.1 16.5 %collective-permute-start.60 = (bf16[192,2048]{1,0:T(8,128)(2,1)S(1)}, bf16[192,2048]{1,0:T(8,128)(2,1)S(1)}, u32[]{:S(2)}, u32[]{:S(2)}) collective-permute-start(bf16[192,2048]{1,0:T(8,128)(2,1)S(1)} %add_convert_fusion), channel_id=1, source_target_pairs={{0,4},{4,0},{8,12},{12,8},{1,5},{5,1},{9,13},{13,9},{2,6},{6,2},{1... | collective-permute-start | bytes 2359304 | tf_op jit(solution)/shard_map/ppermute | solution.py:1088
  508.7 24.9 %collective-permute-done.54 = bf16[256,768]{1,0:T(8,128)(2,1)S(1)} collective-permute-done((bf16[256,768]{1,0:T(8,128)(2,1)S(1)}, bf16[256,768]{1,0:T(8,128)(2,1)S(1)}, u32[]{:S(2)}, u32[]{:S(2)}) %collective-permute-start.54) | collective-permute-done | bytes 393248 | tf_op jit(solution)/shard_map/ppermute | solution.py:1093
  (340 shorter events, 174.2 us)
Async XLA Ops:
  10.1 32.2 %collective-permute-start.11 = (bf16[192,4608]{1,0:T(8,128)(2,1)S(1)}, bf16[192,4608]{1,0:T(8,128)(2,1)S(1)}, u32[]{:S(2)}, u32[]{:S(2)}) collective-permute-start(bf16[192,4608]{1,0:T(8,128)(2,1)S(1)} %get-tuple-element.226), channel_id=1, source_target_pairs={{0,16},{16,0},{1,17},{17,1},{2,18},{18,2},{3,19},{19,3},{4,20},{20... | collective-permute-start | bytes 5308424 | tf_op jit(solution)/shard_map/ppermute | solution.py:1076
  15.7 24.7 %collective-permute-start.2 = (bf16[256,768]{1,0:T(8,128)(2,1)S(1)}, bf16[256,768]{1,0:T(8,128)(2,1)S(1)}, u32[]{:S(2)}, u32[]{:S(2)}) collective-permute-start(bf16[256,768]{1,0:T(8,128)(2,1)S(1)} %dynamic-slice_bitcast_fusion.5), channel_id=1, source_target_pairs={{16,28},{20,24},{24,20},{28,16},{17,29},{21,25},{25,21},{29,17},{1... | collective-permute-start | bytes 1179656 | tf_op jit(solution)/shard_map/ppermute | solution.py:1097
  16.4 24.5 %collective-permute-start.1 = (bf16[256,768]{1,0:T(8,128)(2,1)S(1)}, bf16[256,768]{1,0:T(8,128)(2,1)S(1)}, u32[]{:S(2)}, u32[]{:S(2)}) collective-permute-start(bf16[256,768]{1,0:T(8,128)(2,1)S(1)} %select_bitcast_fusion.5), channel_id=1, source_target_pairs={{0,4},{4,0},{8,12},{12,8},{16,24},{20,28},{24,16},{28,20},{1,5},{5... | collective-permute-start | bytes 1179656 | tf_op jit(solution)/shard_map/ppermute | solution.py:1093
  43.6 40.7 %collective-permute-start.13 = (bf16[192,4608]{1,0:T(8,128)(2,1)}, bf16[192,4608]{1,0:T(8,128)(2,1)S(1)}, u32[]{:S(2)}, u32[]{:S(2)}) collective-permute-start(bf16[192,4608]{1,0:T(8,128)(2,1)} %broadcast_select_fusion.1.refs_8_), channel_id=1, source_target_pairs={{0,2},{1,3},{2,0},{3,1},{4,6},{5,7},{6,4},{7,5},{8,10},{9,11},{10,... | collective-permute-start | bytes 5308424 | tf_op jit(solution)/shard_map/ppermute | solution.py:1084
  45.2 40.6 %collective-permute-start.12 = (bf16[192,4608]{1,0:T(8,128)(2,1)}, bf16[192,4608]{1,0:T(8,128)(2,1)}, u32[]{:S(2)}, u32[]{:S(2)}) collective-permute-start(bf16[192,4608]{1,0:T(8,128)(2,1)} %broadcast_select_fusion.1.refs_8_), channel_id=1, source_target_pairs={{0,1},{1,0},{2,3},{3,2},{4,5},{5,4},{6,7},{7,6},{8,9},{9,8},{10,11... | collective-permute-start | bytes 5308424 | tf_op jit(solution)/shard_map/ppermute | solution.py:1080
  87.5 30.4 %collective-permute-start.17 = (bf16[384,4608]{1,0:T(8,128)(2,1)S(1)}, bf16[384,4608]{1,0:T(8,128)(2,1)S(1)}, u32[]{:S(2)}, u32[]{:S(2)}) collective-permute-start(bf16[384,4608]{1,0:T(8,128)(2,1)S(1)} %pad_maximum_fusion), channel_id=1, source_target_pairs={{0,16},{16,0},{1,17},{17,1},{2,18},{18,2},{3,19},{19,3},{4,20},{20... | collective-permute-start | bytes 10616840 | tf_op jit(solution)/shard_map/ppermute | solution.py:1076
  206.9 88.6 %collective-permute-start.26 = (bf16[512,3072]{1,0:T(8,128)(2,1)}, bf16[512,3072]{1,0:T(8,128)(2,1)}, u32[]{:S(2)}, u32[]{:S(2)}) collective-permute-start(bf16[512,3072]{1,0:T(8,128)(2,1)} %get-tuple-element.165.refs_0_), channel_id=1, source_target_pairs={{0,16},{16,0},{1,17},{17,1},{2,18},{18,2},{3,19},{19,3},{4,20},{20... | collective-permute-start | bytes 9437192 | tf_op jit(solution)/shard_map/ppermute | solution.py:1076
  208.3 24.2 %collective-permute-start.21 = (bf16[256,768]{1,0:T(8,128)(2,1)S(1)}, bf16[256,768]{1,0:T(8,128)(2,1)S(1)}, u32[]{:S(2)}, u32[]{:S(2)}) collective-permute-start(bf16[256,768]{1,0:T(8,128)(2,1)S(1)} %get-tuple-element.211), channel_id=1, source_target_pairs={{0,4},{4,0},{8,12},{12,8},{16,24},{20,28},{24,16},{28,20},{1,5},{5... | collective-permute-start | bytes 1179656 | tf_op jit(solution)/shard_map/ppermute | solution.py:1093
  208.3 24.2 %collective-permute-start.22 = (bf16[256,768]{1,0:T(8,128)(2,1)S(1)}, bf16[256,768]{1,0:T(8,128)(2,1)S(1)}, u32[]{:S(2)}, u32[]{:S(2)}) collective-permute-start(bf16[256,768]{1,0:T(8,128)(2,1)S(1)} %get-tuple-element.212), channel_id=1, source_target_pairs={{16,28},{20,24},{24,20},{28,16},{17,29},{21,25},{25,21},{29,17},{1... | collective-permute-start | bytes 1179656 | tf_op jit(solution)/shard_map/ppermute | solution.py:1097
  322.5 42.3 %collective-permute-start.31 = (bf16[528,768]{1,0:T(8,128)(2,1)}, bf16[528,768]{1,0:T(8,128)(2,1)}, u32[]{:S(2)}, u32[]{:S(2)}) collective-permute-start(bf16[528,768]{1,0:T(8,128)(2,1)} %get-tuple-element.167), channel_id=1, source_target_pairs={{0,16},{16,0},{1,17},{17,1},{2,18},{18,2},{3,19},{19,3},{4,20},{20... | collective-permute-start | bytes 2433032 | tf_op jit(solution)/shard_map/ppermute | solution.py:1076
  333.3 42.7 %collective-permute-start.34 = (bf16[192,1536]{1,0:T(8,128)(2,1)}, bf16[192,1536]{1,0:T(8,128)(2,1)S(1)}, u32[]{:S(2)}, u32[]{:S(2)}) collective-permute-start(bf16[192,1536]{1,0:T(8,128)(2,1)} %get-tuple-element.150), channel_id=1, source_target_pairs={{0,1},{1,0},{2,3},{3,2},{4,5},{5,4},{6,7},{7,6},{8,9},{9,8},{10,11... | collective-permute-start | bytes 1769480 | tf_op jit(solution)/shard_map/ppermute | solution.py:1080
  333.9 43.0 %collective-permute-start.32 = (bf16[192,1536]{1,0:T(8,128)(2,1)}, bf16[192,1536]{1,0:T(8,128)(2,1)S(1)}, u32[]{:S(2)}, u32[]{:S(2)}) collective-permute-start(bf16[192,1536]{1,0:T(8,128)(2,1)} %get-tuple-element.151), channel_id=1, source_target_pairs={{0,2},{1,3},{2,0},{3,1},{4,6},{5,7},{6,4},{7,5},{8,10},{9,11},{10,... | collective-permute-start | bytes 1769480 | tf_op jit(solution)/shard_map/ppermute | solution.py:1084
  388.2 26.1 %collective-permute-start.51 = (bf16[192,1536]{1,0:T(8,128)(2,1)S(1)}, bf16[192,1536]{1,0:T(8,128)(2,1)}, u32[]{:S(2)}, u32[]{:S(2)}) collective-permute-start(bf16[192,1536]{1,0:T(8,128)(2,1)S(1)} %fusion.2), channel_id=1, source_target_pairs={{0,12},{4,8},{8,4},{12,0},{1,13},{5,9},{9,5},{13,1},{2,14},{6,10},... | collective-permute-start | bytes 1769480 | tf_op jit(solution)/shard_map/ppermute | solution.py:1101
  391.0 37.2 %collective-permute-start.49 = (bf16[192,2048]{1,0:T(8,128)(2,1)}, bf16[192,2048]{1,0:T(8,128)(2,1)}, u32[]{:S(2)}, u32[]{:S(2)}) collective-permute-start(bf16[192,2048]{1,0:T(8,128)(2,1)} %get-tuple-element.196), channel_id=1, source_target_pairs={{0,2},{1,3},{2,0},{3,1},{4,6},{5,7},{6,4},{7,5},{8,10},{9,11},{10,... | collective-permute-start | bytes 2359304 | tf_op jit(solution)/shard_map/ppermute | solution.py:1084
  415.6 49.2 %collective-permute-start.62 = (bf16[192,1536]{1,0:T(8,128)(2,1)S(1)}, bf16[192,1536]{1,0:T(8,128)(2,1)S(1)}, u32[]{:S(2)}, u32[]{:S(2)}) collective-permute-start(bf16[192,1536]{1,0:T(8,128)(2,1)S(1)} %add_convert_fusion.2), channel_id=1, source_target_pairs={{0,4},{4,0},{8,12},{12,8},{1,5},{5,1},{9,13},{13,9},{2,6},{6,2},{1... | collective-permute-start | bytes 1769480 | tf_op jit(solution)/shard_map/ppermute | solution.py:1088
  432.5 23.4 %collective-permute-start.44 = (bf16[192,1152]{1,0:T(8,128)(2,1)S(1)}, bf16[192,1152]{1,0:T(8,128)(2,1)S(1)}, u32[]{:S(2)}, u32[]{:S(2)}) collective-permute-start(bf16[192,1152]{1,0:T(8,128)(2,1)S(1)} %copy-done.63), channel_id=1, source_target_pairs={{0,1},{1,0},{2,3},{3,2},{4,5},{5,4},{6,7},{7,6},{8,9},{9,8},{10,11... | collective-permute-start | bytes 1327112 | tf_op jit(solution)/shard_map/ppermute | solution.py:1080
  433.9 23.5 %collective-permute-start.42 = (bf16[192,1152]{1,0:T(8,128)(2,1)S(1)}, bf16[192,1152]{1,0:T(8,128)(2,1)S(1)}, u32[]{:S(2)}, u32[]{:S(2)}) collective-permute-start(bf16[192,1152]{1,0:T(8,128)(2,1)S(1)} %copy-done.62), channel_id=1, source_target_pairs={{0,2},{1,3},{2,0},{3,1},{4,6},{5,7},{6,4},{7,5},{8,10},{9,11},{10,... | collective-permute-start | bytes 1327112 | tf_op jit(solution)/shard_map/ppermute | solution.py:1084
  453.2 31.6 %collective-permute-start.52 = (bf16[192,2048]{1,0:T(8,128)(2,1)S(1)}, bf16[192,2048]{1,0:T(8,128)(2,1)S(1)}, u32[]{:S(2)}, u32[]{:S(2)}) collective-permute-start(bf16[192,2048]{1,0:T(8,128)(2,1)S(1)} %fusion), channel_id=1, source_target_pairs={{0,12},{4,8},{8,4},{12,0},{1,13},{5,9},{9,5},{13,1},{2,14},{6,10},... | collective-permute-start | bytes 2359304 | tf_op jit(solution)/shard_map/ppermute | solution.py:1101
  464.7 42.3 %collective-permute-start.65 = (bf16[192,1536]{1,0:T(8,128)(2,1)S(1)}, bf16[192,1536]{1,0:T(8,128)(2,1)S(1)}, u32[]{:S(2)}, u32[]{:S(2)}) collective-permute-start(bf16[192,1536]{1,0:T(8,128)(2,1)S(1)} %get-tuple-element.221), channel_id=1, source_target_pairs={{0,16},{16,0},{1,17},{17,1},{2,18},{18,2},{3,19},{19,3},{4,20},{20... | collective-permute-start | bytes 1769480 | tf_op jit(solution)/shard_map/ppermute | solution.py:1076
  466.2 35.4 %collective-permute-start.57 = (bf16[192,1152]{1,0:T(8,128)(2,1)S(1)}, bf16[192,1152]{1,0:T(8,128)(2,1)S(1)}, u32[]{:S(2)}, u32[]{:S(2)}) collective-permute-start(bf16[192,1152]{1,0:T(8,128)(2,1)S(1)} %fusion.7), channel_id=1, source_target_pairs={{0,12},{4,8},{8,4},{12,0},{1,13},{5,9},{9,5},{13,1},{2,14},{6,10},... | collective-permute-start | bytes 1327112 | tf_op jit(solution)/shard_map/ppermute | solution.py:1101
  485.1 49.4 %collective-permute-start.60 = (bf16[192,2048]{1,0:T(8,128)(2,1)S(1)}, bf16[192,2048]{1,0:T(8,128)(2,1)S(1)}, u32[]{:S(2)}, u32[]{:S(2)}) collective-permute-start(bf16[192,2048]{1,0:T(8,128)(2,1)S(1)} %add_convert_fusion), channel_id=1, source_target_pairs={{0,4},{4,0},{8,12},{12,8},{1,5},{5,1},{9,13},{13,9},{2,6},{6,2},{1... | collective-permute-start | bytes 2359304 | tf_op jit(solution)/shard_map/ppermute | solution.py:1088
  501.7 32.1 %collective-permute-start.58 = (bf16[192,1152]{1,0:T(8,128)(2,1)S(1)}, bf16[192,1152]{1,0:T(8,128)(2,1)S(1)}, u32[]{:S(2)}, u32[]{:S(2)}) collective-permute-start(bf16[192,1152]{1,0:T(8,128)(2,1)S(1)} %add_convert_fusion.3), channel_id=1, source_target_pairs={{0,4},{4,0},{8,12},{12,8},{1,5},{5,1},{9,13},{13,9},{2,6},{6,2},{1... | collective-permute-start | bytes 1327112 | tf_op jit(solution)/shard_map/ppermute | solution.py:1088
  506.2 27.4 %collective-permute-start.54 = (bf16[256,768]{1,0:T(8,128)(2,1)S(1)}, bf16[256,768]{1,0:T(8,128)(2,1)S(1)}, u32[]{:S(2)}, u32[]{:S(2)}) collective-permute-start(bf16[256,768]{1,0:T(8,128)(2,1)S(1)} %get-tuple-element.209), channel_id=1, source_target_pairs={{0,4},{4,0},{8,12},{12,8},{16,24},{20,28},{24,16},{28,20},{1,5},{5... | collective-permute-start | bytes 1179656 | tf_op jit(solution)/shard_map/ppermute | solution.py:1093
  506.3 27.4 %collective-permute-start.55 = (bf16[256,768]{1,0:T(8,128)(2,1)S(1)}, bf16[256,768]{1,0:T(8,128)(2,1)S(1)}, u32[]{:S(2)}, u32[]{:S(2)}) collective-permute-start(bf16[256,768]{1,0:T(8,128)(2,1)S(1)} %get-tuple-element.210), channel_id=1, source_target_pairs={{16,28},{20,24},{24,20},{28,16},{17,29},{21,25},{25,21},{29,17},{1... | collective-permute-start | bytes 1179656 | tf_op jit(solution)/shard_map/ppermute | solution.py:1097
  (106 other events, 958.8 us)

commit v6 on v5

--- a/solution.py
+++ b/solution.py
@@ -553,14 +553,25 @@
 
 
 def project_rows(place, hidden, cosine, sine, pieces):
-    rows, width = hidden.shape
+    rows, width = hidden[0].shape
     half = 3 * width // 2
-
-    def body(place_ref, hidden_ref, cos_ref, sin_ref, *refs):
-        parts, (q_ref, kv_ref, weight, sems) = refs[:8], refs[8:]
-        wait_all(start_loads(place_ref, parts, 0, half, weight, sems, 0))
+    count = len(hidden)
+
+    def body(place_ref, *refs):
+        hidden_refs, (cos_ref, sin_ref), refs = refs[:count], refs[count : count + 2], refs[count + 2 :]
+        parts, (q_ref, kv_ref, *chosen, weight, sems) = refs[:8], refs[8:]
+        loads = start_loads(place_ref, parts, 0, half, weight, sems, 0)
+        rows_ref = hidden_refs[0]
+        if count == 2:
+            rows_ref = chosen[0]
+            for index in range(2):
+                @pl.when(place_ref[2] == index)
+                def _():
+                    rows_ref[...] = hidden_refs[index][...]
+
+        wait_all(loads)
         for step in range(3 * width // 256):
-            mixed = mm(hidden_ref[...], weight[:, step * 256 : step * 256 + 256])
+            mixed = mm(rows_ref[...], weight[:, step * 256 : step * 256 + 256])
             for pair in range(2):
                 column = step * 256 + pair * 128
                 part = mixed[:, pair * 128 : pair * 128 + 128]
@@ -574,15 +585,16 @@
                 else:
                     kv_ref[which - 1, :, lane : lane + 128] = part.astype(jnp.bfloat16)
 
+    shapes = [shape_of((rows, width), jnp.bfloat16), shape_of((2, rows, width), jnp.bfloat16)]
     return kernel_call(
         body,
-        [shape_of((rows, width), jnp.bfloat16), shape_of((2, rows, width), jnp.bfloat16)],
-        [in_smem()] + [in_vmem()] * 3 + [anywhere()] * 8,
+        shapes + [shape_of((rows, width), jnp.bfloat16)] * (count - 1),
+        [in_smem()] + [in_vmem()] * (count + 2) + [anywhere()] * 8,
         [pltpu.VMEM((width, 3 * width), jnp.bfloat16), pltpu.SemaphoreType.DMA((10,))],
         60,
         3,
         "project_rows",
-    )(place, hidden, cosine, sine, *pieces)
+    )(place, *hidden, cosine, sine, *pieces)
 
 
 def attend_rows(queries, blocks, seg_column, seg_row):
@@ -821,13 +833,15 @@
 
 
 def mlp_rows_back(place, incoming, one, two, gate, up, first_parts, rest_parts, for_weights):
-    rows, width = incoming.shape
+    rows, width = incoming[0].shape
     ff_half = (rest_parts[0].shape[1] - 2 * width) // 2
     ff = 2 * ff_half
     steps, block_of = mlp_blocks(ff)
     extra = 6 if for_weights else 0
 
-    def body(place_ref, in_ref, one_ref, two_ref, gate_ref, up_ref, *refs):
+    def body(place_ref, *refs):
+        in_refs, refs = refs[: len(incoming)], refs[len(incoming) :]
+        (one_ref, two_ref, gate_ref, up_ref), refs = refs[:4], refs[4:]
         parts, outs, rest = refs[:16], refs[16 : 18 + extra], refs[18 + extra :]
         dresid_ref, datt_ref = outs[:2]
         w_out, w_gate, w_up, w_down, w_norm, norm_ref, _, low_ref, sums_ref = rest
@@ -848,7 +862,10 @@
                 start_all(copies)
             wait_all(norm)
             norm_ref[...] = w_norm[:, :128].astype(jnp.float32).T
-            given = in_ref[...].astype(jnp.float32)
+            given = in_refs[0][...]
+            if len(in_refs) == 2:
+                given = jnp.where(place_ref[2] == 0, given, in_refs[1][...])
+            given = given.astype(jnp.float32)
             unit, scaling = unit_of(two_ref[...])
             dresid_two = norm_rows_back(given, unit, scaling, norm_ref[2:3])
             dresid_ref[...] = dresid_two
@@ -915,7 +932,7 @@
     return kernel_call(
         body,
         shapes,
-        [whole, whole, whole, part, part] + [anywhere()] * 16,
+        [whole] * (len(incoming) + 2) + [part, part] + [anywhere()] * 16,
         mlp_scratch(width, ff) + [pltpu.VMEM((rows, width), jnp.bfloat16), pltpu.VMEM((16, width), jnp.float32)],
         60,
         21,
@@ -923,7 +940,7 @@
         specs,
         (steps,),
         True,
-    )(place, incoming, one, two, gate, up, *first_parts, *rest_parts)
+    )(place, *incoming, one, two, gate, up, *first_parts, *rest_parts)
 
 
 def project_rows_back(place, dqueries, sums, dresid_one, cosine, sine, pieces):
@@ -953,14 +970,14 @@
                 send_ref[...] = dmixed_ref[:, (1 - index) * half : (2 - index) * half]
 
         wait_all(loads)
-        dhidden_ref[...] = resid_ref[...] + mm(dmixed_ref[...], weight[...], NT)
+        dhidden_ref[...] = (resid_ref[...] + mm(dmixed_ref[...], weight[...], NT)).astype(jnp.bfloat16)
 
     return kernel_call(
         body,
         [
             shape_of((rows, half), jnp.bfloat16),
             shape_of((rows, half), jnp.bfloat16),
-            shape_of((rows, width), jnp.float32),
+            shape_of((rows, width), jnp.bfloat16),
         ],
         [in_smem()] + [in_vmem()] * 4 + [anywhere()] * 8 + [in_vmem()] * count,
         [
@@ -1204,7 +1221,7 @@
     middle = (ctx_rank == 1) | (ctx_rank == 2)
     role = jnp.where(middle, 1, 0)
     even = ctx_rank % 2 == 0
-    place = jnp.stack([dp_rank, core]).astype(jnp.int32)
+    place = jnp.stack([dp_rank, core, role]).astype(jnp.int32)
     pick = lambda array, index: lax.dynamic_index_in_dim(array, index, 0, keepdims=False)
 
     def in_order(left, right):
@@ -1277,10 +1294,10 @@
     angles = places.astype(jnp.float32)[:, None] * spread[None, :]
     cosine, sine = jnp.cos(angles), jnp.where(lanes < half, -1.0, 1.0) * jnp.sin(angles)
 
-    def attention(hidden):
-        queries, own = project_rows(place, hidden, cosine, sine, first)
+    def attention(*hidden):
+        queries, own, *chosen = project_rows(place, hidden, cosine, sine, first)
         blocks = [own, to_core(own)]
-        return queries, blocks, *attend_rows(queries, blocks, seg_rows[:, None], seg_keys[None, :])
+        return *chosen, queries, blocks, *attend_rows(queries, blocks, seg_rows[:, None], seg_keys[None, :])
 
     first = both_cores(near, far, first_other(near))
     queries, blocks, attended, sums = attention(given)
@@ -1288,11 +1305,10 @@
     rest = both_cores(near_mlp, gather_far(near_mlp), rest_other(near_mlp))
     output = mlp_rows(place, given, attended, first, rest, False)[0]
 
-    hidden = jnp.where(middle, along_z(output), given)
-    queries, blocks, attended, sums = attention(hidden)
+    hidden, queries, blocks, attended, sums = attention(given, along_z(output))
     output, one, two, normed, mids, gate, up = mlp_rows(place, hidden, attended, first, rest, True)
 
-    dresid_one, dattended = mlp_rows_back(place, given, one, two, gate, up, first, rest, False)
+    dresid_one, dattended = mlp_rows_back(place, (given,), one, two, gate, up, first, rest, False)
     sent_outputs = send_rows(output)
     dqueries, own, across = attend_rows_back(
         queries, blocks, seg_rows[None, :], seg_keys[:, None], attended, sums, after(dattended, *sent_outputs)
@@ -1300,13 +1316,13 @@
     dhidden = project_rows_back(
         place, dqueries, (own, to_core(across)), dresid_one, cosine, sine, first
     )[2]
-    incoming = jnp.where(middle, given, along_z(lowered(dhidden)))
+    relayed = along_z(dhidden)
 
     both = lambda value: (value, to_core(value))
     mids, normed, attended, hidden = both(mids), both(normed), both(attended), both(hidden)
-    incoming = after(incoming, mids[1], normed[1], attended[1], hidden[1])
+    relayed = after(relayed, mids[1], normed[1], attended[1], hidden[1])
     dresid_one, dattended, keep, send, keep_gate, keep_up, send_gate, send_up = mlp_rows_back(
-        place, incoming, one, two, gate, up, first, rest, True
+        place, (relayed, given), one, two, gate, up, first, rest, True
     )
     ff = mids[0].shape[1]
     right, right_gate, right_up = (keep, to_core(send)), (keep_gate, to_core(send_gate)), (keep_up, to_core(send_up))
@@ -1341,7 +1357,7 @@
     far.append(reduce_second(parts[3], near[3]))
     pieces = [reduce_last(*group) for group in zip(parts, near, far)]
     totals, nearly = reduce_ctx(pieces, middle, parts[3])
-    sent_grads = send_rows(after(lowered(dhidden), nearly))
+    sent_grads = send_rows(after(dhidden, nearly))
 
     pairs = []
     for first_layer, second_layer in totals:

time: 548 us -> 539 us (0.984)
  waiting for transfers between devices: 146 us -> 156 us
  starting transfers between devices: 109 us -> 99.8 us
  other arithmetic: 40.4 us -> 34.5 us
    ppermute x4, waiting for transfers between devices: 0.01 us -> 10.5 us  [same_role(): return lax.ppermute(value, 'ctx', [(i, i ^ 3) for i in range(4)])]
    ppermute x4, starting transfers between devices: 21.6 us -> 11.3 us  [same_role(): return lax.ppermute(value, 'ctx', [(i, i ^ 3) for i in range(4)])]
    unnamed x133 -> x135, local copies, waits for them, and re-layouts: 13.6 us -> 14 us
  transfers between devices with their start and end apart: 66 -> 66, of which waited for: 20 -> 21; matrix products, arithmetic and copies ran while one was open for 7% -> 6% of each run, Pallas kernels for 25% -> 25%
where the time goes in v6:
time: 539 us; the launch traced here: 535 us
  Pallas kernels  221 us (41%)
  waiting for transfers between devices  156 us (29%)
  starting transfers between devices  99.8 us (19%)
  other arithmetic  34.5 us (6%)
  local copies, waits for them, and re-layouts  21.5 us (4%)
    pallas_call x2, Pallas kernels, mlp_rows_back(): kernel_call(body, shapes, [whole] * (len(incoming) + 2) + [part, part] +...  48.6 us
    ppermute x6, waiting for transfers between devices, along_z(): return lax.ppermute(value, 'ctx', [(i, i ^ 1) for i in range(4)])  45.6 us
    ppermute x6, starting transfers between devices, along_z(): return lax.ppermute(value, 'ctx', [(i, i ^ 1) for i in range(4)])  43.6 us
    ppermute x12, waiting for transfers between devices, along_x(): return lax.ppermute(value, 'dp', [(i, i ^ 1) for i in range(4)])  43 us
    pallas_call x2, Pallas kernels, attend_rows_back(): kernel_call(body, [shape_of((rows, width), jnp.float32), pair_shape, pair...  39.7 us
    pallas_call x2, Pallas kernels, mlp_rows(): kernel_call(body, shapes, [whole, whole] + [anywhere()] * 16, scratch, 60...  37.8 us
    pallas_call x2, Pallas kernels, attend_rows(): kernel_call(body, [shape_of((rows, width), jnp.bfloat16), shape_of((128,...  31.6 us
    pallas_call x4, Pallas kernels, grad_parts(): kernel_call(body, shapes, [in_smem()] + [in_vmem()] * len(arrays), scratc...  30.3 us
  transfers between devices with their start and end apart: 66, of which 21 were waited for; matrix products, arithmetic and copies ran while one was open for 6% of the time, Pallas kernels for 25%

profile of v6, /device:TPU:0, one launch (start us, length us, event | category | flops | bytes accessed | tf_op | source)
XLA Modules:
  0.0 535.4 jit_solution(11595196094906000619)
XLA Ops:
  19.8 7.5 %collective-permute-done.5.refs_4_.refs_1_.refs_5_.refs_6_.refs_7_ = bf16[192,1664]{1,0:T(8,128)(2,1)S(1)} collective-permute-done((bf16[192,1664]{1,0:T(8,128)(2,1)S(1)}, bf16[192,1664]{1,0:T(8,128)(2,1)S(1)}, u32[]{:S(2)}, u32[]{:S(2)}) %collective-permute-start.5) | collective-permute-done | bytes 639008 | tf_op jit(solution)/shard_map/ppermute | solution.py:1097
  47.8 6.5 %project_rows.2 = (bf16[512,768]{1,0:T(8,128)(2,1)}, bf16[2,512,768]{2,1,0:T(8,128)(2,1)}) custom-call(s32[3]{0:T(128)} %pad_add_fusion.1.place_ref, bf16[512,768]{1,0:T(8,128)(2,1)} %maximum_select_fusion.4.refs_0_.hidden_ref.refs_1_, f32[512,128]{1,0:T(8,128)} %get-tuple-element.261.refs_1_.refs_2_.cos_ref, ...), custom_call_target="tpu_custom_call" | custom-call | bytes 9000000 | tf_op jit(solution)/shard_map/project_rows/pallas_call | solution.py:589
  58.1 15.8 %attend_rows.2 = (bf16[512,768]{1,0:T(8,128)(2,1)}, f32[128,512]{1,0:T(8,128)}) custom-call(s32[512,1]{1,0:T(8,128)} %copy.41.col_ref, s32[1,1024]{1,0:T(1,128)} %bitcast.89, bf16[512,768]{1,0:T(8,128)(2,1)} %get-tuple-element.117.q_ref, bf16[2,512,768]{2,1,0:T(8,128)(2,1)} %get-tuple-element.118.b0, bf16[2,512,768]{2,1,0:T(8,128)(2,1)} %collective-permute-done.10.b1), custom_call_target="tpu_custom_call" | custom-call | bytes 24000000 | tf_op jit(solution)/shard_map/attend_rows/pallas_call | solution.py:632
  73.9 10.4 %collective-permute-done.13.refs_10_.refs_15_.refs_16_ = bf16[192,4608]{1,0:T(8,128)(2,1)S(1)} collective-permute-done((bf16[192,4608]{1,0:T(8,128)(2,1)}, bf16[192,4608]{1,0:T(8,128)(2,1)S(1)}, u32[]{:S(2)}, u32[]{:S(2)}) %collective-permute-start.13) | collective-permute-done | bytes 1769504 | tf_op jit(solution)/shard_map/ppermute | solution.py:1101
  92.0 20.1 %collective-permute-done.14.refs_11_.refs_16_.refs_17_ = bf16[96,4608]{1,0:T(8,128)(2,1)S(1)} collective-permute-done((bf16[96,4608]{1,0:T(8,128)(2,1)S(1)}, bf16[96,4608]{1,0:T(8,128)(2,1)S(1)}, u32[]{:S(2)}, u32[]{:S(2)}) %collective-permute-start.14) | collective-permute-done | bytes 884768 | tf_op jit(solution)/shard_map/ppermute | solution.py:1097
  119.6 17.7 %mlp_rows.2 = bf16[512,768]{1,0:T(8,128)(2,1)} custom-call(s32[3]{0:T(128)} %pad_add_fusion.1.place_ref, bf16[512,768]{1,0:T(8,128)(2,1)} %maximum_select_fusion.4.refs_0_.hidden_ref.refs_1_, bf16[512,768]{1,0:T(8,128)(2,1)} %get-tuple-element.119.att_ref, bf16[192,1664]{1,0:T(8,128)(2,1)} %copy-done.5, bf16[192,1664]{1,0:T(8,128)(2,1)} %copy-done.1, ...), custom_call_target="tpu_custom_call" | custom-call | bytes 48000000 | tf_op jit(solution)/shard_map/mlp_rows/pallas_call | solution.py:821
  137.4 19.8 %collective-permute-done.19.refs_1_ = bf16[512,768]{1,0:T(8,128)(2,1)S(1)} collective-permute-done((bf16[512,768]{1,0:T(8,128)(2,1)}, bf16[512,768]{1,0:T(8,128)(2,1)S(1)}, u32[]{:S(2)}, u32[]{:S(2)}) %collective-permute-start.19) | collective-permute-done | bytes 786464 | tf_op jit(solution)/shard_map/ppermute | solution.py:1105
  158.0 7.1 %project_rows.3 = (bf16[512,768]{1,0:T(8,128)(2,1)}, bf16[2,512,768]{2,1,0:T(8,128)(2,1)}, bf16[512,768]{1,0:T(8,128)(2,1)}) custom-call(s32[3]{0:T(128)} %pad_add_fusion.1.place_ref, bf16[512,768]{1,0:T(8,128)(2,1)} %maximum_select_fusion.4.refs_0_.hidden_ref.refs_1_, bf16[512,768]{1,0:T(8,128)(2,1)} %copy-done.32, ...), custom_call_target="tpu_custom_call" | custom-call | bytes 9000000 | tf_op jit(solution)/shard_map/project_rows/pallas_call | solution.py:589
  170.0 15.8 %attend_rows.3 = (bf16[512,768]{1,0:T(8,128)(2,1)}, f32[128,512]{1,0:T(8,128)}) custom-call(s32[512,1]{1,0:T(8,128)} %copy.41.col_ref, s32[1,1024]{1,0:T(1,128)} %bitcast.90, bf16[512,768]{1,0:T(8,128)(2,1)} %get-tuple-element.129.q_ref, bf16[2,512,768]{2,1,0:T(8,128)(2,1)} %get-tuple-element.130.b0, bf16[2,512,768]{2,1,0:T(8,128)(2,1)} %copy-done.11), custom_call_target="tpu_custom_call" | custom-call | bytes 24000000 | tf_op jit(solution)/shard_map/attend_rows/pallas_call | solution.py:632
  185.7 20.0 %mlp_rows.3 = (bf16[512,768]{1,0:T(8,128)(2,1)}, f32[512,768]{1,0:T(8,128)}, f32[512,768]{1,0:T(8,128)}, bf16[512,768]{1,0:T(8,128)(2,1)}, bf16[512,3072]{1,0:T(...) custom-call(s32[3]{0:T(128)} %pad_add_fusion.1.place_ref, ...), custom_call_target="tpu_custom_call" | custom-call | bytes 48000000 | tf_op jit(solution)/shard_map/mlp_rows/pallas_call | solution.py:821
  209.8 21.9 %mlp_rows_back.2 = (f32[512,768]{1,0:T(8,128)}, bf16[512,768]{1,0:T(8,128)(2,1)}) custom-call(s32[3]{0:T(128)} %pad_add_fusion.1.place_ref, bf16[512,768]{1,0:T(8,128)(2,1)} %maximum_select_fusion.4.refs_0_.hidden_ref.refs_1_, f32[512,768]{1,0:T(8,128)} %get-tuple-element.134.refs_1_.refs_2_, f32[512,768]{1,0:T(8,128)} %get-tuple-element.135.refs_2_.refs_3_, ...), custom_call_target="tpu_custom_call" | custom-call | bytes 63000000 | tf_op jit(solution)/shard_map/mlp_rows_back/pallas_call | solution.py:932
  232.6 19.8 %attend_rows_back.2 = (f32[512,768]{1,0:T(8,128)}, bf16[2,512,768]{2,1,0:T(8,128)(2,1)}, bf16[2,512,768]{2,1,0:T(8,128)(2,1)}) custom-call(s32[1,512]{1,0:T(1,128)} %copy-done.59, s32[1024,1]{1,0:T(8,128)} %copy.44.col_ref, f32[128,512]{1,0:T(8,128)} %get-tuple-element.133.sum_ref, bf16[512,768]{1,0:T(8,128)(2,1)} %get-tuple-element.129.q_ref, ...), custom_call_target="tpu_custom_call" | custom-call | bytes 54000000 | tf_op jit(solution)/shard_map/attend_rows_back/pallas_call | solution.py:688
  262.1 9.6 %project_rows_back.2 = (bf16[512,1152]{1,0:T(8,128)(2,1)}, bf16[512,1152]{1,0:T(8,128)(2,1)}, bf16[512,768]{1,0:T(8,128)(2,1)}) custom-call(s32[3]{0:T(128)} %pad_add_fusion.1.place_ref, f32[512,768]{1,0:T(8,128)} %get-tuple-element.140.dq_ref, f32[512,768]{1,0:T(8,128)} %get-tuple-element.141.resid_ref, ...), custom_call_target="tpu_custom_call" | custom-call | bytes 18000000 | tf_op jit(solution)/shard_map/project_rows_back/pallas_call | solution.py:975
  272.3 19.5 %collective-permute-done.25.refs_0_ = bf16[512,768]{1,0:T(8,128)(2,1)} collective-permute-done((bf16[512,768]{1,0:T(8,128)(2,1)}, bf16[512,768]{1,0:T(8,128)(2,1)}, u32[]{:S(2)}, u32[]{:S(2)}) %collective-permute-start.25) | collective-permute-done | bytes 786464 | tf_op jit(solution)/shard_map/ppermute | solution.py:1105
  291.8 26.8 %mlp_rows_back.3 = (f32[512,768]{1,0:T(8,128)}, bf16[512,768]{1,0:T(8,128)(2,1)}, bf16[528,768]{1,0:T(8,128)(2,1)}, bf16[528,768]{1,0:T(8,128)(2,1)}, bf16[512,1...) custom-call(s32[3]{0:T(128)} %pad_add_fusion.1.place_ref, ...), custom_call_target="tpu_custom_call" | custom-call | bytes 63000000 | tf_op jit(solution)/shard_map/mlp_rows_back/pallas_call | solution.py:932
  323.5 6.5 %grad_parts.4 = (bf16[192,1536]{1,0:T(8,128)(2,1)}, bf16[192,1536]{1,0:T(8,128)(2,1)}, bf16[192,1536]{1,0:T(8,128)(2,1)}, bf16[96,1536]{1,0:T(8,128)(2,1)}, bf16[96,1536]{1,0:T(8,128)(2,1)}) custom-call(s32[3]{0:T(128)} %pad_add_fusion.1.place_ref, bf16[512,768]{1,0:T(8,128)(2,1)} %get-tuple-element.156.refs_0_, bf16[512,768]{1,0:T(8,128)(2,1)} %copy-done.17, ...), custom_call_target="tpu_custom_call" | custom-call | bytes 21000000 | tf_op jit(solution)/shard_map/grad_parts/pallas_call | solution.py:1073
  339.6 19.8 %attend_rows_back.3 = (f32[512,768]{1,0:T(8,128)}, bf16[2,512,768]{2,1,0:T(8,128)(2,1)}, bf16[2,512,768]{2,1,0:T(8,128)(2,1)}) custom-call(s32[1,512]{1,0:T(1,128)} %copy-done.59, s32[1024,1]{1,0:T(8,128)} %copy.44.col_ref, f32[128,512]{1,0:T(8,128)} %get-tuple-element.133.sum_ref, bf16[512,768]{1,0:T(8,128)(2,1)} %get-tuple-element.129.q_ref, ...), custom_call_target="tpu_custom_call" | custom-call | bytes 54000000 | tf_op jit(solution)/shard_map/attend_rows_back/pallas_call | solution.py:688
  361.5 11.2 %grad_parts.6 = (bf16[192,2048]{1,0:T(8,128)(2,1)}, bf16[192,2048]{1,0:T(8,128)(2,1)}, bf16[192,2048]{1,0:T(8,128)(2,1)}, bf16[96,2048]{1,0:T(8,128)(2,1)}, bf16[96,2048]{1,0:T(8,128)(2,1)}) custom-call(s32[3]{0:T(128)} %pad_add_fusion.1.place_ref, bf16[512,3072]{1,0:T(8,128)(2,1)} %get-tuple-element.167.refs_0_, ...), custom_call_target="tpu_custom_call" | custom-call | bytes 21000000 | tf_op jit(solution)/shard_map/grad_parts/pallas_call | solution.py:1073
  390.2 9.6 %project_rows_back.3 = (bf16[512,1152]{1,0:T(8,128)(2,1)}, bf16[512,1152]{1,0:T(8,128)(2,1)}, bf16[512,768]{1,0:T(8,128)(2,1)}) custom-call(s32[3]{0:T(128)} %pad_add_fusion.1.place_ref, f32[512,768]{1,0:T(8,128)} %get-tuple-element.165.dq_ref, f32[512,768]{1,0:T(8,128)} %get-tuple-element.179.resid_ref, ...), custom_call_target="tpu_custom_call" | custom-call | bytes 18000000 | tf_op jit(solution)/shard_map/project_rows_back/pallas_call | solution.py:975
  412.9 10.9 %collective-permute-start.62 = (bf16[192,1536]{1,0:T(8,128)(2,1)S(1)}, bf16[192,1536]{1,0:T(8,128)(2,1)S(1)}, u32[]{:S(2)}, u32[]{:S(2)}) collective-permute-start(bf16[192,1536]{1,0:T(8,128)(2,1)S(1)} %add_convert_fusion.2), channel_id=1, source_target_pairs={{0,4},{4,0},{8,12},{12,8},{1,5},{5,1},{9,13},{13,9},{2,6},{6,2},{1... | collective-permute-start | bytes 1769480 | tf_op jit(solution)/shard_map/ppermute | solution.py:1105
  437.0 10.5 %collective-permute-start.64 = (bf16[192,1536]{1,0:T(8,128)(2,1)S(1)}, bf16[192,1536]{1,0:T(8,128)(2,1)S(1)}, u32[]{:S(2)}, u32[]{:S(2)}) collective-permute-start(bf16[192,1536]{1,0:T(8,128)(2,1)S(1)} %add_convert_fusion.1), channel_id=1, source_target_pairs={{0,4},{4,0},{8,12},{12,8},{1,5},{5,1},{9,13},{13,9},{2,6},{6,2},{1... | collective-permute-start | bytes 1769480 | tf_op jit(solution)/shard_map/ppermute | solution.py:1105
  469.5 10.5 %collective-permute-done.52 = bf16[192,2048]{1,0:T(8,128)(2,1)S(1)} collective-permute-done((bf16[192,2048]{1,0:T(8,128)(2,1)S(1)}, bf16[192,2048]{1,0:T(8,128)(2,1)S(1)}, u32[]{:S(2)}, u32[]{:S(2)}) %collective-permute-start.52) | collective-permute-done | bytes 786464 | tf_op jit(solution)/shard_map/ppermute | solution.py:1118
  480.3 16.3 %collective-permute-start.60 = (bf16[192,2048]{1,0:T(8,128)(2,1)S(1)}, bf16[192,2048]{1,0:T(8,128)(2,1)S(1)}, u32[]{:S(2)}, u32[]{:S(2)}) collective-permute-start(bf16[192,2048]{1,0:T(8,128)(2,1)S(1)} %add_convert_fusion), channel_id=1, source_target_pairs={{0,4},{4,0},{8,12},{12,8},{1,5},{5,1},{9,13},{13,9},{2,6},{6,2},{1... | collective-permute-start | bytes 2359304 | tf_op jit(solution)/shard_map/ppermute | solution.py:1105
  504.5 23.1 %collective-permute-done.54 = bf16[256,768]{1,0:T(8,128)(2,1)S(1)} collective-permute-done((bf16[256,768]{1,0:T(8,128)(2,1)S(1)}, bf16[256,768]{1,0:T(8,128)(2,1)S(1)}, u32[]{:S(2)}, u32[]{:S(2)}) %collective-permute-start.54) | collective-permute-done | bytes 393248 | tf_op jit(solution)/shard_map/ppermute | solution.py:1110
  (338 shorter events, 176.2 us)
Async XLA Ops:
  10.1 32.2 %collective-permute-start.11 = (bf16[192,4608]{1,0:T(8,128)(2,1)S(1)}, bf16[192,4608]{1,0:T(8,128)(2,1)S(1)}, u32[]{:S(2)}, u32[]{:S(2)}) collective-permute-start(bf16[192,4608]{1,0:T(8,128)(2,1)S(1)} %get-tuple-element.228), channel_id=1, source_target_pairs={{0,16},{16,0},{1,17},{17,1},{2,18},{18,2},{3,19},{19,3},{4,20},{20... | collective-permute-start | bytes 5308424 | tf_op jit(solution)/shard_map/ppermute | solution.py:1093
  15.6 24.7 %collective-permute-start.2 = (bf16[256,768]{1,0:T(8,128)(2,1)S(1)}, bf16[256,768]{1,0:T(8,128)(2,1)S(1)}, u32[]{:S(2)}, u32[]{:S(2)}) collective-permute-start(bf16[256,768]{1,0:T(8,128)(2,1)S(1)} %dynamic-slice_bitcast_fusion.5), channel_id=1, source_target_pairs={{16,28},{20,24},{24,20},{28,16},{17,29},{21,25},{25,21},{29,17},{1... | collective-permute-start | bytes 1179656 | tf_op jit(solution)/shard_map/ppermute | solution.py:1114
  16.6 24.3 %collective-permute-start.1 = (bf16[256,768]{1,0:T(8,128)(2,1)S(1)}, bf16[256,768]{1,0:T(8,128)(2,1)S(1)}, u32[]{:S(2)}, u32[]{:S(2)}) collective-permute-start(bf16[256,768]{1,0:T(8,128)(2,1)S(1)} %select_bitcast_fusion.5), channel_id=1, source_target_pairs={{0,4},{4,0},{8,12},{12,8},{16,24},{20,28},{24,16},{28,20},{1,5},{5... | collective-permute-start | bytes 1179656 | tf_op jit(solution)/shard_map/ppermute | solution.py:1110
  43.6 40.7 %collective-permute-start.13 = (bf16[192,4608]{1,0:T(8,128)(2,1)}, bf16[192,4608]{1,0:T(8,128)(2,1)S(1)}, u32[]{:S(2)}, u32[]{:S(2)}) collective-permute-start(bf16[192,4608]{1,0:T(8,128)(2,1)} %broadcast_select_fusion.1.refs_8_.refs_13_.refs_14_), channel_id=1, source_target_pairs={{0,2},{1,3},{2,0},{3,1},{4,6},{5,7},{6,4},{7,5},{8,10},{9,11},{10,... | collective-permute-start | bytes 5308424 | tf_op jit(solution)/shard_map/ppermute | solution.py:1101
  45.1 40.6 %collective-permute-start.12 = (bf16[192,4608]{1,0:T(8,128)(2,1)}, bf16[192,4608]{1,0:T(8,128)(2,1)}, u32[]{:S(2)}, u32[]{:S(2)}) collective-permute-start(bf16[192,4608]{1,0:T(8,128)(2,1)} %broadcast_select_fusion.1.refs_8_.refs_13_.refs_14_), channel_id=1, source_target_pairs={{0,1},{1,0},{2,3},{3,2},{4,5},{5,4},{6,7},{7,6},{8,9},{9,8},{10,11... | collective-permute-start | bytes 5308424 | tf_op jit(solution)/shard_map/ppermute | solution.py:1097
  87.4 30.3 %collective-permute-start.17 = (bf16[384,4608]{1,0:T(8,128)(2,1)S(1)}, bf16[384,4608]{1,0:T(8,128)(2,1)S(1)}, u32[]{:S(2)}, u32[]{:S(2)}) collective-permute-start(bf16[384,4608]{1,0:T(8,128)(2,1)S(1)} %pad_maximum_fusion), channel_id=1, source_target_pairs={{0,16},{16,0},{1,17},{17,1},{2,18},{18,2},{3,19},{19,3},{4,20},{20... | collective-permute-start | bytes 10616840 | tf_op jit(solution)/shard_map/ppermute | solution.py:1093
  205.8 86.0 %collective-permute-start.26 = (bf16[512,3072]{1,0:T(8,128)(2,1)}, bf16[512,3072]{1,0:T(8,128)(2,1)}, u32[]{:S(2)}, u32[]{:S(2)}) collective-permute-start(bf16[512,3072]{1,0:T(8,128)(2,1)} %get-tuple-element.167.refs_0_), channel_id=1, source_target_pairs={{0,16},{16,0},{1,17},{17,1},{2,18},{18,2},{3,19},{19,3},{4,20},{20... | collective-permute-start | bytes 9437192 | tf_op jit(solution)/shard_map/ppermute | solution.py:1093
  207.2 24.5 %collective-permute-start.21 = (bf16[256,768]{1,0:T(8,128)(2,1)S(1)}, bf16[256,768]{1,0:T(8,128)(2,1)S(1)}, u32[]{:S(2)}, u32[]{:S(2)}) collective-permute-start(bf16[256,768]{1,0:T(8,128)(2,1)S(1)} %get-tuple-element.213), channel_id=1, source_target_pairs={{0,4},{4,0},{8,12},{12,8},{16,24},{20,28},{24,16},{28,20},{1,5},{5... | collective-permute-start | bytes 1179656 | tf_op jit(solution)/shard_map/ppermute | solution.py:1110
  319.2 42.3 %collective-permute-start.31 = (bf16[528,768]{1,0:T(8,128)(2,1)}, bf16[528,768]{1,0:T(8,128)(2,1)}, u32[]{:S(2)}, u32[]{:S(2)}) collective-permute-start(bf16[528,768]{1,0:T(8,128)(2,1)} %get-tuple-element.169), channel_id=1, source_target_pairs={{0,16},{16,0},{1,17},{17,1},{2,18},{18,2},{3,19},{19,3},{4,20},{20... | collective-permute-start | bytes 2433032 | tf_op jit(solution)/shard_map/ppermute | solution.py:1093
  330.0 42.7 %collective-permute-start.34 = (bf16[192,1536]{1,0:T(8,128)(2,1)}, bf16[192,1536]{1,0:T(8,128)(2,1)S(1)}, u32[]{:S(2)}, u32[]{:S(2)}) collective-permute-start(bf16[192,1536]{1,0:T(8,128)(2,1)} %get-tuple-element.152), channel_id=1, source_target_pairs={{0,1},{1,0},{2,3},{3,2},{4,5},{5,4},{6,7},{7,6},{8,9},{9,8},{10,11... | collective-permute-start | bytes 1769480 | tf_op jit(solution)/shard_map/ppermute | solution.py:1097
  330.7 42.9 %collective-permute-start.32 = (bf16[192,1536]{1,0:T(8,128)(2,1)}, bf16[192,1536]{1,0:T(8,128)(2,1)S(1)}, u32[]{:S(2)}, u32[]{:S(2)}) collective-permute-start(bf16[192,1536]{1,0:T(8,128)(2,1)} %get-tuple-element.153), channel_id=1, source_target_pairs={{0,2},{1,3},{2,0},{3,1},{4,6},{5,7},{6,4},{7,5},{8,10},{9,11},{10,... | collective-permute-start | bytes 1769480 | tf_op jit(solution)/shard_map/ppermute | solution.py:1101
  385.0 27.8 %collective-permute-start.51 = (bf16[192,1536]{1,0:T(8,128)(2,1)S(1)}, bf16[192,1536]{1,0:T(8,128)(2,1)S(1)}, u32[]{:S(2)}, u32[]{:S(2)}) collective-permute-start(bf16[192,1536]{1,0:T(8,128)(2,1)S(1)} %fusion.2), channel_id=1, source_target_pairs={{0,12},{4,8},{8,4},{12,0},{1,13},{5,9},{9,5},{13,1},{2,14},{6,10},... | collective-permute-start | bytes 1769480 | tf_op jit(solution)/shard_map/ppermute | solution.py:1118
  387.7 36.1 %collective-permute-start.49 = (bf16[192,2048]{1,0:T(8,128)(2,1)}, bf16[192,2048]{1,0:T(8,128)(2,1)}, u32[]{:S(2)}, u32[]{:S(2)}) collective-permute-start(bf16[192,2048]{1,0:T(8,128)(2,1)} %get-tuple-element.198), channel_id=1, source_target_pairs={{0,2},{1,3},{2,0},{3,1},{4,6},{5,7},{6,4},{7,5},{8,10},{9,11},{10,... | collective-permute-start | bytes 2359304 | tf_op jit(solution)/shard_map/ppermute | solution.py:1101
  412.9 48.7 %collective-permute-start.62 = (bf16[192,1536]{1,0:T(8,128)(2,1)S(1)}, bf16[192,1536]{1,0:T(8,128)(2,1)S(1)}, u32[]{:S(2)}, u32[]{:S(2)}) collective-permute-start(bf16[192,1536]{1,0:T(8,128)(2,1)S(1)} %add_convert_fusion.2), channel_id=1, source_target_pairs={{0,4},{4,0},{8,12},{12,8},{1,5},{5,1},{9,13},{13,9},{2,6},{6,2},{1... | collective-permute-start | bytes 1769480 | tf_op jit(solution)/shard_map/ppermute | solution.py:1105
  428.2 24.5 %collective-permute-start.44 = (bf16[192,1152]{1,0:T(8,128)(2,1)S(1)}, bf16[192,1152]{1,0:T(8,128)(2,1)S(1)}, u32[]{:S(2)}, u32[]{:S(2)}) collective-permute-start(bf16[192,1152]{1,0:T(8,128)(2,1)S(1)} %copy-done.64), channel_id=1, source_target_pairs={{0,1},{1,0},{2,3},{3,2},{4,5},{5,4},{6,7},{7,6},{8,9},{9,8},{10,11... | collective-permute-start | bytes 1327112 | tf_op jit(solution)/shard_map/ppermute | solution.py:1097
  429.5 24.7 %collective-permute-start.42 = (bf16[192,1152]{1,0:T(8,128)(2,1)S(1)}, bf16[192,1152]{1,0:T(8,128)(2,1)S(1)}, u32[]{:S(2)}, u32[]{:S(2)}) collective-permute-start(bf16[192,1152]{1,0:T(8,128)(2,1)S(1)} %copy-done.63), channel_id=1, source_target_pairs={{0,2},{1,3},{2,0},{3,1},{4,6},{5,7},{6,4},{7,5},{8,10},{9,11},{10,... | collective-permute-start | bytes 1327112 | tf_op jit(solution)/shard_map/ppermute | solution.py:1101
  437.0 24.3 %collective-permute-start.64 = (bf16[192,1536]{1,0:T(8,128)(2,1)S(1)}, bf16[192,1536]{1,0:T(8,128)(2,1)S(1)}, u32[]{:S(2)}, u32[]{:S(2)}) collective-permute-start(bf16[192,1536]{1,0:T(8,128)(2,1)S(1)} %add_convert_fusion.1), channel_id=1, source_target_pairs={{0,4},{4,0},{8,12},{12,8},{1,5},{5,1},{9,13},{13,9},{2,6},{6,2},{1... | collective-permute-start | bytes 1769480 | tf_op jit(solution)/shard_map/ppermute | solution.py:1105
  450.0 30.0 %collective-permute-start.52 = (bf16[192,2048]{1,0:T(8,128)(2,1)S(1)}, bf16[192,2048]{1,0:T(8,128)(2,1)S(1)}, u32[]{:S(2)}, u32[]{:S(2)}) collective-permute-start(bf16[192,2048]{1,0:T(8,128)(2,1)S(1)} %fusion), channel_id=1, source_target_pairs={{0,12},{4,8},{8,4},{12,0},{1,13},{5,9},{9,5},{13,1},{2,14},{6,10},... | collective-permute-start | bytes 2359304 | tf_op jit(solution)/shard_map/ppermute | solution.py:1118
  461.5 41.3 %collective-permute-start.65 = (bf16[192,1536]{1,0:T(8,128)(2,1)S(1)}, bf16[192,1536]{1,0:T(8,128)(2,1)S(1)}, u32[]{:S(2)}, u32[]{:S(2)}) collective-permute-start(bf16[192,1536]{1,0:T(8,128)(2,1)S(1)} %get-tuple-element.223), channel_id=1, source_target_pairs={{0,16},{16,0},{1,17},{17,1},{2,18},{18,2},{3,19},{19,3},{4,20},{20... | collective-permute-start | bytes 1769480 | tf_op jit(solution)/shard_map/ppermute | solution.py:1093
  463.0 33.6 %collective-permute-start.57 = (bf16[192,1152]{1,0:T(8,128)(2,1)S(1)}, bf16[192,1152]{1,0:T(8,128)(2,1)S(1)}, u32[]{:S(2)}, u32[]{:S(2)}) collective-permute-start(bf16[192,1152]{1,0:T(8,128)(2,1)S(1)} %fusion.7), channel_id=1, source_target_pairs={{0,12},{4,8},{8,4},{12,0},{1,13},{5,9},{9,5},{13,1},{2,14},{6,10},... | collective-permute-start | bytes 1327112 | tf_op jit(solution)/shard_map/ppermute | solution.py:1118
  480.3 48.2 %collective-permute-start.60 = (bf16[192,2048]{1,0:T(8,128)(2,1)S(1)}, bf16[192,2048]{1,0:T(8,128)(2,1)S(1)}, u32[]{:S(2)}, u32[]{:S(2)}) collective-permute-start(bf16[192,2048]{1,0:T(8,128)(2,1)S(1)} %add_convert_fusion), channel_id=1, source_target_pairs={{0,4},{4,0},{8,12},{12,8},{1,5},{5,1},{9,13},{13,9},{2,6},{6,2},{1... | collective-permute-start | bytes 2359304 | tf_op jit(solution)/shard_map/ppermute | solution.py:1105
  496.7 31.1 %collective-permute-start.58 = (bf16[192,1152]{1,0:T(8,128)(2,1)S(1)}, bf16[192,1152]{1,0:T(8,128)(2,1)S(1)}, u32[]{:S(2)}, u32[]{:S(2)}) collective-permute-start(bf16[192,1152]{1,0:T(8,128)(2,1)S(1)} %add_convert_fusion.3), channel_id=1, source_target_pairs={{0,4},{4,0},{8,12},{12,8},{1,5},{5,1},{9,13},{13,9},{2,6},{6,2},{1... | collective-permute-start | bytes 1327112 | tf_op jit(solution)/shard_map/ppermute | solution.py:1105
  502.0 25.6 %collective-permute-start.54 = (bf16[256,768]{1,0:T(8,128)(2,1)S(1)}, bf16[256,768]{1,0:T(8,128)(2,1)S(1)}, u32[]{:S(2)}, u32[]{:S(2)}) collective-permute-start(bf16[256,768]{1,0:T(8,128)(2,1)S(1)} %get-tuple-element.211), channel_id=1, source_target_pairs={{0,4},{4,0},{8,12},{12,8},{16,24},{20,28},{24,16},{28,20},{1,5},{5... | collective-permute-start | bytes 1179656 | tf_op jit(solution)/shard_map/ppermute | solution.py:1110
  502.1 25.5 %collective-permute-start.55 = (bf16[256,768]{1,0:T(8,128)(2,1)S(1)}, bf16[256,768]{1,0:T(8,128)(2,1)S(1)}, u32[]{:S(2)}, u32[]{:S(2)}) collective-permute-start(bf16[256,768]{1,0:T(8,128)(2,1)S(1)} %get-tuple-element.212), channel_id=1, source_target_pairs={{16,28},{20,24},{24,20},{28,16},{17,29},{21,25},{25,21},{29,17},{1... | collective-permute-start | bytes 1179656 | tf_op jit(solution)/shard_map/ppermute | solution.py:1114
  (107 other events, 998.0 us)

commit v7 on v6

--- a/solution.py
+++ b/solution.py
@@ -1294,12 +1294,15 @@
     angles = places.astype(jnp.float32)[:, None] * spread[None, :]
     cosine, sine = jnp.cos(angles), jnp.where(lanes < half, -1.0, 1.0) * jnp.sin(angles)
 
+    key_column = seg_keys[:, None]
+
     def attention(*hidden):
         queries, own, *chosen = project_rows(place, hidden, cosine, sine, first)
         blocks = [own, to_core(own)]
         return *chosen, queries, blocks, *attend_rows(queries, blocks, seg_rows[:, None], seg_keys[None, :])
 
     first = both_cores(near, far, first_other(near))
+    key_column, given = lax.optimization_barrier((key_column, given))
     queries, blocks, attended, sums = attention(given)
     near_mlp = [after(part, attended) for part in near_mlp]
     rest = both_cores(near_mlp, gather_far(near_mlp), rest_other(near_mlp))
@@ -1311,10 +1314,10 @@
     dresid_one, dattended = mlp_rows_back(place, (given,), one, two, gate, up, first, rest, False)
     sent_outputs = send_rows(output)
     dqueries, own, across = attend_rows_back(
-        queries, blocks, seg_rows[None, :], seg_keys[:, None], attended, sums, after(dattended, *sent_outputs)
+        queries, blocks, seg_rows[None, :], key_column, attended, sums, dattended
     )
     dhidden = project_rows_back(
-        place, dqueries, (own, to_core(across)), dresid_one, cosine, sine, first
+        place, dqueries, (own, to_core(across)), after(dresid_one, *sent_outputs), cosine, sine, first
     )[2]
     relayed = along_z(dhidden)
 
@@ -1332,7 +1335,7 @@
     parts += grad_parts(place, [[(normed, (0, width), right_up, (0, ff // 2), 1)]])
     near.append(reduce_first(parts[1]))
     dqueries, own, across = attend_rows_back(
-        queries, blocks, seg_rows[None, :], seg_keys[:, None], attended[0], sums, after(dattended, *parts[1])
+        queries, blocks, seg_rows[None, :], key_column, attended[0], sums, after(dattended, *parts[1])
     )
     across = to_core(after(across, *near[0], *near[1]))
     far = [reduce_second(parts[0], near[0], dqueries), reduce_second(parts[1], near[1], dqueries)]

time: 539 us -> 552 us (1.024)
  starting transfers between devices: 99.8 us -> 106 us
  waiting for transfers between devices: 156 us -> 162 us
    ppermute x3, waiting for transfers between devices: 23.1 us -> 30.5 us  [near_blocks(): return lax.ppermute(value, ('section', 'ctx'), pairs)]
  transfers between devices with their start and end apart: 66 -> 66, of which waited for: 21 -> 20; matrix products, arithmetic and copies ran while one was open for 6% -> 6% of each run, Pallas kernels for 25% -> 25%
where the time goes in v7:
time: 552 us; the launch traced here: 548 us
  Pallas kernels  222 us (40%)
  waiting for transfers between devices  162 us (29%)
  starting transfers between devices  106 us (19%)
  other arithmetic  33.5 us (6%)
  local copies, waits for them, and re-layouts  22.8 us (4%)
    pallas_call x2, Pallas kernels, mlp_rows_back(): kernel_call(body, shapes, [whole] * (len(incoming) + 2) + [part, part] +...  48.7 us
    ppermute x6, starting transfers between devices, along_z(): return lax.ppermute(value, 'ctx', [(i, i ^ 1) for i in range(4)])  46.9 us
    ppermute x6, waiting for transfers between devices, along_z(): return lax.ppermute(value, 'ctx', [(i, i ^ 1) for i in range(4)])  45.9 us
    ppermute x12, waiting for transfers between devices, along_x(): return lax.ppermute(value, 'dp', [(i, i ^ 1) for i in range(4)])  42.7 us
    pallas_call x2, Pallas kernels, attend_rows_back(): kernel_call(body, [shape_of((rows, width), jnp.float32), pair_shape, pair...  40 us
    pallas_call x2, Pallas kernels, mlp_rows(): kernel_call(body, shapes, [whole, whole] + [anywhere()] * 16, scratch, 60...  37.8 us
    pallas_call x2, Pallas kernels, attend_rows(): kernel_call(body, [shape_of((rows, width), jnp.bfloat16), shape_of((128,...  31.6 us
    ppermute x3, waiting for transfers between devices, near_blocks(): return lax.ppermute(value, ('section', 'ctx'), pairs)  30.5 us
  transfers between devices with their start and end apart: 66, of which 20 were waited for; matrix products, arithmetic and copies ran while one was open for 6% of the time, Pallas kernels for 25%

profile of v7, /device:TPU:0, one launch (start us, length us, event | category | flops | bytes accessed | tf_op | source)
XLA Modules:
  0.0 548.3 jit_solution(14257674991271302702)
XLA Ops:
  20.3 7.6 %collective-permute-done.5.refs_4_.refs_1_.refs_5_.refs_6_.refs_7_ = bf16[192,1664]{1,0:T(8,128)(2,1)S(1)} collective-permute-done((bf16[192,1664]{1,0:T(8,128)(2,1)S(1)}, bf16[192,1664]{1,0:T(8,128)(2,1)S(1)}, u32[]{:S(2)}, u32[]{:S(2)}) %collective-permute-start.5) | collective-permute-done | bytes 639008 | tf_op jit(solution)/shard_map/ppermute | solution.py:1097
  48.3 6.5 %project_rows.2 = (bf16[512,768]{1,0:T(8,128)(2,1)}, bf16[2,512,768]{2,1,0:T(8,128)(2,1)}) custom-call(s32[3]{0:T(128)} %pad_add_fusion.1.place_ref, bf16[512,768]{1,0:T(8,128)(2,1)} %maximum_select_fusion.4.refs_0_.hidden_ref.refs_1_, f32[512,128]{1,0:T(8,128)} %get-tuple-element.265.refs_1_.refs_2_.cos_ref, ...), custom_call_target="tpu_custom_call" | custom-call | bytes 9000000 | tf_op jit(solution)/shard_map/project_rows/pallas_call | solution.py:589
  58.7 15.8 %attend_rows.2 = (bf16[512,768]{1,0:T(8,128)(2,1)}, f32[128,512]{1,0:T(8,128)}) custom-call(s32[512,1]{1,0:T(8,128)} %copy.41.col_ref, s32[1,1024]{1,0:T(1,128)} %bitcast.89, bf16[512,768]{1,0:T(8,128)(2,1)} %get-tuple-element.120.q_ref, bf16[2,512,768]{2,1,0:T(8,128)(2,1)} %get-tuple-element.121.b0, bf16[2,512,768]{2,1,0:T(8,128)(2,1)} %collective-permute-done.10.b1), custom_call_target="tpu_custom_call" | custom-call | bytes 24000000 | tf_op jit(solution)/shard_map/attend_rows/pallas_call | solution.py:632
  74.5 10.4 %collective-permute-done.13.refs_10_.refs_15_.refs_16_ = bf16[192,4608]{1,0:T(8,128)(2,1)S(1)} collective-permute-done((bf16[192,4608]{1,0:T(8,128)(2,1)}, bf16[192,4608]{1,0:T(8,128)(2,1)S(1)}, u32[]{:S(2)}, u32[]{:S(2)}) %collective-permute-start.13) | collective-permute-done | bytes 1769504 | tf_op jit(solution)/shard_map/ppermute | solution.py:1101
  92.6 20.0 %collective-permute-done.14.refs_11_.refs_16_.refs_17_ = bf16[96,4608]{1,0:T(8,128)(2,1)S(1)} collective-permute-done((bf16[96,4608]{1,0:T(8,128)(2,1)S(1)}, bf16[96,4608]{1,0:T(8,128)(2,1)S(1)}, u32[]{:S(2)}, u32[]{:S(2)}) %collective-permute-start.14) | collective-permute-done | bytes 884768 | tf_op jit(solution)/shard_map/ppermute | solution.py:1097
  120.2 17.7 %mlp_rows.2 = bf16[512,768]{1,0:T(8,128)(2,1)} custom-call(s32[3]{0:T(128)} %pad_add_fusion.1.place_ref, bf16[512,768]{1,0:T(8,128)(2,1)} %maximum_select_fusion.4.refs_0_.hidden_ref.refs_1_, bf16[512,768]{1,0:T(8,128)(2,1)} %get-tuple-element.122.att_ref, bf16[192,1664]{1,0:T(8,128)(2,1)} %copy-done.5, bf16[192,1664]{1,0:T(8,128)(2,1)} %copy-done.1, ...), custom_call_target="tpu_custom_call" | custom-call | bytes 48000000 | tf_op jit(solution)/shard_map/mlp_rows/pallas_call | solution.py:821
  138.0 19.8 %collective-permute-done.19.refs_1_ = bf16[512,768]{1,0:T(8,128)(2,1)S(1)} collective-permute-done((bf16[512,768]{1,0:T(8,128)(2,1)}, bf16[512,768]{1,0:T(8,128)(2,1)S(1)}, u32[]{:S(2)}, u32[]{:S(2)}) %collective-permute-start.19) | collective-permute-done | bytes 786464 | tf_op jit(solution)/shard_map/ppermute | solution.py:1105
  158.7 7.1 %project_rows.3 = (bf16[512,768]{1,0:T(8,128)(2,1)}, bf16[2,512,768]{2,1,0:T(8,128)(2,1)}, bf16[512,768]{1,0:T(8,128)(2,1)}) custom-call(s32[3]{0:T(128)} %pad_add_fusion.1.place_ref, bf16[512,768]{1,0:T(8,128)(2,1)} %maximum_select_fusion.4.refs_0_.hidden_ref.refs_1_, bf16[512,768]{1,0:T(8,128)(2,1)} %copy-done.32, ...), custom_call_target="tpu_custom_call" | custom-call | bytes 9000000 | tf_op jit(solution)/shard_map/project_rows/pallas_call | solution.py:589
  170.6 15.8 %attend_rows.3 = (bf16[512,768]{1,0:T(8,128)(2,1)}, f32[128,512]{1,0:T(8,128)}) custom-call(s32[512,1]{1,0:T(8,128)} %copy.41.col_ref, s32[1,1024]{1,0:T(1,128)} %bitcast.90, bf16[512,768]{1,0:T(8,128)(2,1)} %get-tuple-element.132.q_ref, bf16[2,512,768]{2,1,0:T(8,128)(2,1)} %get-tuple-element.133.b0, bf16[2,512,768]{2,1,0:T(8,128)(2,1)} %copy-done.11), custom_call_target="tpu_custom_call" | custom-call | bytes 24000000 | tf_op jit(solution)/shard_map/attend_rows/pallas_call | solution.py:632
  186.4 20.1 %mlp_rows.3 = (bf16[512,768]{1,0:T(8,128)(2,1)}, f32[512,768]{1,0:T(8,128)}, f32[512,768]{1,0:T(8,128)}, bf16[512,768]{1,0:T(8,128)(2,1)}, bf16[512,3072]{1,0:T(...) custom-call(s32[3]{0:T(128)} %pad_add_fusion.1.place_ref, ...), custom_call_target="tpu_custom_call" | custom-call | bytes 48000000 | tf_op jit(solution)/shard_map/mlp_rows/pallas_call | solution.py:821
  207.7 21.9 %mlp_rows_back.2 = (f32[512,768]{1,0:T(8,128)}, bf16[512,768]{1,0:T(8,128)(2,1)}) custom-call(s32[3]{0:T(128)} %pad_add_fusion.1.place_ref, bf16[512,768]{1,0:T(8,128)(2,1)} %maximum_select_fusion.4.refs_0_.hidden_ref.refs_1_, f32[512,768]{1,0:T(8,128)} %get-tuple-element.138.refs_1_.refs_2_, f32[512,768]{1,0:T(8,128)} %get-tuple-element.139.refs_2_.refs_3_, ...), custom_call_target="tpu_custom_call" | custom-call | bytes 63000000 | tf_op jit(solution)/shard_map/mlp_rows_back/pallas_call | solution.py:932
  229.6 20.2 %attend_rows_back.2 = (f32[512,768]{1,0:T(8,128)}, bf16[2,512,768]{2,1,0:T(8,128)(2,1)}, bf16[2,512,768]{2,1,0:T(8,128)(2,1)}) custom-call(s32[1,512]{1,0:T(1,128)} %copy-done.59, s32[1024,1]{1,0:T(8,128)} %copy.44.col_ref, f32[128,512]{1,0:T(8,128)} %get-tuple-element.137.sum_ref, bf16[512,768]{1,0:T(8,128)(2,1)} %get-tuple-element.132.q_ref, ...), custom_call_target="tpu_custom_call" | custom-call | bytes 54000000 | tf_op jit(solution)/shard_map/attend_rows_back/pallas_call | solution.py:688
  268.3 9.6 %project_rows_back.2 = (bf16[512,1152]{1,0:T(8,128)(2,1)}, bf16[512,1152]{1,0:T(8,128)(2,1)}, bf16[512,768]{1,0:T(8,128)(2,1)}) custom-call(s32[3]{0:T(128)} %pad_add_fusion.1.place_ref, f32[512,768]{1,0:T(8,128)} %get-tuple-element.143.dq_ref, f32[512,768]{1,0:T(8,128)} %get-tuple-element.145.resid_ref, ...), custom_call_target="tpu_custom_call" | custom-call | bytes 18000000 | tf_op jit(solution)/shard_map/project_rows_back/pallas_call | solution.py:975
  282.1 18.0 %collective-permute-done.25.refs_0_ = bf16[512,768]{1,0:T(8,128)(2,1)} collective-permute-done((bf16[512,768]{1,0:T(8,128)(2,1)}, bf16[512,768]{1,0:T(8,128)(2,1)}, u32[]{:S(2)}, u32[]{:S(2)}) %collective-permute-start.25) | collective-permute-done | bytes 786464 | tf_op jit(solution)/shard_map/ppermute | solution.py:1105
  300.1 26.8 %mlp_rows_back.3 = (f32[512,768]{1,0:T(8,128)}, bf16[512,768]{1,0:T(8,128)(2,1)}, bf16[528,768]{1,0:T(8,128)(2,1)}, bf16[528,768]{1,0:T(8,128)(2,1)}, bf16[512,1...) custom-call(s32[3]{0:T(128)} %pad_add_fusion.1.place_ref, ...), custom_call_target="tpu_custom_call" | custom-call | bytes 63000000 | tf_op jit(solution)/shard_map/mlp_rows_back/pallas_call | solution.py:932
  347.8 19.8 %attend_rows_back.3 = (f32[512,768]{1,0:T(8,128)}, bf16[2,512,768]{2,1,0:T(8,128)(2,1)}, bf16[2,512,768]{2,1,0:T(8,128)(2,1)}) custom-call(s32[1,512]{1,0:T(1,128)} %copy-done.59, s32[1024,1]{1,0:T(8,128)} %copy.44.col_ref, f32[128,512]{1,0:T(8,128)} %get-tuple-element.137.sum_ref, bf16[512,768]{1,0:T(8,128)(2,1)} %get-tuple-element.132.q_ref, ...), custom_call_target="tpu_custom_call" | custom-call | bytes 54000000 | tf_op jit(solution)/shard_map/attend_rows_back/pallas_call | solution.py:688
  369.8 11.2 %grad_parts.6 = (bf16[192,2048]{1,0:T(8,128)(2,1)}, bf16[192,2048]{1,0:T(8,128)(2,1)}, bf16[192,2048]{1,0:T(8,128)(2,1)}, bf16[96,2048]{1,0:T(8,128)(2,1)}, bf16[96,2048]{1,0:T(8,128)(2,1)}) custom-call(s32[3]{0:T(128)} %pad_add_fusion.1.place_ref, bf16[512,3072]{1,0:T(8,128)(2,1)} %get-tuple-element.171.refs_0_, ...), custom_call_target="tpu_custom_call" | custom-call | bytes 21000000 | tf_op jit(solution)/shard_map/grad_parts/pallas_call | solution.py:1073
  400.6 9.6 %project_rows_back.3 = (bf16[512,1152]{1,0:T(8,128)(2,1)}, bf16[512,1152]{1,0:T(8,128)(2,1)}, bf16[512,768]{1,0:T(8,128)(2,1)}) custom-call(s32[3]{0:T(128)} %pad_add_fusion.1.place_ref, f32[512,768]{1,0:T(8,128)} %get-tuple-element.169.dq_ref, f32[512,768]{1,0:T(8,128)} %get-tuple-element.183.resid_ref, ...), custom_call_target="tpu_custom_call" | custom-call | bytes 18000000 | tf_op jit(solution)/shard_map/project_rows_back/pallas_call | solution.py:975
  424.8 10.0 %collective-permute-start.62 = (bf16[192,1536]{1,0:T(8,128)(2,1)S(1)}, bf16[192,1536]{1,0:T(8,128)(2,1)S(1)}, u32[]{:S(2)}, u32[]{:S(2)}) collective-permute-start(bf16[192,1536]{1,0:T(8,128)(2,1)S(1)} %add_convert_fusion.2), channel_id=1, source_target_pairs={{0,4},{4,0},{8,12},{12,8},{1,5},{5,1},{9,13},{13,9},{2,6},{6,2},{1... | collective-permute-start | bytes 1769480 | tf_op jit(solution)/shard_map/ppermute | solution.py:1105
  447.0 11.0 %collective-permute-start.64 = (bf16[192,1536]{1,0:T(8,128)(2,1)S(1)}, bf16[192,1536]{1,0:T(8,128)(2,1)S(1)}, u32[]{:S(2)}, u32[]{:S(2)}) collective-permute-start(bf16[192,1536]{1,0:T(8,128)(2,1)S(1)} %add_convert_fusion.1), channel_id=1, source_target_pairs={{0,4},{4,0},{8,12},{12,8},{1,5},{5,1},{9,13},{13,9},{2,6},{6,2},{1... | collective-permute-start | bytes 1769480 | tf_op jit(solution)/shard_map/ppermute | solution.py:1105
  464.2 8.2 %collective-permute-done.64 = bf16[192,1536]{1,0:T(8,128)(2,1)S(1)} collective-permute-done((bf16[192,1536]{1,0:T(8,128)(2,1)S(1)}, bf16[192,1536]{1,0:T(8,128)(2,1)S(1)}, u32[]{:S(2)}, u32[]{:S(2)}) %collective-permute-start.64) | collective-permute-done | bytes 589856 | tf_op jit(solution)/shard_map/ppermute | solution.py:1105
  478.9 13.0 %collective-permute-done.52 = bf16[192,2048]{1,0:T(8,128)(2,1)S(1)} collective-permute-done((bf16[192,2048]{1,0:T(8,128)(2,1)S(1)}, bf16[192,2048]{1,0:T(8,128)(2,1)S(1)}, u32[]{:S(2)}, u32[]{:S(2)}) %collective-permute-start.52) | collective-permute-done | bytes 786464 | tf_op jit(solution)/shard_map/ppermute | solution.py:1118
  492.1 16.3 %collective-permute-start.60 = (bf16[192,2048]{1,0:T(8,128)(2,1)S(1)}, bf16[192,2048]{1,0:T(8,128)(2,1)S(1)}, u32[]{:S(2)}, u32[]{:S(2)}) collective-permute-start(bf16[192,2048]{1,0:T(8,128)(2,1)S(1)} %add_convert_fusion), channel_id=1, source_target_pairs={{0,4},{4,0},{8,12},{12,8},{1,5},{5,1},{9,13},{13,9},{2,6},{6,2},{1... | collective-permute-start | bytes 2359304 | tf_op jit(solution)/shard_map/ppermute | solution.py:1105
  516.4 24.1 %collective-permute-done.54 = bf16[256,768]{1,0:T(8,128)(2,1)S(1)} collective-permute-done((bf16[256,768]{1,0:T(8,128)(2,1)S(1)}, bf16[256,768]{1,0:T(8,128)(2,1)S(1)}, u32[]{:S(2)}, u32[]{:S(2)}) %collective-permute-start.54) | collective-permute-done | bytes 393248 | tf_op jit(solution)/shard_map/ppermute | solution.py:1110
  (338 shorter events, 185.5 us)
Async XLA Ops:
  10.6 32.2 %collective-permute-start.11 = (bf16[192,4608]{1,0:T(8,128)(2,1)S(1)}, bf16[192,4608]{1,0:T(8,128)(2,1)S(1)}, u32[]{:S(2)}, u32[]{:S(2)}) collective-permute-start(bf16[192,4608]{1,0:T(8,128)(2,1)S(1)} %get-tuple-element.232), channel_id=1, source_target_pairs={{0,16},{16,0},{1,17},{17,1},{2,18},{18,2},{3,19},{19,3},{4,20},{20... | collective-permute-start | bytes 5308424 | tf_op jit(solution)/shard_map/ppermute | solution.py:1093
  16.2 24.7 %collective-permute-start.2 = (bf16[256,768]{1,0:T(8,128)(2,1)S(1)}, bf16[256,768]{1,0:T(8,128)(2,1)S(1)}, u32[]{:S(2)}, u32[]{:S(2)}) collective-permute-start(bf16[256,768]{1,0:T(8,128)(2,1)S(1)} %dynamic-slice_bitcast_fusion.5), channel_id=1, source_target_pairs={{16,28},{20,24},{24,20},{28,16},{17,29},{21,25},{25,21},{29,17},{1... | collective-permute-start | bytes 1179656 | tf_op jit(solution)/shard_map/ppermute | solution.py:1114
  17.2 24.3 %collective-permute-start.1 = (bf16[256,768]{1,0:T(8,128)(2,1)S(1)}, bf16[256,768]{1,0:T(8,128)(2,1)S(1)}, u32[]{:S(2)}, u32[]{:S(2)}) collective-permute-start(bf16[256,768]{1,0:T(8,128)(2,1)S(1)} %select_bitcast_fusion.5), channel_id=1, source_target_pairs={{0,4},{4,0},{8,12},{12,8},{16,24},{20,28},{24,16},{28,20},{1,5},{5... | collective-permute-start | bytes 1179656 | tf_op jit(solution)/shard_map/ppermute | solution.py:1110
  44.2 40.7 %collective-permute-start.13 = (bf16[192,4608]{1,0:T(8,128)(2,1)}, bf16[192,4608]{1,0:T(8,128)(2,1)S(1)}, u32[]{:S(2)}, u32[]{:S(2)}) collective-permute-start(bf16[192,4608]{1,0:T(8,128)(2,1)} %broadcast_select_fusion.1.refs_8_.refs_13_.refs_14_), channel_id=1, source_target_pairs={{0,2},{1,3},{2,0},{3,1},{4,6},{5,7},{6,4},{7,5},{8,10},{9,11},{10,... | collective-permute-start | bytes 5308424 | tf_op jit(solution)/shard_map/ppermute | solution.py:1101
  45.7 40.6 %collective-permute-start.12 = (bf16[192,4608]{1,0:T(8,128)(2,1)}, bf16[192,4608]{1,0:T(8,128)(2,1)}, u32[]{:S(2)}, u32[]{:S(2)}) collective-permute-start(bf16[192,4608]{1,0:T(8,128)(2,1)} %broadcast_select_fusion.1.refs_8_.refs_13_.refs_14_), channel_id=1, source_target_pairs={{0,1},{1,0},{2,3},{3,2},{4,5},{5,4},{6,7},{7,6},{8,9},{9,8},{10,11... | collective-permute-start | bytes 5308424 | tf_op jit(solution)/shard_map/ppermute | solution.py:1097
  88.0 30.3 %collective-permute-start.17 = (bf16[384,4608]{1,0:T(8,128)(2,1)S(1)}, bf16[384,4608]{1,0:T(8,128)(2,1)S(1)}, u32[]{:S(2)}, u32[]{:S(2)}) collective-permute-start(bf16[384,4608]{1,0:T(8,128)(2,1)S(1)} %pad_maximum_fusion), channel_id=1, source_target_pairs={{0,16},{16,0},{1,17},{17,1},{2,18},{18,2},{3,19},{19,3},{4,20},{20... | collective-permute-start | bytes 10616840 | tf_op jit(solution)/shard_map/ppermute | solution.py:1093
  206.5 93.7 %collective-permute-start.26 = (bf16[512,3072]{1,0:T(8,128)(2,1)}, bf16[512,3072]{1,0:T(8,128)(2,1)}, u32[]{:S(2)}, u32[]{:S(2)}) collective-permute-start(bf16[512,3072]{1,0:T(8,128)(2,1)} %get-tuple-element.171.refs_0_), channel_id=1, source_target_pairs={{0,16},{16,0},{1,17},{17,1},{2,18},{18,2},{3,19},{19,3},{4,20},{20... | collective-permute-start | bytes 9437192 | tf_op jit(solution)/shard_map/ppermute | solution.py:1093
  251.4 30.7 %collective-permute-start.23 = (bf16[512,768]{1,0:T(8,128)(2,1)S(1)}, bf16[512,768]{1,0:T(8,128)(2,1)}, u32[]{:S(2)}, u32[]{:S(2)}) collective-permute-start(bf16[512,768]{1,0:T(8,128)(2,1)S(1)} %copy-done.15), channel_id=1, source_target_pairs={{0,16},{16,0},{1,17},{17,1},{2,18},{18,2},{3,19},{19,3},{4,20},{20... | collective-permute-start | bytes 2359304 | tf_op jit(solution)/shard_map/ppermute | solution.py:1093
  327.5 42.3 %collective-permute-start.31 = (bf16[528,768]{1,0:T(8,128)(2,1)}, bf16[528,768]{1,0:T(8,128)(2,1)}, u32[]{:S(2)}, u32[]{:S(2)}) collective-permute-start(bf16[528,768]{1,0:T(8,128)(2,1)} %get-tuple-element.173), channel_id=1, source_target_pairs={{0,16},{16,0},{1,17},{17,1},{2,18},{18,2},{3,19},{19,3},{4,20},{20... | collective-permute-start | bytes 2433032 | tf_op jit(solution)/shard_map/ppermute | solution.py:1093
  338.3 42.8 %collective-permute-start.34 = (bf16[192,1536]{1,0:T(8,128)(2,1)}, bf16[192,1536]{1,0:T(8,128)(2,1)S(1)}, u32[]{:S(2)}, u32[]{:S(2)}) collective-permute-start(bf16[192,1536]{1,0:T(8,128)(2,1)} %get-tuple-element.156), channel_id=1, source_target_pairs={{0,1},{1,0},{2,3},{3,2},{4,5},{5,4},{6,7},{7,6},{8,9},{9,8},{10,11... | collective-permute-start | bytes 1769480 | tf_op jit(solution)/shard_map/ppermute | solution.py:1097
  339.0 42.9 %collective-permute-start.32 = (bf16[192,1536]{1,0:T(8,128)(2,1)}, bf16[192,1536]{1,0:T(8,128)(2,1)}, u32[]{:S(2)}, u32[]{:S(2)}) collective-permute-start(bf16[192,1536]{1,0:T(8,128)(2,1)} %get-tuple-element.157), channel_id=1, source_target_pairs={{0,2},{1,3},{2,0},{3,1},{4,6},{5,7},{6,4},{7,5},{8,10},{9,11},{10,... | collective-permute-start | bytes 1769480 | tf_op jit(solution)/shard_map/ppermute | solution.py:1101
  394.2 29.3 %collective-permute-start.51 = (bf16[192,1536]{1,0:T(8,128)(2,1)S(1)}, bf16[192,1536]{1,0:T(8,128)(2,1)}, u32[]{:S(2)}, u32[]{:S(2)}) collective-permute-start(bf16[192,1536]{1,0:T(8,128)(2,1)S(1)} %fusion.2), channel_id=1, source_target_pairs={{0,12},{4,8},{8,4},{12,0},{1,13},{5,9},{9,5},{13,1},{2,14},{6,10},... | collective-permute-start | bytes 1769480 | tf_op jit(solution)/shard_map/ppermute | solution.py:1118
  398.1 36.6 %collective-permute-start.49 = (bf16[192,2048]{1,0:T(8,128)(2,1)}, bf16[192,2048]{1,0:T(8,128)(2,1)S(1)}, u32[]{:S(2)}, u32[]{:S(2)}) collective-permute-start(bf16[192,2048]{1,0:T(8,128)(2,1)} %get-tuple-element.202), channel_id=1, source_target_pairs={{0,2},{1,3},{2,0},{3,1},{4,6},{5,7},{6,4},{7,5},{8,10},{9,11},{10,... | collective-permute-start | bytes 2359304 | tf_op jit(solution)/shard_map/ppermute | solution.py:1101
  424.8 47.8 %collective-permute-start.62 = (bf16[192,1536]{1,0:T(8,128)(2,1)S(1)}, bf16[192,1536]{1,0:T(8,128)(2,1)S(1)}, u32[]{:S(2)}, u32[]{:S(2)}) collective-permute-start(bf16[192,1536]{1,0:T(8,128)(2,1)S(1)} %add_convert_fusion.2), channel_id=1, source_target_pairs={{0,4},{4,0},{8,12},{12,8},{1,5},{5,1},{9,13},{13,9},{2,6},{6,2},{1... | collective-permute-start | bytes 1769480 | tf_op jit(solution)/shard_map/ppermute | solution.py:1105
  437.9 24.4 %collective-permute-start.44 = (bf16[192,1152]{1,0:T(8,128)(2,1)S(1)}, bf16[192,1152]{1,0:T(8,128)(2,1)S(1)}, u32[]{:S(2)}, u32[]{:S(2)}) collective-permute-start(bf16[192,1152]{1,0:T(8,128)(2,1)S(1)} %copy-done.64), channel_id=1, source_target_pairs={{0,1},{1,0},{2,3},{3,2},{4,5},{5,4},{6,7},{7,6},{8,9},{9,8},{10,11... | collective-permute-start | bytes 1327112 | tf_op jit(solution)/shard_map/ppermute | solution.py:1097
  438.9 24.2 %collective-permute-start.42 = (bf16[192,1152]{1,0:T(8,128)(2,1)S(1)}, bf16[192,1152]{1,0:T(8,128)(2,1)S(1)}, u32[]{:S(2)}, u32[]{:S(2)}) collective-permute-start(bf16[192,1152]{1,0:T(8,128)(2,1)S(1)} %copy-done.63), channel_id=1, source_target_pairs={{0,2},{1,3},{2,0},{3,1},{4,6},{5,7},{6,4},{7,5},{8,10},{9,11},{10,... | collective-permute-start | bytes 1327112 | tf_op jit(solution)/shard_map/ppermute | solution.py:1101
  447.0 25.4 %collective-permute-start.64 = (bf16[192,1536]{1,0:T(8,128)(2,1)S(1)}, bf16[192,1536]{1,0:T(8,128)(2,1)S(1)}, u32[]{:S(2)}, u32[]{:S(2)}) collective-permute-start(bf16[192,1536]{1,0:T(8,128)(2,1)S(1)} %add_convert_fusion.1), channel_id=1, source_target_pairs={{0,4},{4,0},{8,12},{12,8},{1,5},{5,1},{9,13},{13,9},{2,6},{6,2},{1... | collective-permute-start | bytes 1769480 | tf_op jit(solution)/shard_map/ppermute | solution.py:1105
  459.4 32.4 %collective-permute-start.52 = (bf16[192,2048]{1,0:T(8,128)(2,1)S(1)}, bf16[192,2048]{1,0:T(8,128)(2,1)S(1)}, u32[]{:S(2)}, u32[]{:S(2)}) collective-permute-start(bf16[192,2048]{1,0:T(8,128)(2,1)S(1)} %fusion), channel_id=1, source_target_pairs={{0,12},{4,8},{8,4},{12,0},{1,13},{5,9},{9,5},{13,1},{2,14},{6,10},... | collective-permute-start | bytes 2359304 | tf_op jit(solution)/shard_map/ppermute | solution.py:1118
  472.5 42.2 %collective-permute-start.65 = (bf16[192,1536]{1,0:T(8,128)(2,1)S(1)}, bf16[192,1536]{1,0:T(8,128)(2,1)S(1)}, u32[]{:S(2)}, u32[]{:S(2)}) collective-permute-start(bf16[192,1536]{1,0:T(8,128)(2,1)S(1)} %get-tuple-element.227), channel_id=1, source_target_pairs={{0,16},{16,0},{1,17},{17,1},{2,18},{18,2},{3,19},{19,3},{4,20},{20... | collective-permute-start | bytes 1769480 | tf_op jit(solution)/shard_map/ppermute | solution.py:1093
  473.9 34.5 %collective-permute-start.57 = (bf16[192,1152]{1,0:T(8,128)(2,1)S(1)}, bf16[192,1152]{1,0:T(8,128)(2,1)S(1)}, u32[]{:S(2)}, u32[]{:S(2)}) collective-permute-start(bf16[192,1152]{1,0:T(8,128)(2,1)S(1)} %fusion.7), channel_id=1, source_target_pairs={{0,12},{4,8},{8,4},{12,0},{1,13},{5,9},{9,5},{13,1},{2,14},{6,10},... | collective-permute-start | bytes 1327112 | tf_op jit(solution)/shard_map/ppermute | solution.py:1118
  492.1 49.2 %collective-permute-start.60 = (bf16[192,2048]{1,0:T(8,128)(2,1)S(1)}, bf16[192,2048]{1,0:T(8,128)(2,1)S(1)}, u32[]{:S(2)}, u32[]{:S(2)}) collective-permute-start(bf16[192,2048]{1,0:T(8,128)(2,1)S(1)} %add_convert_fusion), channel_id=1, source_target_pairs={{0,4},{4,0},{8,12},{12,8},{1,5},{5,1},{9,13},{13,9},{2,6},{6,2},{1... | collective-permute-start | bytes 2359304 | tf_op jit(solution)/shard_map/ppermute | solution.py:1105
  508.5 32.2 %collective-permute-start.58 = (bf16[192,1152]{1,0:T(8,128)(2,1)S(1)}, bf16[192,1152]{1,0:T(8,128)(2,1)S(1)}, u32[]{:S(2)}, u32[]{:S(2)}) collective-permute-start(bf16[192,1152]{1,0:T(8,128)(2,1)S(1)} %add_convert_fusion.3), channel_id=1, source_target_pairs={{0,4},{4,0},{8,12},{12,8},{1,5},{5,1},{9,13},{13,9},{2,6},{6,2},{1... | collective-permute-start | bytes 1327112 | tf_op jit(solution)/shard_map/ppermute | solution.py:1105
  513.9 26.6 %collective-permute-start.54 = (bf16[256,768]{1,0:T(8,128)(2,1)S(1)}, bf16[256,768]{1,0:T(8,128)(2,1)S(1)}, u32[]{:S(2)}, u32[]{:S(2)}) collective-permute-start(bf16[256,768]{1,0:T(8,128)(2,1)S(1)} %get-tuple-element.215), channel_id=1, source_target_pairs={{0,4},{4,0},{8,12},{12,8},{16,24},{20,28},{24,16},{28,20},{1,5},{5... | collective-permute-start | bytes 1179656 | tf_op jit(solution)/shard_map/ppermute | solution.py:1110
  514.0 26.5 %collective-permute-start.55 = (bf16[256,768]{1,0:T(8,128)(2,1)S(1)}, bf16[256,768]{1,0:T(8,128)(2,1)S(1)}, u32[]{:S(2)}, u32[]{:S(2)}) collective-permute-start(bf16[256,768]{1,0:T(8,128)(2,1)S(1)} %get-tuple-element.216), channel_id=1, source_target_pairs={{16,28},{20,24},{24,20},{28,16},{17,29},{21,25},{25,21},{29,17},{1... | collective-permute-start | bytes 1179656 | tf_op jit(solution)/shard_map/ppermute | solution.py:1114
  (107 other events, 1004.8 us)
